TPU v7x, 32 devices: a whole 2x2x4 slice. The times are simulated.
32 devices in a mesh: src: 16 (over z, y, x), tgt: 2 (over core).
Axes of the slice: x: 2, y: 2, z: 4, core: 2. Of those that a mesh axis runs over, the one named last changes fastest.
Arguments:
- sources: bfloat16 [6144, 1024], P('src'), may hold values from -72 to 72
- targets: bfloat16 [64, 1024, 1024], P(('src', 'tgt')), may hold values from -72 to 72
- picks: int32 [6144, 4], P('src'), may hold values from 0 to 63, all different within a row; in each aligned block of 384 rows (0 to 383, 384 to 767, ...) at most 48 rows name the same one
- cluster_home: int32 [64], replicated, may hold values from 0 to 63, each once
- row_count: int32 [64], replicated, may hold values from 512 to 1024, as said below
Outputs:
- pooled: bfloat16 [6144, 1024], P('src')
- confidence: bfloat16 [6144], P('src')
Inputs may be any that keep to these rules, and one draw needn't show every extreme that they name: `picks`: the 4 clusters of a source are different; among the 384 sources of one index of src no cluster is picked by more than 48 sources; every cluster is picked by some source. Cluster c's block is targets[cluster_home[c]]; each position is used once. Rows of a block at or past row_count of its cluster are not part of it; some cluster uses all 1024 rows.
All inputs are finite; a program needn't handle non-finite values.
Results may differ from a plain program's by a relative error of at most 0.0046.
Values may be sent and summed in bfloat16 or wider, within the bound.
No kernel may reach another device: no remote copies, remote signals or barrier semaphores. Data moves between devices by JAX's collectives and lax.ppermute only.
A program may use at most 64 MiB of HBM per device.

v0:
```python
import math

import jax
import jax.numpy as jnp
from jax import lax
from jax.sharding import PartitionSpec as P

NEGATIVE = -1e30
SHARPNESS = 2.5


def joined(value, axis, join):
    pieces = jax.tree.map(lambda part: lax.all_gather(part, axis), value)
    head = jax.tree.map(lambda part: part[0], pieces)
    tail = jax.tree.map(lambda part: part[1:], pieces)
    running, _ = lax.scan(lambda running, share: (join(running, share), None), head, tail)
    return running


def masked_lse(values, allowed, along):
    highest = jnp.max(jnp.where(allowed, values, NEGATIVE), axis=along, keepdims=True)
    summed = jnp.sum(jnp.where(allowed, jnp.exp(values - highest), 0.0), axis=along, keepdims=True)
    return jnp.squeeze(highest + jnp.log(jnp.where(summed > 0.0, summed, 1.0)), axis=along)


def plain_lse(values, along):
    highest = jnp.max(values, axis=along, keepdims=True)
    summed = jnp.sum(jnp.exp(values - highest), axis=along, keepdims=True)
    return jnp.squeeze(highest + jnp.log(summed), axis=along)


def pair_lse(first, second):
    highest = jnp.maximum(first, second)
    return highest + jnp.log(jnp.exp(first - highest) + jnp.exp(second - highest))


def combine_parts(first, second):
    forward = pair_lse(first[0], second[0])
    margin = pair_lse(first[1], second[1])
    pooled = (
        first[2] * jnp.exp(first[1] - margin)[:, None]
        + second[2] * jnp.exp(second[1] - margin)[:, None]
    )
    return (forward, margin, pooled)


def place_requests(picks, cluster_home, group, n_src, n_tgt, per_device, capacity):
    n_rows, n_picks = picks.shape
    cluster_ids = jnp.arange(cluster_home.shape[0], dtype=jnp.int32)
    stored_at = jnp.sum(
        jnp.where(picks[:, :, None] == cluster_ids[None, None, :], cluster_home[None, None, :], 0),
        axis=2,
    )
    holder = stored_at // per_device
    inside = holder % n_tgt == group
    bucket = holder // n_tgt * per_device + stored_at % per_device
    n_buckets = n_src * per_device
    flat_bucket = bucket.reshape(-1)
    flat_inside = inside.reshape(-1)
    one_hot = (
        (flat_bucket[:, None] == jnp.arange(n_buckets, dtype=jnp.int32)[None, :])
        & flat_inside[:, None]
    ).astype(jnp.int32)
    before = jnp.cumsum(one_hot, axis=0) - one_hot
    ordinal = jnp.sum(before * one_hot, axis=1).reshape(n_rows, n_picks)
    return (inside, bucket * capacity + ordinal)


def shards(sources, targets, picks, cluster_home, row_count):
    n_src = lax.axis_size("src")
    n_tgt = lax.axis_size("tgt")
    src_rows, width = sources.shape
    per_device, rows_cluster, _ = targets.shape
    n_clusters = cluster_home.shape[0]
    n_picks = picks.shape[1]
    capacity = 2 * n_picks * src_rows // n_clusters
    group = lax.axis_index("tgt")
    inside, position = place_requests(
        picks, cluster_home, group, n_src, n_tgt, per_device, capacity
    )
    n_slots = n_src * per_device * capacity
    row_ids = jnp.broadcast_to(jnp.arange(src_rows, dtype=jnp.int32)[:, None], (src_rows, n_picks))
    slot_rows = jnp.full((n_slots,), src_rows, jnp.int32)
    slot_rows = slot_rows.at[jnp.where(inside, position, n_slots).reshape(-1)].set(
        row_ids.reshape(-1), mode="drop"
    )
    occupied = slot_rows < src_rows
    fetched = jnp.take(sources, jnp.minimum(slot_rows, src_rows - 1), axis=0)
    queries = jnp.where(occupied[:, None], fetched, jnp.zeros((), jnp.bfloat16)).reshape(
        n_src, per_device, capacity, width
    )
    flags = occupied.astype(jnp.bfloat16).reshape(n_src, per_device, capacity)
    arrived, arrived_flags = (
        lax.all_to_all(queries, "src", split_axis=0, concat_axis=0, tiled=True),
        lax.all_to_all(flags, "src", split_axis=0, concat_axis=0, tiled=True),
    )
    here = lax.axis_index("src") * n_tgt + group
    own_slots = here * per_device + jnp.arange(per_device, dtype=jnp.int32)
    own_counts = jnp.sum(
        jnp.where(cluster_home[None, :] == own_slots[:, None], row_count[None, :], 0), axis=1
    )
    row_valid = jnp.arange(rows_cluster, dtype=jnp.int32)[None, :] < own_counts[:, None]
    row_bias = jnp.where(row_valid, 0.0, NEGATIVE).astype(jnp.float32)
    slot_bias = jnp.where(arrived_flags > 0, 0.0, NEGATIVE).astype(jnp.float32)
    scores = jnp.einsum("jlcd,lrd->jlcr", arrived, targets, preferred_element_type=jnp.float32) * (
        SHARPNESS / math.sqrt(width)
    )
    biased = scores + row_bias[None, :, None, :] + slot_bias[..., None]
    reverse = plain_lse(biased, (0, 2))
    forward_part = plain_lse(biased, 3)
    shifted = biased - 0.5 * reverse[None, :, None, :]
    margin_part = plain_lse(shifted, 3)
    weights = jnp.exp(shifted - margin_part[..., None]).astype(jnp.bfloat16)
    pool_part = jnp.einsum("jlcr,lrd->jlcd", weights, targets, preferred_element_type=jnp.float32)
    back_pool, back_forward, back_margin = (
        lax.all_to_all(pool_part, "src", split_axis=0, concat_axis=0, tiled=True),
        lax.all_to_all(forward_part, "src", split_axis=0, concat_axis=0, tiled=True),
        lax.all_to_all(margin_part, "src", split_axis=0, concat_axis=0, tiled=True),
    )
    flat_pool = back_pool.reshape(n_slots, width)
    safe_position = jnp.where(inside, position, 0)
    forward_picks = jnp.take(back_forward.reshape(-1), safe_position)
    margin_picks = jnp.take(back_margin.reshape(-1), safe_position)
    forward_group = masked_lse(forward_picks, inside, 1)
    margin_group = masked_lse(margin_picks, inside, 1)
    factors = jnp.where(inside, jnp.exp(margin_picks - margin_group[:, None]), 0.0)
    pooled_group = jnp.zeros((src_rows, width), jnp.float32)
    for pick_no in range(n_picks):
        pooled_group = pooled_group + factors[:, pick_no, None] * jnp.take(
            flat_pool, safe_position[:, pick_no], axis=0
        )
    forward, margin_total, pooled = joined(
        (forward_group, margin_group, pooled_group), "tgt", combine_parts
    )
    return (pooled.astype(jnp.bfloat16), (margin_total - 0.5 * forward).astype(jnp.bfloat16))


def solution(mesh):
    placed = (P("src", None), P(("src", "tgt"), None, None), P("src", None), P(), P())
    return jax.shard_map(
        shards, mesh=mesh, in_specs=placed, out_specs=(P("src", None), P("src")), check_vma=False
    )
```

profile of v0, /device:TPU:0, one launch (start us, length us, event | category | flops | bytes accessed | tf_op | source)
XLA Modules:
  0.0 351.0 jit_solution(801832820251880937)
XLA Ops:
  7.2 0.9 select_reduce_fusion
  8.1 0.1 copy.35
  8.2 0.1 reduce_sum.87
  8.4 0.1 reduce_sum.86
  8.6 0.2 reduce_sum.85
  8.8 9.1 %reduce-window.6 = s32[32,12,128]{2,1,0:T(8,128)S(1)} reduce-window(s32[32,12,128]{2,1,0:T(8,128)S(1)} %fusion.20, s32[]{:T(128)} %constant.107.clone.1), window={size=1x1x128 pad=0_0x0_0x127_0}, to_apply=%region_1.2 | reduce-window | flops 6242304 | bytes 393220 | tf_op jit(solution)/shard_map/reduce-window
  17.9 0.1 slice.84
  18.0 0.2 copy.37
  18.3 0.1 copy.38
  18.4 0.1 broadcast_add_fusion
  18.5 0.1 reshape.521
  18.7 0.1 fusion.23
  18.8 0.1 fusion.36
  18.9 6.2 %scatter_custom_fusion = s32[1536]{0:T(1024)S(1)} fusion(s32[1536]{0:T(1024)S(1)} %fusion.36, s32[1536]{0:T(1024)S(1)} %reshape.521, s32[]{:T(128)} %constant.112.clone.1), kind=kCustom, calls=%fused_computation.146 | custom fusion | bytes 6148 | tf_op jit(solution)/shard_map/scatter | solution.py:84
  25.1 0.1 broadcast_in_dim.142
  25.2 0.6 reshape.456
  25.8 8.3 %all-to-all-start.1 = ((bf16[16,2,48]{2,1,0:T(2,128)(2,1)}), bf16[16,2,48]{2,1,0:T(2,128)(2,1)S(1)}, u32[]{:S(2)}, u32[]{:S(2)}) async-start(bf16[16,2,48]{2,1,0:T(2,128)(2,1)} %reshape.456), calls=%async_computation.1 | async-start | bytes 16384 | tf_op jit(solution)/shard_map/all_to_all | solution.py:95
  34.1 0.1 broadcast_in_dim.144
  34.2 5.8 %gather_fusion = bf16[1536,1024]{1,0:T(8,128)(2,1)} fusion(bf16[384,1024]{1,0:T(8,128)(2,1)S(1)} %copy-done, s32[2048]{0:T(1024)S(1)} %pad_clamp_fusion.1), kind=kCustom, calls=%fused_computation.6 | custom fusion | bytes 6297600 | tf_op jit(solution)/shard_map/jit(_take)/gather | solution.py:88
  40.1 3.4 select_select_fusion
  43.5 7.1 %all-to-all-start = ((bf16[16,2,48,1024]{3,2,1,0:T(8,128)(2,1)}), bf16[16,2,48,1024]{3,2,1,0:T(8,128)(2,1)}, u32[]{:S(2)}, u32[]{:S(2)}) async-start(bf16[16,2,48,1024]{3,2,1,0:T(8,128)(2,1)} %select_select_fusion), calls=%async_computation | async-start | bytes 6291456 | tf_op jit(solution)/shard_map/all_to_all | solution.py:94
  50.6 0.2 fusion.61
  50.8 0.1 compare_select_fusion.5
  50.9 60.5 %all-to-all-done = bf16[16,2,48,1024]{3,2,1,0:T(8,128)(2,1)} async-done(((bf16[16,2,48,1024]{3,2,1,0:T(8,128)(2,1)}), bf16[16,2,48,1024]{3,2,1,0:T(8,128)(2,1)}, u32[]{:S(2)}, u32[]{:S(2)}) %all-to-all-start) | async-done | bytes 3145760 | tf_op jit(solution)/shard_map/all_to_all | solution.py:94
  111.4 6.7 %fusion.65 = (f32[2,1024]{1,0:T(2,128)S(1)}, f32[16,2,48,1024]{3,2,0,1:T(8,128)S(1)}) fusion(f32[16,2,48]{2,0,1:T(8,128)S(1)} %copy.42, f32[2,1024]{1,0:T(2,128)S(1)} %compare_select_fusion.5, bf16[2,1024,1024]{2,1,0:T(8,128)(2,1)} %param.10, bf16[16,2,48,1024]{3,2,1,0:T(8,128)(2,1)} %all-to-all-done), kind=kOutput, calls=%fused_computation.188 | convolution fusion | flops 3227514880 | bytes 13654016 | tf_op jit(solution)/shard_map/jlcd,lrd->jlcr/dot_general | solution.py:105
  118.1 0.9 exponential_reduce_fusion.2
  119.0 1.1 fusion.62
  120.0 0.7 copy-done.1
  120.7 2.4 exponential_reduce_fusion
  123.1 0.6 copy.47
  123.8 14.1 %all-to-all-start.4 = ((f32[16,2,48]{2,1,0:T(2,128)}), f32[16,2,48]{2,1,0:T(2,128)S(1)}, u32[]{:S(2)}, u32[]{:S(2)}) async-start(f32[16,2,48]{2,1,0:T(2,128)} %copy.47), calls=%async_computation.4 | async-start | bytes 32768 | tf_op jit(solution)/shard_map/all_to_all | solution.py:117
  137.9 0.6 copy.43
  138.5 6.7 %all-to-all-done.4 = f32[16,2,48]{2,1,0:T(2,128)S(1)} async-done(((f32[16,2,48]{2,1,0:T(2,128)}), f32[16,2,48]{2,1,0:T(2,128)S(1)}, u32[]{:S(2)}, u32[]{:S(2)}) %all-to-all-start.4) | async-done | bytes 6176 | tf_op jit(solution)/shard_map/all_to_all | solution.py:117
  145.2 3.7 %all-to-all-start.2 = ((f32[16,2,48]{2,1,0:T(2,128)}), f32[16,2,48]{2,1,0:T(2,128)S(1)}, u32[]{:S(2)}, u32[]{:S(2)}) async-start(f32[16,2,48]{2,1,0:T(2,128)} %copy.43), calls=%async_computation.2 | async-start | bytes 32768 | tf_op jit(solution)/shard_map/all_to_all | solution.py:118
  148.9 6.9 %fusion.7 = f32[16,2,48,1024]{3,2,0,1:T(8,128)S(1)} fusion(bf16[2,1024,1024]{2,1,0:T(8,128)(2,1)} %param.10, f32[16,2,48,1024]{3,2,0,1:T(8,128)} %copy-done.1, f32[16,2,48]{2,0,1:T(8,128)S(1)} %log_add_fusion.1, f32[2,1024]{1,0:T(2,128)S(1)} %add_multiply_fusion), kind=kOutput, calls=%fused_computation.22 | convolution fusion | flops 3225944064 | bytes 16791552 | tf_op jit(solution)/shard_map/jlcr,lrd->jlcd/dot_general | solution.py:114
  155.8 3.2 copy.46
  159.0 6.7 %all-to-all-start.3 = ((f32[16,2,48,1024]{3,2,1,0:T(8,128)}), f32[16,2,48,1024]{3,2,1,0:T(8,128)}, u32[]{:S(2)}, u32[]{:S(2)}) async-start(f32[16,2,48,1024]{3,2,1,0:T(8,128)} %copy.46), calls=%async_computation.3 | async-start | bytes 12582912 | tf_op jit(solution)/shard_map/all_to_all | solution.py:116
  165.8 0.0 all-gather.5.cloned.1.call-start
  165.8 0.2 reshape.458
  166.0 0.1 copy.39
  166.1 0.1 compare_select_fusion.4
  166.2 0.1 copy.44
  166.3 0.1 reshape.551
  166.6 0.1 reshape.460
  166.7 8.4 %gather_fusion.6 = f32[1536]{0:T(1024)S(1)} fusion(f32[1536]{0:T(1024)S(1)} %reshape.460, s32[2048]{0:T(1024)S(1)} %pad_clamp_fusion), kind=kCustom, calls=%fused_computation.2.clone | custom fusion | bytes 18432 | tf_op jit(solution)/shard_map/jit(_take)/gather | solution.py:122
  175.1 0.2 reshape.566
  175.3 0.1 copy.49
  175.4 0.1 reshape.457
  175.5 8.4 %gather_fusion.1 = f32[1536]{0:T(1024)S(1)} fusion(f32[1536]{0:T(1024)S(1)} %reshape.457, s32[2048]{0:T(1024)S(1)} %pad_clamp_fusion), kind=kCustom, calls=%fused_computation.clone | custom fusion | bytes 18432 | tf_op jit(solution)/shard_map/jit(_take)/gather | solution.py:123
  183.9 0.2 reshape.554
  184.1 0.1 copy.45
  184.2 0.1 select_reduce_fusion.2
  184.4 95.3 %all-to-all-done.3 = f32[16,2,48,1024]{3,2,1,0:T(8,128)} async-done(((f32[16,2,48,1024]{3,2,1,0:T(8,128)}), f32[16,2,48,1024]{3,2,1,0:T(8,128)}, u32[]{:S(2)}, u32[]{:S(2)}) %all-to-all-start.3) | async-done | bytes 6291488 | tf_op jit(solution)/shard_map/all_to_all | solution.py:116
  279.6 5.6 %gather_fusion.2 = f32[384,1024]{1,0:T(8,128)S(1)} fusion(f32[1536,1024]{1,0:T(8,128)} %bitcast.8, s32[1024]{0:T(1024)S(1)} %pad_clamp_fusion.5), kind=kCustom, calls=%fused_computation.1.clone | custom fusion | bytes 3147264 | tf_op jit(solution)/shard_map/jit(_take)/gather | solution.py:129
  285.2 6.3 %gather_fusion.3 = f32[384,1024]{1,0:T(8,128)} fusion(f32[1536,1024]{1,0:T(8,128)} %bitcast.8, s32[1024]{0:T(1024)S(1)} %pad_clamp_fusion.4), kind=kCustom, calls=%fused_computation.3.clone | custom fusion | bytes 3147264 | tf_op jit(solution)/shard_map/jit(_take)/gather | solution.py:129
  291.5 6.2 %gather_fusion.4 = f32[384,1024]{1,0:T(8,128)} fusion(f32[1536,1024]{1,0:T(8,128)} %bitcast.8, s32[1024]{0:T(1024)S(1)} %pad_clamp_fusion.3), kind=kCustom, calls=%fused_computation.4.clone | custom fusion | bytes 3147264 | tf_op jit(solution)/shard_map/jit(_take)/gather | solution.py:129
  297.7 6.2 %gather_fusion.5 = f32[384,1024]{1,0:T(8,128)} fusion(f32[1536,1024]{1,0:T(8,128)} %bitcast.8, s32[1024]{0:T(1024)S(1)} %pad_clamp_fusion.2), kind=kCustom, calls=%fused_computation.5.clone | custom fusion | bytes 3147264 | tf_op jit(solution)/shard_map/jit(_take)/gather | solution.py:129
  303.9 3.7 %fusion.16 = f32[384,1024]{1,0:T(8,128)} fusion(f32[384,1024]{1,0:T(8,128)} %gather_fusion.5, f32[384,1024]{1,0:T(8,128)} %gather_fusion.4, f32[384,1024]{1,0:T(8,128)} %gather_fusion.3, f32[384,1024]{1,0:T(8,128)S(1)} %gather_fusion.2, f32[384]{0:T(512)S(1)} %get-tuple-element.30, f32[384]{0:T(512)S(1)} %get-tuple-element.31, f32[384]{0:T(512)S(1)} %get-tuple-element.32, ...), kind=kLoop, calls=%fused_computation.28 | loop fusion | flops 4325376 | bytes 7872000 | tf_op jit(solution)/shard_map/add | solution.py:129
  307.6 0.0 all-gather.5.cloned.1.call-update
  307.6 1.8 all-gather.1
  309.4 1.8 all-gather.2
  311.2 0.6 subtract_convert_fusion
  311.8 29.3 %all-gather.5.cloned.1.call-done = f32[768,1024]{1,0:T(8,128)} async-done(((f32[384,1024]{1,0:T(8,128)}), f32[768,1024]{1,0:T(8,128)}) %all-gather.5.cloned.1.call-update) | async-done | bytes 3145744 | tf_op jit(solution)/shard_map/all_gather | solution.py:13
  341.2 3.0 fusion.15
  (43 shorter events, 0.5 us)
Async XLA Ops:
  7.2 27.1 %copy-start = (bf16[384,1024]{1,0:T(8,128)(2,1)S(1)}, bf16[384,1024]{1,0:T(8,128)(2,1)}, u32[]{:S(2)}) copy-start(bf16[384,1024]{1,0:T(8,128)(2,1)} %param.9) | copy-start | bytes 2359300
  25.8 17.7 %all-to-all-start.1 = ((bf16[16,2,48]{2,1,0:T(2,128)(2,1)}), bf16[16,2,48]{2,1,0:T(2,128)(2,1)S(1)}, u32[]{:S(2)}, u32[]{:S(2)}) async-start(bf16[16,2,48]{2,1,0:T(2,128)(2,1)} %reshape.456), calls=%async_computation.1 | async-start | bytes 16384 | tf_op jit(solution)/shard_map/all_to_all | solution.py:95
  43.5 7.1 %copy-start.2 = (s32[64]{0:T(128)S(1)}, s32[64]{0:T(128)}, u32[]{:S(2)}) copy-start(s32[64]{0:T(128)} %param.12) | copy-start | bytes 772
  43.5 7.1 %copy-start.3 = (s32[64]{0:T(128)S(1)}, s32[64]{0:T(128)}, u32[]{:S(2)}) copy-start(s32[64]{0:T(128)} %param.13) | copy-start | bytes 772
  43.5 67.9 %all-to-all-start = ((bf16[16,2,48,1024]{3,2,1,0:T(8,128)(2,1)}), bf16[16,2,48,1024]{3,2,1,0:T(8,128)(2,1)}, u32[]{:S(2)}, u32[]{:S(2)}) async-start(bf16[16,2,48,1024]{3,2,1,0:T(8,128)(2,1)} %select_select_fusion), calls=%async_computation | async-start | bytes 6291456 | tf_op jit(solution)/shard_map/all_to_all | solution.py:94
  118.1 2.7 copy-start.1
  123.8 21.5 %all-to-all-start.4 = ((f32[16,2,48]{2,1,0:T(2,128)}), f32[16,2,48]{2,1,0:T(2,128)S(1)}, u32[]{:S(2)}, u32[]{:S(2)}) async-start(f32[16,2,48]{2,1,0:T(2,128)} %copy.47), calls=%async_computation.4 | async-start | bytes 32768 | tf_op jit(solution)/shard_map/all_to_all | solution.py:117
  145.2 13.8 %all-to-all-start.2 = ((f32[16,2,48]{2,1,0:T(2,128)}), f32[16,2,48]{2,1,0:T(2,128)S(1)}, u32[]{:S(2)}, u32[]{:S(2)}) async-start(f32[16,2,48]{2,1,0:T(2,128)} %copy.43), calls=%async_computation.2 | async-start | bytes 32768 | tf_op jit(solution)/shard_map/all_to_all | solution.py:118
  159.0 120.6 %all-to-all-start.3 = ((f32[16,2,48,1024]{3,2,1,0:T(8,128)}), f32[16,2,48,1024]{3,2,1,0:T(8,128)}, u32[]{:S(2)}, u32[]{:S(2)}) async-start(f32[16,2,48,1024]{3,2,1,0:T(8,128)} %copy.46), calls=%async_computation.3 | async-start | bytes 12582912 | tf_op jit(solution)/shard_map/all_to_all | solution.py:116
  165.8 175.4 %all-gather.5.cloned.1.call-start = ((), (), s32[]{:S(2)}) async-start(), calls=%async_computation.5 | async-start | bytes 4718592 | tf_op jit(solution)/shard_map/all_gather | solution.py:13
Sparse Core Ops, SparseCore 0:
  307.7 33.3 all-gather.4
where the time goes:
time: 352 us; the launch traced here: 351 us
  waiting for transfers between devices  192 us (55%)
  local copies, waits for them, and re-layouts  61 us (17%)
  starting transfers between devices  40 us (11%)
  other arithmetic  26.6 us (8%)
  between operations  14.5 us (4%)
  matrix products  13.6 us (4%)
  blocking collectives  3.56 us (1%)
    all_to_all x1, waiting for transfers between devices, shards(): lax.all_to_all(pool_part, 'src', split_axis=0, concat_axis=0, tiled=True)  95.3 us
    all_to_all x1, waiting for transfers between devices, shards(): lax.all_to_all(queries, 'src', split_axis=0, concat_axis=0, tiled=True)  60.5 us
    all_gather x1, waiting for transfers between devices, joined(): pieces = jax.tree.map(lambda part: lax.all_gather(part, axis), value)  29.3 us
    gather x4, local copies, waits for them, and re-layouts, shards(): jnp.take(flat_pool, safe_position[:, pick_no], axis=0)  24.3 us
    all_to_all x1, starting transfers between devices, shards(): lax.all_to_all(forward_part, 'src', split_axis=0, concat_axis=0, tiled=True)  14.1 us
    another operation x3, other arithmetic  9.24 us
    gather x3, local copies, waits for them, and re-layouts, shards(): margin_picks = jnp.take(back_margin.reshape(-1), safe_position)  8.67 us
    gather x3, local copies, waits for them, and re-layouts, shards(): forward_picks = jnp.take(back_forward.reshape(-1), safe_position)  8.67 us
  transfers between devices with their start and end apart: 6, of which 4 were waited for; matrix products, arithmetic and copies ran while one was open for 11% of the time, Pallas kernels for 0%

commit v1 on v0

v1 whole, which is shorter than its diff:
```python
import functools
import math

import jax
import jax.numpy as jnp
from jax import lax
from jax.experimental import pallas as pl
from jax.experimental.pallas import tpu as pltpu
from jax.sharding import PartitionSpec as P

NEGATIVE = -1e30
SHARPNESS = 2.5
EXTRA = 16
F32, BF16 = jnp.float32, jnp.bfloat16
MIB = 1 << 20


def iota(shape, axis):
    return lax.broadcasted_iota(jnp.int32, shape, axis)


def call(kernel, out_shape, scratch=(), smem=0, n_in=0, limit=32, flops=0, moved=0, exps=0, **kw):
    if not kw:
        kw = dict(
            in_specs=[pl.BlockSpec(memory_space=pltpu.SMEM)] * smem
            + [pl.BlockSpec(memory_space=pltpu.VMEM)] * (n_in - smem),
            out_specs=jax.tree.map(lambda _: pl.BlockSpec(memory_space=pltpu.VMEM), out_shape),
        )
    return pl.pallas_call(
        kernel,
        out_shape=out_shape,
        scratch_shapes=list(scratch),
        compiler_params=pltpu.CompilerParams(vmem_limit_bytes=limit * MIB),
        cost_estimate=pl.CostEstimate(flops=flops, bytes_accessed=moved, transcendentals=exps),
        **kw,
    )


def columns(rows, width):
    stacked = jnp.concatenate(rows + [jnp.zeros((128 - len(rows), width), F32)], axis=0)
    return stacked.T


def three(row):
    high = row.astype(BF16).astype(F32)
    middle = (row - high).astype(BF16).astype(F32)
    return [high, middle, row - high - middle]


def extra_rows(first, second, width):
    parts = three(first) + three(second)
    body = jnp.concatenate(parts + [jnp.zeros((EXTRA - len(parts), first.shape[1]), F32)], axis=0)
    rest = jnp.zeros((EXTRA, width - first.shape[1]), F32)
    return jnp.concatenate([body, rest], axis=1).astype(BF16)


def read_extra(ref, start, length):
    block = ref[start : start + EXTRA, :length].astype(F32)
    first = (block[0:1] + block[1:2]) + block[2:3]
    second = (block[3:4] + block[4:5]) + block[5:6]
    return first, second


def one_hot_slots(code, start, group, capacity):
    rows = code.shape[1]
    order = iota((capacity, rows), 0).astype(F32)
    return jnp.concatenate(
        [jnp.where(order == code[b : b + 1, :], 1.0, 0.0) for b in range(start, start + group)], axis=0
    )


def gather_body(info, picks_ref, home_ref, source, q_ref, code_ref, *, n_tgt, per_device, capacity, group):
    n_buckets, rows = code_ref.shape
    n_clusters = home_ref.shape[1]
    width = q_ref.shape[2]
    cluster = iota((n_clusters, rows), 0)
    member = jnp.zeros((n_clusters, rows), F32)
    for k in range(picks_ref.shape[0]):
        member = jnp.where(cluster == picks_ref[k : k + 1, :], 1.0, member)
    bucket = iota((n_buckets, n_clusters), 0)
    holder = (info[0] + lax.div(bucket, per_device)) * n_tgt + info[1]
    place = holder * per_device + lax.rem(bucket, per_device)
    chosen = jnp.where(home_ref[...] == place, 1.0, 0.0).astype(BF16)
    inside = jnp.dot(chosen, member.astype(BF16), preferred_element_type=F32)
    earlier = jnp.where(iota((rows, rows), 0) < iota((rows, rows), 1), 1.0, 0.0).astype(BF16)
    rank = jnp.dot(inside.astype(BF16), earlier, preferred_element_type=F32)
    code = jnp.where(inside > 0.5, rank, -1.0)
    code_ref[...] = code
    per_message = group // per_device
    for start in range(0, n_buckets, group):
        slots = one_hot_slots(code, start, group, capacity)
        filled = jnp.sum(slots, axis=1, keepdims=True)
        found = jnp.dot(slots.astype(BF16), source, preferred_element_type=F32)
        head = found[:, :128]
        head = jnp.where((iota(head.shape, 1) == 0) & (filled < 0.5), jnp.inf, head)
        found = jnp.concatenate([head, found[:, 128:]], axis=1).astype(BF16)
        d = start // per_device
        q_ref[d : d + per_message] = found.reshape(per_message, per_device * capacity, width)


def gather_own(info, picks_ref, home_ref, src_ref, q_ref, code_ref, **sizes):
    gather_body(info, picks_ref, home_ref, src_ref[...], q_ref, code_ref, **sizes)


def gather_partner(info, picks_ref, home_ref, mine_ref, other_ref, q_ref, code_ref, src_ref, **sizes):
    half = mine_ref.shape[0]
    src_ref[pl.ds(pl.multiple_of(info[1] * half, 16), half), :] = mine_ref[...]
    src_ref[pl.ds(pl.multiple_of((1 - info[1]) * half, 16), half), :] = other_ref[...]
    gather_body(info, picks_ref, home_ref, src_ref[...], q_ref, code_ref, **sizes)


def owner_kernel(count_ref, q1_ref, q2_ref, t_ref, p1_ref, p2_ref, mf_ref, s_ref, w_ref, bias_ref, mf_scr, *, block):
    n_msg, capacity, width = q1_ref.shape
    n_half = n_msg * capacity
    n_rows, n_cols = s_ref.shape
    count = count_ref[pl.program_id(0)]
    column_bias = jnp.where(iota((1, n_cols), 1) < count, 0.0, NEGATIVE).astype(F32)
    sharp = SHARPNESS / math.sqrt(width)
    highest = jnp.full((1, n_cols), NEGATIVE * 4, F32)
    for h, q_ref in enumerate((q1_ref, q2_ref)):
        q = q_ref[...].reshape(n_half, width)
        head = q[:, :128].astype(F32)
        empty = head > 1e38
        slot_bias = jnp.where(empty[:, 0:1], NEGATIVE, 0.0).astype(F32)
        bias_ref[h * n_half : (h + 1) * n_half, :] = jnp.broadcast_to(slot_bias, (n_half, 128))
        q = jnp.concatenate([jnp.where(empty, 0.0, head).astype(BF16), q[:, 128:]], axis=1)
        s = lax.dot_general(q, t_ref[0], (((1,), (1,)), ((), ())), preferred_element_type=F32)
        s = s * sharp + column_bias
        s_ref[h * n_half : (h + 1) * n_half, :] = s
        highest = jnp.maximum(highest, jnp.max(s + slot_bias, axis=0, keepdims=True))

    def column_sums(i, total):
        at = pl.ds(pl.multiple_of(i * block, block), block)
        part = jnp.exp(s_ref[at, :] + bias_ref[at, 0:1] - highest)
        return total + jnp.sum(part.reshape(block // 8, 8, n_cols), axis=0)

    total = lax.fori_loop(0, n_rows // block, column_sums, jnp.zeros((8, n_cols), F32))
    half_reverse = 0.5 * (highest + jnp.log(jnp.sum(total, axis=0, keepdims=True)))

    def row_parts(i, _):
        at = pl.ds(pl.multiple_of(i * block, block), block)
        s = s_ref[at, :]
        top = jnp.max(s, axis=1, keepdims=True)
        forward = top + jnp.log(jnp.sum(jnp.exp(s - top), axis=1, keepdims=True))
        shifted = s - half_reverse
        top = jnp.max(shifted, axis=1, keepdims=True)
        margin = top + jnp.log(jnp.sum(jnp.exp(shifted - top), axis=1, keepdims=True))
        w_ref[at, :] = jnp.exp(shifted - margin).astype(BF16)
        lane = iota((block, 128), 1)
        mf_scr[at, :] = jnp.where(lane == 0, margin, jnp.where(lane == 1, forward, 0.0))
        return 0

    lax.fori_loop(0, n_rows // block, row_parts, 0)
    mf_ref[0] = mf_scr[...].T[:8]
    for h, p_ref in enumerate((p1_ref, p2_ref)):
        w = w_ref[h * n_half : (h + 1) * n_half, :]
        p = jnp.dot(w, t_ref[0], preferred_element_type=F32)
        p_ref[...] = p.astype(BF16).reshape(n_msg, capacity, width)


def combine_kernel(info, code_ref, mf_ref, r_ref, keep_ref, send_ref, kmf_ref, scr, *, capacity, group):
    n_buckets, rows = code_ref.shape
    n_slots = n_buckets * capacity
    width = r_ref.shape[2]
    half = rows // 2
    cols = columns([mf_ref[0:1, :], mf_ref[1:2, :]], n_slots)
    margin, forward = cols[:, 0:1], cols[:, 1:2]
    code = code_ref[...]
    slots = one_hot_slots(code, 0, n_buckets, capacity) > 0.5

    def merged(column):
        top = jnp.max(jnp.where(slots, column, NEGATIVE), axis=0, keepdims=True)
        total = jnp.sum(jnp.where(slots, jnp.exp(column - top), 0.0), axis=0, keepdims=True)
        return jnp.where(total > 0.0, top + jnp.log(jnp.where(total > 0.0, total, 1.0)), NEGATIVE)

    margin_row, forward_row = merged(margin), merged(forward)
    factor = jnp.where(slots, jnp.exp(margin - margin_row), 0.0)
    high = factor.astype(BF16)
    low = (factor - high.astype(F32)).astype(BF16)
    r = r_ref[...].reshape(n_slots, width)
    over = (((0,), (0,)), ((), ()))
    pooled = lax.dot_general(high, r, over, preferred_element_type=F32)
    scr[...] = pooled + lax.dot_general(low, r, over, preferred_element_type=F32)
    keep_ref[...] = scr[pl.ds(pl.multiple_of(info[1] * half, 16), half), :]
    send_ref[:half, :] = scr[pl.ds(pl.multiple_of((1 - info[1]) * half, 16), half), :].astype(BF16)
    send_ref[half:, :] = extra_rows(margin_row, forward_row, width)
    kmf_ref[...] = jnp.concatenate([margin_row, forward_row, jnp.zeros((6, rows), F32)], axis=0)


def log_sum(first, second, third=None):
    top = jnp.maximum(first, second)
    if third is not None:
        top = jnp.maximum(top, third)
    total = jnp.exp(first - top) + jnp.exp(second - top)
    if third is not None:
        total = total + jnp.exp(third - top)
    return top + jnp.log(total)


def merge_pair(info, keep_ref, kmf_ref, got_ref, out_ref, scr):
    half, width = keep_ref.shape
    rows = kmf_ref.shape[1]
    margin, forward = kmf_ref[0:1, :], kmf_ref[1:2, :]
    margin_b, forward_b = read_extra(got_ref, half, rows)
    margin_all, forward_all = log_sum(margin, margin_b), log_sum(forward, forward_b)
    scr[...] = columns([jnp.exp(margin - margin_all), jnp.exp(margin_b - margin_all)], rows)
    factors = scr[pl.ds(pl.multiple_of(info[1] * half, 16), half), :]
    out = keep_ref[...] * factors[:, 0:1] + got_ref[:half, :].astype(F32) * factors[:, 1:2]
    out_ref[:half, :] = out.astype(BF16)
    out_ref[half:, :] = extra_rows(margin_all, forward_all, width)


def merge_last(info, keep_ref, kmf_ref, got_ref, far_ref, out_ref, conf_ref, scr):
    half, width = keep_ref.shape
    rows = kmf_ref.shape[1]
    margin, forward = kmf_ref[0:1, :], kmf_ref[1:2, :]
    margin_b, forward_b = read_extra(got_ref, half, rows)
    margin_c, forward_c = read_extra(far_ref, half, rows)
    margin_all = log_sum(margin, margin_b, margin_c)
    forward_all = log_sum(forward, forward_b, forward_c)
    scr[...] = columns(
        [jnp.exp(margin - margin_all), jnp.exp(margin_b - margin_all), jnp.exp(margin_c - margin_all)], rows
    )
    factors = scr[pl.ds(pl.multiple_of(info[1] * half, 16), half), :]
    out = keep_ref[...] * factors[:, 0:1] + got_ref[:half, :].astype(F32) * factors[:, 1:2]
    out_ref[...] = (out + far_ref[:half, :].astype(F32) * factors[:, 2:3]).astype(BF16)
    conf_ref[...] = margin_all - 0.5 * forward_all


def shards(sources, targets, picks, cluster_home, row_count):
    n_src, n_tgt = lax.axis_size("src"), lax.axis_size("tgt")
    rows, width = sources.shape
    per_device, n_cols, _ = targets.shape
    n_clusters = cluster_home.shape[0]
    n_picks = picks.shape[1]
    capacity = -(-(2 * n_picks * rows // n_clusters) // 16) * 16
    side = n_src // 2
    half = rows // 2
    message = per_device * capacity
    n_buckets = side * per_device
    n_slots = n_buckets * capacity
    group = max(g for g in range(per_device, n_buckets + 1, per_device) if n_buckets % g == 0 and g * capacity <= 400)
    sds = jax.ShapeDtypeStruct

    me, core = lax.axis_index("src"), lax.axis_index("tgt")
    info = jnp.stack([me // side * side, core]).astype(jnp.int32)
    partner = [(i, (i + side) % n_src) for i in range(n_src)]
    twin = [(i, 1 - i) for i in range(n_tgt)]
    halves = [list(range(side)), list(range(side, n_src))]

    def exchange(x):
        return lax.all_to_all(x, "src", split_axis=0, concat_axis=0, axis_index_groups=halves, tiled=True)

    picks_t = picks.T
    home = cluster_home[None, :]
    far_picks = lax.ppermute(picks_t, "src", partner)
    far_mine = lax.ppermute(lax.dynamic_slice_in_dim(sources, core * half, half, 0), "src", partner)
    far_other = lax.ppermute(far_mine, "tgt", twin)

    sizes = dict(n_tgt=n_tgt, per_device=per_device, capacity=capacity, group=group)
    gather_out = (sds((side, message, width), BF16), sds((n_buckets, rows), F32))
    cost = dict(flops=2 * n_slots * rows * width, moved=2 * (n_slots + rows) * width)
    near_q, near_code = call(
        functools.partial(gather_own, **sizes), gather_out, smem=1, n_in=4, **cost
    )(info, picks_t, home, sources)
    near_in = exchange(near_q)
    far_q, far_code = call(
        functools.partial(gather_partner, **sizes),
        gather_out,
        [pltpu.VMEM((rows, width), BF16)],
        smem=1,
        n_in=5,
        **cost,
    )(info, far_picks, home, far_mine, far_other)
    far_in = exchange(far_q)

    here = (me * n_tgt + core) * per_device + jnp.arange(per_device, dtype=jnp.int32)
    counts = jnp.sum(jnp.where(home == here[:, None], row_count[None, :], 0), axis=1)
    n_rows = 2 * side * capacity
    piece = pl.BlockSpec((side, capacity, width), lambda l: (0, l, 0))
    near_pool, far_pool, mf = call(
        functools.partial(owner_kernel, block=64),
        (
            sds((side, message, width), BF16),
            sds((side, message, width), BF16),
            sds((per_device, 8, n_rows), F32),
        ),
        [
            pltpu.VMEM((n_rows, n_cols), F32),
            pltpu.VMEM((n_rows, n_cols), BF16),
            pltpu.VMEM((n_rows, 128), F32),
            pltpu.VMEM((n_rows, 128), F32),
        ],
        limit=48,
        flops=4 * 2 * n_slots * n_cols * width,
        moved=2 * (4 * n_slots + per_device * n_cols) * width,
        exps=8 * n_slots * n_cols,
        grid=(per_device,),
        in_specs=[
            pl.BlockSpec(memory_space=pltpu.SMEM),
            piece,
            piece,
            pl.BlockSpec((1, n_cols, width), lambda l: (l, 0, 0)),
        ],
        out_specs=(piece, piece, pl.BlockSpec((1, 8, n_rows), lambda l: (l, 0, 0))),
    )(counts, near_in, far_in, targets)

    back_far = exchange(far_pool)
    back_near = exchange(near_pool)
    parts = mf[:, :2].reshape(per_device, 2, 2, side, capacity)
    parts = parts.transpose(3, 2, 1, 0, 4).reshape(side, 4 * message)
    parts = exchange(parts).reshape(side, 2, 2, message)
    parts = parts.transpose(1, 2, 0, 3).reshape(2, 2, n_slots)

    combine = call(
        functools.partial(combine_kernel, capacity=capacity, group=group),
        (sds((half, width), F32), sds((half + EXTRA, width), BF16), sds((8, rows), F32)),
        [pltpu.VMEM((rows, width), F32)],
        smem=1,
        n_in=4,
        limit=40,
        flops=4 * n_slots * rows * width,
        moved=2 * (n_slots + 2 * rows) * width,
    )
    keep, send, kmf = combine(info, far_code, parts[1], back_far)
    got = lax.ppermute(send, "tgt", twin)
    factors = [pltpu.VMEM((rows, 128), F32)]
    joined = call(merge_pair, sds((half + EXTRA, width), BF16), factors, smem=1, n_in=4, moved=10 * half * width)(
        info, keep, kmf, got
    )
    from_far = lax.ppermute(joined, "src", partner)

    keep, send, kmf = combine(info, near_code, parts[0], back_near)
    got = lax.ppermute(send, "tgt", twin)
    mine, confidence = call(
        merge_last,
        (sds((half, width), BF16), sds((1, rows), F32)),
        factors,
        smem=1,
        n_in=5,
        moved=10 * half * width,
    )(info, keep, kmf, got, from_far)
    other = lax.ppermute(mine, "tgt", twin)
    first = jnp.where(core == 0, mine, other)
    second = jnp.where(core == 0, other, mine)
    return (jnp.concatenate([first, second], axis=0), confidence[0].astype(BF16))


def solution(mesh):
    placed = (P("src", None), P(("src", "tgt"), None, None), P("src", None), P(), P())
    return jax.shard_map(
        shards, mesh=mesh, in_specs=placed, out_specs=(P("src", None), P("src")), check_vma=False
    )
```

time: 352 us -> 180 us (0.51)
  waiting for transfers between devices: 192 us -> 80.3 us
  local copies, waits for them, and re-layouts: 61 us -> 5.02 us
  Pallas kernels: 0 us -> 34.1 us
  blocking collectives: 3.56 us -> 32.2 us
  other arithmetic: 26.6 us -> 1.91 us
  starting transfers between devices: 40 us -> 25.3 us
  between operations: 14.5 us -> 0.8 us
  matrix products: 13.6 us -> 0 us
    all_to_all x5 -> x3, waiting for transfers between devices: 162 us -> 32.8 us  [exchange(): lax.all_to_all(x, 'src', split_axis=0, concat_axis=0, axis_index_groups=h...]
    ppermute x0 -> x7, waiting for transfers between devices: none -> 47.5 us  [the longest x1 22.9 us: shards(): lax.ppermute(lax.dynamic_slice_in_dim(sources, core * half, half, 0), 'sr...]
    gather x11 -> x0, local copies, waits for them, and re-layouts: 47.5 us -> none  [the longest x4 24.3 us: shards(): jnp.take(flat_pool, safe_position[:, pick_no], axis=0)]
    pallas_call x0 -> x7, Pallas kernels: none -> 34.1 us  [the longest x1 19 us: shards(): call(functools.partial(owner_kernel, block=64), (sds((side, message, widt...]
    all_to_all x0 -> x2, blocking collectives: none -> 32.2 us  [exchange(): lax.all_to_all(x, 'src', split_axis=0, concat_axis=0, axis_index_groups=h...]
    all_gather x1 -> x0, waiting for transfers between devices: 29.3 us -> none  [joined(): pieces = jax.tree.map(lambda part: lax.all_gather(part, axis), value)]
    all_to_all x5 -> x3, starting transfers between devices: 39.9 us -> 18.7 us  [exchange(): lax.all_to_all(x, 'src', split_axis=0, concat_axis=0, axis_index_groups=h...]
    dot_general x2 -> x0, matrix products: 13.6 us -> none  [the longest x1 6.91 us: shards(): jnp.einsum('jlcr,lrd->jlcd', weights, targets, preferred_element_type=jnp...]
  transfers between devices with their start and end apart: 6 -> 10, of which waited for: 4 -> 7; matrix products, arithmetic and copies ran while one was open for 11% -> 1% of each run, Pallas kernels for 0% -> 6%
where the time goes in v1:
time: 180 us
  waiting for transfers between devices  80.3 us (45%)
  Pallas kernels  34.1 us (19%)
  blocking collectives  32.2 us (18%)
  starting transfers between devices  25.3 us (14%)
  local copies, waits for them, and re-layouts  5.02 us (3%)
  other arithmetic  1.91 us (1%)
    all_to_all x3, waiting for transfers between devices, exchange(): lax.all_to_all(x, 'src', split_axis=0, concat_axis=0, axis_index_groups=h...  32.8 us
    all_to_all x2, blocking collectives, exchange(): lax.all_to_all(x, 'src', split_axis=0, concat_axis=0, axis_index_groups=h...  32.2 us
    ppermute x1, waiting for transfers between devices, shards(): lax.ppermute(lax.dynamic_slice_in_dim(sources, core * half, half, 0), 'sr...  22.9 us
    ppermute x1, waiting for transfers between devices, shards(): from_far = lax.ppermute(joined, 'src', partner)  21.5 us
    pallas_call x1, Pallas kernels, shards(): call(functools.partial(owner_kernel, block=64), (sds((side, message, widt...  19 us
    all_to_all x3, starting transfers between devices, exchange(): lax.all_to_all(x, 'src', split_axis=0, concat_axis=0, axis_index_groups=h...  18.7 us
    unnamed x20, local copies, waits for them, and re-layouts  4.51 us
    pallas_call x1, Pallas kernels, shards(): keep, send, kmf = combine(info, far_code, parts[1], back_far)  3.97 us
  transfers between devices with their start and end apart: 10, of which 7 were waited for; matrix products, arithmetic and copies ran while one was open for 1% of the time, Pallas kernels for 6%

profile of v1, /device:TPU:0, one launch (start us, length us, event | category | flops | bytes accessed | tf_op | source)
XLA Modules:
  0.0 179.6 jit_solution(17793120817591535954)
XLA Ops:
  0.6 0.1 pad_add_fusion.info
  0.7 0.0 copy-start.3
  0.7 1.1 copy-done.3
  1.9 0.0 copy-start.5
  1.9 0.7 copy-done.5
  2.5 0.0 copy-start.7
  2.5 0.7 copy-done.7
  3.2 3.0 %shard_map.68 = (bf16[8,96,1024]{2,1,0:T(8,128)(2,1)}, f32[16,384]{1,0:T(8,128)S(1)}) custom-call(s32[2]{0:T(128)S(1)} %pad_add_fusion.info, s32[4,384]{1,0:T(4,128)S(1)} %bitcast.14, s32[1,64]{1,0:T(1,128)S(1)} %bitcast.12, bf16[384,1024]{1,0:T(8,128)(2,1)S(1)} %copy-done.3), custom_call_target="tpu_custom_call" | custom-call | flops 603979776 | bytes 2359296 | tf_op jit(solution)/shard_map/pallas_call | solution.py:263
  6.2 0.0 copy-start.4
  6.2 0.0 copy-start.8
  6.2 0.0 copy-start.6
  6.2 6.3 %all-to-all-start = ((bf16[8,96,1024]{2,1,0:T(8,128)(2,1)}), bf16[8,96,1024]{2,1,0:T(8,128)(2,1)S(1)}, u32[]{:S(2)}, u32[]{:S(2)}) async-start(bf16[8,96,1024]{2,1,0:T(8,128)(2,1)} %get-tuple-element.18), calls=%async_computation | async-start | bytes 3145728 | tf_op jit(solution)/shard_map/all_to_all | solution.py:252
  12.5 0.0 copy-done.4
  12.6 2.7 %collective-permute-start.1 = (bf16[192,1024]{1,0:T(8,128)(2,1)S(1)}, bf16[192,1024]{1,0:T(8,128)(2,1)S(1)}, u32[]{:S(2)}, u32[]{:S(2)}) collective-permute-start(bf16[192,1024]{1,0:T(8,128)(2,1)S(1)} %constant_dynamic-slice_fusion), channel_id=1, source_target_pairs={{0,16},{2,18},{4,20},{6,22},{8,24},{10,26},{12,28},{14,30},{16,0},... | collective-permute-start | bytes 1179656 | tf_op jit(solution)/shard_map/ppermute | solution.py:257
  15.2 22.9 %collective-permute-done.1.mine_ref = bf16[192,1024]{1,0:T(8,128)(2,1)S(1)} collective-permute-done((bf16[192,1024]{1,0:T(8,128)(2,1)S(1)}, bf16[192,1024]{1,0:T(8,128)(2,1)S(1)}, u32[]{:S(2)}, u32[]{:S(2)}) %collective-permute-start.1) | collective-permute-done | bytes 393248 | tf_op jit(solution)/shard_map/ppermute | solution.py:257
  38.1 0.0 collective-permute-start.2
  38.1 0.0 copy-done.8
  38.1 3.4 %collective-permute-start = (s32[4,384]{1,0:T(4,128)S(1)}, s32[4,384]{1,0:T(4,128)S(1)}, u32[]{:S(2)}, u32[]{:S(2)}) collective-permute-start(s32[4,384]{1,0:T(4,128)S(1)} %bitcast.15), channel_id=1, source_target_pairs={{0,16},{2,18},{4,20},{6,22},{8,24},{10,26},{12,28},{14,30},{16,0},... | collective-permute-start | bytes 18440 | tf_op jit(solution)/shard_map/ppermute | solution.py:256
  41.5 1.6 collective-permute-done.picks_ref
  43.1 0.0 collective-permute-done.2.other_ref
  43.1 0.0 copy-done.6
  43.1 3.0 %shard_map.69 = (bf16[8,96,1024]{2,1,0:T(8,128)(2,1)}, f32[16,384]{1,0:T(8,128)S(1)}) custom-call(s32[2]{0:T(128)S(1)} %pad_add_fusion.info, s32[4,384]{1,0:T(4,128)S(1)} %collective-permute-done.picks_ref, s32[1,64]{1,0:T(1,128)S(1)} %bitcast.13, bf16[192,1024]{1,0:T(8,128)(2,1)S(1)} %collective-permute-done.1.mine_ref, ...), custom_call_target="tpu_custom_call" | custom-call | flops 603979776 | bytes 2359296 | tf_op jit(solution)/shard_map/pallas_call | solution.py:267
  46.1 0.0 all-to-all-done.q1_ref
  46.1 0.0 copy-start.9
  46.1 8.6 %all-to-all-start.1 = ((bf16[8,96,1024]{2,1,0:T(8,128)(2,1)}), bf16[8,96,1024]{2,1,0:T(8,128)(2,1)}, u32[]{:S(2)}, u32[]{:S(2)}) async-start(bf16[8,96,1024]{2,1,0:T(8,128)(2,1)} %get-tuple-element.19), calls=%async_computation.1 | async-start | bytes 3145728 | tf_op jit(solution)/shard_map/all_to_all | solution.py:252
  54.7 0.0 copy-done.9
  54.7 0.2 fusion.count_ref
  54.9 20.0 %all-to-all-done.1.q2_ref = bf16[8,96,1024]{2,1,0:T(8,128)(2,1)} async-done(((bf16[8,96,1024]{2,1,0:T(8,128)(2,1)}), bf16[8,96,1024]{2,1,0:T(8,128)(2,1)}, u32[]{:S(2)}, u32[]{:S(2)}) %all-to-all-start.1) | async-done | bytes 1572896 | tf_op jit(solution)/shard_map/all_to_all | solution.py:252
  74.9 19.0 %shard_map.70 = (bf16[8,96,1024]{2,1,0:T(8,128)(2,1)}, bf16[8,96,1024]{2,1,0:T(8,128)(2,1)S(1)}, f32[2,8,768]{2,1,0:T(8,128)S(1)}) custom-call(s32[2]{0:T(128)S(1)} %fusion.count_ref, bf16[8,96,1024]{2,1,0:T(8,128)(2,1)S(1)} %all-to-all-done.q1_ref, bf16[8,96,1024]{2,1,0:T(8,128)(2,1)} %all-to-all-done.1.q2_ref, bf16[2,1024,1024]{2,1,0:T(8,128)(2,1)} %t_ref.1), custom_call_target="tpu_custom_call" | custom-call | flops 6442450944 | bytes 10485760 | tf_op jit(solution)/shard_map/pallas_call | solution.py:281
  93.9 0.0 copy-start
  93.9 1.1 copy-done
  95.1 0.1 reshape.27
  95.2 0.1 all_to_all.24
  95.3 9.0 %all_to_all.30 = f32[8,1,384]{2,1,0:T(1,128)S(1)} all-to-all(f32[8,1,384]{2,1,0:T(1,128)S(1)} %all_to_all.24), channel_id=1, replica_groups={{0,2,4,6,8,10,12,14},{16,18,20,22,24,26,28,30},{1,3,5,7,9,11,13,15},{17..., dimensions={0} | all-to-all | bytes 24576 | tf_op jit(solution)/shard_map/all_to_all | solution.py:252
  104.3 23.2 %all_to_all.31.r_ref = bf16[8,96,1024]{2,1,0:T(8,128)(2,1)S(1)} all-to-all(bf16[8,96,1024]{2,1,0:T(8,128)(2,1)} %copy-done), channel_id=1, replica_groups={{0,2,4,6,8,10,12,14},{16,18,20,22,24,26,28,30},{1,3,5,7,9,11,13,15},{17..., dimensions={0} | all-to-all | bytes 3145728 | tf_op jit(solution)/shard_map/all_to_all | solution.py:252
  127.5 3.8 %all-to-all-start.3 = ((bf16[8,96,1024]{2,1,0:T(8,128)(2,1)}), bf16[8,96,1024]{2,1,0:T(8,128)(2,1)S(1)}, u32[]{:S(2)}, u32[]{:S(2)}) async-start(bf16[8,96,1024]{2,1,0:T(8,128)(2,1)} %get-tuple-element.21), calls=%async_computation.3 | async-start | bytes 3145728 | tf_op jit(solution)/shard_map/all_to_all | solution.py:252
  131.3 0.1 reshape.28
  131.4 0.1 squeeze.8.mf_ref
  131.5 4.0 %shard_map.72 = (f32[192,1024]{1,0:T(8,128)S(1)}, bf16[208,1024]{1,0:T(8,128)(2,1)}, f32[8,384]{1,0:T(8,128)S(1)}) custom-call(s32[2]{0:T(128)S(1)} %pad_add_fusion.info, f32[16,384]{1,0:T(8,128)S(1)} %get-tuple-element.25.code_ref, f32[2,768]{1,0:T(2,128)S(1)} %squeeze.8.mf_ref, bf16[8,96,1024]{2,1,0:T(8,128)(2,1)S(1)} %all_to_all.31.r_ref), custom_call_target="tpu_custom_call" | custom-call | flops 1207959552 | bytes 3145728 | tf_op jit(solution)/shard_map/pallas_call | solution.py:325
  135.4 0.0 copy-start.1
  135.4 0.9 copy-done.1
  136.3 0.0 collective-permute-start.4
  136.3 0.1 squeeze.7.mf_ref
  136.4 12.8 %all-to-all-done.3.r_ref = bf16[8,96,1024]{2,1,0:T(8,128)(2,1)S(1)} async-done(((bf16[8,96,1024]{2,1,0:T(8,128)(2,1)}), bf16[8,96,1024]{2,1,0:T(8,128)(2,1)S(1)}, u32[]{:S(2)}, u32[]{:S(2)}) %all-to-all-start.3) | async-done | bytes 1572896 | tf_op jit(solution)/shard_map/all_to_all | solution.py:252
  149.2 0.0 copy-start.2
  149.2 3.2 %shard_map.71 = (f32[192,1024]{1,0:T(8,128)S(1)}, bf16[208,1024]{1,0:T(8,128)(2,1)S(1)}, f32[8,384]{1,0:T(8,128)S(1)}) custom-call(s32[2]{0:T(128)S(1)} %pad_add_fusion.info, f32[16,384]{1,0:T(8,128)S(1)} %get-tuple-element.17.code_ref, f32[2,768]{1,0:T(2,128)S(1)} %squeeze.7.mf_ref, bf16[8,96,1024]{2,1,0:T(8,128)(2,1)S(1)} %all-to-all-done.3.r_ref), custom_call_target="tpu_custom_call" | custom-call | flops 1207959552 | bytes 3145728 | tf_op jit(solution)/shard_map/pallas_call | solution.py:333
  152.4 0.1 collective-permute-start.3
  152.5 0.0 collective-permute-done.4.got_ref
  152.5 0.0 copy-done.2
  152.5 0.9 shard_map.73
  153.4 0.4 collective-permute-start.5
  153.8 0.4 collective-permute-done.3.got_ref
  154.2 21.5 %collective-permute-done.5.far_ref = bf16[208,1024]{1,0:T(8,128)(2,1)S(1)} collective-permute-done((bf16[208,1024]{1,0:T(8,128)(2,1)S(1)}, bf16[208,1024]{1,0:T(8,128)(2,1)S(1)}, u32[]{:S(2)}, u32[]{:S(2)}) %collective-permute-start.5) | collective-permute-done | bytes 426016 | tf_op jit(solution)/shard_map/ppermute | solution.py:331
  175.7 1.0 shard_map.74
  176.8 0.1 collective-permute-start.6
  176.9 0.6 convert_reduce_fusion
  177.4 1.1 collective-permute-done.6
  178.6 0.1 broadcast_select_fusion.1
  178.7 0.9 pad_maximum_fusion
  (8 shorter events, 0.1 us)
Async XLA Ops:
  0.7 1.1 copy-start.3
  1.9 0.7 copy-start.5
  2.5 0.7 copy-start.7
  6.2 6.3 %copy-start.4 = (bf16[384,1024]{1,0:T(8,128)(2,1)S(1)}, bf16[384,1024]{1,0:T(8,128)(2,1)}, u32[]{:S(2)}) copy-start(bf16[384,1024]{1,0:T(8,128)(2,1)} %src_ref.1) | copy-start | bytes 2359300
  6.2 31.9 %copy-start.8 = (s32[384,4]{0,1:T(4,128)S(1)}, s32[384,4]{0,1:T(4,128)}, u32[]{:S(2)}) copy-start(s32[384,4]{0,1:T(4,128)} %param.7) | copy-start | bytes 18436
  6.2 36.9 %copy-start.6 = (s32[64]{0:T(128)S(1)}, s32[64]{0:T(128)}, u32[]{:S(2)}) copy-start(s32[64]{0:T(128)} %param.8) | copy-start | bytes 772
  6.2 39.9 %all-to-all-start = ((bf16[8,96,1024]{2,1,0:T(8,128)(2,1)}), bf16[8,96,1024]{2,1,0:T(8,128)(2,1)S(1)}, u32[]{:S(2)}, u32[]{:S(2)}) async-start(bf16[8,96,1024]{2,1,0:T(8,128)(2,1)} %get-tuple-element.18), calls=%async_computation | async-start | bytes 3145728 | tf_op jit(solution)/shard_map/all_to_all | solution.py:252
  12.6 25.5 %collective-permute-start.1 = (bf16[192,1024]{1,0:T(8,128)(2,1)S(1)}, bf16[192,1024]{1,0:T(8,128)(2,1)S(1)}, u32[]{:S(2)}, u32[]{:S(2)}) collective-permute-start(bf16[192,1024]{1,0:T(8,128)(2,1)S(1)} %constant_dynamic-slice_fusion), channel_id=1, source_target_pairs={{0,16},{2,18},{4,20},{6,22},{8,24},{10,26},{12,28},{14,30},{16,0},... | collective-permute-start | bytes 1179656 | tf_op jit(solution)/shard_map/ppermute | solution.py:257
  38.1 5.0 %collective-permute-start.2 = (bf16[192,1024]{1,0:T(8,128)(2,1)S(1)}, bf16[192,1024]{1,0:T(8,128)(2,1)S(1)}, u32[]{:S(2)}, u32[]{:S(2)}) collective-permute-start(bf16[192,1024]{1,0:T(8,128)(2,1)S(1)} %collective-permute-done.1.mine_ref), channel_id=1, source_target_pairs={{0,1},{1,0},{2,3},{3,2},{4,5},{5,4},{6,7},{7,6},{8,9},{9,8},{10,11... | collective-permute-start | bytes 1179656 | tf_op jit(solution)/shard_map/ppermute | solution.py:258
  38.1 5.0 %collective-permute-start = (s32[4,384]{1,0:T(4,128)S(1)}, s32[4,384]{1,0:T(4,128)S(1)}, u32[]{:S(2)}, u32[]{:S(2)}) collective-permute-start(s32[4,384]{1,0:T(4,128)S(1)} %bitcast.15), channel_id=1, source_target_pairs={{0,16},{2,18},{4,20},{6,22},{8,24},{10,26},{12,28},{14,30},{16,0},... | collective-permute-start | bytes 18440 | tf_op jit(solution)/shard_map/ppermute | solution.py:256
  46.1 8.6 %copy-start.9 = (s32[64]{0:T(128)S(1)}, s32[64]{0:T(128)}, u32[]{:S(2)}) copy-start(s32[64]{0:T(128)} %param.9) | copy-start | bytes 772
  46.1 28.8 %all-to-all-start.1 = ((bf16[8,96,1024]{2,1,0:T(8,128)(2,1)}), bf16[8,96,1024]{2,1,0:T(8,128)(2,1)}, u32[]{:S(2)}, u32[]{:S(2)}) async-start(bf16[8,96,1024]{2,1,0:T(8,128)(2,1)} %get-tuple-element.19), calls=%async_computation.1 | async-start | bytes 3145728 | tf_op jit(solution)/shard_map/all_to_all | solution.py:252
  93.9 1.1 copy-start
  127.5 21.7 %all-to-all-start.3 = ((bf16[8,96,1024]{2,1,0:T(8,128)(2,1)}), bf16[8,96,1024]{2,1,0:T(8,128)(2,1)S(1)}, u32[]{:S(2)}, u32[]{:S(2)}) async-start(bf16[8,96,1024]{2,1,0:T(8,128)(2,1)} %get-tuple-element.21), calls=%async_computation.3 | async-start | bytes 3145728 | tf_op jit(solution)/shard_map/all_to_all | solution.py:252
  135.4 0.9 copy-start.1
  136.3 16.2 %collective-permute-start.4 = (bf16[208,1024]{1,0:T(8,128)(2,1)}, bf16[208,1024]{1,0:T(8,128)(2,1)S(1)}, u32[]{:S(2)}, u32[]{:S(2)}) collective-permute-start(bf16[208,1024]{1,0:T(8,128)(2,1)} %get-tuple-element.29), channel_id=1, source_target_pairs={{0,1},{1,0},{2,3},{3,2},{4,5},{5,4},{6,7},{7,6},{8,9},{9,8},{10,11... | collective-permute-start | bytes 1277960 | tf_op jit(solution)/shard_map/ppermute | solution.py:326
  149.2 3.3 %copy-start.2 = (f32[192,1024]{1,0:T(8,128)S(1)}, f32[192,1024]{1,0:T(8,128)}, u32[]{:S(2)}) copy-start(f32[192,1024]{1,0:T(8,128)} %copy-done.1) | copy-start | bytes 2359300
  152.4 1.8 %collective-permute-start.3 = (bf16[208,1024]{1,0:T(8,128)(2,1)S(1)}, bf16[208,1024]{1,0:T(8,128)(2,1)S(1)}, u32[]{:S(2)}, u32[]{:S(2)}) collective-permute-start(bf16[208,1024]{1,0:T(8,128)(2,1)S(1)} %get-tuple-element.24), channel_id=1, source_target_pairs={{0,1},{1,0},{2,3},{3,2},{4,5},{5,4},{6,7},{7,6},{8,9},{9,8},{10,11... | collective-permute-start | bytes 1277960 | tf_op jit(solution)/shard_map/ppermute | solution.py:334
  153.4 22.3 %collective-permute-start.5 = (bf16[208,1024]{1,0:T(8,128)(2,1)S(1)}, bf16[208,1024]{1,0:T(8,128)(2,1)S(1)}, u32[]{:S(2)}, u32[]{:S(2)}) collective-permute-start(bf16[208,1024]{1,0:T(8,128)(2,1)S(1)} %shard_map.73), channel_id=1, source_target_pairs={{0,16},{2,18},{4,20},{6,22},{8,24},{10,26},{12,28},{14,30},{16,0},... | collective-permute-start | bytes 1277960 | tf_op jit(solution)/shard_map/ppermute | solution.py:331
  176.8 1.8 collective-permute-start.6

commit v2 on v1

v2 whole, which is shorter than its diff:
```python
import functools
import math

import jax
import jax.numpy as jnp
from jax import lax
from jax.experimental import pallas as pl
from jax.experimental.pallas import tpu as pltpu
from jax.sharding import PartitionSpec as P

NEGATIVE = -1e30
SHARPNESS = 2.5
EXTRA = 16
F32, BF16 = jnp.float32, jnp.bfloat16
MIB = 1 << 20
LOG2E = math.log2(math.e)
LN2 = math.log(2.0)
BLOCK = 32
HIDE = 23_000_000_000


def iota(shape, axis):
    return lax.broadcasted_iota(jnp.int32, shape, axis)


def call(kernel, out_shape, scratch=(), smem=0, n_in=0, limit=32, flops=0, moved=0, exps=0, **kw):
    if not kw:
        kw = dict(
            in_specs=[pl.BlockSpec(memory_space=pltpu.SMEM)] * smem
            + [pl.BlockSpec(memory_space=pltpu.VMEM)] * (n_in - smem),
            out_specs=jax.tree.map(lambda _: pl.BlockSpec(memory_space=pltpu.VMEM), out_shape),
        )
    return pl.pallas_call(
        kernel,
        out_shape=out_shape,
        scratch_shapes=list(scratch),
        compiler_params=pltpu.CompilerParams(vmem_limit_bytes=limit * MIB),
        cost_estimate=pl.CostEstimate(flops=flops, bytes_accessed=moved, transcendentals=exps),
        **kw,
    )


def columns(rows, width):
    stacked = jnp.concatenate(rows + [jnp.zeros((128 - len(rows), width), F32)], axis=0)
    return stacked.T


def three(row):
    high = row.astype(BF16).astype(F32)
    middle = (row - high).astype(BF16).astype(F32)
    return [high, middle, row - high - middle]


def extra_rows(first, second, width):
    parts = three(first) + three(second)
    body = jnp.concatenate(parts + [jnp.zeros((EXTRA - len(parts), first.shape[1]), F32)], axis=0)
    rest = jnp.zeros((EXTRA, width - first.shape[1]), F32)
    return jnp.concatenate([body, rest], axis=1).astype(BF16)


def read_extra(ref, start, length):
    block = ref[start : start + EXTRA, :length].astype(F32)
    first = (block[0:1] + block[1:2]) + block[2:3]
    second = (block[3:4] + block[4:5]) + block[5:6]
    return first, second


def one_hot_slots(code, start, group, capacity):
    rows = code.shape[1]
    order = iota((capacity, rows), 0).astype(F32)
    return jnp.concatenate(
        [jnp.where(order == code[b : b + 1, :], 1.0, 0.0) for b in range(start, start + group)], axis=0
    )


def gather_body(info, picks, home_ref, source, q_ref, code_ref, *, n_tgt, per_device, capacity, group):
    n_buckets, rows = code_ref.shape
    n_clusters = home_ref.shape[1]
    width = q_ref.shape[2]
    cluster = iota((n_clusters, rows), 0).astype(F32)
    member = jnp.zeros((n_clusters, rows), F32)
    for pick in picks:
        member = jnp.where(cluster == pick, 1.0, member)
    bucket = iota((n_buckets, n_clusters), 0)
    holder = (info[0] + lax.div(bucket, per_device)) * n_tgt + info[1]
    place = holder * per_device + lax.rem(bucket, per_device)
    chosen = jnp.where(home_ref[...] == place, 1.0, 0.0).astype(BF16)
    inside = jnp.dot(chosen, member.astype(BF16), preferred_element_type=F32)
    earlier = jnp.where(iota((rows, rows), 0) < iota((rows, rows), 1), 1.0, 0.0).astype(BF16)
    rank = jnp.dot(inside.astype(BF16), earlier, preferred_element_type=F32)
    code = jnp.where(inside > 0.5, rank, -1.0)
    code_ref[...] = code
    per_message = group // per_device
    for start in range(0, n_buckets, group):
        slots = one_hot_slots(code, start, group, capacity)
        filled = jnp.sum(slots, axis=1, keepdims=True)
        found = jnp.dot(slots.astype(BF16), source, preferred_element_type=F32)
        head = found[:, :128]
        head = jnp.where((iota(head.shape, 1) == 0) & (filled < 0.5), jnp.inf, head)
        found = jnp.concatenate([head, found[:, 128:]], axis=1).astype(BF16)
        d = start // per_device
        q_ref[d : d + per_message] = found.reshape(per_message, per_device * capacity, width)


def half_with_picks(info, picks_ref, src_ref, out_ref):
    n_picks, rows = picks_ref.shape
    width = src_ref.shape[1]
    half = rows // 2
    out_ref[:half, :] = src_ref[pl.ds(pl.multiple_of(info[1] * half, 16), half), :]
    body = jnp.concatenate([picks_ref[...].astype(F32), jnp.zeros((EXTRA - n_picks, rows), F32)], axis=0)
    rest = jnp.zeros((EXTRA, width - rows), F32)
    out_ref[half:, :] = jnp.concatenate([body, rest], axis=1).astype(BF16)


def gather_own(info, picks_ref, home_ref, src_ref, q_ref, code_ref, **sizes):
    picks = [picks_ref[k : k + 1, :].astype(F32) for k in range(picks_ref.shape[0])]
    gather_body(info, picks, home_ref, src_ref[...], q_ref, code_ref, **sizes)


def gather_partner(info, home_ref, mine_ref, other_ref, q_ref, code_ref, src_ref, *, n_picks, **sizes):
    rows = src_ref.shape[0]
    half = rows // 2
    src_ref[pl.ds(pl.multiple_of(info[1] * half, 16), half), :] = mine_ref[:half, :]
    src_ref[pl.ds(pl.multiple_of((1 - info[1]) * half, 16), half), :] = other_ref[:half, :]
    block = mine_ref[half : half + EXTRA, :rows].astype(F32)
    picks = [block[k : k + 1, :] for k in range(n_picks)]
    gather_body(info, picks, home_ref, src_ref[...], q_ref, code_ref, **sizes)


def scores_of(q_ref, t, count, l, capacity):
    width = q_ref.shape[2]
    n_cols = t.shape[0]
    q = q_ref[:, l * capacity : (l + 1) * capacity, :].reshape(-1, width)
    head = q[:, :128].astype(F32)
    empty = head > 1e38
    q = jnp.concatenate([jnp.where(empty, 0.0, head).astype(BF16), q[:, 128:]], axis=1)
    s = lax.dot_general(q, t, (((1,), (1,)), ((), ())), preferred_element_type=F32)
    column_bias = jnp.where(iota((1, n_cols), 1) < count, 0.0, NEGATIVE).astype(F32)
    slot_bias = jnp.where(empty[:, 0:1], NEGATIVE, 0.0).astype(F32)
    return s * (SHARPNESS / math.sqrt(width) * LOG2E) + column_bias + slot_bias


def column_part(s_ref, highest, block):
    n_rows, n_cols = s_ref.shape

    def add(i, total):
        part = jnp.exp2(s_ref[pl.ds(pl.multiple_of(i * block, block), block), :] - highest)
        return total + jnp.sum(part.reshape(block // 8, 8, n_cols), axis=0)

    total = lax.fori_loop(0, n_rows // block, add, jnp.zeros((8, n_cols), F32))
    return jnp.sum(total, axis=0, keepdims=True)


def row_log_sum(s):
    top = jnp.max(s, axis=1, keepdims=True)
    return top + jnp.log2(jnp.sum(jnp.exp2(s - top), axis=1, keepdims=True))


def weigh(s, half_reverse):
    shifted = s - half_reverse
    top = jnp.max(shifted, axis=1, keepdims=True)
    e = jnp.exp2(shifted - top)
    total = jnp.sum(e, axis=1, keepdims=True)
    return (e * (1.0 / total)).astype(BF16), top + jnp.log2(total)


def tail(margin, forward, lane):
    out = jnp.zeros(lane.shape, F32)
    for i, part in enumerate(three(margin) + three(forward)):
        out = jnp.where(lane == i, part, out)
    return out.astype(BF16)


def near_scores(count_ref, q_ref, t_ref, s_ref, col_ref, fwd_ref, *, capacity, block):
    per_device, n_half, n_cols = s_ref.shape
    for l in range(per_device):
        s = scores_of(q_ref, t_ref[l], count_ref[l], l, capacity)
        s_ref[l] = s
        highest = jnp.max(s, axis=0, keepdims=True)
        total = column_part(s_ref.at[l], highest, block)
        col_ref[l] = jnp.concatenate([highest, total, jnp.zeros((6, n_cols), F32)], axis=0)

        def forward(i, _):
            at = pl.ds(pl.multiple_of(i * block, block), block)
            fwd_ref[l, at, :] = jnp.broadcast_to(row_log_sum(s_ref[l, at, :]), (block, 128))
            return 0

        lax.fori_loop(0, n_half // block, forward, 0)


def far_owner(count_ref, q_ref, t_ref, col_ref, p_ref, rev_ref, s_ref, w_ref, tail_ref, *, capacity, block):
    n_msg, _, full = p_ref.shape
    per_device = t_ref.shape[0]
    n_half, n_cols = s_ref.shape
    width = full - 128
    for l in range(per_device):
        s = scores_of(q_ref, t_ref[l], count_ref[l], l, capacity)
        s_ref[...] = s
        highest = jnp.max(s, axis=0, keepdims=True)
        total = column_part(s_ref, highest, block)
        top = jnp.maximum(highest, col_ref[l, 0:1, :])
        total = total * jnp.exp2(highest - top) + col_ref[l, 1:2, :] * jnp.exp2(col_ref[l, 0:1, :] - top)
        half_reverse = 0.5 * (top + jnp.log2(total))
        rev_ref[l] = jnp.broadcast_to(half_reverse, (8, n_cols))

        def rows(i, _):
            at = pl.ds(pl.multiple_of(i * block, block), block)
            s = s_ref[at, :]
            forward = row_log_sum(s)
            w, margin = weigh(s, half_reverse)
            w_ref[at, :] = w
            tail_ref[at, :] = tail(margin, forward, iota((block, 128), 1))
            return 0

        lax.fori_loop(0, n_half // block, rows, 0)
        at = slice(l * capacity, (l + 1) * capacity)
        p = jnp.dot(w_ref[...], t_ref[l], preferred_element_type=F32)
        p_ref[:, at, :width] = p.astype(BF16).reshape(n_msg, capacity, width)
        p_ref[:, at, width:] = tail_ref[...].reshape(n_msg, capacity, 128)


def near_owner(s_ref, rev_ref, fwd_ref, t_ref, p_ref, w_ref, tail_ref, *, capacity, block):
    n_msg, _, full = p_ref.shape
    per_device, n_half, _ = s_ref.shape
    width = full - 128
    for l in range(per_device):
        half_reverse = rev_ref[l, 0:1, :]

        def rows(i, _):
            at = pl.ds(pl.multiple_of(i * block, block), block)
            w, margin = weigh(s_ref[l, at, :], half_reverse)
            w_ref[at, :] = w
            tail_ref[at, :] = tail(margin, fwd_ref[l, at, 0:1], iota((block, 128), 1))
            return 0

        lax.fori_loop(0, n_half // block, rows, 0)
        at = slice(l * capacity, (l + 1) * capacity)
        p = jnp.dot(w_ref[...], t_ref[l], preferred_element_type=F32)
        p_ref[:, at, :width] = p.astype(BF16).reshape(n_msg, capacity, width)
        p_ref[:, at, width:] = tail_ref[...].reshape(n_msg, capacity, 128)


def combine_kernel(info, code_ref, r_ref, _, keep_ref, kmf_ref, *refs, capacity):
    *send_refs, scr = refs
    n_buckets, rows = code_ref.shape
    n_slots = n_buckets * capacity
    width = r_ref.shape[2] - 128
    half = rows // 2
    parts = r_ref[:, :, width:].reshape(n_slots, 128).astype(F32)
    margin = (parts[:, 0:1] + parts[:, 1:2]) + parts[:, 2:3]
    forward = (parts[:, 3:4] + parts[:, 4:5]) + parts[:, 5:6]
    slots = one_hot_slots(code_ref[...], 0, n_buckets, capacity) > 0.5

    def merged(column):
        top = jnp.max(jnp.where(slots, column, NEGATIVE), axis=0, keepdims=True)
        total = jnp.sum(jnp.where(slots, jnp.exp2(column - top), 0.0), axis=0, keepdims=True)
        return jnp.where(total > 0.0, top + jnp.log2(jnp.where(total > 0.0, total, 1.0)), NEGATIVE)

    margin_row, forward_row = merged(margin), merged(forward)
    factor = jnp.where(slots, jnp.exp2(margin - margin_row), 0.0)
    high = factor.astype(BF16)
    low = (factor - high.astype(F32)).astype(BF16)
    r = r_ref[:, :, :width].reshape(n_slots, width)
    over = (((0,), (0,)), ((), ()))
    pooled = lax.dot_general(high, r, over, preferred_element_type=F32)
    scr[...] = pooled + lax.dot_general(low, r, over, preferred_element_type=F32)
    keep_ref[...] = scr[pl.ds(pl.multiple_of(info[1] * half, 16), half), :]
    start = 0
    for ref in send_refs:
        count = min(ref.shape[0], half - start)
        at = pl.ds(pl.multiple_of((1 - info[1]) * half + start, 16), count)
        ref[:count, :] = scr[at, :].astype(BF16)
        start = start + count
    send_refs[-1][count:, :] = extra_rows(margin_row, forward_row, width)
    kmf_ref[...] = jnp.concatenate([margin_row, forward_row, jnp.zeros((6, rows), F32)], axis=0)


def log_sum(first, second, third=None):
    top = jnp.maximum(first, second)
    if third is not None:
        top = jnp.maximum(top, third)
    total = jnp.exp2(first - top) + jnp.exp2(second - top)
    if third is not None:
        total = total + jnp.exp2(third - top)
    return top + jnp.log2(total)


def merge_pair(info, keep_ref, kmf_ref, got_ref, out_ref, scr):
    half, width = keep_ref.shape
    rows = kmf_ref.shape[1]
    margin, forward = kmf_ref[0:1, :], kmf_ref[1:2, :]
    margin_b, forward_b = read_extra(got_ref, half, rows)
    margin_all, forward_all = log_sum(margin, margin_b), log_sum(forward, forward_b)
    scr[...] = columns([jnp.exp2(margin - margin_all), jnp.exp2(margin_b - margin_all)], rows)
    factors = scr[pl.ds(pl.multiple_of(info[1] * half, 16), half), :]
    out = keep_ref[...] * factors[:, 0:1] + got_ref[:half, :].astype(F32) * factors[:, 1:2]
    out_ref[:half, :] = out.astype(BF16)
    out_ref[half:, :] = extra_rows(margin_all, forward_all, width)


def merge_last(info, keep_ref, kmf_ref, got_ref, last_ref, far_ref, out_ref, conf_ref, scr):
    half, width = keep_ref.shape
    rows = kmf_ref.shape[1]
    margin, forward = kmf_ref[0:1, :], kmf_ref[1:2, :]
    first = got_ref.shape[0]
    margin_b, forward_b = read_extra(last_ref, half - first, rows)
    margin_c, forward_c = read_extra(far_ref, half, rows)
    margin_all = log_sum(margin, margin_b, margin_c)
    forward_all = log_sum(forward, forward_b, forward_c)
    scr[...] = columns(
        [jnp.exp2(margin - margin_all), jnp.exp2(margin_b - margin_all), jnp.exp2(margin_c - margin_all)], rows
    )
    factors = scr[pl.ds(pl.multiple_of(info[1] * half, 16), half), :]
    for at, ref in ((slice(0, first), got_ref), (slice(first, half), last_ref)):
        out = keep_ref[at, :] * factors[at, 0:1] + ref[: at.stop - at.start, :].astype(F32) * factors[at, 1:2]
        out_ref[at, :] = (out + far_ref[at, :].astype(F32) * factors[at, 2:3]).astype(BF16)
    conf_ref[...] = (margin_all - 0.5 * forward_all) * LN2


def shards(sources, targets, picks, cluster_home, row_count):
    n_src, n_tgt = lax.axis_size("src"), lax.axis_size("tgt")
    rows, width = sources.shape
    per_device, n_cols, _ = targets.shape
    n_clusters = cluster_home.shape[0]
    n_picks = picks.shape[1]
    capacity = -(-(2 * n_picks * rows // n_clusters) // 16) * 16
    side = n_src // 2
    half = rows // 2
    message = per_device * capacity
    n_buckets = side * per_device
    n_slots = n_buckets * capacity
    group = max(g for g in range(per_device, n_buckets + 1, per_device) if n_buckets % g == 0 and g * capacity <= 400)
    sds = jax.ShapeDtypeStruct

    me, core = lax.axis_index("src"), lax.axis_index("tgt")
    info = jnp.stack([me // side * side, core]).astype(jnp.int32)
    partner = [(i, (i + side) % n_src) for i in range(n_src)]
    twin = [(i, 1 - i) for i in range(n_tgt)]
    halves = [list(range(side)), list(range(side, n_src))]

    def exchange(x):
        return lax.all_to_all(x, "src", split_axis=0, concat_axis=0, axis_index_groups=halves, tiled=True)

    picks_t = picks.T
    home = cluster_home[None, :]
    letter = sds((half + EXTRA, width), BF16)
    far_mine = lax.ppermute(
        call(half_with_picks, letter, smem=1, n_in=3, moved=4 * half * width)(info, picks_t, sources), "src", partner
    )
    far_other = lax.ppermute(far_mine, "tgt", twin)

    sizes = dict(n_tgt=n_tgt, per_device=per_device, capacity=capacity, group=group)
    gather_out = (sds((side, message, width), BF16), sds((n_buckets, rows), F32))
    moved = 2 * (n_slots + rows) * width
    near_q, near_code = call(
        functools.partial(gather_own, **sizes), gather_out, smem=1, n_in=4, flops=2 * n_slots * rows * width, moved=moved
    )(info, picks_t, home, sources)
    near_in = exchange(near_q)
    far_q, far_code = call(
        functools.partial(gather_partner, n_picks=n_picks, **sizes),
        gather_out,
        [pltpu.VMEM((rows, width), BF16)],
        smem=1,
        n_in=4,
        flops=HIDE,
        moved=moved,
    )(info, home, far_mine, far_other)
    far_in = exchange(far_q)

    here = (me * n_tgt + core) * per_device + jnp.arange(per_device, dtype=jnp.int32)
    counts = jnp.sum(jnp.where(home == here[:, None], row_count[None, :], 0), axis=1)
    n_half = side * capacity
    options = dict(capacity=capacity, block=BLOCK)
    work = dict(flops=2 * n_slots * n_cols * width, moved=2 * (n_slots + per_device * n_cols) * width, limit=40)
    pooled = sds((side, message, width + 128), BF16)
    near_s, near_col, near_fwd = call(
        functools.partial(near_scores, **options),
        (
            sds((per_device, n_half, n_cols), F32),
            sds((per_device, 8, n_cols), F32),
            sds((per_device, n_half, 128), F32),
        ),
        smem=1,
        n_in=3,
        exps=2 * n_slots * n_cols,
        **work,
    )(counts, near_in, targets)
    weights = [pltpu.VMEM((n_half, n_cols), BF16), pltpu.VMEM((n_half, 128), BF16)]
    far_pool, reverse = call(
        functools.partial(far_owner, **options),
        (pooled, sds((per_device, 8, n_cols), F32)),
        [pltpu.VMEM((n_half, n_cols), F32)] + weights,
        smem=1,
        n_in=4,
        exps=3 * n_slots * n_cols,
        **work,
    )(counts, far_in, targets, near_col)
    back_far = exchange(far_pool)
    near_pool = call(
        functools.partial(near_owner, **options), pooled, weights, n_in=4, exps=n_slots * n_cols, **work
    )(near_s, reverse, near_fwd, targets)
    back_near = exchange(near_pool)

    def combine(code, back, after, pieces, weight):
        return pl.pallas_call(
            functools.partial(combine_kernel, capacity=capacity),
            out_shape=(sds((half, width), F32), sds((8, rows), F32)) + tuple(sds((n, width), BF16) for n in pieces),
            in_specs=[
                pl.BlockSpec(memory_space=pltpu.SMEM),
                pl.BlockSpec(memory_space=pltpu.VMEM),
                pl.BlockSpec(memory_space=pltpu.VMEM),
                pl.BlockSpec(memory_space=pl.ANY),
            ],
            out_specs=tuple([pl.BlockSpec(memory_space=pltpu.VMEM)] * (2 + len(pieces))),
            scratch_shapes=[pltpu.VMEM((rows, width), F32)],
            compiler_params=pltpu.CompilerParams(vmem_limit_bytes=40 * MIB),
            cost_estimate=pl.CostEstimate(
                flops=weight * 4 * n_slots * rows * width,
                bytes_accessed=weight * 2 * (n_slots + 2 * rows) * width,
                transcendentals=0,
            ),
        )(info, code, back, after)

    keep, kmf, send = combine(far_code, back_far, info, [half + EXTRA], 1)
    got = lax.ppermute(send, "tgt", twin)
    factors = [pltpu.VMEM((rows, 128), F32)]
    joined = call(merge_pair, letter, factors, smem=1, n_in=4, moved=10 * half * width)(info, keep, kmf, got)
    from_far = lax.ppermute(joined, "src", partner)

    first = half // 32 * 16
    keep, kmf, *send = combine(near_code, back_near, joined, [first, half - first + EXTRA], 0)
    got = [lax.ppermute(piece, "tgt", twin) for piece in send]
    mine, confidence = call(
        merge_last,
        (sds((half, width), BF16), sds((1, rows), F32)),
        factors,
        smem=1,
        n_in=6,
        moved=10 * half * width,
    )(info, keep, kmf, *got, from_far)
    other = lax.ppermute(mine, "tgt", twin)
    first = jnp.where(core == 0, mine, other)
    second = jnp.where(core == 0, other, mine)
    return (jnp.concatenate([first, second], axis=0), confidence[0].astype(BF16))


def solution(mesh):
    placed = (P("src", None), P(("src", "tgt"), None, None), P("src", None), P(), P())
    return jax.shard_map(
        shards, mesh=mesh, in_specs=placed, out_specs=(P("src", None), P("src")), check_vma=False
    )
```

time: 180 us -> 157 us (0.87)
  blocking collectives: 32.2 us -> 0 us
  local copies, waits for them, and re-layouts: 5.02 us -> 17.5 us
  waiting for transfers between devices: 80.3 us -> 69.4 us
  Pallas kernels: 34.1 us -> 43.8 us
  starting transfers between devices: 25.3 us -> 22.6 us
    all_to_all x2 -> x0, blocking collectives: 32.2 us -> none  [exchange(): lax.all_to_all(x, 'src', split_axis=0, concat_axis=0, axis_index_groups=h...]
    all_to_all x3 -> x4, waiting for transfers between devices: 32.8 us -> 54.8 us  [exchange(): lax.all_to_all(x, 'src', split_axis=0, concat_axis=0, axis_index_groups=h...]
    ppermute x1, waiting for transfers between devices: 21.5 us -> 0.01 us  [shards(): from_far = lax.ppermute(joined, 'src', partner)]
    ppermute x2 -> x3, waiting for transfers between devices: 24.5 us -> 10.2 us  [the longest x1 8.92 us: shards(): lax.ppermute(call(half_with_picks, letter, smem=1, n_in=3, moved=4 * half...]
    unnamed x20 -> x38, local copies, waits for them, and re-layouts: 4.51 us -> 17.5 us
    pallas_call x5 -> x8, Pallas kernels: 30.1 us -> 39.7 us  [the longest x1 11.2 us: shards(): call(functools.partial(far_owner, **options), (pooled, sds((per_device, 8...]
    ppermute x2 -> x3, starting transfers between devices: 6.03 us -> 4.67 us  [the longest x1 4.1 us: shards(): lax.ppermute(call(half_with_picks, letter, smem=1, n_in=3, moved=4 * half...]
    all_to_all x3 -> x4, starting transfers between devices: 18.7 us -> 17.5 us  [exchange(): lax.all_to_all(x, 'src', split_axis=0, concat_axis=0, axis_index_groups=h...]
  transfers between devices with their start and end apart: 10 -> 11, of which waited for: 7 -> 9; matrix products, arithmetic and copies ran while one was open for 1% -> 0% of each run, Pallas kernels for 6% -> 20%
where the time goes in v2:
time: 157 us; the launch traced here: 156 us
  waiting for transfers between devices  69.4 us (44%)
  Pallas kernels  43.8 us (28%)
  starting transfers between devices  22.6 us (14%)
  local copies, waits for them, and re-layouts  17.5 us (11%)
  other arithmetic  1.83 us (1%)
    all_to_all x4, waiting for transfers between devices, exchange(): lax.all_to_all(x, 'src', split_axis=0, concat_axis=0, axis_index_groups=h...  54.8 us
    unnamed x38, local copies, waits for them, and re-layouts  17.5 us
    all_to_all x4, starting transfers between devices, exchange(): lax.all_to_all(x, 'src', split_axis=0, concat_axis=0, axis_index_groups=h...  17.5 us
    pallas_call x1, Pallas kernels, shards(): call(functools.partial(far_owner, **options), (pooled, sds((per_device, 8...  11.2 us
    pallas_call x1, Pallas kernels, shards(): call(functools.partial(near_owner, **options), pooled, weights, n_in=4, e...  9.27 us
    ppermute x1, waiting for transfers between devices, shards(): lax.ppermute(call(half_with_picks, letter, smem=1, n_in=3, moved=4 * half...  8.92 us
    pallas_call x1, Pallas kernels, shards(): call(functools.partial(near_scores, **options), (sds((per_device, n_half,...  7.86 us
    pallas_call x2, Pallas kernels, combine(): pl.pallas_call(functools.partial(combine_kernel, capacity=capacity), out_...  6.93 us
  transfers between devices with their start and end apart: 11, of which 9 were waited for; matrix products, arithmetic and copies ran while one was open for 0% of the time, Pallas kernels for 20%

profile of v2, /device:TPU:0, one launch (start us, length us, event | category | flops | bytes accessed | tf_op | source)
XLA Modules:
  0.0 155.9 jit_solution(15644600741190182293)
XLA Ops:
  0.6 0.1 pad_add_fusion.info._
  0.7 0.0 copy-start.6
  0.7 1.1 copy-done.6
  1.9 0.0 copy-start.12
  1.9 0.7 copy-done.12
  2.5 0.6 shard_map.70
  3.1 4.1 %collective-permute-start = (bf16[208,1024]{1,0:T(8,128)(2,1)S(1)}, bf16[208,1024]{1,0:T(8,128)(2,1)S(1)}, u32[]{:S(2)}, u32[]{:S(2)}) collective-permute-start(bf16[208,1024]{1,0:T(8,128)(2,1)S(1)} %shard_map.70), channel_id=1, source_target_pairs={{0,16},{2,18},{4,20},{6,22},{8,24},{10,26},{12,28},{14,30},{16,0},... | collective-permute-start | bytes 1277960 | tf_op jit(solution)/shard_map/ppermute | solution.py:347
  7.2 0.0 copy-start.7
  7.2 1.1 copy-done.7
  8.4 0.0 copy-start.13
  8.4 0.7 copy-done.13
  9.0 3.0 %shard_map.68 = (bf16[8,96,1024]{2,1,0:T(8,128)(2,1)}, f32[16,384]{1,0:T(8,128)S(1)}) custom-call(s32[2]{0:T(128)S(1)} %pad_add_fusion.info._, s32[4,384]{1,0:T(4,128)S(1)} %bitcast.5, s32[1,64]{1,0:T(1,128)S(1)} %bitcast.6, bf16[384,1024]{1,0:T(8,128)(2,1)S(1)} %copy-done.7), custom_call_target="tpu_custom_call" | custom-call | flops 603979776 | bytes 2359296 | tf_op jit(solution)/shard_map/pallas_call | solution.py:355
  12.0 0.0 copy-start.10
  12.0 0.6 copy-done.10
  12.6 4.7 %all-to-all-start = ((bf16[8,96,1024]{2,1,0:T(8,128)(2,1)}), bf16[8,96,1024]{2,1,0:T(8,128)(2,1)S(1)}, u32[]{:S(2)}, u32[]{:S(2)}) async-start(bf16[8,96,1024]{2,1,0:T(8,128)(2,1)} %get-tuple-element.21), calls=%async_computation | async-start | bytes 3145728 | tf_op jit(solution)/shard_map/all_to_all | solution.py:342
  17.4 8.9 %collective-permute-done.mine_ref = bf16[208,1024]{1,0:T(8,128)(2,1)S(1)} collective-permute-done((bf16[208,1024]{1,0:T(8,128)(2,1)S(1)}, bf16[208,1024]{1,0:T(8,128)(2,1)S(1)}, u32[]{:S(2)}, u32[]{:S(2)}) %collective-permute-start) | collective-permute-done | bytes 426016 | tf_op jit(solution)/shard_map/ppermute | solution.py:347
  26.3 0.0 collective-permute-start.1
  26.3 1.8 %collective-permute-done.1.other_ref = bf16[208,1024]{1,0:T(8,128)(2,1)S(1)} collective-permute-done((bf16[208,1024]{1,0:T(8,128)(2,1)S(1)}, bf16[208,1024]{1,0:T(8,128)(2,1)S(1)}, u32[]{:S(2)}, u32[]{:S(2)}) %collective-permute-start.1) | collective-permute-done | bytes 426016 | tf_op jit(solution)/shard_map/ppermute | solution.py:350
  28.0 3.0 %shard_map.71 = (bf16[8,96,1024]{2,1,0:T(8,128)(2,1)}, f32[16,384]{1,0:T(8,128)S(1)}) custom-call(s32[2]{0:T(128)S(1)} %pad_add_fusion.info._, s32[1,64]{1,0:T(1,128)S(1)} %bitcast.7, bf16[208,1024]{1,0:T(8,128)(2,1)S(1)} %collective-permute-done.mine_ref, bf16[208,1024]{1,0:T(8,128)(2,1)S(1)} %collective-permute-done.1.other_ref), custom_call_target="tpu_custom_call" | custom-call | flops 23000000512 | bytes 2359296 | tf_op jit(solution)/shard_map/pallas_call | solution.py:359
  31.1 12.6 %all-to-all-done.q_ref = bf16[8,96,1024]{2,1,0:T(8,128)(2,1)S(1)} async-done(((bf16[8,96,1024]{2,1,0:T(8,128)(2,1)}), bf16[8,96,1024]{2,1,0:T(8,128)(2,1)S(1)}, u32[]{:S(2)}, u32[]{:S(2)}) %all-to-all-start) | async-done | bytes 1572896 | tf_op jit(solution)/shard_map/all_to_all | solution.py:342
  43.6 0.0 copy-done.16
  43.6 1.1 copy-done.4
  44.8 4.3 %all-to-all-start.1 = ((bf16[8,96,1024]{2,1,0:T(8,128)(2,1)}), bf16[8,96,1024]{2,1,0:T(8,128)(2,1)}, u32[]{:S(2)}, u32[]{:S(2)}) async-start(bf16[8,96,1024]{2,1,0:T(8,128)(2,1)} %get-tuple-element.23), calls=%async_computation.1 | async-start | bytes 3145728 | tf_op jit(solution)/shard_map/all_to_all | solution.py:342
  49.1 0.0 copy-done.18
  49.1 0.2 fusion.count_ref
  49.3 2.2 %copy-done = bf16[2,1024,1024]{2,1,0:T(8,128)(2,1)S(1)} copy-done((bf16[2,1024,1024]{2,1,0:T(8,128)(2,1)S(1)}, bf16[2,1024,1024]{2,1,0:T(8,128)(2,1)}, u32[]{:S(2)}) %copy-start) | copy-done | bytes 4194328
  51.5 1.4 copy-done.5
  52.9 7.9 %shard_map.69 = (f32[2,384,1024]{2,1,0:T(8,128)S(1)}, f32[2,8,1024]{2,1,0:T(8,128)S(1)}, f32[2,384,128]{2,1,0:T(8,128)S(1)}) custom-call(s32[2]{0:T(128)S(1)} %fusion.count_ref, bf16[8,96,1024]{2,1,0:T(8,128)(2,1)S(1)} %copy-done.5, bf16[2,1024,1024]{2,1,0:T(8,128)(2,1)S(1)} %copy-done), custom_call_target="tpu_custom_call" | custom-call | flops 1610612736 | bytes 5767168 | tf_op jit(solution)/shard_map/pallas_call | solution.py:376
  60.8 0.0 copy-start.14
  60.8 0.6 copy-done.14
  61.4 8.4 %all-to-all-done.1.q_ref = bf16[8,96,1024]{2,1,0:T(8,128)(2,1)} async-done(((bf16[8,96,1024]{2,1,0:T(8,128)(2,1)}), bf16[8,96,1024]{2,1,0:T(8,128)(2,1)}, u32[]{:S(2)}, u32[]{:S(2)}) %all-to-all-start.1) | async-done | bytes 1572896 | tf_op jit(solution)/shard_map/all_to_all | solution.py:342
  69.7 2.2 %copy-done.1 = bf16[2,1024,1024]{2,1,0:T(8,128)(2,1)S(1)} copy-done((bf16[2,1024,1024]{2,1,0:T(8,128)(2,1)S(1)}, bf16[2,1024,1024]{2,1,0:T(8,128)(2,1)}, u32[]{:S(2)}) %copy-start.1) | copy-done | bytes 4194328
  71.9 0.8 copy-done.15
  72.8 11.2 %shard_map.72 = (bf16[8,96,1152]{2,1,0:T(8,128)(2,1)S(1)}, f32[2,8,1024]{2,1,0:T(8,128)S(1)}) custom-call(s32[2]{0:T(128)S(1)} %fusion.count_ref, bf16[8,96,1024]{2,1,0:T(8,128)(2,1)} %all-to-all-done.1.q_ref, bf16[2,1024,1024]{2,1,0:T(8,128)(2,1)S(1)} %copy-done.1, f32[2,8,1024]{2,1,0:T(8,128)S(1)} %copy-done.15), custom_call_target="tpu_custom_call" | custom-call | flops 1610612736 | bytes 5767168 | tf_op jit(solution)/shard_map/pallas_call | solution.py:389
  83.9 0.0 copy-start.3
  84.0 1.2 copy-done.3
  85.2 0.6 copy-done.8
  85.8 4.6 %all-to-all-start.3 = ((bf16[8,96,1152]{2,1,0:T(8,128)(2,1)}), bf16[8,96,1152]{2,1,0:T(8,128)(2,1)}, u32[]{:S(2)}, u32[]{:S(2)}) async-start(bf16[8,96,1152]{2,1,0:T(8,128)(2,1)} %copy-done.3), calls=%async_computation.3 | async-start | bytes 3538944 | tf_op jit(solution)/shard_map/all_to_all | solution.py:342
  90.5 2.2 %copy-done.2 = bf16[2,1024,1024]{2,1,0:T(8,128)(2,1)S(1)} copy-done((bf16[2,1024,1024]{2,1,0:T(8,128)(2,1)S(1)}, bf16[2,1024,1024]{2,1,0:T(8,128)(2,1)}, u32[]{:S(2)}) %copy-start.2) | copy-done | bytes 4194328
  92.6 0.8 copy-done.9
  93.5 9.3 %shard_map.73 = bf16[8,96,1152]{2,1,0:T(8,128)(2,1)} custom-call(f32[2,384,1024]{2,1,0:T(8,128)S(1)} %get-tuple-element.22.s_ref, f32[2,8,1024]{2,1,0:T(8,128)S(1)} %copy-done.9, f32[2,384,128]{2,1,0:T(8,128)S(1)} %get-tuple-element.26.fwd_ref, bf16[2,1024,1024]{2,1,0:T(8,128)(2,1)S(1)} %copy-done.2), custom_call_target="tpu_custom_call" | custom-call | flops 1610612736 | bytes 5767168 | tf_op jit(solution)/shard_map/pallas_call | solution.py:399
  102.8 10.3 %all-to-all-done.3.r_ref = bf16[8,96,1152]{2,1,0:T(8,128)(2,1)} async-done(((bf16[8,96,1152]{2,1,0:T(8,128)(2,1)}), bf16[8,96,1152]{2,1,0:T(8,128)(2,1)}, u32[]{:S(2)}, u32[]{:S(2)}) %all-to-all-start.3) | async-done | bytes 1769504 | tf_op jit(solution)/shard_map/all_to_all | solution.py:342
  113.1 3.8 %all-to-all-start.2 = ((bf16[8,96,1152]{2,1,0:T(8,128)(2,1)}), bf16[8,96,1152]{2,1,0:T(8,128)(2,1)S(1)}, u32[]{:S(2)}, u32[]{:S(2)}) async-start(bf16[8,96,1152]{2,1,0:T(8,128)(2,1)} %shard_map.73), calls=%async_computation.2 | async-start | bytes 3538944 | tf_op jit(solution)/shard_map/all_to_all | solution.py:342
  116.8 0.0 copy-done.17
  116.8 3.9 %shard_map.74 = (f32[192,1024]{1,0:T(8,128)S(1)}, f32[8,384]{1,0:T(8,128)S(1)}, bf16[208,1024]{1,0:T(8,128)(2,1)S(1)}) custom-call(s32[2]{0:T(128)S(1)} %pad_add_fusion.info._, f32[16,384]{1,0:T(8,128)S(1)} %copy-done.17, bf16[8,96,1152]{2,1,0:T(8,128)(2,1)} %all-to-all-done.3.r_ref, s32[2]{0:T(128)S(1)} %pad_add_fusion.info._), custom_call_target="tpu_custom_call" | custom-call | flops 1207959552 | bytes 3145728 | tf_op jit(solution)/shard_map/pallas_call | solution.py:405
  120.8 0.0 copy-start.11
  120.8 0.1 collective-permute-start.2
  120.9 1.8 %collective-permute-done.2.got_ref = bf16[208,1024]{1,0:T(8,128)(2,1)S(1)} collective-permute-done((bf16[208,1024]{1,0:T(8,128)(2,1)S(1)}, bf16[208,1024]{1,0:T(8,128)(2,1)S(1)}, u32[]{:S(2)}, u32[]{:S(2)}) %collective-permute-start.2) | collective-permute-done | bytes 426016 | tf_op jit(solution)/shard_map/ppermute | solution.py:425
  122.6 0.9 shard_map.75._
  123.6 0.1 collective-permute-start.5
  123.7 23.6 %all-to-all-done.2.r_ref = bf16[8,96,1152]{2,1,0:T(8,128)(2,1)S(1)} async-done(((bf16[8,96,1152]{2,1,0:T(8,128)(2,1)}), bf16[8,96,1152]{2,1,0:T(8,128)(2,1)S(1)}, u32[]{:S(2)}, u32[]{:S(2)}) %all-to-all-start.2) | async-done | bytes 1769504 | tf_op jit(solution)/shard_map/all_to_all | solution.py:342
  147.2 0.0 copy-done.11
  147.2 3.0 %shard_map.76 = (f32[192,1024]{1,0:T(8,128)S(1)}, f32[8,384]{1,0:T(8,128)S(1)}, bf16[96,1024]{1,0:T(8,128)(2,1)S(1)}, bf16[112,1024]{1,0:T(8,128)(2,1)S(1)}) custom-call(s32[2]{0:T(128)S(1)} %pad_add_fusion.info._, f32[16,384]{1,0:T(8,128)S(1)} %copy-done.11, bf16[8,96,1152]{2,1,0:T(8,128)(2,1)S(1)} %all-to-all-done.2.r_ref, bf16[208,1024]{1,0:T(8,128)(2,1)S(1)} %shard_map.75._), custom_call_target="tpu_custom_call" | custom-call | tf_op jit(solution)/shard_map/pallas_call | solution.py:405
  150.2 0.1 collective-permute-start.4
  150.3 0.5 collective-permute-start.3
  150.8 1.3 collective-permute-done.3.got_ref
  152.1 0.0 collective-permute-done.4.last_ref
  152.1 0.0 collective-permute-done.5.far_ref
  152.1 1.0 shard_map.77
  153.1 0.3 collective-permute-start.6
  153.4 0.6 convert_reduce_fusion
  153.9 1.0 collective-permute-done.6
  154.9 0.1 broadcast_select_fusion.1
  155.0 0.9 pad_maximum_fusion
  (12 shorter events, 0.0 us)
Async XLA Ops:
  0.7 1.1 copy-start.6
  1.9 0.7 copy-start.12
  3.1 23.1 %collective-permute-start = (bf16[208,1024]{1,0:T(8,128)(2,1)S(1)}, bf16[208,1024]{1,0:T(8,128)(2,1)S(1)}, u32[]{:S(2)}, u32[]{:S(2)}) collective-permute-start(bf16[208,1024]{1,0:T(8,128)(2,1)S(1)} %shard_map.70), channel_id=1, source_target_pairs={{0,16},{2,18},{4,20},{6,22},{8,24},{10,26},{12,28},{14,30},{16,0},... | collective-permute-start | bytes 1277960 | tf_op jit(solution)/shard_map/ppermute | solution.py:347
  7.2 1.1 copy-start.7
  8.4 0.7 copy-start.13
  12.0 0.6 copy-start.10
  12.6 31.0 %all-to-all-start = ((bf16[8,96,1024]{2,1,0:T(8,128)(2,1)}), bf16[8,96,1024]{2,1,0:T(8,128)(2,1)S(1)}, u32[]{:S(2)}, u32[]{:S(2)}) async-start(bf16[8,96,1024]{2,1,0:T(8,128)(2,1)} %get-tuple-element.21), calls=%async_computation | async-start | bytes 3145728 | tf_op jit(solution)/shard_map/all_to_all | solution.py:342
  26.3 1.8 %collective-permute-start.1 = (bf16[208,1024]{1,0:T(8,128)(2,1)S(1)}, bf16[208,1024]{1,0:T(8,128)(2,1)S(1)}, u32[]{:S(2)}, u32[]{:S(2)}) collective-permute-start(bf16[208,1024]{1,0:T(8,128)(2,1)S(1)} %collective-permute-done.mine_ref), channel_id=1, source_target_pairs={{0,1},{1,0},{2,3},{3,2},{4,5},{5,4},{6,7},{7,6},{8,9},{9,8},{10,11... | collective-permute-start | bytes 1277960 | tf_op jit(solution)/shard_map/ppermute | solution.py:350
  31.0 12.6 %copy-start.16 = (f32[16,384]{1,0:T(8,128)}, f32[16,384]{1,0:T(8,128)S(1)}, u32[]{:S(2)}) copy-start(f32[16,384]{1,0:T(8,128)S(1)} %get-tuple-element.27.code_ref) | copy-start | bytes 73732
  43.6 1.2 copy-start.4
  43.6 5.5 %copy-start.18 = (s32[64]{0:T(128)S(1)}, s32[64]{0:T(128)}, u32[]{:S(2)}) copy-start(s32[64]{0:T(128)} %param.9) | copy-start | bytes 772
  44.8 25.0 %all-to-all-start.1 = ((bf16[8,96,1024]{2,1,0:T(8,128)(2,1)}), bf16[8,96,1024]{2,1,0:T(8,128)(2,1)}, u32[]{:S(2)}, u32[]{:S(2)}) async-start(bf16[8,96,1024]{2,1,0:T(8,128)(2,1)} %get-tuple-element.23), calls=%async_computation.1 | async-start | bytes 3145728 | tf_op jit(solution)/shard_map/all_to_all | solution.py:342
  49.3 2.2 %copy-start = (bf16[2,1024,1024]{2,1,0:T(8,128)(2,1)S(1)}, bf16[2,1024,1024]{2,1,0:T(8,128)(2,1)}, u32[]{:S(2)}) copy-start(bf16[2,1024,1024]{2,1,0:T(8,128)(2,1)} %t_ref.5) | copy-start | bytes 12582916
  51.5 1.4 copy-start.5
  60.8 0.6 copy-start.14
  69.7 2.2 %copy-start.1 = (bf16[2,1024,1024]{2,1,0:T(8,128)(2,1)S(1)}, bf16[2,1024,1024]{2,1,0:T(8,128)(2,1)}, u32[]{:S(2)}) copy-start(bf16[2,1024,1024]{2,1,0:T(8,128)(2,1)} %t_ref.5) | copy-start | bytes 12582916
  71.9 0.8 copy-start.15
  83.9 1.2 copy-start.3
  85.2 0.6 copy-start.8
  85.8 27.2 %all-to-all-start.3 = ((bf16[8,96,1152]{2,1,0:T(8,128)(2,1)}), bf16[8,96,1152]{2,1,0:T(8,128)(2,1)}, u32[]{:S(2)}, u32[]{:S(2)}) async-start(bf16[8,96,1152]{2,1,0:T(8,128)(2,1)} %copy-done.3), calls=%async_computation.3 | async-start | bytes 3538944 | tf_op jit(solution)/shard_map/all_to_all | solution.py:342
  90.5 2.2 %copy-start.2 = (bf16[2,1024,1024]{2,1,0:T(8,128)(2,1)S(1)}, bf16[2,1024,1024]{2,1,0:T(8,128)(2,1)}, u32[]{:S(2)}) copy-start(bf16[2,1024,1024]{2,1,0:T(8,128)(2,1)} %t_ref.5) | copy-start | bytes 12582916
  92.6 0.8 copy-start.9
  102.8 14.1 %copy-start.17 = (f32[16,384]{1,0:T(8,128)S(1)}, f32[16,384]{1,0:T(8,128)}, u32[]{:S(2)}) copy-start(f32[16,384]{1,0:T(8,128)} %copy-done.16) | copy-start | bytes 73732
  113.1 34.2 %all-to-all-start.2 = ((bf16[8,96,1152]{2,1,0:T(8,128)(2,1)}), bf16[8,96,1152]{2,1,0:T(8,128)(2,1)S(1)}, u32[]{:S(2)}, u32[]{:S(2)}) async-start(bf16[8,96,1152]{2,1,0:T(8,128)(2,1)} %shard_map.73), calls=%async_computation.2 | async-start | bytes 3538944 | tf_op jit(solution)/shard_map/all_to_all | solution.py:342
  120.8 26.4 %copy-start.11 = (f32[16,384]{1,0:T(8,128)S(1)}, f32[16,384]{1,0:T(8,128)}, u32[]{:S(2)}) copy-start(f32[16,384]{1,0:T(8,128)} %copy-done.10) | copy-start | bytes 73732
  120.8 1.8 %collective-permute-start.2 = (bf16[208,1024]{1,0:T(8,128)(2,1)S(1)}, bf16[208,1024]{1,0:T(8,128)(2,1)S(1)}, u32[]{:S(2)}, u32[]{:S(2)}) collective-permute-start(bf16[208,1024]{1,0:T(8,128)(2,1)S(1)} %get-tuple-element.31), channel_id=1, source_target_pairs={{0,1},{1,0},{2,3},{3,2},{4,5},{5,4},{6,7},{7,6},{8,9},{9,8},{10,11... | collective-permute-start | bytes 1277960 | tf_op jit(solution)/shard_map/ppermute | solution.py:425
  123.6 28.5 %collective-permute-start.5 = (bf16[208,1024]{1,0:T(8,128)(2,1)S(1)}, bf16[208,1024]{1,0:T(8,128)(2,1)S(1)}, u32[]{:S(2)}, u32[]{:S(2)}) collective-permute-start(bf16[208,1024]{1,0:T(8,128)(2,1)S(1)} %shard_map.75._), channel_id=1, source_target_pairs={{0,16},{2,18},{4,20},{6,22},{8,24},{10,26},{12,28},{14,30},{16,0},... | collective-permute-start | bytes 1277960 | tf_op jit(solution)/shard_map/ppermute | solution.py:428
  150.2 1.8 %collective-permute-start.4 = (bf16[112,1024]{1,0:T(8,128)(2,1)S(1)}, bf16[112,1024]{1,0:T(8,128)(2,1)S(1)}, u32[]{:S(2)}, u32[]{:S(2)}) collective-permute-start(bf16[112,1024]{1,0:T(8,128)(2,1)S(1)} %get-tuple-element.35), channel_id=1, source_target_pairs={{0,1},{1,0},{2,3},{3,2},{4,5},{5,4},{6,7},{7,6},{8,9},{9,8},{10,11... | collective-permute-start | bytes 688136 | tf_op jit(solution)/shard_map/ppermute | solution.py:432
  150.3 1.8 %collective-permute-start.3 = (bf16[96,1024]{1,0:T(8,128)(2,1)S(1)}, bf16[96,1024]{1,0:T(8,128)(2,1)S(1)}, u32[]{:S(2)}, u32[]{:S(2)}) collective-permute-start(bf16[96,1024]{1,0:T(8,128)(2,1)S(1)} %get-tuple-element.34), channel_id=1, source_target_pairs={{0,1},{1,0},{2,3},{3,2},{4,5},{5,4},{6,7},{7,6},{8,9},{9,8},{10,11... | collective-permute-start | bytes 589832 | tf_op jit(solution)/shard_map/ppermute | solution.py:432
  153.1 1.8 %collective-permute-start.6 = (bf16[192,1024]{1,0:T(8,128)(2,1)S(1)}, bf16[192,1024]{1,0:T(8,128)(2,1)S(1)}, u32[]{:S(2)}, u32[]{:S(2)}) collective-permute-start(bf16[192,1024]{1,0:T(8,128)(2,1)S(1)} %get-tuple-element.36), channel_id=1, source_target_pairs={{0,1},{1,0},{2,3},{3,2},{4,5},{5,4},{6,7},{7,6},{8,9},{9,8},{10,11... | collective-permute-start | bytes 1179656 | tf_op jit(solution)/shard_map/ppermute | solution.py:441

commit v3 on v2

--- a/solution.py
+++ b/solution.py
@@ -15,7 +15,10 @@
 MIB = 1 << 20
 LOG2E = math.log2(math.e)
 LN2 = math.log(2.0)
-BLOCK = 32
+BLOCK = 128
+ROW_GROUPS = 8
+LIMIT = 24
+FULL = 63
 HIDE = 23_000_000_000
 
 
@@ -23,7 +26,7 @@
     return lax.broadcasted_iota(jnp.int32, shape, axis)
 
 
-def call(kernel, out_shape, scratch=(), smem=0, n_in=0, limit=32, flops=0, moved=0, exps=0, **kw):
+def call(kernel, out_shape, scratch=(), smem=0, n_in=0, limit=LIMIT, flops=0, moved=0, exps=0, **kw):
     if not kw:
         kw = dict(
             in_specs=[pl.BlockSpec(memory_space=pltpu.SMEM)] * smem
@@ -73,7 +76,9 @@
     )
 
 
-def gather_body(info, picks, home_ref, source, q_ref, code_ref, *, n_tgt, per_device, capacity, group):
+def gather_body(
+    info, picks, home_ref, source, q_hbm, code_hbm, q_ref, code_ref, sem, *, n_tgt, per_device, capacity, group
+):
     n_buckets, rows = code_ref.shape
     n_clusters = home_ref.shape[1]
     width = q_ref.shape[2]
@@ -90,6 +95,8 @@
     rank = jnp.dot(inside.astype(BF16), earlier, preferred_element_type=F32)
     code = jnp.where(inside > 0.5, rank, -1.0)
     code_ref[...] = code
+    leave = [pltpu.make_async_copy(code_ref, code_hbm, sem.at[0])]
+    leave[0].start()
     per_message = group // per_device
     for start in range(0, n_buckets, group):
         slots = one_hot_slots(code, start, group, capacity)
@@ -99,7 +106,12 @@
         head = jnp.where((iota(head.shape, 1) == 0) & (filled < 0.5), jnp.inf, head)
         found = jnp.concatenate([head, found[:, 128:]], axis=1).astype(BF16)
         d = start // per_device
-        q_ref[d : d + per_message] = found.reshape(per_message, per_device * capacity, width)
+        at = pl.ds(d, per_message)
+        q_ref[at] = found.reshape(per_message, per_device * capacity, width)
+        leave.append(pltpu.make_async_copy(q_ref.at[at], q_hbm.at[at], sem.at[1 + start // group]))
+        leave[-1].start()
+    for copy in leave:
+        copy.wait()
 
 
 def half_with_picks(info, picks_ref, src_ref, out_ref):
@@ -112,25 +124,25 @@
     out_ref[half:, :] = jnp.concatenate([body, rest], axis=1).astype(BF16)
 
 
-def gather_own(info, picks_ref, home_ref, src_ref, q_ref, code_ref, **sizes):
+def gather_own(info, picks_ref, home_ref, src_ref, *refs, **sizes):
     picks = [picks_ref[k : k + 1, :].astype(F32) for k in range(picks_ref.shape[0])]
-    gather_body(info, picks, home_ref, src_ref[...], q_ref, code_ref, **sizes)
-
-
-def gather_partner(info, home_ref, mine_ref, other_ref, q_ref, code_ref, src_ref, *, n_picks, **sizes):
+    gather_body(info, picks, home_ref, src_ref[...], *refs, **sizes)
+
+
+def gather_partner(info, home_ref, mine_ref, other_ref, *refs, n_picks, **sizes):
+    *refs, src_ref = refs
     rows = src_ref.shape[0]
     half = rows // 2
     src_ref[pl.ds(pl.multiple_of(info[1] * half, 16), half), :] = mine_ref[:half, :]
     src_ref[pl.ds(pl.multiple_of((1 - info[1]) * half, 16), half), :] = other_ref[:half, :]
     block = mine_ref[half : half + EXTRA, :rows].astype(F32)
     picks = [block[k : k + 1, :] for k in range(n_picks)]
-    gather_body(info, picks, home_ref, src_ref[...], q_ref, code_ref, **sizes)
-
-
-def scores_of(q_ref, t, count, l, capacity):
-    width = q_ref.shape[2]
+    gather_body(info, picks, home_ref, src_ref[...], *refs, **sizes)
+
+
+def scores_of(q, t, count):
+    width = q.shape[1]
     n_cols = t.shape[0]
-    q = q_ref[:, l * capacity : (l + 1) * capacity, :].reshape(-1, width)
     head = q[:, :128].astype(F32)
     empty = head > 1e38
     q = jnp.concatenate([jnp.where(empty, 0.0, head).astype(BF16), q[:, 128:]], axis=1)
@@ -142,12 +154,10 @@
 
 def column_part(s_ref, highest, block):
     n_rows, n_cols = s_ref.shape
-
-    def add(i, total):
-        part = jnp.exp2(s_ref[pl.ds(pl.multiple_of(i * block, block), block), :] - highest)
-        return total + jnp.sum(part.reshape(block // 8, 8, n_cols), axis=0)
-
-    total = lax.fori_loop(0, n_rows // block, add, jnp.zeros((8, n_cols), F32))
+    total = jnp.zeros((8, n_cols), F32)
+    for start in range(0, n_rows, block):
+        part = jnp.exp2(s_ref[start : start + block, :] - highest)
+        total = total + jnp.sum(part.reshape(block // 8, 8, n_cols), axis=0)
     return jnp.sum(total, axis=0, keepdims=True)
 
 
@@ -174,7 +184,8 @@
 def near_scores(count_ref, q_ref, t_ref, s_ref, col_ref, fwd_ref, *, capacity, block):
     per_device, n_half, n_cols = s_ref.shape
     for l in range(per_device):
-        s = scores_of(q_ref, t_ref[l], count_ref[l], l, capacity)
+        q = q_ref[:, l * capacity : (l + 1) * capacity, :].reshape(n_half, -1)
+        s = scores_of(q, t_ref[l], count_ref[l])
         s_ref[l] = s
         highest = jnp.max(s, axis=0, keepdims=True)
         total = column_part(s_ref.at[l], highest, block)
@@ -188,35 +199,48 @@
         lax.fori_loop(0, n_half // block, forward, 0)
 
 
-def far_owner(count_ref, q_ref, t_ref, col_ref, p_ref, rev_ref, s_ref, w_ref, tail_ref, *, capacity, block):
-    n_msg, _, full = p_ref.shape
-    per_device = t_ref.shape[0]
-    n_half, n_cols = s_ref.shape
-    width = full - 128
+def far_owner(
+    count_ref, q_hbm, t_hbm, col_ref, p_hbm, rev_hbm, q_ref, t_ref, s_ref, w_ref, p_ref, rev_ref, sems, rev_sem, *, block
+):
+    per_device, n_msg, capacity, width = q_ref.shape
+    _, n_half, n_cols = s_ref.shape
+    places = [pl.ds(l * capacity, capacity) for l in range(per_device)]
+    arrive = []
+    for l, at in enumerate(places):
+        arrive.append(pltpu.make_async_copy(q_hbm.at[:, at, :], q_ref.at[l], sems.at[0, l]))
+        arrive.append(pltpu.make_async_copy(t_hbm.at[l], t_ref.at[l], sems.at[1, l]))
+    for copy in arrive:
+        copy.start()
+    rev_leave = pltpu.make_async_copy(rev_ref, rev_hbm, rev_sem)
+    leave = [pltpu.make_async_copy(p_ref.at[l], p_hbm.at[:, at, :], sems.at[2, l]) for l, at in enumerate(places)]
+    half_reverse = []
     for l in range(per_device):
-        s = scores_of(q_ref, t_ref[l], count_ref[l], l, capacity)
-        s_ref[...] = s
+        arrive[2 * l].wait()
+        arrive[2 * l + 1].wait()
+        s = scores_of(q_ref[l].reshape(n_half, width), t_ref[l], count_ref[l])
+        s_ref[l] = s
         highest = jnp.max(s, axis=0, keepdims=True)
-        total = column_part(s_ref, highest, block)
+        total = column_part(s_ref.at[l], highest, block)
         top = jnp.maximum(highest, col_ref[l, 0:1, :])
         total = total * jnp.exp2(highest - top) + col_ref[l, 1:2, :] * jnp.exp2(col_ref[l, 0:1, :] - top)
-        half_reverse = 0.5 * (top + jnp.log2(total))
-        rev_ref[l] = jnp.broadcast_to(half_reverse, (8, n_cols))
-
-        def rows(i, _):
-            at = pl.ds(pl.multiple_of(i * block, block), block)
-            s = s_ref[at, :]
+        half_reverse.append(0.5 * (top + jnp.log2(total)))
+        rev_ref[l] = jnp.broadcast_to(half_reverse[l], (8, n_cols))
+    rev_leave.start()
+    for l in range(per_device):
+        for start in range(0, n_half, block):
+            at = slice(start, start + block)
+            s = s_ref[l, at, :]
             forward = row_log_sum(s)
-            w, margin = weigh(s, half_reverse)
-            w_ref[at, :] = w
-            tail_ref[at, :] = tail(margin, forward, iota((block, 128), 1))
-            return 0
-
-        lax.fori_loop(0, n_half // block, rows, 0)
-        at = slice(l * capacity, (l + 1) * capacity)
-        p = jnp.dot(w_ref[...], t_ref[l], preferred_element_type=F32)
-        p_ref[:, at, :width] = p.astype(BF16).reshape(n_msg, capacity, width)
-        p_ref[:, at, width:] = tail_ref[...].reshape(n_msg, capacity, 128)
+            w, margin = weigh(s, half_reverse[l])
+            w_ref[l, at, :] = w
+            part = tail(margin, forward, iota((block, 128), 1))
+            first = start // capacity
+            p_ref[l, first : first + block // capacity, :, width:] = part.reshape(block // capacity, capacity, 128)
+        p = jnp.dot(w_ref[l], t_ref[l], preferred_element_type=F32)
+        p_ref[l, :, :, :width] = p.astype(BF16).reshape(n_msg, capacity, width)
+        leave[l].start()
+    for copy in leave + [rev_leave]:
+        copy.wait()
 
 
 def near_owner(s_ref, rev_ref, fwd_ref, t_ref, p_ref, w_ref, tail_ref, *, capacity, block):
@@ -345,25 +369,41 @@
     home = cluster_home[None, :]
     letter = sds((half + EXTRA, width), BF16)
     far_mine = lax.ppermute(
-        call(half_with_picks, letter, smem=1, n_in=3, moved=4 * half * width)(info, picks_t, sources), "src", partner
+        call(half_with_picks, letter, smem=1, n_in=3, moved=4 * half * width, limit=FULL)(info, picks_t, sources), "src", partner
     )
     far_other = lax.ppermute(far_mine, "tgt", twin)
 
     sizes = dict(n_tgt=n_tgt, per_device=per_device, capacity=capacity, group=group)
     gather_out = (sds((side, message, width), BF16), sds((n_buckets, rows), F32))
     moved = 2 * (n_slots + rows) * width
+    hbm = pl.BlockSpec(memory_space=pltpu.HBM)
+    vmem = pl.BlockSpec(memory_space=pltpu.VMEM)
+    smem = pl.BlockSpec(memory_space=pltpu.SMEM)
+    gather_scratch = [
+        pltpu.VMEM((side, message, width), BF16),
+        pltpu.VMEM((n_buckets, rows), F32),
+        pltpu.SemaphoreType.DMA((1 + n_buckets // group,)),
+    ]
     near_q, near_code = call(
-        functools.partial(gather_own, **sizes), gather_out, smem=1, n_in=4, flops=2 * n_slots * rows * width, moved=moved
+        functools.partial(gather_own, **sizes),
+        gather_out,
+        gather_scratch,
+        flops=2 * n_slots * rows * width,
+        moved=moved,
+        limit=FULL,
+        in_specs=[smem] + [vmem] * 3,
+        out_specs=(hbm, hbm),
     )(info, picks_t, home, sources)
     near_in = exchange(near_q)
     far_q, far_code = call(
         functools.partial(gather_partner, n_picks=n_picks, **sizes),
         gather_out,
-        [pltpu.VMEM((rows, width), BF16)],
-        smem=1,
-        n_in=4,
+        gather_scratch + [pltpu.VMEM((rows, width), BF16)],
         flops=HIDE,
         moved=moved,
+        limit=FULL,
+        in_specs=[smem] + [vmem] * 3,
+        out_specs=(hbm, hbm),
     )(info, home, far_mine, far_other)
     far_in = exchange(far_q)
 
@@ -371,7 +411,7 @@
     counts = jnp.sum(jnp.where(home == here[:, None], row_count[None, :], 0), axis=1)
     n_half = side * capacity
     options = dict(capacity=capacity, block=BLOCK)
-    work = dict(flops=2 * n_slots * n_cols * width, moved=2 * (n_slots + per_device * n_cols) * width, limit=40)
+    work = dict(flops=2 * n_slots * n_cols * width, moved=2 * (n_slots + per_device * n_cols) * width)
     pooled = sds((side, message, width + 128), BF16)
     near_s, near_col, near_fwd = call(
         functools.partial(near_scores, **options),
@@ -382,17 +422,28 @@
         ),
         smem=1,
         n_in=3,
+        limit=FULL,
         exps=2 * n_slots * n_cols,
         **work,
     )(counts, near_in, targets)
     weights = [pltpu.VMEM((n_half, n_cols), BF16), pltpu.VMEM((n_half, 128), BF16)]
     far_pool, reverse = call(
-        functools.partial(far_owner, **options),
+        functools.partial(far_owner, block=capacity * math.gcd(side, ROW_GROUPS)),
         (pooled, sds((per_device, 8, n_cols), F32)),
-        [pltpu.VMEM((n_half, n_cols), F32)] + weights,
-        smem=1,
-        n_in=4,
+        [
+            pltpu.VMEM((per_device, side, capacity, width), BF16),
+            pltpu.VMEM((per_device, n_cols, width), BF16),
+            pltpu.VMEM((per_device, n_half, n_cols), F32),
+            pltpu.VMEM((per_device, n_half, n_cols), BF16),
+            pltpu.VMEM((per_device, side, capacity, width + 128), BF16),
+            pltpu.VMEM((per_device, 8, n_cols), F32),
+            pltpu.SemaphoreType.DMA((3, per_device)),
+            pltpu.SemaphoreType.DMA,
+        ],
+        limit=FULL,
         exps=3 * n_slots * n_cols,
+        in_specs=[smem, hbm, hbm, vmem],
+        out_specs=(hbm, hbm),
         **work,
     )(counts, far_in, targets, near_col)
     back_far = exchange(far_pool)
@@ -413,7 +464,7 @@
             ],
             out_specs=tuple([pl.BlockSpec(memory_space=pltpu.VMEM)] * (2 + len(pieces))),
             scratch_shapes=[pltpu.VMEM((rows, width), F32)],
-            compiler_params=pltpu.CompilerParams(vmem_limit_bytes=40 * MIB),
+            compiler_params=pltpu.CompilerParams(vmem_limit_bytes=LIMIT * MIB),
             cost_estimate=pl.CostEstimate(
                 flops=weight * 4 * n_slots * rows * width,
                 bytes_accessed=weight * 2 * (n_slots + 2 * rows) * width,

time: 157 us -> 146 us (0.930)
  local copies, waits for them, and re-layouts: 17.5 us -> 3.84 us
  waiting for transfers between devices: 69.4 us -> 76.1 us
  Pallas kernels: 43.8 us -> 39.2 us
    unnamed x38 -> x22, local copies, waits for them, and re-layouts: 17.5 us -> 3.84 us
    all_to_all x4, waiting for transfers between devices: 54.8 us -> 59.3 us  [exchange(): lax.all_to_all(x, 'src', split_axis=0, concat_axis=0, axis_index_groups=h...]
    pallas_call x1, Pallas kernels: 9.27 us -> 4.79 us  [shards(): call(functools.partial(near_owner, **options), pooled, weights, n_in=4, e...]
    ppermute x1, waiting for transfers between devices: 8.92 us -> 11.1 us  [shards(): lax.ppermute(call(half_with_picks, letter, smem=1, n_in=3, moved=4 * half...]
  transfers between devices with their start and end apart: 11 -> 11, of which waited for: 9 -> 9; matrix products, arithmetic and copies ran while one was open for 0% -> 1% of each run, Pallas kernels for 20% -> 19%
where the time goes in v3:
time: 146 us
  waiting for transfers between devices  76.1 us (52%)
  Pallas kernels  39.2 us (27%)
  starting transfers between devices  22.7 us (16%)
  local copies, waits for them, and re-layouts  3.84 us (3%)
  other arithmetic  2.95 us (2%)
    all_to_all x4, waiting for transfers between devices, exchange(): lax.all_to_all(x, 'src', split_axis=0, concat_axis=0, axis_index_groups=h...  59.3 us
    all_to_all x4, starting transfers between devices, exchange(): lax.all_to_all(x, 'src', split_axis=0, concat_axis=0, axis_index_groups=h...  17.7 us
    ppermute x1, waiting for transfers between devices, shards(): lax.ppermute(call(half_with_picks, letter, smem=1, n_in=3, moved=4 * half...  11.1 us
    pallas_call x1, Pallas kernels, shards(): call(functools.partial(far_owner, block=capacity * math.gcd(side, ROW_GRO...  8.53 us
    pallas_call x1, Pallas kernels, shards(): call(functools.partial(near_scores, **options), (sds((per_device, n_half,...  8.22 us
    pallas_call x2, Pallas kernels, combine(): pl.pallas_call(functools.partial(combine_kernel, capacity=capacity), out_...  7.01 us
    pallas_call x1, Pallas kernels, shards(): call(functools.partial(near_owner, **options), pooled, weights, n_in=4, e...  4.79 us
    ppermute x1, starting transfers between devices, shards(): lax.ppermute(call(half_with_picks, letter, smem=1, n_in=3, moved=4 * half...  4.04 us
  transfers between devices with their start and end apart: 11, of which 9 were waited for; matrix products, arithmetic and copies ran while one was open for 1% of the time, Pallas kernels for 19%

profile of v3, /device:TPU:0, one launch (start us, length us, event | category | flops | bytes accessed | tf_op | source)
XLA Modules:
  0.0 145.7 jit_solution(648006110330571367)
XLA Ops:
  0.6 0.6 pad_add_fusion.info._
  1.3 1.9 %shard_map.70 = bf16[208,1024]{1,0:T(8,128)(2,1)} custom-call(s32[2]{0:T(128)} %pad_add_fusion.info._, s32[4,384]{1,0:T(4,128)} %bitcast.4, bf16[384,1024]{1,0:T(8,128)(2,1)} %src_ref.3), custom_call_target="tpu_custom_call" | custom-call | bytes 786432 | tf_op jit(solution)/shard_map/pallas_call | solution.py:372
  3.2 4.0 %collective-permute-start = (bf16[208,1024]{1,0:T(8,128)(2,1)}, bf16[208,1024]{1,0:T(8,128)(2,1)S(1)}, u32[]{:S(2)}, u32[]{:S(2)}) collective-permute-start(bf16[208,1024]{1,0:T(8,128)(2,1)} %shard_map.70), channel_id=1, source_target_pairs={{0,16},{2,18},{4,20},{6,22},{8,24},{10,26},{12,28},{14,30},{16,0},... | collective-permute-start | bytes 1277960 | tf_op jit(solution)/shard_map/ppermute | solution.py:371
  7.2 3.4 %shard_map.68 = (bf16[8,96,1024]{2,1,0:T(8,128)(2,1)}, f32[16,384]{1,0:T(8,128)}) custom-call(s32[2]{0:T(128)} %pad_add_fusion.info._, s32[4,384]{1,0:T(4,128)} %bitcast.5, s32[1,64]{1,0:T(1,128)} %bitcast.6, bf16[384,1024]{1,0:T(8,128)(2,1)} %src_ref.3), custom_call_target="tpu_custom_call" | custom-call | flops 603979776 | bytes 2359296 | tf_op jit(solution)/shard_map/pallas_call | solution.py:387
  10.7 4.7 %all-to-all-start = ((bf16[8,96,1024]{2,1,0:T(8,128)(2,1)}), bf16[8,96,1024]{2,1,0:T(8,128)(2,1)}, u32[]{:S(2)}, u32[]{:S(2)}) async-start(bf16[8,96,1024]{2,1,0:T(8,128)(2,1)} %get-tuple-element.21), calls=%async_computation | async-start | bytes 3145728 | tf_op jit(solution)/shard_map/all_to_all | solution.py:366
  15.4 11.1 %collective-permute-done.mine_ref = bf16[208,1024]{1,0:T(8,128)(2,1)S(1)} collective-permute-done((bf16[208,1024]{1,0:T(8,128)(2,1)}, bf16[208,1024]{1,0:T(8,128)(2,1)S(1)}, u32[]{:S(2)}, u32[]{:S(2)}) %collective-permute-start) | collective-permute-done | bytes 426016 | tf_op jit(solution)/shard_map/ppermute | solution.py:371
  26.5 0.0 copy-start.9
  26.5 0.0 collective-permute-start.1
  26.5 1.8 %collective-permute-done.1.other_ref = bf16[208,1024]{1,0:T(8,128)(2,1)S(1)} collective-permute-done((bf16[208,1024]{1,0:T(8,128)(2,1)S(1)}, bf16[208,1024]{1,0:T(8,128)(2,1)S(1)}, u32[]{:S(2)}, u32[]{:S(2)}) %collective-permute-start.1) | collective-permute-done | bytes 426016 | tf_op jit(solution)/shard_map/ppermute | solution.py:374
  28.3 0.0 copy-done.9
  28.3 0.0 copy-start.10
  28.3 0.8 copy-done.10
  29.1 3.4 %shard_map.71 = (bf16[8,96,1024]{2,1,0:T(8,128)(2,1)}, f32[16,384]{1,0:T(8,128)}) custom-call(s32[2]{0:T(128)} %pad_add_fusion.info._, s32[1,64]{1,0:T(1,128)} %bitcast.7, bf16[208,1024]{1,0:T(8,128)(2,1)} %copy-done.9, bf16[208,1024]{1,0:T(8,128)(2,1)} %copy-done.10), custom_call_target="tpu_custom_call" | custom-call | flops 23000000512 | bytes 2359296 | tf_op jit(solution)/shard_map/pallas_call | solution.py:398
  32.4 9.9 %all-to-all-done.q_ref = bf16[8,96,1024]{2,1,0:T(8,128)(2,1)} async-done(((bf16[8,96,1024]{2,1,0:T(8,128)(2,1)}), bf16[8,96,1024]{2,1,0:T(8,128)(2,1)}, u32[]{:S(2)}, u32[]{:S(2)}) %all-to-all-start) | async-done | bytes 1572896 | tf_op jit(solution)/shard_map/all_to_all | solution.py:366
  42.4 0.0 copy-start.7
  42.4 0.0 copy-start.8
  42.4 4.4 %all-to-all-start.1 = ((bf16[8,96,1024]{2,1,0:T(8,128)(2,1)}), bf16[8,96,1024]{2,1,0:T(8,128)(2,1)}, u32[]{:S(2)}, u32[]{:S(2)}) async-start(bf16[8,96,1024]{2,1,0:T(8,128)(2,1)} %get-tuple-element.23), calls=%async_computation.1 | async-start | bytes 3145728 | tf_op jit(solution)/shard_map/all_to_all | solution.py:366
  46.8 0.0 copy-done.7
  46.8 0.0 copy-done.8
  46.8 0.8 fusion.count_ref
  47.6 8.2 %shard_map.69 = (f32[2,384,1024]{2,1,0:T(8,128)}, f32[2,8,1024]{2,1,0:T(8,128)}, f32[2,384,128]{2,1,0:T(8,128)}) custom-call(s32[2]{0:T(128)} %fusion.count_ref, bf16[8,96,1024]{2,1,0:T(8,128)(2,1)} %all-to-all-done.q_ref, bf16[2,1024,1024]{2,1,0:T(8,128)(2,1)} %t_ref.3), custom_call_target="tpu_custom_call" | custom-call | flops 1610612736 | bytes 5767168 | tf_op jit(solution)/shard_map/pallas_call | solution.py:416
  55.8 11.1 %all-to-all-done.1.q_hbm = bf16[8,96,1024]{2,1,0:T(8,128)(2,1)} async-done(((bf16[8,96,1024]{2,1,0:T(8,128)(2,1)}), bf16[8,96,1024]{2,1,0:T(8,128)(2,1)}, u32[]{:S(2)}, u32[]{:S(2)}) %all-to-all-start.1) | async-done | bytes 1572896 | tf_op jit(solution)/shard_map/all_to_all | solution.py:366
  66.9 8.5 %shard_map.72 = (bf16[8,96,1152]{2,1,0:T(8,128)(2,1)}, f32[2,8,1024]{2,1,0:T(8,128)}) custom-call(s32[2]{0:T(128)} %fusion.count_ref, bf16[8,96,1024]{2,1,0:T(8,128)(2,1)} %all-to-all-done.1.q_hbm, bf16[2,1024,1024]{2,1,0:T(8,128)(2,1)} %t_ref.3, f32[2,8,1024]{2,1,0:T(8,128)} %get-tuple-element.24.col_ref), custom_call_target="tpu_custom_call" | custom-call | flops 1610612736 | bytes 5767168 | tf_op jit(solution)/shard_map/pallas_call | solution.py:430
  75.5 0.0 copy-start.1
  75.5 0.0 copy-start.2
  75.5 4.6 %all-to-all-start.3 = ((bf16[8,96,1152]{2,1,0:T(8,128)(2,1)}), bf16[8,96,1152]{2,1,0:T(8,128)(2,1)}, u32[]{:S(2)}, u32[]{:S(2)}) async-start(bf16[8,96,1152]{2,1,0:T(8,128)(2,1)} %get-tuple-element.28), calls=%async_computation.3 | async-start | bytes 3538944 | tf_op jit(solution)/shard_map/all_to_all | solution.py:366
  80.1 0.0 copy-done.1
  80.1 0.0 copy-done.2
  80.1 0.0 copy-start
  80.1 2.2 %copy-done = bf16[2,1024,1024]{2,1,0:T(8,128)(2,1)S(1)} copy-done((bf16[2,1024,1024]{2,1,0:T(8,128)(2,1)S(1)}, bf16[2,1024,1024]{2,1,0:T(8,128)(2,1)}, u32[]{:S(2)}) %copy-start) | copy-done | bytes 4194328
  82.3 0.0 copy-start.3
  82.3 0.8 copy-done.3
  83.2 4.8 %shard_map.73 = bf16[8,96,1152]{2,1,0:T(8,128)(2,1)} custom-call(f32[2,384,1024]{2,1,0:T(8,128)S(1)} %copy-done.1, f32[2,8,1024]{2,1,0:T(8,128)S(1)} %copy-done.3, f32[2,384,128]{2,1,0:T(8,128)S(1)} %copy-done.2, bf16[2,1024,1024]{2,1,0:T(8,128)(2,1)S(1)} %copy-done), custom_call_target="tpu_custom_call" | custom-call | flops 1610612736 | bytes 5767168 | tf_op jit(solution)/shard_map/pallas_call | solution.py:450
  87.9 0.0 copy-start.5
  87.9 0.0 copy-start.6
  87.9 14.4 %all-to-all-done.3.r_ref = bf16[8,96,1152]{2,1,0:T(8,128)(2,1)} async-done(((bf16[8,96,1152]{2,1,0:T(8,128)(2,1)}), bf16[8,96,1152]{2,1,0:T(8,128)(2,1)}, u32[]{:S(2)}, u32[]{:S(2)}) %all-to-all-start.3) | async-done | bytes 1769504 | tf_op jit(solution)/shard_map/all_to_all | solution.py:366
  102.3 3.9 %all-to-all-start.2 = ((bf16[8,96,1152]{2,1,0:T(8,128)(2,1)}), bf16[8,96,1152]{2,1,0:T(8,128)(2,1)S(1)}, u32[]{:S(2)}, u32[]{:S(2)}) async-start(bf16[8,96,1152]{2,1,0:T(8,128)(2,1)} %shard_map.73), calls=%async_computation.2 | async-start | bytes 3538944 | tf_op jit(solution)/shard_map/all_to_all | solution.py:366
  106.3 0.0 copy-done.5
  106.3 0.0 copy-done.6
  106.3 4.0 %shard_map.74 = (f32[192,1024]{1,0:T(8,128)S(1)}, f32[8,384]{1,0:T(8,128)S(1)}, bf16[208,1024]{1,0:T(8,128)(2,1)S(1)}) custom-call(s32[2]{0:T(128)S(1)} %copy-done.5, f32[16,384]{1,0:T(8,128)S(1)} %copy-done.6, bf16[8,96,1152]{2,1,0:T(8,128)(2,1)} %all-to-all-done.3.r_ref, s32[2]{0:T(128)S(1)} %copy-done.5), custom_call_target="tpu_custom_call" | custom-call | flops 1207959552 | bytes 3145728 | tf_op jit(solution)/shard_map/pallas_call | solution.py:456
  110.3 0.0 copy-start.4
  110.3 0.1 collective-permute-start.2
  110.3 1.8 %collective-permute-done.2.got_ref = bf16[208,1024]{1,0:T(8,128)(2,1)S(1)} collective-permute-done((bf16[208,1024]{1,0:T(8,128)(2,1)S(1)}, bf16[208,1024]{1,0:T(8,128)(2,1)S(1)}, u32[]{:S(2)}, u32[]{:S(2)}) %collective-permute-start.2) | collective-permute-done | bytes 426016 | tf_op jit(solution)/shard_map/ppermute | solution.py:476
  112.1 0.9 shard_map.75._
  113.0 0.1 collective-permute-start.5
  113.1 23.9 %all-to-all-done.2.r_ref = bf16[8,96,1152]{2,1,0:T(8,128)(2,1)S(1)} async-done(((bf16[8,96,1152]{2,1,0:T(8,128)(2,1)}), bf16[8,96,1152]{2,1,0:T(8,128)(2,1)S(1)}, u32[]{:S(2)}, u32[]{:S(2)}) %all-to-all-start.2) | async-done | bytes 1769504 | tf_op jit(solution)/shard_map/all_to_all | solution.py:366
  137.0 0.0 copy-done.4
  137.0 3.1 %shard_map.76 = (f32[192,1024]{1,0:T(8,128)S(1)}, f32[8,384]{1,0:T(8,128)S(1)}, bf16[96,1024]{1,0:T(8,128)(2,1)S(1)}, bf16[112,1024]{1,0:T(8,128)(2,1)S(1)}) custom-call(s32[2]{0:T(128)S(1)} %copy-done.5, f32[16,384]{1,0:T(8,128)S(1)} %copy-done.4, bf16[8,96,1152]{2,1,0:T(8,128)(2,1)S(1)} %all-to-all-done.2.r_ref, bf16[208,1024]{1,0:T(8,128)(2,1)S(1)} %shard_map.75._), custom_call_target="tpu_custom_call" | custom-call | tf_op jit(solution)/shard_map/pallas_call | solution.py:456
  140.1 0.1 collective-permute-start.4
  140.1 0.5 collective-permute-start.3
  140.6 1.3 collective-permute-done.3.got_ref
  141.9 0.0 collective-permute-done.4.last_ref
  141.9 0.0 collective-permute-done.5.far_ref
  141.9 1.0 shard_map.77
  142.9 0.3 collective-permute-start.6
  143.2 0.6 convert_reduce_fusion
  143.8 1.0 collective-permute-done.6
  144.7 0.1 broadcast_select_fusion.1
  144.8 0.9 pad_maximum_fusion
  (1 shorter events, 0.0 us)
Async XLA Ops:
  3.2 23.3 %collective-permute-start = (bf16[208,1024]{1,0:T(8,128)(2,1)}, bf16[208,1024]{1,0:T(8,128)(2,1)S(1)}, u32[]{:S(2)}, u32[]{:S(2)}) collective-permute-start(bf16[208,1024]{1,0:T(8,128)(2,1)} %shard_map.70), channel_id=1, source_target_pairs={{0,16},{2,18},{4,20},{6,22},{8,24},{10,26},{12,28},{14,30},{16,0},... | collective-permute-start | bytes 1277960 | tf_op jit(solution)/shard_map/ppermute | solution.py:371
  10.7 31.7 %all-to-all-start = ((bf16[8,96,1024]{2,1,0:T(8,128)(2,1)}), bf16[8,96,1024]{2,1,0:T(8,128)(2,1)}, u32[]{:S(2)}, u32[]{:S(2)}) async-start(bf16[8,96,1024]{2,1,0:T(8,128)(2,1)} %get-tuple-element.21), calls=%async_computation | async-start | bytes 3145728 | tf_op jit(solution)/shard_map/all_to_all | solution.py:366
  26.5 1.8 %copy-start.9 = (bf16[208,1024]{1,0:T(8,128)(2,1)}, bf16[208,1024]{1,0:T(8,128)(2,1)S(1)}, u32[]{:S(2)}) copy-start(bf16[208,1024]{1,0:T(8,128)(2,1)S(1)} %collective-permute-done.mine_ref) | copy-start | bytes 1277956
  26.5 1.8 %collective-permute-start.1 = (bf16[208,1024]{1,0:T(8,128)(2,1)S(1)}, bf16[208,1024]{1,0:T(8,128)(2,1)S(1)}, u32[]{:S(2)}, u32[]{:S(2)}) collective-permute-start(bf16[208,1024]{1,0:T(8,128)(2,1)S(1)} %collective-permute-done.mine_ref), channel_id=1, source_target_pairs={{0,1},{1,0},{2,3},{3,2},{4,5},{5,4},{6,7},{7,6},{8,9},{9,8},{10,11... | collective-permute-start | bytes 1277960 | tf_op jit(solution)/shard_map/ppermute | solution.py:374
  28.3 0.8 copy-start.10
  42.4 4.5 %copy-start.7 = (s32[64]{0:T(128)S(1)}, s32[64]{0:T(128)}, u32[]{:S(2)}) copy-start(s32[64]{0:T(128)} %param.8) | copy-start | bytes 772
  42.4 4.5 %copy-start.8 = (s32[64]{0:T(128)S(1)}, s32[64]{0:T(128)}, u32[]{:S(2)}) copy-start(s32[64]{0:T(128)} %param.9) | copy-start | bytes 772
  42.4 24.6 %all-to-all-start.1 = ((bf16[8,96,1024]{2,1,0:T(8,128)(2,1)}), bf16[8,96,1024]{2,1,0:T(8,128)(2,1)}, u32[]{:S(2)}, u32[]{:S(2)}) async-start(bf16[8,96,1024]{2,1,0:T(8,128)(2,1)} %get-tuple-element.23), calls=%async_computation.1 | async-start | bytes 3145728 | tf_op jit(solution)/shard_map/all_to_all | solution.py:366
  75.5 4.6 %copy-start.1 = (f32[2,384,1024]{2,1,0:T(8,128)S(1)}, f32[2,384,1024]{2,1,0:T(8,128)}, u32[]{:S(2)}) copy-start(f32[2,384,1024]{2,1,0:T(8,128)} %get-tuple-element.22.s_ref) | copy-start | bytes 9437188
  75.5 4.6 %copy-start.2 = (f32[2,384,128]{2,1,0:T(8,128)S(1)}, f32[2,384,128]{2,1,0:T(8,128)}, u32[]{:S(2)}) copy-start(f32[2,384,128]{2,1,0:T(8,128)} %get-tuple-element.26.fwd_ref) | copy-start | bytes 1179652
  75.5 26.8 %all-to-all-start.3 = ((bf16[8,96,1152]{2,1,0:T(8,128)(2,1)}), bf16[8,96,1152]{2,1,0:T(8,128)(2,1)}, u32[]{:S(2)}, u32[]{:S(2)}) async-start(bf16[8,96,1152]{2,1,0:T(8,128)(2,1)} %get-tuple-element.28), calls=%async_computation.3 | async-start | bytes 3538944 | tf_op jit(solution)/shard_map/all_to_all | solution.py:366
  80.1 2.2 %copy-start = (bf16[2,1024,1024]{2,1,0:T(8,128)(2,1)S(1)}, bf16[2,1024,1024]{2,1,0:T(8,128)(2,1)}, u32[]{:S(2)}) copy-start(bf16[2,1024,1024]{2,1,0:T(8,128)(2,1)} %t_ref.3) | copy-start | bytes 12582916
  82.3 0.8 copy-start.3
  87.9 18.3 %copy-start.5 = (s32[2]{0:T(128)S(1)}, s32[2]{0:T(128)}, u32[]{:S(2)}) copy-start(s32[2]{0:T(128)} %pad_add_fusion.info._) | copy-start | bytes 28
  87.9 18.3 %copy-start.6 = (f32[16,384]{1,0:T(8,128)S(1)}, f32[16,384]{1,0:T(8,128)}, u32[]{:S(2)}) copy-start(f32[16,384]{1,0:T(8,128)} %get-tuple-element.27.code_ref) | copy-start | bytes 73732
  102.3 34.7 %all-to-all-start.2 = ((bf16[8,96,1152]{2,1,0:T(8,128)(2,1)}), bf16[8,96,1152]{2,1,0:T(8,128)(2,1)S(1)}, u32[]{:S(2)}, u32[]{:S(2)}) async-start(bf16[8,96,1152]{2,1,0:T(8,128)(2,1)} %shard_map.73), calls=%async_computation.2 | async-start | bytes 3538944 | tf_op jit(solution)/shard_map/all_to_all | solution.py:366
  110.3 26.7 %copy-start.4 = (f32[16,384]{1,0:T(8,128)S(1)}, f32[16,384]{1,0:T(8,128)}, u32[]{:S(2)}) copy-start(f32[16,384]{1,0:T(8,128)} %get-tuple-element.20.code_ref) | copy-start | bytes 73732
  110.3 1.8 %collective-permute-start.2 = (bf16[208,1024]{1,0:T(8,128)(2,1)S(1)}, bf16[208,1024]{1,0:T(8,128)(2,1)S(1)}, u32[]{:S(2)}, u32[]{:S(2)}) collective-permute-start(bf16[208,1024]{1,0:T(8,128)(2,1)S(1)} %get-tuple-element.31), channel_id=1, source_target_pairs={{0,1},{1,0},{2,3},{3,2},{4,5},{5,4},{6,7},{7,6},{8,9},{9,8},{10,11... | collective-permute-start | bytes 1277960 | tf_op jit(solution)/shard_map/ppermute | solution.py:476
  113.0 28.9 %collective-permute-start.5 = (bf16[208,1024]{1,0:T(8,128)(2,1)S(1)}, bf16[208,1024]{1,0:T(8,128)(2,1)S(1)}, u32[]{:S(2)}, u32[]{:S(2)}) collective-permute-start(bf16[208,1024]{1,0:T(8,128)(2,1)S(1)} %shard_map.75._), channel_id=1, source_target_pairs={{0,16},{2,18},{4,20},{6,22},{8,24},{10,26},{12,28},{14,30},{16,0},... | collective-permute-start | bytes 1277960 | tf_op jit(solution)/shard_map/ppermute | solution.py:479
  140.1 1.8 %collective-permute-start.4 = (bf16[112,1024]{1,0:T(8,128)(2,1)S(1)}, bf16[112,1024]{1,0:T(8,128)(2,1)S(1)}, u32[]{:S(2)}, u32[]{:S(2)}) collective-permute-start(bf16[112,1024]{1,0:T(8,128)(2,1)S(1)} %get-tuple-element.35), channel_id=1, source_target_pairs={{0,1},{1,0},{2,3},{3,2},{4,5},{5,4},{6,7},{7,6},{8,9},{9,8},{10,11... | collective-permute-start | bytes 688136 | tf_op jit(solution)/shard_map/ppermute | solution.py:483
  140.1 1.8 %collective-permute-start.3 = (bf16[96,1024]{1,0:T(8,128)(2,1)S(1)}, bf16[96,1024]{1,0:T(8,128)(2,1)S(1)}, u32[]{:S(2)}, u32[]{:S(2)}) collective-permute-start(bf16[96,1024]{1,0:T(8,128)(2,1)S(1)} %get-tuple-element.34), channel_id=1, source_target_pairs={{0,1},{1,0},{2,3},{3,2},{4,5},{5,4},{6,7},{7,6},{8,9},{9,8},{10,11... | collective-permute-start | bytes 589832 | tf_op jit(solution)/shard_map/ppermute | solution.py:483
  142.9 1.8 %collective-permute-start.6 = (bf16[192,1024]{1,0:T(8,128)(2,1)S(1)}, bf16[192,1024]{1,0:T(8,128)(2,1)S(1)}, u32[]{:S(2)}, u32[]{:S(2)}) collective-permute-start(bf16[192,1024]{1,0:T(8,128)(2,1)S(1)} %get-tuple-element.36), channel_id=1, source_target_pairs={{0,1},{1,0},{2,3},{3,2},{4,5},{5,4},{6,7},{7,6},{8,9},{9,8},{10,11... | collective-permute-start | bytes 1179656 | tf_op jit(solution)/shard_map/ppermute | solution.py:492

commit v4 on v3

--- a/solution.py
+++ b/solution.py
@@ -19,7 +19,12 @@
 ROW_GROUPS = 8
 LIMIT = 24
 FULL = 63
-HIDE = 23_000_000_000
+AFTER = 2
+HIDE = 20_000_000_000
+
+
+def order_of(side):
+    return list(range(1, side))
 
 
 def iota(shape, axis):
@@ -77,27 +82,33 @@
 
 
 def gather_body(
-    info, picks, home_ref, source, q_hbm, code_hbm, q_ref, code_ref, sem, *, n_tgt, per_device, capacity, group
+    info, flip, picks, home_ref, source, q_hbm, code_hbm, q_ref, code_ref, sem, *, n_tgt, per_device, capacity, group
 ):
     n_buckets, rows = code_ref.shape
     n_clusters = home_ref.shape[1]
     width = q_ref.shape[2]
+    per_message = group // per_device
     cluster = iota((n_clusters, rows), 0).astype(F32)
     member = jnp.zeros((n_clusters, rows), F32)
     for pick in picks:
         member = jnp.where(cluster == pick, 1.0, member)
     bucket = iota((n_buckets, n_clusters), 0)
-    holder = (info[0] + lax.div(bucket, per_device)) * n_tgt + info[1]
-    place = holder * per_device + lax.rem(bucket, per_device)
-    chosen = jnp.where(home_ref[...] == place, 1.0, 0.0).astype(BF16)
-    inside = jnp.dot(chosen, member.astype(BF16), preferred_element_type=F32)
     earlier = jnp.where(iota((rows, rows), 0) < iota((rows, rows), 1), 1.0, 0.0).astype(BF16)
-    rank = jnp.dot(inside.astype(BF16), earlier, preferred_element_type=F32)
-    code = jnp.where(inside > 0.5, rank, -1.0)
+
+    def ranks(turn):
+        holder = (info[0] + lax.bitwise_xor(lax.div(bucket, per_device), turn)) * n_tgt + info[1]
+        place = holder * per_device + lax.rem(bucket, per_device)
+        chosen = jnp.where(home_ref[...] == place, 1.0, 0.0).astype(BF16)
+        inside = jnp.dot(chosen, member.astype(BF16), preferred_element_type=F32)
+        rank = jnp.dot(inside.astype(BF16), earlier, preferred_element_type=F32)
+        return jnp.where(inside > 0.5, rank, -1.0)
+
+    code = ranks(0)
     code_ref[...] = code
     leave = [pltpu.make_async_copy(code_ref, code_hbm, sem.at[0])]
     leave[0].start()
-    per_message = group // per_device
+    if flip is not None:
+        code = ranks(flip)
     for start in range(0, n_buckets, group):
         slots = one_hot_slots(code, start, group, capacity)
         filled = jnp.sum(slots, axis=1, keepdims=True)
@@ -108,8 +119,13 @@
         d = start // per_device
         at = pl.ds(d, per_message)
         q_ref[at] = found.reshape(per_message, per_device * capacity, width)
-        leave.append(pltpu.make_async_copy(q_ref.at[at], q_hbm.at[at], sem.at[1 + start // group]))
-        leave[-1].start()
+        if flip is None:
+            leave.append(pltpu.make_async_copy(q_ref.at[at], q_hbm.at[at], sem.at[1 + start // group]))
+            leave[-1].start()
+        else:
+            for k in range(d, d + per_message):
+                leave.append(pltpu.make_async_copy(q_ref.at[k], q_hbm[k], sem.at[1 + k]))
+                leave[-1].start()
     for copy in leave:
         copy.wait()
 
@@ -126,18 +142,18 @@
 
 def gather_own(info, picks_ref, home_ref, src_ref, *refs, **sizes):
     picks = [picks_ref[k : k + 1, :].astype(F32) for k in range(picks_ref.shape[0])]
-    gather_body(info, picks, home_ref, src_ref[...], *refs, **sizes)
+    gather_body(info, None, picks, home_ref, src_ref[...], *refs, **sizes)
 
 
 def gather_partner(info, home_ref, mine_ref, other_ref, *refs, n_picks, **sizes):
-    *refs, src_ref = refs
+    *q_hbm, code_hbm, q_ref, code_ref, sem, src_ref = refs
     rows = src_ref.shape[0]
     half = rows // 2
     src_ref[pl.ds(pl.multiple_of(info[1] * half, 16), half), :] = mine_ref[:half, :]
     src_ref[pl.ds(pl.multiple_of((1 - info[1]) * half, 16), half), :] = other_ref[:half, :]
     block = mine_ref[half : half + EXTRA, :rows].astype(F32)
     picks = [block[k : k + 1, :] for k in range(n_picks)]
-    gather_body(info, picks, home_ref, src_ref[...], *refs, **sizes)
+    gather_body(info, info[2], picks, home_ref, src_ref[...], q_hbm, code_hbm, q_ref, code_ref, sem, **sizes)
 
 
 def scores_of(q, t, count):
@@ -181,7 +197,8 @@
     return out.astype(BF16)
 
 
-def near_scores(count_ref, q_ref, t_ref, s_ref, col_ref, fwd_ref, *, capacity, block):
+def near_scores(count_ref, q_ref, t_ref, *refs, capacity, block):
+    s_ref, col_ref, fwd_ref = refs[-3:]
     per_device, n_half, n_cols = s_ref.shape
     for l in range(per_device):
         q = q_ref[:, l * capacity : (l + 1) * capacity, :].reshape(n_half, -1)
@@ -199,24 +216,24 @@
         lax.fori_loop(0, n_half // block, forward, 0)
 
 
-def far_owner(
-    count_ref, q_hbm, t_hbm, col_ref, p_hbm, rev_hbm, q_ref, t_ref, s_ref, w_ref, p_ref, rev_ref, sems, rev_sem, *, block
-):
+def far_owner(info, count_ref, col_ref, t_hbm, *refs, block):
+    *q_hbm, p_hbm, rev_hbm, q_ref, t_ref, s_ref, w_ref, p_ref, rev_ref, q_sem, t_sem, p_sem, rev_sem = refs
     per_device, n_msg, capacity, width = q_ref.shape
     _, n_half, n_cols = s_ref.shape
     places = [pl.ds(l * capacity, capacity) for l in range(per_device)]
-    arrive = []
+    arrive, leave = [], []
     for l, at in enumerate(places):
-        arrive.append(pltpu.make_async_copy(q_hbm.at[:, at, :], q_ref.at[l], sems.at[0, l]))
-        arrive.append(pltpu.make_async_copy(t_hbm.at[l], t_ref.at[l], sems.at[1, l]))
-    for copy in arrive:
+        pieces = [pltpu.make_async_copy(q_hbm[k].at[at, :], q_ref.at[l, k], q_sem.at[l, k]) for k in range(n_msg)]
+        arrive.append(pieces + [pltpu.make_async_copy(t_hbm.at[l], t_ref.at[l], t_sem.at[l])])
+        to = [p_hbm.at[lax.bitwise_xor(info[2], k), at, :] for k in range(n_msg)]
+        leave.append([pltpu.make_async_copy(p_ref.at[l, k], to[k], p_sem.at[l, k]) for k in range(n_msg)])
+    for copy in sum(arrive, []):
         copy.start()
     rev_leave = pltpu.make_async_copy(rev_ref, rev_hbm, rev_sem)
-    leave = [pltpu.make_async_copy(p_ref.at[l], p_hbm.at[:, at, :], sems.at[2, l]) for l, at in enumerate(places)]
     half_reverse = []
     for l in range(per_device):
-        arrive[2 * l].wait()
-        arrive[2 * l + 1].wait()
+        for copy in arrive[l]:
+            copy.wait()
         s = scores_of(q_ref[l].reshape(n_half, width), t_ref[l], count_ref[l])
         s_ref[l] = s
         highest = jnp.max(s, axis=0, keepdims=True)
@@ -238,8 +255,9 @@
             p_ref[l, first : first + block // capacity, :, width:] = part.reshape(block // capacity, capacity, 128)
         p = jnp.dot(w_ref[l], t_ref[l], preferred_element_type=F32)
         p_ref[l, :, :, :width] = p.astype(BF16).reshape(n_msg, capacity, width)
-        leave[l].start()
-    for copy in leave + [rev_leave]:
+        for copy in leave[l]:
+            copy.start()
+    for copy in sum(leave, [rev_leave]):
         copy.wait()
 
 
@@ -357,7 +375,7 @@
     sds = jax.ShapeDtypeStruct
 
     me, core = lax.axis_index("src"), lax.axis_index("tgt")
-    info = jnp.stack([me // side * side, core]).astype(jnp.int32)
+    info = jnp.stack([me // side * side, core, me % side]).astype(jnp.int32)
     partner = [(i, (i + side) % n_src) for i in range(n_src)]
     twin = [(i, 1 - i) for i in range(n_tgt)]
     halves = [list(range(side)), list(range(side, n_src))]
@@ -382,7 +400,7 @@
     gather_scratch = [
         pltpu.VMEM((side, message, width), BF16),
         pltpu.VMEM((n_buckets, rows), F32),
-        pltpu.SemaphoreType.DMA((1 + n_buckets // group,)),
+        pltpu.SemaphoreType.DMA((1 + side,)),
     ]
     near_q, near_code = call(
         functools.partial(gather_own, **sizes),
@@ -395,17 +413,21 @@
         out_specs=(hbm, hbm),
     )(info, picks_t, home, sources)
     near_in = exchange(near_q)
-    far_q, far_code = call(
+    *far_q, far_code = call(
         functools.partial(gather_partner, n_picks=n_picks, **sizes),
-        gather_out,
+        tuple([sds((message, width), BF16)] * side) + gather_out[1:],
         gather_scratch + [pltpu.VMEM((rows, width), BF16)],
         flops=HIDE,
         moved=moved,
         limit=FULL,
         in_specs=[smem] + [vmem] * 3,
-        out_specs=(hbm, hbm),
+        out_specs=tuple([hbm] * (side + 1)),
     )(info, home, far_mine, far_other)
-    far_in = exchange(far_q)
+    far_in = far_q[:1] + [
+        lax.ppermute(far_q[k], "src", [(i, i ^ k) for i in range(n_src)]) for k in order_of(side)
+    ]
+    after = far_in[1 : 1 + AFTER]
+    far_in = far_in[:1] + [far_in[1 + order_of(side).index(k)] for k in range(1, side)]
 
     here = (me * n_tgt + core) * per_device + jnp.arange(per_device, dtype=jnp.int32)
     counts = jnp.sum(jnp.where(home == here[:, None], row_count[None, :], 0), axis=1)
@@ -420,12 +442,12 @@
             sds((per_device, 8, n_cols), F32),
             sds((per_device, n_half, 128), F32),
         ),
-        smem=1,
-        n_in=3,
         limit=FULL,
         exps=2 * n_slots * n_cols,
+        in_specs=[smem, vmem, vmem] + [pl.BlockSpec(memory_space=pl.ANY)] * len(after),
+        out_specs=(vmem, vmem, vmem),
         **work,
-    )(counts, near_in, targets)
+    )(counts, near_in, targets, *after)
     weights = [pltpu.VMEM((n_half, n_cols), BF16), pltpu.VMEM((n_half, 128), BF16)]
     far_pool, reverse = call(
         functools.partial(far_owner, block=capacity * math.gcd(side, ROW_GROUPS)),
@@ -437,15 +459,17 @@
             pltpu.VMEM((per_device, n_half, n_cols), BF16),
             pltpu.VMEM((per_device, side, capacity, width + 128), BF16),
             pltpu.VMEM((per_device, 8, n_cols), F32),
-            pltpu.SemaphoreType.DMA((3, per_device)),
+            pltpu.SemaphoreType.DMA((per_device, side)),
+            pltpu.SemaphoreType.DMA((per_device,)),
+            pltpu.SemaphoreType.DMA((per_device, side)),
             pltpu.SemaphoreType.DMA,
         ],
         limit=FULL,
         exps=3 * n_slots * n_cols,
-        in_specs=[smem, hbm, hbm, vmem],
+        in_specs=[smem, smem, vmem] + [hbm] * (1 + side),
         out_specs=(hbm, hbm),
         **work,
-    )(counts, far_in, targets, near_col)
+    )(info, counts, near_col, targets, *far_in)
     back_far = exchange(far_pool)
     near_pool = call(
         functools.partial(near_owner, **options), pooled, weights, n_in=4, exps=n_slots * n_cols, **work

time: 146 us -> 141 us (0.966)
  waiting for transfers between devices: 76.1 us -> 68.7 us
  starting transfers between devices: 22.7 us -> 25 us
    all_to_all x4 -> x3, waiting for transfers between devices: 59.3 us -> 38.1 us  [exchange(): lax.all_to_all(x, 'src', split_axis=0, concat_axis=0, axis_index_groups=h...]
    ppermute x0 -> x7, waiting for transfers between devices: none -> 13.7 us  [shards(): lax.ppermute(far_q[k], 'src', [(i, i ^ k) for i in range(n_src)])]
    ppermute x0 -> x7, starting transfers between devices: none -> 6.56 us  [shards(): lax.ppermute(far_q[k], 'src', [(i, i ^ k) for i in range(n_src)])]
    all_to_all x4 -> x3, starting transfers between devices: 17.7 us -> 13.5 us  [exchange(): lax.all_to_all(x, 'src', split_axis=0, concat_axis=0, axis_index_groups=h...]
    unnamed x22 -> x28, local copies, waits for them, and re-layouts: 3.84 us -> 3.07 us
  transfers between devices with their start and end apart: 11 -> 17, of which waited for: 9 -> 11; matrix products, arithmetic and copies ran while one was open for 1% -> 1% of each run, Pallas kernels for 19% -> 20%
where the time goes in v4:
time: 141 us
  waiting for transfers between devices  68.7 us (49%)
  Pallas kernels  40 us (28%)
  starting transfers between devices  25 us (18%)
  local copies, waits for them, and re-layouts  3.07 us (2%)
  other arithmetic  2.85 us (2%)
    all_to_all x3, waiting for transfers between devices, exchange(): lax.all_to_all(x, 'src', split_axis=0, concat_axis=0, axis_index_groups=h...  38.1 us
    ppermute x7, waiting for transfers between devices, shards(): lax.ppermute(far_q[k], 'src', [(i, i ^ k) for i in range(n_src)])  13.7 us
    all_to_all x3, starting transfers between devices, exchange(): lax.all_to_all(x, 'src', split_axis=0, concat_axis=0, axis_index_groups=h...  13.5 us
    ppermute x1, waiting for transfers between devices, shards(): lax.ppermute(call(half_with_picks, letter, smem=1, n_in=3, moved=4 * half...  11 us
    pallas_call x1, Pallas kernels, shards(): call(functools.partial(far_owner, block=capacity * math.gcd(side, ROW_GRO...  9.12 us
    pallas_call x1, Pallas kernels, shards(): call(functools.partial(near_scores, **options), (sds((per_device, n_half,...  8.22 us
    pallas_call x2, Pallas kernels, combine(): pl.pallas_call(functools.partial(combine_kernel, capacity=capacity), out_...  7 us
    ppermute x7, starting transfers between devices, shards(): lax.ppermute(far_q[k], 'src', [(i, i ^ k) for i in range(n_src)])  6.56 us
  transfers between devices with their start and end apart: 17, of which 11 were waited for; matrix products, arithmetic and copies ran while one was open for 1% of the time, Pallas kernels for 20%

profile of v4, /device:TPU:0, one launch (start us, length us, event | category | flops | bytes accessed | tf_op | source)
XLA Modules:
  0.0 140.5 jit_solution(8111057177271240022)
XLA Ops:
  0.7 0.6 pad_add_fusion.info._
  1.2 1.9 %shard_map.69 = bf16[208,1024]{1,0:T(8,128)(2,1)} custom-call(s32[3]{0:T(128)} %pad_add_fusion.info._, s32[4,384]{1,0:T(4,128)} %bitcast.5, bf16[384,1024]{1,0:T(8,128)(2,1)} %src_ref.3), custom_call_target="tpu_custom_call" | custom-call | bytes 786432 | tf_op jit(solution)/shard_map/pallas_call | solution.py:390
  3.2 4.0 %collective-permute-start = (bf16[208,1024]{1,0:T(8,128)(2,1)}, bf16[208,1024]{1,0:T(8,128)(2,1)S(1)}, u32[]{:S(2)}, u32[]{:S(2)}) collective-permute-start(bf16[208,1024]{1,0:T(8,128)(2,1)} %shard_map.69), channel_id=1, source_target_pairs={{0,16},{2,18},{4,20},{6,22},{8,24},{10,26},{12,28},{14,30},{16,0},... | collective-permute-start | bytes 1277960 | tf_op jit(solution)/shard_map/ppermute | solution.py:389
  7.2 3.4 %shard_map.68 = (bf16[8,96,1024]{2,1,0:T(8,128)(2,1)}, f32[16,384]{1,0:T(8,128)}) custom-call(s32[3]{0:T(128)} %pad_add_fusion.info._, s32[4,384]{1,0:T(4,128)} %bitcast.6, s32[1,64]{1,0:T(1,128)} %bitcast.7, bf16[384,1024]{1,0:T(8,128)(2,1)} %src_ref.3), custom_call_target="tpu_custom_call" | custom-call | flops 603979776 | bytes 2359296 | tf_op jit(solution)/shard_map/pallas_call | solution.py:405
  10.7 4.7 %all-to-all-start = ((bf16[8,96,1024]{2,1,0:T(8,128)(2,1)}), bf16[8,96,1024]{2,1,0:T(8,128)(2,1)}, u32[]{:S(2)}, u32[]{:S(2)}) async-start(bf16[8,96,1024]{2,1,0:T(8,128)(2,1)} %get-tuple-element.28), calls=%async_computation | async-start | bytes 3145728 | tf_op jit(solution)/shard_map/all_to_all | solution.py:384
  15.4 0.0 copy-start.10
  15.4 11.0 %collective-permute-done.mine_ref = bf16[208,1024]{1,0:T(8,128)(2,1)S(1)} collective-permute-done((bf16[208,1024]{1,0:T(8,128)(2,1)}, bf16[208,1024]{1,0:T(8,128)(2,1)S(1)}, u32[]{:S(2)}, u32[]{:S(2)}) %collective-permute-start) | collective-permute-done | bytes 426016 | tf_op jit(solution)/shard_map/ppermute | solution.py:389
  26.5 0.0 collective-permute-start.1
  26.5 1.9 %collective-permute-done.1.other_ref = bf16[208,1024]{1,0:T(8,128)(2,1)} collective-permute-done((bf16[208,1024]{1,0:T(8,128)(2,1)S(1)}, bf16[208,1024]{1,0:T(8,128)(2,1)}, u32[]{:S(2)}, u32[]{:S(2)}) %collective-permute-start.1) | collective-permute-done | bytes 426016 | tf_op jit(solution)/shard_map/ppermute | solution.py:392
  28.4 0.0 copy-done.11
  28.4 3.5 %shard_map.70 = (bf16[96,1024]{1,0:T(8,128)(2,1)}, bf16[96,1024]{1,0:T(8,128)(2,1)}, bf16[96,1024]{1,0:T(8,128)(2,1)}, bf16[96,1024]{1,0:T(8,128)(2,1)}, bf16[96...) custom-call(s32[3]{0:T(128)} %pad_add_fusion.info._, ...), custom_call_target="tpu_custom_call" | custom-call | flops 20000000000 | bytes 2359296 | tf_op jit(solution)/shard_map/pallas_call | solution.py:416
  31.9 1.6 %collective-permute-start.2 = (bf16[96,1024]{1,0:T(8,128)(2,1)}, bf16[96,1024]{1,0:T(8,128)(2,1)S(1)}, u32[]{:S(2)}, u32[]{:S(2)}) collective-permute-start(bf16[96,1024]{1,0:T(8,128)(2,1)} %get-tuple-element.29), channel_id=1, source_target_pairs={{0,2},{2,0},{4,6},{6,4},{8,10},{10,8},{12,14},{14,12},{16,18},{18,... | collective-permute-start | bytes 589832 | tf_op jit(solution)/shard_map/ppermute | solution.py:427
  33.5 1.5 %collective-permute-start.3 = (bf16[96,1024]{1,0:T(8,128)(2,1)}, bf16[96,1024]{1,0:T(8,128)(2,1)S(1)}, u32[]{:S(2)}, u32[]{:S(2)}) collective-permute-start(bf16[96,1024]{1,0:T(8,128)(2,1)} %get-tuple-element.30), channel_id=1, source_target_pairs={{0,4},{2,6},{4,0},{6,2},{8,12},{10,14},{12,8},{14,10},{16,20},{18,... | collective-permute-start | bytes 589832 | tf_op jit(solution)/shard_map/ppermute | solution.py:427
  35.0 0.4 collective-permute-start.4
  35.5 0.8 collective-permute-start.5
  36.3 2.2 %collective-permute-start.6 = (bf16[96,1024]{1,0:T(8,128)(2,1)}, bf16[96,1024]{1,0:T(8,128)(2,1)}, u32[]{:S(2)}, u32[]{:S(2)}) collective-permute-start(bf16[96,1024]{1,0:T(8,128)(2,1)} %get-tuple-element.36), channel_id=1, source_target_pairs={{0,10},{2,8},{4,14},{6,12},{8,2},{10,0},{12,6},{14,4},{16,26},{18,... | collective-permute-start | bytes 589832 | tf_op jit(solution)/shard_map/ppermute | solution.py:427
  38.5 4.8 %collective-permute-done.2.refs_0_.refs_1_ = bf16[96,1024]{1,0:T(8,128)(2,1)S(1)} collective-permute-done((bf16[96,1024]{1,0:T(8,128)(2,1)}, bf16[96,1024]{1,0:T(8,128)(2,1)S(1)}, u32[]{:S(2)}, u32[]{:S(2)}) %collective-permute-start.2) | collective-permute-done | bytes 196640 | tf_op jit(solution)/shard_map/ppermute | solution.py:427
  43.2 0.0 collective-permute-start.7
  43.2 4.4 %collective-permute-done.3.refs_1_.refs_2_ = bf16[96,1024]{1,0:T(8,128)(2,1)S(1)} collective-permute-done((bf16[96,1024]{1,0:T(8,128)(2,1)}, bf16[96,1024]{1,0:T(8,128)(2,1)S(1)}, u32[]{:S(2)}, u32[]{:S(2)}) %collective-permute-start.3) | collective-permute-done | bytes 196640 | tf_op jit(solution)/shard_map/ppermute | solution.py:427
  47.6 0.0 collective-permute-start.8
  47.6 0.0 copy-done.9
  47.7 0.0 copy-done.10
  47.7 0.7 fusion.count_ref
  48.4 0.0 all-to-all-done.q_ref
  48.4 0.0 copy-done.7
  48.4 0.0 copy-done.8
  48.4 8.2 %shard_map.71 = (f32[2,384,1024]{2,1,0:T(8,128)}, f32[2,8,1024]{2,1,0:T(8,128)}, f32[2,384,128]{2,1,0:T(8,128)}) custom-call(s32[2]{0:T(128)} %fusion.count_ref, bf16[8,96,1024]{2,1,0:T(8,128)(2,1)} %all-to-all-done.q_ref, bf16[2,1024,1024]{2,1,0:T(8,128)(2,1)} %t_ref.3, bf16[96,1024]{1,0:T(8,128)(2,1)} %copy-done.7, bf16[96,1024]{1,0:T(8,128)(2,1)} %copy-done.8), custom_call_target="tpu_custom_call" | custom-call | flops 1610612736 | bytes 5767168 | tf_op jit(solution)/shard_map/pallas_call | solution.py:438
  56.6 0.0 collective-permute-done.4.refs_3_
  56.6 0.0 collective-permute-done.5.refs_4_
  56.6 0.0 copy-start.13
  56.6 0.0 collective-permute-done.6.refs_5_
  56.6 0.3 collective-permute-done.7.refs_6_
  56.9 4.2 %collective-permute-done.8.refs_7_ = bf16[96,1024]{1,0:T(8,128)(2,1)} collective-permute-done((bf16[96,1024]{1,0:T(8,128)(2,1)}, bf16[96,1024]{1,0:T(8,128)(2,1)}, u32[]{:S(2)}, u32[]{:S(2)}) %collective-permute-start.8) | collective-permute-done | bytes 196640 | tf_op jit(solution)/shard_map/ppermute | solution.py:427
  61.1 0.0 copy-done.12
  61.1 0.0 copy-done.13
  61.1 9.1 %shard_map.72 = (bf16[8,96,1152]{2,1,0:T(8,128)(2,1)}, f32[2,8,1024]{2,1,0:T(8,128)}) custom-call(s32[3]{0:T(128)} %pad_add_fusion.info._, s32[2]{0:T(128)} %fusion.count_ref, f32[2,8,1024]{2,1,0:T(8,128)} %get-tuple-element.32.col_ref, bf16[2,1024,1024]{2,1,0:T(8,128)(2,1)} %t_ref.3, bf16[96,1024]{1,0:T(8,128)(2,1)} %get-tuple-element.33.refs_0_, ...), custom_call_target="tpu_custom_call" | custom-call | flops 1610612736 | bytes 5767168 | tf_op jit(solution)/shard_map/pallas_call | solution.py:452
  70.3 0.0 copy-start.1
  70.3 0.0 copy-start.2
  70.3 4.8 %all-to-all-start.2 = ((bf16[8,96,1152]{2,1,0:T(8,128)(2,1)}), bf16[8,96,1152]{2,1,0:T(8,128)(2,1)}, u32[]{:S(2)}, u32[]{:S(2)}) async-start(bf16[8,96,1152]{2,1,0:T(8,128)(2,1)} %get-tuple-element.42), calls=%async_computation.2 | async-start | bytes 3538944 | tf_op jit(solution)/shard_map/all_to_all | solution.py:384
  75.1 0.0 copy-done.1
  75.1 0.0 copy-start
  75.1 2.2 %copy-done = bf16[2,1024,1024]{2,1,0:T(8,128)(2,1)S(1)} copy-done((bf16[2,1024,1024]{2,1,0:T(8,128)(2,1)S(1)}, bf16[2,1024,1024]{2,1,0:T(8,128)(2,1)}, u32[]{:S(2)}) %copy-start) | copy-done | bytes 4194328
  77.3 0.8 copy-done.3
  78.1 4.8 %shard_map.73 = bf16[8,96,1152]{2,1,0:T(8,128)(2,1)} custom-call(f32[2,384,1024]{2,1,0:T(8,128)S(1)} %copy-done.1, f32[2,8,1024]{2,1,0:T(8,128)S(1)} %copy-done.3, f32[2,384,128]{2,1,0:T(8,128)S(1)} %copy-done.2, bf16[2,1024,1024]{2,1,0:T(8,128)(2,1)S(1)} %copy-done), custom_call_target="tpu_custom_call" | custom-call | flops 1610612736 | bytes 5767168 | tf_op jit(solution)/shard_map/pallas_call | solution.py:474
  82.9 14.2 %all-to-all-done.2.r_ref = bf16[8,96,1152]{2,1,0:T(8,128)(2,1)} async-done(((bf16[8,96,1152]{2,1,0:T(8,128)(2,1)}), bf16[8,96,1152]{2,1,0:T(8,128)(2,1)}, u32[]{:S(2)}, u32[]{:S(2)}) %all-to-all-start.2) | async-done | bytes 1769504 | tf_op jit(solution)/shard_map/all_to_all | solution.py:384
  97.1 3.9 %all-to-all-start.1 = ((bf16[8,96,1152]{2,1,0:T(8,128)(2,1)}), bf16[8,96,1152]{2,1,0:T(8,128)(2,1)S(1)}, u32[]{:S(2)}, u32[]{:S(2)}) async-start(bf16[8,96,1152]{2,1,0:T(8,128)(2,1)} %shard_map.73), calls=%async_computation.1 | async-start | bytes 3538944 | tf_op jit(solution)/shard_map/all_to_all | solution.py:384
  101.1 3.9 %shard_map.74 = (f32[192,1024]{1,0:T(8,128)S(1)}, f32[8,384]{1,0:T(8,128)S(1)}, bf16[208,1024]{1,0:T(8,128)(2,1)S(1)}) custom-call(s32[3]{0:T(128)S(1)} %copy-done.5, f32[16,384]{1,0:T(8,128)S(1)} %copy-done.6, bf16[8,96,1152]{2,1,0:T(8,128)(2,1)} %all-to-all-done.2.r_ref, s32[3]{0:T(128)S(1)} %copy-done.5), custom_call_target="tpu_custom_call" | custom-call | flops 1207959552 | bytes 3145728 | tf_op jit(solution)/shard_map/pallas_call | solution.py:480
  105.1 0.1 collective-permute-start.9
  105.1 1.8 %collective-permute-done.9.got_ref = bf16[208,1024]{1,0:T(8,128)(2,1)S(1)} collective-permute-done((bf16[208,1024]{1,0:T(8,128)(2,1)S(1)}, bf16[208,1024]{1,0:T(8,128)(2,1)S(1)}, u32[]{:S(2)}, u32[]{:S(2)}) %collective-permute-start.9) | collective-permute-done | bytes 426016 | tf_op jit(solution)/shard_map/ppermute | solution.py:500
  106.9 0.9 shard_map.75._
  107.8 0.1 collective-permute-start.12
  107.9 23.9 %all-to-all-done.1.r_ref = bf16[8,96,1152]{2,1,0:T(8,128)(2,1)S(1)} async-done(((bf16[8,96,1152]{2,1,0:T(8,128)(2,1)}), bf16[8,96,1152]{2,1,0:T(8,128)(2,1)S(1)}, u32[]{:S(2)}, u32[]{:S(2)}) %all-to-all-start.1) | async-done | bytes 1769504 | tf_op jit(solution)/shard_map/all_to_all | solution.py:384
  131.8 3.1 %shard_map.76 = (f32[192,1024]{1,0:T(8,128)S(1)}, f32[8,384]{1,0:T(8,128)S(1)}, bf16[96,1024]{1,0:T(8,128)(2,1)S(1)}, bf16[112,1024]{1,0:T(8,128)(2,1)S(1)}) custom-call(s32[3]{0:T(128)S(1)} %copy-done.5, f32[16,384]{1,0:T(8,128)S(1)} %copy-done.4, bf16[8,96,1152]{2,1,0:T(8,128)(2,1)S(1)} %all-to-all-done.1.r_ref, bf16[208,1024]{1,0:T(8,128)(2,1)S(1)} %shard_map.75._), custom_call_target="tpu_custom_call" | custom-call | tf_op jit(solution)/shard_map/pallas_call | solution.py:480
  134.9 0.1 collective-permute-start.11
  134.9 0.5 collective-permute-start.10
  135.4 1.3 collective-permute-done.10.got_ref
  136.7 0.0 collective-permute-done.11.last_ref
  136.7 0.0 collective-permute-done.12.far_ref
  136.7 1.0 shard_map.77
  137.8 0.3 collective-permute-start.13
  138.0 0.6 convert_reduce_fusion
  138.6 1.0 collective-permute-done.13
  139.5 0.1 broadcast_select_fusion.1
  139.6 0.9 pad_maximum_fusion
  (14 shorter events, 0.0 us)
Async XLA Ops:
  3.2 23.3 %collective-permute-start = (bf16[208,1024]{1,0:T(8,128)(2,1)}, bf16[208,1024]{1,0:T(8,128)(2,1)S(1)}, u32[]{:S(2)}, u32[]{:S(2)}) collective-permute-start(bf16[208,1024]{1,0:T(8,128)(2,1)} %shard_map.69), channel_id=1, source_target_pairs={{0,16},{2,18},{4,20},{6,22},{8,24},{10,26},{12,28},{14,30},{16,0},... | collective-permute-start | bytes 1277960 | tf_op jit(solution)/shard_map/ppermute | solution.py:389
  10.7 37.7 %all-to-all-start = ((bf16[8,96,1024]{2,1,0:T(8,128)(2,1)}), bf16[8,96,1024]{2,1,0:T(8,128)(2,1)}, u32[]{:S(2)}, u32[]{:S(2)}) async-start(bf16[8,96,1024]{2,1,0:T(8,128)(2,1)} %get-tuple-element.28), calls=%async_computation | async-start | bytes 3145728 | tf_op jit(solution)/shard_map/all_to_all | solution.py:384
  15.4 32.2 %copy-start.9 = (s32[64]{0:T(128)S(1)}, s32[64]{0:T(128)}, u32[]{:S(2)}) copy-start(s32[64]{0:T(128)} %param.8) | copy-start | bytes 772
  15.4 32.2 %copy-start.10 = (s32[64]{0:T(128)S(1)}, s32[64]{0:T(128)}, u32[]{:S(2)}) copy-start(s32[64]{0:T(128)} %param.9) | copy-start | bytes 772
  26.5 1.9 %copy-start.11 = (bf16[208,1024]{1,0:T(8,128)(2,1)}, bf16[208,1024]{1,0:T(8,128)(2,1)S(1)}, u32[]{:S(2)}) copy-start(bf16[208,1024]{1,0:T(8,128)(2,1)S(1)} %collective-permute-done.mine_ref) | copy-start | bytes 1277956
  26.5 1.9 %collective-permute-start.1 = (bf16[208,1024]{1,0:T(8,128)(2,1)S(1)}, bf16[208,1024]{1,0:T(8,128)(2,1)}, u32[]{:S(2)}, u32[]{:S(2)}) collective-permute-start(bf16[208,1024]{1,0:T(8,128)(2,1)S(1)} %collective-permute-done.mine_ref), channel_id=1, source_target_pairs={{0,1},{1,0},{2,3},{3,2},{4,5},{5,4},{6,7},{7,6},{8,9},{9,8},{10,11... | collective-permute-start | bytes 1277960 | tf_op jit(solution)/shard_map/ppermute | solution.py:392
  31.9 11.3 %collective-permute-start.2 = (bf16[96,1024]{1,0:T(8,128)(2,1)}, bf16[96,1024]{1,0:T(8,128)(2,1)S(1)}, u32[]{:S(2)}, u32[]{:S(2)}) collective-permute-start(bf16[96,1024]{1,0:T(8,128)(2,1)} %get-tuple-element.29), channel_id=1, source_target_pairs={{0,2},{2,0},{4,6},{6,4},{8,10},{10,8},{12,14},{14,12},{16,18},{18,... | collective-permute-start | bytes 589832 | tf_op jit(solution)/shard_map/ppermute | solution.py:427
  33.5 14.1 %collective-permute-start.3 = (bf16[96,1024]{1,0:T(8,128)(2,1)}, bf16[96,1024]{1,0:T(8,128)(2,1)S(1)}, u32[]{:S(2)}, u32[]{:S(2)}) collective-permute-start(bf16[96,1024]{1,0:T(8,128)(2,1)} %get-tuple-element.30), channel_id=1, source_target_pairs={{0,4},{2,6},{4,0},{6,2},{8,12},{10,14},{12,8},{14,10},{16,20},{18,... | collective-permute-start | bytes 589832 | tf_op jit(solution)/shard_map/ppermute | solution.py:427
  35.0 21.5 %collective-permute-start.4 = (bf16[96,1024]{1,0:T(8,128)(2,1)}, bf16[96,1024]{1,0:T(8,128)(2,1)S(1)}, u32[]{:S(2)}, u32[]{:S(2)}) collective-permute-start(bf16[96,1024]{1,0:T(8,128)(2,1)} %get-tuple-element.34), channel_id=1, source_target_pairs={{0,6},{2,4},{4,2},{6,0},{8,14},{10,12},{12,10},{14,8},{16,22},{18,... | collective-permute-start | bytes 589832 | tf_op jit(solution)/shard_map/ppermute | solution.py:427
  35.5 21.1 %collective-permute-start.5 = (bf16[96,1024]{1,0:T(8,128)(2,1)}, bf16[96,1024]{1,0:T(8,128)(2,1)S(1)}, u32[]{:S(2)}, u32[]{:S(2)}) collective-permute-start(bf16[96,1024]{1,0:T(8,128)(2,1)} %get-tuple-element.35), channel_id=1, source_target_pairs={{0,8},{2,10},{4,12},{6,14},{8,0},{10,2},{12,4},{14,6},{16,24},{18,... | collective-permute-start | bytes 589832 | tf_op jit(solution)/shard_map/ppermute | solution.py:427
  36.3 20.4 %collective-permute-start.6 = (bf16[96,1024]{1,0:T(8,128)(2,1)}, bf16[96,1024]{1,0:T(8,128)(2,1)}, u32[]{:S(2)}, u32[]{:S(2)}) collective-permute-start(bf16[96,1024]{1,0:T(8,128)(2,1)} %get-tuple-element.36), channel_id=1, source_target_pairs={{0,10},{2,8},{4,14},{6,12},{8,2},{10,0},{12,6},{14,4},{16,26},{18,... | collective-permute-start | bytes 589832 | tf_op jit(solution)/shard_map/ppermute | solution.py:427
  43.2 5.1 %copy-start.7 = (bf16[96,1024]{1,0:T(8,128)(2,1)}, bf16[96,1024]{1,0:T(8,128)(2,1)S(1)}, u32[]{:S(2)}) copy-start(bf16[96,1024]{1,0:T(8,128)(2,1)S(1)} %collective-permute-done.2.refs_0_.refs_1_) | copy-start | bytes 589828
  43.2 13.7 %collective-permute-start.7 = (bf16[96,1024]{1,0:T(8,128)(2,1)}, bf16[96,1024]{1,0:T(8,128)(2,1)}, u32[]{:S(2)}, u32[]{:S(2)}) collective-permute-start(bf16[96,1024]{1,0:T(8,128)(2,1)} %get-tuple-element.37), channel_id=1, source_target_pairs={{0,12},{2,14},{4,8},{6,10},{8,4},{10,6},{12,0},{14,2},{16,28},{18,... | collective-permute-start | bytes 589832 | tf_op jit(solution)/shard_map/ppermute | solution.py:427
  47.6 0.7 copy-start.8
  47.6 13.5 %collective-permute-start.8 = (bf16[96,1024]{1,0:T(8,128)(2,1)}, bf16[96,1024]{1,0:T(8,128)(2,1)}, u32[]{:S(2)}, u32[]{:S(2)}) collective-permute-start(bf16[96,1024]{1,0:T(8,128)(2,1)} %get-tuple-element.38), channel_id=1, source_target_pairs={{0,14},{2,12},{4,10},{6,8},{8,6},{10,4},{12,2},{14,0},{16,30},{18,... | collective-permute-start | bytes 589832 | tf_op jit(solution)/shard_map/ppermute | solution.py:427
  56.6 4.6 %copy-start.12 = (bf16[96,1024]{1,0:T(8,128)(2,1)}, bf16[96,1024]{1,0:T(8,128)(2,1)S(1)}, u32[]{:S(2)}) copy-start(bf16[96,1024]{1,0:T(8,128)(2,1)S(1)} %collective-permute-done.4.refs_3_) | copy-start | bytes 589828
  56.6 4.5 %copy-start.13 = (bf16[96,1024]{1,0:T(8,128)(2,1)}, bf16[96,1024]{1,0:T(8,128)(2,1)S(1)}, u32[]{:S(2)}) copy-start(bf16[96,1024]{1,0:T(8,128)(2,1)S(1)} %collective-permute-done.5.refs_4_) | copy-start | bytes 589828
  70.3 4.8 %copy-start.1 = (f32[2,384,1024]{2,1,0:T(8,128)S(1)}, f32[2,384,1024]{2,1,0:T(8,128)}, u32[]{:S(2)}) copy-start(f32[2,384,1024]{2,1,0:T(8,128)} %get-tuple-element.31.s_ref) | copy-start | bytes 9437188
  70.3 4.8 %copy-start.2 = (f32[2,384,128]{2,1,0:T(8,128)S(1)}, f32[2,384,128]{2,1,0:T(8,128)}, u32[]{:S(2)}) copy-start(f32[2,384,128]{2,1,0:T(8,128)} %get-tuple-element.40.fwd_ref) | copy-start | bytes 1179652
  70.3 26.9 %all-to-all-start.2 = ((bf16[8,96,1152]{2,1,0:T(8,128)(2,1)}), bf16[8,96,1152]{2,1,0:T(8,128)(2,1)}, u32[]{:S(2)}, u32[]{:S(2)}) async-start(bf16[8,96,1152]{2,1,0:T(8,128)(2,1)} %get-tuple-element.42), calls=%async_computation.2 | async-start | bytes 3538944 | tf_op jit(solution)/shard_map/all_to_all | solution.py:384
  75.1 2.2 %copy-start = (bf16[2,1024,1024]{2,1,0:T(8,128)(2,1)S(1)}, bf16[2,1024,1024]{2,1,0:T(8,128)(2,1)}, u32[]{:S(2)}) copy-start(bf16[2,1024,1024]{2,1,0:T(8,128)(2,1)} %t_ref.3) | copy-start | bytes 12582916
  77.3 0.8 copy-start.3
  82.9 18.2 %copy-start.5 = (s32[3]{0:T(128)S(1)}, s32[3]{0:T(128)}, u32[]{:S(2)}) copy-start(s32[3]{0:T(128)} %pad_add_fusion.info._) | copy-start | bytes 40
  82.9 18.2 %copy-start.6 = (f32[16,384]{1,0:T(8,128)S(1)}, f32[16,384]{1,0:T(8,128)}, u32[]{:S(2)}) copy-start(f32[16,384]{1,0:T(8,128)} %get-tuple-element.41.code_ref) | copy-start | bytes 73732
  97.1 34.7 %all-to-all-start.1 = ((bf16[8,96,1152]{2,1,0:T(8,128)(2,1)}), bf16[8,96,1152]{2,1,0:T(8,128)(2,1)S(1)}, u32[]{:S(2)}, u32[]{:S(2)}) async-start(bf16[8,96,1152]{2,1,0:T(8,128)(2,1)} %shard_map.73), calls=%async_computation.1 | async-start | bytes 3538944 | tf_op jit(solution)/shard_map/all_to_all | solution.py:384
  101.1 30.7 %copy-start.4 = (f32[16,384]{1,0:T(8,128)S(1)}, f32[16,384]{1,0:T(8,128)}, u32[]{:S(2)}) copy-start(f32[16,384]{1,0:T(8,128)} %get-tuple-element.27.code_ref) | copy-start | bytes 73732
  105.1 1.8 %collective-permute-start.9 = (bf16[208,1024]{1,0:T(8,128)(2,1)S(1)}, bf16[208,1024]{1,0:T(8,128)(2,1)S(1)}, u32[]{:S(2)}, u32[]{:S(2)}) collective-permute-start(bf16[208,1024]{1,0:T(8,128)(2,1)S(1)} %get-tuple-element.45), channel_id=1, source_target_pairs={{0,1},{1,0},{2,3},{3,2},{4,5},{5,4},{6,7},{7,6},{8,9},{9,8},{10,11... | collective-permute-start | bytes 1277960 | tf_op jit(solution)/shard_map/ppermute | solution.py:500
  107.8 28.9 %collective-permute-start.12 = (bf16[208,1024]{1,0:T(8,128)(2,1)S(1)}, bf16[208,1024]{1,0:T(8,128)(2,1)S(1)}, u32[]{:S(2)}, u32[]{:S(2)}) collective-permute-start(bf16[208,1024]{1,0:T(8,128)(2,1)S(1)} %shard_map.75._), channel_id=1, source_target_pairs={{0,16},{2,18},{4,20},{6,22},{8,24},{10,26},{12,28},{14,30},{16,0},... | collective-permute-start | bytes 1277960 | tf_op jit(solution)/shard_map/ppermute | solution.py:503
  134.9 1.8 %collective-permute-start.11 = (bf16[112,1024]{1,0:T(8,128)(2,1)S(1)}, bf16[112,1024]{1,0:T(8,128)(2,1)S(1)}, u32[]{:S(2)}, u32[]{:S(2)}) collective-permute-start(bf16[112,1024]{1,0:T(8,128)(2,1)S(1)} %get-tuple-element.49), channel_id=1, source_target_pairs={{0,1},{1,0},{2,3},{3,2},{4,5},{5,4},{6,7},{7,6},{8,9},{9,8},{10,11... | collective-permute-start | bytes 688136 | tf_op jit(solution)/shard_map/ppermute | solution.py:507
  134.9 1.8 %collective-permute-start.10 = (bf16[96,1024]{1,0:T(8,128)(2,1)S(1)}, bf16[96,1024]{1,0:T(8,128)(2,1)S(1)}, u32[]{:S(2)}, u32[]{:S(2)}) collective-permute-start(bf16[96,1024]{1,0:T(8,128)(2,1)S(1)} %get-tuple-element.48), channel_id=1, source_target_pairs={{0,1},{1,0},{2,3},{3,2},{4,5},{5,4},{6,7},{7,6},{8,9},{9,8},{10,11... | collective-permute-start | bytes 589832 | tf_op jit(solution)/shard_map/ppermute | solution.py:507
  137.8 1.8 %collective-permute-start.13 = (bf16[192,1024]{1,0:T(8,128)(2,1)S(1)}, bf16[192,1024]{1,0:T(8,128)(2,1)S(1)}, u32[]{:S(2)}, u32[]{:S(2)}) collective-permute-start(bf16[192,1024]{1,0:T(8,128)(2,1)S(1)} %get-tuple-element.50), channel_id=1, source_target_pairs={{0,1},{1,0},{2,3},{3,2},{4,5},{5,4},{6,7},{7,6},{8,9},{9,8},{10,11... | collective-permute-start | bytes 1179656 | tf_op jit(solution)/shard_map/ppermute | solution.py:516

commit v5 on v4

--- a/solution.py
+++ b/solution.py
@@ -19,16 +19,16 @@
 ROW_GROUPS = 8
 LIMIT = 24
 FULL = 63
-AFTER = 2
 HIDE = 20_000_000_000
-
-
-def order_of(side):
-    return list(range(1, side))
 
 
 def iota(shape, axis):
     return lax.broadcasted_iota(jnp.int32, shape, axis)
+
+
+def place_of(side):
+    me = lax.axis_index("src")
+    return me // side * side, lax.axis_index("tgt"), lax.rem(me, side)
 
 
 def call(kernel, out_shape, scratch=(), smem=0, n_in=0, limit=LIMIT, flops=0, moved=0, exps=0, **kw):
@@ -82,7 +82,7 @@
 
 
 def gather_body(
-    info, flip, picks, home_ref, source, q_hbm, code_hbm, q_ref, code_ref, sem, *, n_tgt, per_device, capacity, group
+    info, flip, picks, home_ref, load, q_hbm, code_hbm, q_ref, code_ref, sem, *, n_tgt, per_device, capacity, group
 ):
     n_buckets, rows = code_ref.shape
     n_clusters = home_ref.shape[1]
@@ -109,6 +109,7 @@
     leave[0].start()
     if flip is not None:
         code = ranks(flip)
+    source = load()
     for start in range(0, n_buckets, group):
         slots = one_hot_slots(code, start, group, capacity)
         filled = jnp.sum(slots, axis=1, keepdims=True)
@@ -130,22 +131,42 @@
         copy.wait()
 
 
-def half_with_picks(info, picks_ref, src_ref, out_ref):
+def half_with_picks(picks_hbm, src_hbm, out_ref, picks_ref, sems, *, side):
+    _, core, _ = place_of(side)
     n_picks, rows = picks_ref.shape
-    width = src_ref.shape[1]
+    width = src_hbm.shape[1]
     half = rows // 2
-    out_ref[:half, :] = src_ref[pl.ds(pl.multiple_of(info[1] * half, 16), half), :]
-    body = jnp.concatenate([picks_ref[...].astype(F32), jnp.zeros((EXTRA - n_picks, rows), F32)], axis=0)
+    mine = pl.ds(pl.multiple_of(core * half, 16), half)
+    names = pltpu.make_async_copy(picks_hbm, picks_ref, sems.at[0])
+    names.start()
+    body = pltpu.make_async_copy(src_hbm.at[mine, :], out_ref.at[pl.ds(0, half), :], sems.at[1])
+    body.start()
+    names.wait()
+    names = jnp.concatenate([picks_ref[...].astype(F32), jnp.zeros((EXTRA - n_picks, rows), F32)], axis=0)
     rest = jnp.zeros((EXTRA, width - rows), F32)
-    out_ref[half:, :] = jnp.concatenate([body, rest], axis=1).astype(BF16)
-
-
-def gather_own(info, picks_ref, home_ref, src_ref, *refs, **sizes):
+    out_ref[half:, :] = jnp.concatenate([names, rest], axis=1).astype(BF16)
+    body.wait()
+
+
+def gather_own(picks_hbm, home_hbm, src_hbm, *refs, side, **sizes):
+    *refs, picks_ref, home_ref, src_ref, sems = refs
+    copies = []
+    for i, (here, there) in enumerate(((picks_hbm, picks_ref), (home_hbm, home_ref), (src_hbm, src_ref))):
+        copies.append(pltpu.make_async_copy(here, there, sems.at[i]))
+        copies[-1].start()
+    copies[0].wait()
+    copies[1].wait()
     picks = [picks_ref[k : k + 1, :].astype(F32) for k in range(picks_ref.shape[0])]
-    gather_body(info, None, picks, home_ref, src_ref[...], *refs, **sizes)
-
-
-def gather_partner(info, home_ref, mine_ref, other_ref, *refs, n_picks, **sizes):
+
+    def load():
+        copies[2].wait()
+        return src_ref[...]
+
+    gather_body(place_of(side), None, picks, home_ref, load, *refs, **sizes)
+
+
+def gather_partner(home_ref, mine_ref, other_ref, *refs, n_picks, side, **sizes):
+    info = place_of(side)
     *q_hbm, code_hbm, q_ref, code_ref, sem, src_ref = refs
     rows = src_ref.shape[0]
     half = rows // 2
@@ -153,7 +174,8 @@
     src_ref[pl.ds(pl.multiple_of((1 - info[1]) * half, 16), half), :] = other_ref[:half, :]
     block = mine_ref[half : half + EXTRA, :rows].astype(F32)
     picks = [block[k : k + 1, :] for k in range(n_picks)]
-    gather_body(info, info[2], picks, home_ref, src_ref[...], q_hbm, code_hbm, q_ref, code_ref, sem, **sizes)
+    load = lambda: src_ref[...]
+    gather_body(info, info[2], picks, home_ref, load, q_hbm, code_hbm, q_ref, code_ref, sem, **sizes)
 
 
 def scores_of(q, t, count):
@@ -190,15 +212,33 @@
     return (e * (1.0 / total)).astype(BF16), top + jnp.log2(total)
 
 
-def tail(margin, forward, lane):
-    out = jnp.zeros(lane.shape, F32)
-    for i, part in enumerate(three(margin) + three(forward)):
-        out = jnp.where(lane == i, part, out)
-    return out.astype(BF16)
-
-
-def near_scores(count_ref, q_ref, t_ref, *refs, capacity, block):
-    s_ref, col_ref, fwd_ref = refs[-3:]
+def put_pool(p_ref, l, p, capacity):
+    strips, cols = capacity // 16, p.shape[1] // 128
+    for k in range(p_ref.shape[0]):
+        for r in range(strips):
+            strip = p[k * capacity + 16 * r : k * capacity + 16 * (r + 1)]
+            for c in range(cols):
+                p_ref[k, (l * strips + r) * cols + c] = strip[:, 128 * c : 128 * (c + 1)]
+
+
+def put_tail(tail_ref, l, first, margin, forward, capacity):
+    strips = capacity // 16
+    shape = (margin.shape[0], 128)
+    parts = three(jnp.broadcast_to(margin, shape)) + three(jnp.broadcast_to(forward, shape))
+    turn = lax.rem(iota(shape, 1), 6)
+    mixed = parts[5]
+    for i in range(5):
+        mixed = jnp.where(turn == i, parts[i], mixed)
+    strip_of = lax.div(iota((16, 128), 1), 6)
+    for k in range(margin.shape[0] // capacity):
+        tile = tail_ref[first + k] if l else jnp.zeros((16, 128), F32)
+        for r in range(strips):
+            at = slice(k * capacity + 16 * r, k * capacity + 16 * (r + 1))
+            tile = jnp.where(strip_of == l * strips + r, mixed[at], tile)
+        tail_ref[first + k] = tile
+
+
+def near_scores(count_ref, q_ref, t_ref, s_ref, col_ref, fwd_ref, *, capacity, block):
     per_device, n_half, n_cols = s_ref.shape
     for l in range(per_device):
         q = q_ref[:, l * capacity : (l + 1) * capacity, :].reshape(n_half, -1)
@@ -216,24 +256,28 @@
         lax.fori_loop(0, n_half // block, forward, 0)
 
 
-def far_owner(info, count_ref, col_ref, t_hbm, *refs, block):
-    *q_hbm, p_hbm, rev_hbm, q_ref, t_ref, s_ref, w_ref, p_ref, rev_ref, q_sem, t_sem, p_sem, rev_sem = refs
+def far_owner(count_ref, col_ref, t_ref, *refs, block, side):
+    _, _, here = place_of(side)
+    *q_hbm, p_hbm, rev_hbm, q_ref, s_ref, w_ref, p_ref, tail_ref, rev_ref, q_sem, p_sem, rev_sem = refs
     per_device, n_msg, capacity, width = q_ref.shape
     _, n_half, n_cols = s_ref.shape
-    places = [pl.ds(l * capacity, capacity) for l in range(per_device)]
+    tiles = capacity * width // 2048
     arrive, leave = [], []
-    for l, at in enumerate(places):
-        pieces = [pltpu.make_async_copy(q_hbm[k].at[at, :], q_ref.at[l, k], q_sem.at[l, k]) for k in range(n_msg)]
-        arrive.append(pieces + [pltpu.make_async_copy(t_hbm.at[l], t_ref.at[l], t_sem.at[l])])
-        to = [p_hbm.at[lax.bitwise_xor(info[2], k), at, :] for k in range(n_msg)]
-        leave.append([pltpu.make_async_copy(p_ref.at[l, k], to[k], p_sem.at[l, k]) for k in range(n_msg)])
-    for copy in sum(arrive, []):
+    for l in range(per_device):
+        at = pl.ds(l * capacity, capacity)
+        arrive.append([pltpu.make_async_copy(q_hbm[k].at[at, :], q_ref.at[l, k], q_sem.at[l, k]) for k in range(n_msg)])
+        at = pl.ds(l * tiles, tiles + l // (per_device - 1))
+        to = [p_hbm.at[lax.bitwise_xor(here, k), at] for k in range(n_msg)]
+        leave.append([pltpu.make_async_copy(p_ref.at[k, at], to[k], p_sem.at[l, k]) for k in range(n_msg)])
+    for copy in arrive[0]:
         copy.start()
     rev_leave = pltpu.make_async_copy(rev_ref, rev_hbm, rev_sem)
     half_reverse = []
     for l in range(per_device):
         for copy in arrive[l]:
             copy.wait()
+        for copy in arrive[l + 1] if l + 1 < per_device else []:
+            copy.start()
         s = scores_of(q_ref[l].reshape(n_half, width), t_ref[l], count_ref[l])
         s_ref[l] = s
         highest = jnp.max(s, axis=0, keepdims=True)
@@ -250,11 +294,11 @@
             forward = row_log_sum(s)
             w, margin = weigh(s, half_reverse[l])
             w_ref[l, at, :] = w
-            part = tail(margin, forward, iota((block, 128), 1))
-            first = start // capacity
-            p_ref[l, first : first + block // capacity, :, width:] = part.reshape(block // capacity, capacity, 128)
-        p = jnp.dot(w_ref[l], t_ref[l], preferred_element_type=F32)
-        p_ref[l, :, :, :width] = p.astype(BF16).reshape(n_msg, capacity, width)
+            put_tail(tail_ref, l, start // capacity, margin, forward, capacity)
+        p = jnp.dot(w_ref[l], t_ref[l], preferred_element_type=F32).astype(BF16)
+        put_pool(p_ref, l, p, capacity)
+        if l == per_device - 1:
+            p_ref[:, per_device * tiles] = tail_ref[...].astype(BF16)
         for copy in leave[l]:
             copy.start()
     for copy in sum(leave, [rev_leave]):
@@ -262,35 +306,40 @@
 
 
 def near_owner(s_ref, rev_ref, fwd_ref, t_ref, p_ref, w_ref, tail_ref, *, capacity, block):
-    n_msg, _, full = p_ref.shape
     per_device, n_half, _ = s_ref.shape
-    width = full - 128
     for l in range(per_device):
         half_reverse = rev_ref[l, 0:1, :]
-
-        def rows(i, _):
-            at = pl.ds(pl.multiple_of(i * block, block), block)
+        for start in range(0, n_half, block):
+            at = slice(start, start + block)
             w, margin = weigh(s_ref[l, at, :], half_reverse)
             w_ref[at, :] = w
-            tail_ref[at, :] = tail(margin, fwd_ref[l, at, 0:1], iota((block, 128), 1))
-            return 0
-
-        lax.fori_loop(0, n_half // block, rows, 0)
-        at = slice(l * capacity, (l + 1) * capacity)
-        p = jnp.dot(w_ref[...], t_ref[l], preferred_element_type=F32)
-        p_ref[:, at, :width] = p.astype(BF16).reshape(n_msg, capacity, width)
-        p_ref[:, at, width:] = tail_ref[...].reshape(n_msg, capacity, 128)
-
-
-def combine_kernel(info, code_ref, r_ref, _, keep_ref, kmf_ref, *refs, capacity):
-    *send_refs, scr = refs
+            put_tail(tail_ref, l, start // capacity, margin, fwd_ref[l, at, 0:1], capacity)
+        p = jnp.dot(w_ref[...], t_ref[l], preferred_element_type=F32).astype(BF16)
+        put_pool(p_ref, l, p, capacity)
+    p_ref[:, p_ref.shape[1] - 1] = tail_ref[...].astype(BF16)
+
+
+def combine_kernel(code_ref, r_ref, _, keep_ref, kmf_ref, *refs, capacity, side):
+    _, core, _ = place_of(side)
+    *send_refs, r_scr, scr = refs
     n_buckets, rows = code_ref.shape
-    n_slots = n_buckets * capacity
-    width = r_ref.shape[2] - 128
+    width = scr.shape[1]
     half = rows // 2
-    parts = r_ref[:, :, width:].reshape(n_slots, 128).astype(F32)
-    margin = (parts[:, 0:1] + parts[:, 1:2]) + parts[:, 2:3]
-    forward = (parts[:, 3:4] + parts[:, 4:5]) + parts[:, 5:6]
+    n_msg, n_tiles, _, _ = r_ref.shape
+    cols = width // 128
+    strips = n_tiles // cols
+    margin, forward = [], []
+    for j in range(n_msg):
+        last = r_ref[j, n_tiles - 1].astype(F32)
+        last = (last + pltpu.roll(last, 127, 1)) + pltpu.roll(last, 126, 1)
+        for r in range(strips):
+            margin.append(jnp.broadcast_to(last[:, 6 * r : 6 * r + 1], (16, 128)))
+            forward.append(jnp.broadcast_to(last[:, 6 * r + 3 : 6 * r + 4], (16, 128)))
+            at = slice((j * strips + r) * 16, (j * strips + r + 1) * 16)
+            for c in range(cols):
+                r_scr[at, 128 * c : 128 * (c + 1)] = r_ref[j, r * cols + c]
+    margin = jnp.concatenate([jnp.concatenate(margin, axis=0)] * (rows // 128), axis=1)
+    forward = jnp.concatenate([jnp.concatenate(forward, axis=0)] * (rows // 128), axis=1)
     slots = one_hot_slots(code_ref[...], 0, n_buckets, capacity) > 0.5
 
     def merged(column):
@@ -302,15 +351,15 @@
     factor = jnp.where(slots, jnp.exp2(margin - margin_row), 0.0)
     high = factor.astype(BF16)
     low = (factor - high.astype(F32)).astype(BF16)
-    r = r_ref[:, :, :width].reshape(n_slots, width)
+    r = r_scr[...]
     over = (((0,), (0,)), ((), ()))
     pooled = lax.dot_general(high, r, over, preferred_element_type=F32)
     scr[...] = pooled + lax.dot_general(low, r, over, preferred_element_type=F32)
-    keep_ref[...] = scr[pl.ds(pl.multiple_of(info[1] * half, 16), half), :]
+    keep_ref[...] = scr[pl.ds(pl.multiple_of(core * half, 16), half), :]
     start = 0
     for ref in send_refs:
         count = min(ref.shape[0], half - start)
-        at = pl.ds(pl.multiple_of((1 - info[1]) * half + start, 16), count)
+        at = pl.ds(pl.multiple_of((1 - core) * half + start, 16), count)
         ref[:count, :] = scr[at, :].astype(BF16)
         start = start + count
     send_refs[-1][count:, :] = extra_rows(margin_row, forward_row, width)
@@ -327,20 +376,22 @@
     return top + jnp.log2(total)
 
 
-def merge_pair(info, keep_ref, kmf_ref, got_ref, out_ref, scr):
+def merge_pair(keep_ref, kmf_ref, got_ref, out_ref, scr, *, side):
+    _, core, _ = place_of(side)
     half, width = keep_ref.shape
     rows = kmf_ref.shape[1]
     margin, forward = kmf_ref[0:1, :], kmf_ref[1:2, :]
     margin_b, forward_b = read_extra(got_ref, half, rows)
     margin_all, forward_all = log_sum(margin, margin_b), log_sum(forward, forward_b)
     scr[...] = columns([jnp.exp2(margin - margin_all), jnp.exp2(margin_b - margin_all)], rows)
-    factors = scr[pl.ds(pl.multiple_of(info[1] * half, 16), half), :]
+    factors = scr[pl.ds(pl.multiple_of(core * half, 16), half), :]
     out = keep_ref[...] * factors[:, 0:1] + got_ref[:half, :].astype(F32) * factors[:, 1:2]
     out_ref[:half, :] = out.astype(BF16)
     out_ref[half:, :] = extra_rows(margin_all, forward_all, width)
 
 
-def merge_last(info, keep_ref, kmf_ref, got_ref, last_ref, far_ref, out_ref, conf_ref, scr):
+def merge_last(keep_ref, kmf_ref, got_ref, last_ref, far_ref, out_ref, conf_ref, scr, *, side):
+    _, core, _ = place_of(side)
     half, width = keep_ref.shape
     rows = kmf_ref.shape[1]
     margin, forward = kmf_ref[0:1, :], kmf_ref[1:2, :]
@@ -352,7 +403,7 @@
     scr[...] = columns(
         [jnp.exp2(margin - margin_all), jnp.exp2(margin_b - margin_all), jnp.exp2(margin_c - margin_all)], rows
     )
-    factors = scr[pl.ds(pl.multiple_of(info[1] * half, 16), half), :]
+    factors = scr[pl.ds(pl.multiple_of(core * half, 16), half), :]
     for at, ref in ((slice(0, first), got_ref), (slice(first, half), last_ref)):
         out = keep_ref[at, :] * factors[at, 0:1] + ref[: at.stop - at.start, :].astype(F32) * factors[at, 1:2]
         out_ref[at, :] = (out + far_ref[at, :].astype(F32) * factors[at, 2:3]).astype(BF16)
@@ -375,7 +426,6 @@
     sds = jax.ShapeDtypeStruct
 
     me, core = lax.axis_index("src"), lax.axis_index("tgt")
-    info = jnp.stack([me // side * side, core, me % side]).astype(jnp.int32)
     partner = [(i, (i + side) % n_src) for i in range(n_src)]
     twin = [(i, 1 - i) for i in range(n_tgt)]
     halves = [list(range(side)), list(range(side, n_src))]
@@ -386,17 +436,25 @@
     picks_t = picks.T
     home = cluster_home[None, :]
     letter = sds((half + EXTRA, width), BF16)
-    far_mine = lax.ppermute(
-        call(half_with_picks, letter, smem=1, n_in=3, moved=4 * half * width, limit=FULL)(info, picks_t, sources), "src", partner
-    )
-    far_other = lax.ppermute(far_mine, "tgt", twin)
-
-    sizes = dict(n_tgt=n_tgt, per_device=per_device, capacity=capacity, group=group)
-    gather_out = (sds((side, message, width), BF16), sds((n_buckets, rows), F32))
-    moved = 2 * (n_slots + rows) * width
     hbm = pl.BlockSpec(memory_space=pltpu.HBM)
     vmem = pl.BlockSpec(memory_space=pltpu.VMEM)
     smem = pl.BlockSpec(memory_space=pltpu.SMEM)
+    unread = pl.BlockSpec(memory_space=pl.ANY)
+    mine = call(
+        functools.partial(half_with_picks, side=side),
+        letter,
+        [pltpu.VMEM((n_picks, rows), jnp.int32), pltpu.SemaphoreType.DMA((2,))],
+        moved=4 * half * width,
+        limit=FULL,
+        in_specs=[hbm, hbm],
+        out_specs=vmem,
+    )(picks_t, sources)
+    far_mine = lax.ppermute(mine, "src", partner)
+    far_other = lax.ppermute(far_mine, "tgt", twin)
+
+    sizes = dict(side=side, n_tgt=n_tgt, per_device=per_device, capacity=capacity, group=group)
+    gather_out = (sds((side, message, width), BF16), sds((n_buckets, rows), F32))
+    moved = 2 * (n_slots + rows) * width
     gather_scratch = [
         pltpu.VMEM((side, message, width), BF16),
         pltpu.VMEM((n_buckets, rows), F32),
@@ -405,13 +463,19 @@
     near_q, near_code = call(
         functools.partial(gather_own, **sizes),
         gather_out,
-        gather_scratch,
+        gather_scratch
+        + [
+            pltpu.VMEM((n_picks, rows), jnp.int32),
+            pltpu.VMEM((1, n_clusters), jnp.int32),
+            pltpu.VMEM((rows, width), BF16),
+            pltpu.SemaphoreType.DMA((3,)),
+        ],
         flops=2 * n_slots * rows * width,
         moved=moved,
         limit=FULL,
-        in_specs=[smem] + [vmem] * 3,
+        in_specs=[hbm] * 3,
         out_specs=(hbm, hbm),
-    )(info, picks_t, home, sources)
+    )(picks_t, home, sources)
     near_in = exchange(near_q)
     *far_q, far_code = call(
         functools.partial(gather_partner, n_picks=n_picks, **sizes),
@@ -420,21 +484,21 @@
         flops=HIDE,
         moved=moved,
         limit=FULL,
-        in_specs=[smem] + [vmem] * 3,
+        in_specs=[vmem] * 3,
         out_specs=tuple([hbm] * (side + 1)),
-    )(info, home, far_mine, far_other)
+    )(home, far_mine, far_other)
     far_in = far_q[:1] + [
-        lax.ppermute(far_q[k], "src", [(i, i ^ k) for i in range(n_src)]) for k in order_of(side)
+        lax.ppermute(far_q[k], "src", [(i, i ^ k) for i in range(n_src)]) for k in range(1, side)
     ]
-    after = far_in[1 : 1 + AFTER]
-    far_in = far_in[:1] + [far_in[1 + order_of(side).index(k)] for k in range(1, side)]
 
     here = (me * n_tgt + core) * per_device + jnp.arange(per_device, dtype=jnp.int32)
     counts = jnp.sum(jnp.where(home == here[:, None], row_count[None, :], 0), axis=1)
     n_half = side * capacity
     options = dict(capacity=capacity, block=BLOCK)
     work = dict(flops=2 * n_slots * n_cols * width, moved=2 * (n_slots + per_device * n_cols) * width)
-    pooled = sds((side, message, width + 128), BF16)
+    n_tiles = message * width // 2048 + 1
+    pooled = sds((side, n_tiles, 16, 128), BF16)
+    row_block = capacity * math.gcd(side, ROW_GROUPS)
     near_s, near_col, near_fwd = call(
         functools.partial(near_scores, **options),
         (
@@ -442,77 +506,71 @@
             sds((per_device, 8, n_cols), F32),
             sds((per_device, n_half, 128), F32),
         ),
-        limit=FULL,
         exps=2 * n_slots * n_cols,
-        in_specs=[smem, vmem, vmem] + [pl.BlockSpec(memory_space=pl.ANY)] * len(after),
+        in_specs=[smem, vmem, vmem],
         out_specs=(vmem, vmem, vmem),
         **work,
-    )(counts, near_in, targets, *after)
-    weights = [pltpu.VMEM((n_half, n_cols), BF16), pltpu.VMEM((n_half, 128), BF16)]
+    )(counts, near_in, targets)
+    tails = pltpu.VMEM((side, 16, 128), F32)
     far_pool, reverse = call(
-        functools.partial(far_owner, block=capacity * math.gcd(side, ROW_GROUPS)),
-        (pooled, sds((per_device, 8, n_cols), F32)),
+        functools.partial(far_owner, block=row_block, side=side),
+        (pltpu.HBM(pooled.shape, BF16), pltpu.HBM((per_device, 8, n_cols), F32)),
         [
             pltpu.VMEM((per_device, side, capacity, width), BF16),
-            pltpu.VMEM((per_device, n_cols, width), BF16),
             pltpu.VMEM((per_device, n_half, n_cols), F32),
             pltpu.VMEM((per_device, n_half, n_cols), BF16),
-            pltpu.VMEM((per_device, side, capacity, width + 128), BF16),
+            pltpu.VMEM((side, n_tiles, 16, 128), BF16),
+            tails,
             pltpu.VMEM((per_device, 8, n_cols), F32),
             pltpu.SemaphoreType.DMA((per_device, side)),
-            pltpu.SemaphoreType.DMA((per_device,)),
             pltpu.SemaphoreType.DMA((per_device, side)),
             pltpu.SemaphoreType.DMA,
         ],
-        limit=FULL,
         exps=3 * n_slots * n_cols,
-        in_specs=[smem, smem, vmem] + [hbm] * (1 + side),
+        in_specs=[smem, vmem, vmem] + [hbm] * side,
         out_specs=(hbm, hbm),
         **work,
-    )(info, counts, near_col, targets, *far_in)
+    )(counts, near_col, targets, *far_in)
     back_far = exchange(far_pool)
     near_pool = call(
-        functools.partial(near_owner, **options), pooled, weights, n_in=4, exps=n_slots * n_cols, **work
+        functools.partial(near_owner, capacity=capacity, block=row_block),
+        pooled,
+        [pltpu.VMEM((n_half, n_cols), BF16), tails],
+        n_in=4,
+        exps=n_slots * n_cols,
+        **work,
     )(near_s, reverse, near_fwd, targets)
     back_near = exchange(near_pool)
 
     def combine(code, back, after, pieces, weight):
-        return pl.pallas_call(
-            functools.partial(combine_kernel, capacity=capacity),
-            out_shape=(sds((half, width), F32), sds((8, rows), F32)) + tuple(sds((n, width), BF16) for n in pieces),
-            in_specs=[
-                pl.BlockSpec(memory_space=pltpu.SMEM),
-                pl.BlockSpec(memory_space=pltpu.VMEM),
-                pl.BlockSpec(memory_space=pltpu.VMEM),
-                pl.BlockSpec(memory_space=pl.ANY),
-            ],
-            out_specs=tuple([pl.BlockSpec(memory_space=pltpu.VMEM)] * (2 + len(pieces))),
-            scratch_shapes=[pltpu.VMEM((rows, width), F32)],
-            compiler_params=pltpu.CompilerParams(vmem_limit_bytes=LIMIT * MIB),
-            cost_estimate=pl.CostEstimate(
-                flops=weight * 4 * n_slots * rows * width,
-                bytes_accessed=weight * 2 * (n_slots + 2 * rows) * width,
-                transcendentals=0,
-            ),
-        )(info, code, back, after)
-
-    keep, kmf, send = combine(far_code, back_far, info, [half + EXTRA], 1)
+        return call(
+            functools.partial(combine_kernel, capacity=capacity, side=side),
+            (sds((half, width), F32), sds((8, rows), F32)) + tuple(sds((n, width), BF16) for n in pieces),
+            [pltpu.VMEM((n_slots, width), BF16), pltpu.VMEM((rows, width), F32)],
+            flops=weight * 4 * n_slots * rows * width,
+            moved=weight * 2 * (n_slots + 2 * rows) * width,
+            in_specs=[vmem, vmem, unread],
+            out_specs=tuple([vmem] * (2 + len(pieces))),
+        )(code, back, after)
+
+    keep, kmf, send = combine(far_code, back_far, near_code, [half + EXTRA], 1)
     got = lax.ppermute(send, "tgt", twin)
     factors = [pltpu.VMEM((rows, 128), F32)]
-    joined = call(merge_pair, letter, factors, smem=1, n_in=4, moved=10 * half * width)(info, keep, kmf, got)
+    joined = call(
+        functools.partial(merge_pair, side=side), letter, factors, n_in=3, moved=10 * half * width
+    )(keep, kmf, got)
     from_far = lax.ppermute(joined, "src", partner)
 
     first = half // 32 * 16
     keep, kmf, *send = combine(near_code, back_near, joined, [first, half - first + EXTRA], 0)
     got = [lax.ppermute(piece, "tgt", twin) for piece in send]
     mine, confidence = call(
-        merge_last,
+        functools.partial(merge_last, side=side),
         (sds((half, width), BF16), sds((1, rows), F32)),
         factors,
-        smem=1,
-        n_in=6,
+        n_in=5,
         moved=10 * half * width,
-    )(info, keep, kmf, *got, from_far)
+    )(keep, kmf, *got, from_far)
     other = lax.ppermute(mine, "tgt", twin)
     first = jnp.where(core == 0, mine, other)
     second = jnp.where(core == 0, other, mine)

time: 141 us -> 134 us (0.950)
  Pallas kernels: 40 us -> 34 us
  waiting for transfers between devices: 68.7 us -> 62.9 us
  local copies, waits for them, and re-layouts: 3.07 us -> 7.36 us
  starting transfers between devices: 25 us -> 27.1 us
    unnamed x28 -> x30, local copies, waits for them, and re-layouts: 3.07 us -> 7.36 us
    ppermute x7, waiting for transfers between devices: 13.7 us -> 9.89 us  [shards(): lax.ppermute(far_q[k], 'src', [(i, i ^ k) for i in range(n_src)])]
    pallas_call x8, Pallas kernels: 28.2 us -> 25 us  [the longest x1 8.39 us: shards(): call(functools.partial(far_owner, block=row_block, side=side), (pltpu.HBM...]
    pallas_call x1, Pallas kernels: 8.22 us -> 5.46 us  [shards(): call(functools.partial(near_scores, **options), (sds((per_device, n_half,...]
    ppermute x7, starting transfers between devices: 6.56 us -> 9.18 us  [shards(): lax.ppermute(far_q[k], 'src', [(i, i ^ k) for i in range(n_src)])]
    all_to_all x3, waiting for transfers between devices: 38.1 us -> 35.9 us  [exchange(): lax.all_to_all(x, 'src', split_axis=0, concat_axis=0, axis_index_groups=h...]
  transfers between devices with their start and end apart: 17 -> 17, of which waited for: 11 -> 11; matrix products, arithmetic and copies ran while one was open for 1% -> 1% of each run, Pallas kernels for 20% -> 17%
where the time goes in v5:
time: 134 us
  waiting for transfers between devices  62.9 us (47%)
  Pallas kernels  34 us (25%)
  starting transfers between devices  27.1 us (20%)
  local copies, waits for them, and re-layouts  7.36 us (5%)
  other arithmetic  1.75 us (1%)
    all_to_all x3, waiting for transfers between devices, exchange(): lax.all_to_all(x, 'src', split_axis=0, concat_axis=0, axis_index_groups=h...  35.9 us
    all_to_all x3, starting transfers between devices, exchange(): lax.all_to_all(x, 'src', split_axis=0, concat_axis=0, axis_index_groups=h...  12.9 us
    ppermute x1, waiting for transfers between devices, shards(): far_mine = lax.ppermute(mine, 'src', partner)  11.3 us
    ppermute x7, waiting for transfers between devices, shards(): lax.ppermute(far_q[k], 'src', [(i, i ^ k) for i in range(n_src)])  9.89 us
    ppermute x7, starting transfers between devices, shards(): lax.ppermute(far_q[k], 'src', [(i, i ^ k) for i in range(n_src)])  9.18 us
    pallas_call x1, Pallas kernels, shards(): call(functools.partial(far_owner, block=row_block, side=side), (pltpu.HBM...  8.39 us
    unnamed x30, local copies, waits for them, and re-layouts  7.36 us
    pallas_call x2, Pallas kernels, combine(): call(functools.partial(combine_kernel, capacity=capacity, side=side), (sd...  7.15 us
  transfers between devices with their start and end apart: 17, of which 11 were waited for; matrix products, arithmetic and copies ran while one was open for 1% of the time, Pallas kernels for 17%

profile of v5, /device:TPU:0, one launch (start us, length us, event | category | flops | bytes accessed | tf_op | source)
XLA Modules:
  0.0 133.9 jit_solution(1420770902394184614)
XLA Ops:
  0.6 1.8 %shard_map.70 = bf16[208,1024]{1,0:T(8,128)(2,1)} custom-call(s32[4,384]{1,0:T(4,128)} %bitcast.2, bf16[384,1024]{1,0:T(8,128)(2,1)} %src_hbm.3), custom_call_target="tpu_custom_call" | custom-call | bytes 786432 | tf_op jit(solution)/shard_map/pallas_call | solution.py:443
  2.4 4.1 %collective-permute-start = (bf16[208,1024]{1,0:T(8,128)(2,1)}, bf16[208,1024]{1,0:T(8,128)(2,1)S(1)}, u32[]{:S(2)}, u32[]{:S(2)}) collective-permute-start(bf16[208,1024]{1,0:T(8,128)(2,1)} %shard_map.70), channel_id=1, source_target_pairs={{0,16},{2,18},{4,20},{6,22},{8,24},{10,26},{12,28},{14,30},{16,0},... | collective-permute-start | bytes 1277960 | tf_op jit(solution)/shard_map/ppermute | solution.py:452
  6.5 3.1 %shard_map.68 = (bf16[8,96,1024]{2,1,0:T(8,128)(2,1)}, f32[16,384]{1,0:T(8,128)}) custom-call(s32[4,384]{1,0:T(4,128)} %bitcast.3, s32[1,64]{1,0:T(1,128)} %bitcast.4, bf16[384,1024]{1,0:T(8,128)(2,1)} %src_hbm.3), custom_call_target="tpu_custom_call" | custom-call | flops 603979776 | bytes 2359296 | tf_op jit(solution)/shard_map/pallas_call | solution.py:463
  9.7 4.8 %all-to-all-start = ((bf16[8,96,1024]{2,1,0:T(8,128)(2,1)}), bf16[8,96,1024]{2,1,0:T(8,128)(2,1)}, u32[]{:S(2)}, u32[]{:S(2)}) async-start(bf16[8,96,1024]{2,1,0:T(8,128)(2,1)} %get-tuple-element.28), calls=%async_computation | async-start | bytes 3145728 | tf_op jit(solution)/shard_map/all_to_all | solution.py:434
  14.4 0.0 copy-start.12
  14.5 11.3 %collective-permute-done.mine_ref = bf16[208,1024]{1,0:T(8,128)(2,1)S(1)} collective-permute-done((bf16[208,1024]{1,0:T(8,128)(2,1)}, bf16[208,1024]{1,0:T(8,128)(2,1)S(1)}, u32[]{:S(2)}, u32[]{:S(2)}) %collective-permute-start) | collective-permute-done | bytes 426016 | tf_op jit(solution)/shard_map/ppermute | solution.py:452
  25.8 0.0 collective-permute-start.1
  25.8 1.8 %collective-permute-done.1.other_ref = bf16[208,1024]{1,0:T(8,128)(2,1)S(1)} collective-permute-done((bf16[208,1024]{1,0:T(8,128)(2,1)S(1)}, bf16[208,1024]{1,0:T(8,128)(2,1)S(1)}, u32[]{:S(2)}, u32[]{:S(2)}) %collective-permute-start.1) | collective-permute-done | bytes 426016 | tf_op jit(solution)/shard_map/ppermute | solution.py:453
  27.6 0.0 copy-done.13
  27.6 0.8 copy-done.14
  28.3 3.5 %shard_map.71 = (bf16[96,1024]{1,0:T(8,128)(2,1)}, bf16[96,1024]{1,0:T(8,128)(2,1)}, bf16[96,1024]{1,0:T(8,128)(2,1)}, bf16[96,1024]{1,0:T(8,128)(2,1)}, bf16[96...) custom-call(s32[1,64]{1,0:T(1,128)} %bitcast.5, ...), custom_call_target="tpu_custom_call" | custom-call | flops 20000000000 | bytes 2359296 | tf_op jit(solution)/shard_map/pallas_call | solution.py:480
  31.9 1.6 %collective-permute-start.2 = (bf16[96,1024]{1,0:T(8,128)(2,1)}, bf16[96,1024]{1,0:T(8,128)(2,1)S(1)}, u32[]{:S(2)}, u32[]{:S(2)}) collective-permute-start(bf16[96,1024]{1,0:T(8,128)(2,1)} %get-tuple-element.32), channel_id=1, source_target_pairs={{0,2},{2,0},{4,6},{6,4},{8,10},{10,8},{12,14},{14,12},{16,18},{18,... | collective-permute-start | bytes 589832 | tf_op jit(solution)/shard_map/ppermute | solution.py:491
  33.5 1.5 %collective-permute-start.3 = (bf16[96,1024]{1,0:T(8,128)(2,1)}, bf16[96,1024]{1,0:T(8,128)(2,1)S(1)}, u32[]{:S(2)}, u32[]{:S(2)}) collective-permute-start(bf16[96,1024]{1,0:T(8,128)(2,1)} %get-tuple-element.33), channel_id=1, source_target_pairs={{0,4},{2,6},{4,0},{6,2},{8,12},{10,14},{12,8},{14,10},{16,20},{18,... | collective-permute-start | bytes 589832 | tf_op jit(solution)/shard_map/ppermute | solution.py:491
  35.0 0.4 collective-permute-start.4
  35.4 0.8 collective-permute-start.5
  36.2 2.2 %collective-permute-start.6 = (bf16[96,1024]{1,0:T(8,128)(2,1)}, bf16[96,1024]{1,0:T(8,128)(2,1)}, u32[]{:S(2)}, u32[]{:S(2)}) collective-permute-start(bf16[96,1024]{1,0:T(8,128)(2,1)} %get-tuple-element.36), channel_id=1, source_target_pairs={{0,10},{2,8},{4,14},{6,12},{8,2},{10,0},{12,6},{14,4},{16,26},{18,... | collective-permute-start | bytes 589832 | tf_op jit(solution)/shard_map/ppermute | solution.py:491
  38.4 3.9 %collective-permute-done.2.refs_1_ = bf16[96,1024]{1,0:T(8,128)(2,1)S(1)} collective-permute-done((bf16[96,1024]{1,0:T(8,128)(2,1)}, bf16[96,1024]{1,0:T(8,128)(2,1)S(1)}, u32[]{:S(2)}, u32[]{:S(2)}) %collective-permute-start.2) | collective-permute-done | bytes 196640 | tf_op jit(solution)/shard_map/ppermute | solution.py:491
  42.3 0.7 copy-done.5
  43.0 0.0 collective-permute-start.7
  43.0 0.3 collective-permute-done.3.refs_2_
  43.3 0.7 copy-done.7
  44.0 2.6 %collective-permute-start.8 = (bf16[96,1024]{1,0:T(8,128)(2,1)}, bf16[96,1024]{1,0:T(8,128)(2,1)}, u32[]{:S(2)}, u32[]{:S(2)}) collective-permute-start(bf16[96,1024]{1,0:T(8,128)(2,1)} %get-tuple-element.38), channel_id=1, source_target_pairs={{0,14},{2,12},{4,10},{6,8},{8,6},{10,4},{12,2},{14,0},{16,30},{18,... | collective-permute-start | bytes 589832 | tf_op jit(solution)/shard_map/ppermute | solution.py:491
  46.6 0.0 copy-done.11
  46.6 0.0 copy-done.12
  46.6 0.2 fusion.count_ref
  46.8 0.0 all-to-all-done.q_ref
  46.8 0.0 copy-start
  46.8 2.2 %copy-done = bf16[2,1024,1024]{2,1,0:T(8,128)(2,1)S(1)} copy-done((bf16[2,1024,1024]{2,1,0:T(8,128)(2,1)S(1)}, bf16[2,1024,1024]{2,1,0:T(8,128)(2,1)}, u32[]{:S(2)}) %copy-start) | copy-done | bytes 4194328
  49.0 5.5 %shard_map.69 = (f32[2,384,1024]{2,1,0:T(8,128)S(1)}, f32[2,8,1024]{2,1,0:T(8,128)S(1)}, f32[2,384,128]{2,1,0:T(8,128)S(1)}) custom-call(s32[2]{0:T(128)S(1)} %fusion.count_ref, bf16[8,96,1024]{2,1,0:T(8,128)(2,1)} %all-to-all-done.q_ref, bf16[2,1024,1024]{2,1,0:T(8,128)(2,1)S(1)} %copy-done), custom_call_target="tpu_custom_call" | custom-call | flops 1610612736 | bytes 5767168 | tf_op jit(solution)/shard_map/pallas_call | solution.py:502
  54.4 0.0 collective-permute-done.4.refs_3_
  54.5 0.0 collective-permute-done.5.refs_4_
  54.5 0.0 collective-permute-done.6.refs_5_
  54.5 1.6 %collective-permute-done.7.refs_6_ = bf16[96,1024]{1,0:T(8,128)(2,1)} collective-permute-done((bf16[96,1024]{1,0:T(8,128)(2,1)}, bf16[96,1024]{1,0:T(8,128)(2,1)}, u32[]{:S(2)}, u32[]{:S(2)}) %collective-permute-start.7) | collective-permute-done | bytes 196640 | tf_op jit(solution)/shard_map/ppermute | solution.py:491
  56.0 4.1 %collective-permute-done.8.refs_7_ = bf16[96,1024]{1,0:T(8,128)(2,1)} collective-permute-done((bf16[96,1024]{1,0:T(8,128)(2,1)}, bf16[96,1024]{1,0:T(8,128)(2,1)}, u32[]{:S(2)}, u32[]{:S(2)}) %collective-permute-start.8) | collective-permute-done | bytes 196640 | tf_op jit(solution)/shard_map/ppermute | solution.py:491
  60.2 0.0 copy-done.1
  60.2 0.0 copy-done.6
  60.2 0.0 copy-done.8
  60.2 0.0 copy-done.9
  60.2 8.4 %shard_map.72 = (bf16[8,49,16,128]{3,2,1,0:T(8,128)(2,1)}, f32[2,8,1024]{2,1,0:T(8,128)}) custom-call(s32[2]{0:T(128)S(1)} %fusion.count_ref, f32[2,8,1024]{2,1,0:T(8,128)S(1)} %get-tuple-element.30.col_ref, bf16[2,1024,1024]{2,1,0:T(8,128)(2,1)S(1)} %copy-done.1, bf16[96,1024]{1,0:T(8,128)(2,1)S(1)} %copy-done.9, bf16[96,1024]{1,0:T(8,128)(2,1)S(1)} %copy-done.6, ...), custom_call_target="tpu_custom_call" | custom-call | flops 1610612736 | bytes 5767168 | tf_op jit(solution)/shard_map/pallas_call | solution.py:515
  68.6 4.5 %all-to-all-start.2 = ((bf16[8,49,16,128]{3,2,1,0:T(8,128)(2,1)}), bf16[8,49,16,128]{3,2,1,0:T(8,128)(2,1)}, u32[]{:S(2)}, u32[]{:S(2)}) async-start(bf16[8,49,16,128]{3,2,1,0:T(8,128)(2,1)} %get-tuple-element.42), calls=%async_computation.2 | async-start | bytes 3211264 | tf_op jit(solution)/shard_map/all_to_all | solution.py:434
  73.1 0.0 copy-start.2
  73.1 2.2 %copy-done.2 = bf16[2,1024,1024]{2,1,0:T(8,128)(2,1)S(1)} copy-done((bf16[2,1024,1024]{2,1,0:T(8,128)(2,1)S(1)}, bf16[2,1024,1024]{2,1,0:T(8,128)(2,1)}, u32[]{:S(2)}) %copy-start.2) | copy-done | bytes 4194328
  75.3 0.8 copy-done.3
  76.1 3.6 %shard_map.73 = bf16[8,49,16,128]{3,2,1,0:T(8,128)(2,1)} custom-call(f32[2,384,1024]{2,1,0:T(8,128)S(1)} %get-tuple-element.29.s_ref, f32[2,8,1024]{2,1,0:T(8,128)S(1)} %copy-done.3, f32[2,384,128]{2,1,0:T(8,128)S(1)} %get-tuple-element.40.fwd_ref, bf16[2,1024,1024]{2,1,0:T(8,128)(2,1)S(1)} %copy-done.2), custom_call_target="tpu_custom_call" | custom-call | flops 1610612736 | bytes 5767168 | tf_op jit(solution)/shard_map/pallas_call | solution.py:535
  79.8 13.6 %all-to-all-done.2.r_ref = bf16[8,49,16,128]{3,2,1,0:T(8,128)(2,1)} async-done(((bf16[8,49,16,128]{3,2,1,0:T(8,128)(2,1)}), bf16[8,49,16,128]{3,2,1,0:T(8,128)(2,1)}, u32[]{:S(2)}, u32[]{:S(2)}) %all-to-all-start.2) | async-done | bytes 1605664 | tf_op jit(solution)/shard_map/all_to_all | solution.py:434
  93.3 3.6 %all-to-all-start.1 = ((bf16[8,49,16,128]{3,2,1,0:T(8,128)(2,1)}), bf16[8,49,16,128]{3,2,1,0:T(8,128)(2,1)S(1)}, u32[]{:S(2)}, u32[]{:S(2)}) async-start(bf16[8,49,16,128]{3,2,1,0:T(8,128)(2,1)} %shard_map.73), calls=%async_computation.1 | async-start | bytes 3211264 | tf_op jit(solution)/shard_map/all_to_all | solution.py:434
  97.0 4.3 %shard_map.74 = (f32[192,1024]{1,0:T(8,128)S(1)}, f32[8,384]{1,0:T(8,128)S(1)}, bf16[208,1024]{1,0:T(8,128)(2,1)S(1)}) custom-call(f32[16,384]{1,0:T(8,128)S(1)} %copy-done.10, bf16[8,49,16,128]{3,2,1,0:T(8,128)(2,1)} %all-to-all-done.2.r_ref, f32[16,384]{1,0:T(8,128)S(1)} %copy-done.4), custom_call_target="tpu_custom_call" | custom-call | flops 1207959552 | bytes 3145728 | tf_op jit(solution)/shard_map/pallas_call | solution.py:546
  101.2 0.1 collective-permute-start.9
  101.3 1.8 %collective-permute-done.9.got_ref = bf16[208,1024]{1,0:T(8,128)(2,1)S(1)} collective-permute-done((bf16[208,1024]{1,0:T(8,128)(2,1)S(1)}, bf16[208,1024]{1,0:T(8,128)(2,1)S(1)}, u32[]{:S(2)}, u32[]{:S(2)}) %collective-permute-start.9) | collective-permute-done | bytes 426016 | tf_op jit(solution)/shard_map/ppermute | solution.py:557
  103.1 0.4 shard_map.75._
  103.5 0.1 collective-permute-start.12
  103.5 22.4 %all-to-all-done.1.r_ref = bf16[8,49,16,128]{3,2,1,0:T(8,128)(2,1)S(1)} async-done(((bf16[8,49,16,128]{3,2,1,0:T(8,128)(2,1)}), bf16[8,49,16,128]{3,2,1,0:T(8,128)(2,1)S(1)}, u32[]{:S(2)}, u32[]{:S(2)}) %all-to-all-start.1) | async-done | bytes 1605664 | tf_op jit(solution)/shard_map/all_to_all | solution.py:434
  125.9 2.9 %shard_map.76 = (f32[192,1024]{1,0:T(8,128)S(1)}, f32[8,384]{1,0:T(8,128)S(1)}, bf16[96,1024]{1,0:T(8,128)(2,1)S(1)}, bf16[112,1024]{1,0:T(8,128)(2,1)S(1)}) custom-call(f32[16,384]{1,0:T(8,128)S(1)} %copy-done.4, bf16[8,49,16,128]{3,2,1,0:T(8,128)(2,1)S(1)} %all-to-all-done.1.r_ref, bf16[208,1024]{1,0:T(8,128)(2,1)S(1)} %shard_map.75._), custom_call_target="tpu_custom_call" | custom-call | tf_op jit(solution)/shard_map/pallas_call | solution.py:546
  128.8 0.1 collective-permute-start.11
  128.9 0.5 collective-permute-start.10
  129.4 1.3 collective-permute-done.10.got_ref
  130.6 0.0 collective-permute-done.11.last_ref
  130.6 0.0 collective-permute-done.12.far_ref
  130.7 0.5 shard_map.77
  131.1 0.2 collective-permute-start.13
  131.4 0.6 convert_reduce_fusion
  132.0 1.0 collective-permute-done.13
  132.9 0.1 broadcast_select_fusion.1
  133.0 0.9 pad_maximum_fusion
  (15 shorter events, 0.0 us)
Async XLA Ops:
  2.4 23.4 %collective-permute-start = (bf16[208,1024]{1,0:T(8,128)(2,1)}, bf16[208,1024]{1,0:T(8,128)(2,1)S(1)}, u32[]{:S(2)}, u32[]{:S(2)}) collective-permute-start(bf16[208,1024]{1,0:T(8,128)(2,1)} %shard_map.70), channel_id=1, source_target_pairs={{0,16},{2,18},{4,20},{6,22},{8,24},{10,26},{12,28},{14,30},{16,0},... | collective-permute-start | bytes 1277960 | tf_op jit(solution)/shard_map/ppermute | solution.py:452
  9.7 37.1 %all-to-all-start = ((bf16[8,96,1024]{2,1,0:T(8,128)(2,1)}), bf16[8,96,1024]{2,1,0:T(8,128)(2,1)}, u32[]{:S(2)}, u32[]{:S(2)}) async-start(bf16[8,96,1024]{2,1,0:T(8,128)(2,1)} %get-tuple-element.28), calls=%async_computation | async-start | bytes 3145728 | tf_op jit(solution)/shard_map/all_to_all | solution.py:434
  14.4 32.1 %copy-start.11 = (s32[64]{0:T(128)S(1)}, s32[64]{0:T(128)}, u32[]{:S(2)}) copy-start(s32[64]{0:T(128)} %param.8) | copy-start | bytes 772
  14.4 32.1 %copy-start.12 = (s32[64]{0:T(128)S(1)}, s32[64]{0:T(128)}, u32[]{:S(2)}) copy-start(s32[64]{0:T(128)} %param.9) | copy-start | bytes 772
  25.8 1.8 %copy-start.13 = (bf16[208,1024]{1,0:T(8,128)(2,1)}, bf16[208,1024]{1,0:T(8,128)(2,1)S(1)}, u32[]{:S(2)}) copy-start(bf16[208,1024]{1,0:T(8,128)(2,1)S(1)} %collective-permute-done.mine_ref) | copy-start | bytes 1277956
  25.8 1.8 %collective-permute-start.1 = (bf16[208,1024]{1,0:T(8,128)(2,1)S(1)}, bf16[208,1024]{1,0:T(8,128)(2,1)S(1)}, u32[]{:S(2)}, u32[]{:S(2)}) collective-permute-start(bf16[208,1024]{1,0:T(8,128)(2,1)S(1)} %collective-permute-done.mine_ref), channel_id=1, source_target_pairs={{0,1},{1,0},{2,3},{3,2},{4,5},{5,4},{6,7},{7,6},{8,9},{9,8},{10,11... | collective-permute-start | bytes 1277960 | tf_op jit(solution)/shard_map/ppermute | solution.py:453
  27.6 0.8 copy-start.14
  31.9 10.5 %collective-permute-start.2 = (bf16[96,1024]{1,0:T(8,128)(2,1)}, bf16[96,1024]{1,0:T(8,128)(2,1)S(1)}, u32[]{:S(2)}, u32[]{:S(2)}) collective-permute-start(bf16[96,1024]{1,0:T(8,128)(2,1)} %get-tuple-element.32), channel_id=1, source_target_pairs={{0,2},{2,0},{4,6},{6,4},{8,10},{10,8},{12,14},{14,12},{16,18},{18,... | collective-permute-start | bytes 589832 | tf_op jit(solution)/shard_map/ppermute | solution.py:491
  33.5 9.8 %collective-permute-start.3 = (bf16[96,1024]{1,0:T(8,128)(2,1)}, bf16[96,1024]{1,0:T(8,128)(2,1)S(1)}, u32[]{:S(2)}, u32[]{:S(2)}) collective-permute-start(bf16[96,1024]{1,0:T(8,128)(2,1)} %get-tuple-element.33), channel_id=1, source_target_pairs={{0,4},{2,6},{4,0},{6,2},{8,12},{10,14},{12,8},{14,10},{16,20},{18,... | collective-permute-start | bytes 589832 | tf_op jit(solution)/shard_map/ppermute | solution.py:491
  35.0 19.5 %collective-permute-start.4 = (bf16[96,1024]{1,0:T(8,128)(2,1)}, bf16[96,1024]{1,0:T(8,128)(2,1)}, u32[]{:S(2)}, u32[]{:S(2)}) collective-permute-start(bf16[96,1024]{1,0:T(8,128)(2,1)} %get-tuple-element.34), channel_id=1, source_target_pairs={{0,6},{2,4},{4,2},{6,0},{8,14},{10,12},{12,10},{14,8},{16,22},{18,... | collective-permute-start | bytes 589832 | tf_op jit(solution)/shard_map/ppermute | solution.py:491
  35.4 19.0 %collective-permute-start.5 = (bf16[96,1024]{1,0:T(8,128)(2,1)}, bf16[96,1024]{1,0:T(8,128)(2,1)}, u32[]{:S(2)}, u32[]{:S(2)}) collective-permute-start(bf16[96,1024]{1,0:T(8,128)(2,1)} %get-tuple-element.35), channel_id=1, source_target_pairs={{0,8},{2,10},{4,12},{6,14},{8,0},{10,2},{12,4},{14,6},{16,24},{18,... | collective-permute-start | bytes 589832 | tf_op jit(solution)/shard_map/ppermute | solution.py:491
  36.2 18.3 %collective-permute-start.6 = (bf16[96,1024]{1,0:T(8,128)(2,1)}, bf16[96,1024]{1,0:T(8,128)(2,1)}, u32[]{:S(2)}, u32[]{:S(2)}) collective-permute-start(bf16[96,1024]{1,0:T(8,128)(2,1)} %get-tuple-element.36), channel_id=1, source_target_pairs={{0,10},{2,8},{4,14},{6,12},{8,2},{10,0},{12,6},{14,4},{16,26},{18,... | collective-permute-start | bytes 589832 | tf_op jit(solution)/shard_map/ppermute | solution.py:491
  42.3 0.7 copy-start.5
  43.0 13.0 %collective-permute-start.7 = (bf16[96,1024]{1,0:T(8,128)(2,1)}, bf16[96,1024]{1,0:T(8,128)(2,1)}, u32[]{:S(2)}, u32[]{:S(2)}) collective-permute-start(bf16[96,1024]{1,0:T(8,128)(2,1)} %get-tuple-element.37), channel_id=1, source_target_pairs={{0,12},{2,14},{4,8},{6,10},{8,4},{10,6},{12,0},{14,2},{16,28},{18,... | collective-permute-start | bytes 589832 | tf_op jit(solution)/shard_map/ppermute | solution.py:491
  43.3 0.7 copy-start.7
  44.0 16.2 %collective-permute-start.8 = (bf16[96,1024]{1,0:T(8,128)(2,1)}, bf16[96,1024]{1,0:T(8,128)(2,1)}, u32[]{:S(2)}, u32[]{:S(2)}) collective-permute-start(bf16[96,1024]{1,0:T(8,128)(2,1)} %get-tuple-element.38), channel_id=1, source_target_pairs={{0,14},{2,12},{4,10},{6,8},{8,6},{10,4},{12,2},{14,0},{16,30},{18,... | collective-permute-start | bytes 589832 | tf_op jit(solution)/shard_map/ppermute | solution.py:491
  46.8 2.2 %copy-start = (bf16[2,1024,1024]{2,1,0:T(8,128)(2,1)S(1)}, bf16[2,1024,1024]{2,1,0:T(8,128)(2,1)}, u32[]{:S(2)}) copy-start(bf16[2,1024,1024]{2,1,0:T(8,128)(2,1)} %t_ref.5) | copy-start | bytes 12582916
  49.0 11.2 %copy-start.1 = (bf16[2,1024,1024]{2,1,0:T(8,128)(2,1)S(1)}, bf16[2,1024,1024]{2,1,0:T(8,128)(2,1)}, u32[]{:S(2)}) copy-start(bf16[2,1024,1024]{2,1,0:T(8,128)(2,1)} %t_ref.5) | copy-start | bytes 12582916
  49.0 11.2 %copy-start.6 = (bf16[96,1024]{1,0:T(8,128)(2,1)S(1)}, bf16[96,1024]{1,0:T(8,128)(2,1)}, u32[]{:S(2)}) copy-start(bf16[96,1024]{1,0:T(8,128)(2,1)} %copy-done.5) | copy-start | bytes 589828
  49.0 11.2 %copy-start.8 = (bf16[96,1024]{1,0:T(8,128)(2,1)S(1)}, bf16[96,1024]{1,0:T(8,128)(2,1)}, u32[]{:S(2)}) copy-start(bf16[96,1024]{1,0:T(8,128)(2,1)} %copy-done.7) | copy-start | bytes 589828
  49.0 11.2 %copy-start.9 = (bf16[96,1024]{1,0:T(8,128)(2,1)S(1)}, bf16[96,1024]{1,0:T(8,128)(2,1)}, u32[]{:S(2)}) copy-start(bf16[96,1024]{1,0:T(8,128)(2,1)} %get-tuple-element.31.refs_0_) | copy-start | bytes 589828
  68.6 24.7 %all-to-all-start.2 = ((bf16[8,49,16,128]{3,2,1,0:T(8,128)(2,1)}), bf16[8,49,16,128]{3,2,1,0:T(8,128)(2,1)}, u32[]{:S(2)}, u32[]{:S(2)}) async-start(bf16[8,49,16,128]{3,2,1,0:T(8,128)(2,1)} %get-tuple-element.42), calls=%async_computation.2 | async-start | bytes 3211264 | tf_op jit(solution)/shard_map/all_to_all | solution.py:434
  73.1 2.2 %copy-start.2 = (bf16[2,1024,1024]{2,1,0:T(8,128)(2,1)S(1)}, bf16[2,1024,1024]{2,1,0:T(8,128)(2,1)}, u32[]{:S(2)}) copy-start(bf16[2,1024,1024]{2,1,0:T(8,128)(2,1)} %t_ref.5) | copy-start | bytes 12582916
  75.3 0.8 copy-start.3
  79.8 17.2 %copy-start.4 = (f32[16,384]{1,0:T(8,128)S(1)}, f32[16,384]{1,0:T(8,128)}, u32[]{:S(2)}) copy-start(f32[16,384]{1,0:T(8,128)} %get-tuple-element.27._.code_ref) | copy-start | bytes 73732
  79.8 17.2 %copy-start.10 = (f32[16,384]{1,0:T(8,128)S(1)}, f32[16,384]{1,0:T(8,128)}, u32[]{:S(2)}) copy-start(f32[16,384]{1,0:T(8,128)} %get-tuple-element.41.code_ref) | copy-start | bytes 73732
  93.3 32.6 %all-to-all-start.1 = ((bf16[8,49,16,128]{3,2,1,0:T(8,128)(2,1)}), bf16[8,49,16,128]{3,2,1,0:T(8,128)(2,1)S(1)}, u32[]{:S(2)}, u32[]{:S(2)}) async-start(bf16[8,49,16,128]{3,2,1,0:T(8,128)(2,1)} %shard_map.73), calls=%async_computation.1 | async-start | bytes 3211264 | tf_op jit(solution)/shard_map/all_to_all | solution.py:434
  101.2 1.8 %collective-permute-start.9 = (bf16[208,1024]{1,0:T(8,128)(2,1)S(1)}, bf16[208,1024]{1,0:T(8,128)(2,1)S(1)}, u32[]{:S(2)}, u32[]{:S(2)}) collective-permute-start(bf16[208,1024]{1,0:T(8,128)(2,1)S(1)} %get-tuple-element.45), channel_id=1, source_target_pairs={{0,1},{1,0},{2,3},{3,2},{4,5},{5,4},{6,7},{7,6},{8,9},{9,8},{10,11... | collective-permute-start | bytes 1277960 | tf_op jit(solution)/shard_map/ppermute | solution.py:557
  103.5 27.2 %collective-permute-start.12 = (bf16[208,1024]{1,0:T(8,128)(2,1)S(1)}, bf16[208,1024]{1,0:T(8,128)(2,1)S(1)}, u32[]{:S(2)}, u32[]{:S(2)}) collective-permute-start(bf16[208,1024]{1,0:T(8,128)(2,1)S(1)} %shard_map.75._), channel_id=1, source_target_pairs={{0,16},{2,18},{4,20},{6,22},{8,24},{10,26},{12,28},{14,30},{16,0},... | collective-permute-start | bytes 1277960 | tf_op jit(solution)/shard_map/ppermute | solution.py:562
  128.8 1.8 %collective-permute-start.11 = (bf16[112,1024]{1,0:T(8,128)(2,1)S(1)}, bf16[112,1024]{1,0:T(8,128)(2,1)S(1)}, u32[]{:S(2)}, u32[]{:S(2)}) collective-permute-start(bf16[112,1024]{1,0:T(8,128)(2,1)S(1)} %get-tuple-element.49), channel_id=1, source_target_pairs={{0,1},{1,0},{2,3},{3,2},{4,5},{5,4},{6,7},{7,6},{8,9},{9,8},{10,11... | collective-permute-start | bytes 688136 | tf_op jit(solution)/shard_map/ppermute | solution.py:566
  128.9 1.8 %collective-permute-start.10 = (bf16[96,1024]{1,0:T(8,128)(2,1)S(1)}, bf16[96,1024]{1,0:T(8,128)(2,1)S(1)}, u32[]{:S(2)}, u32[]{:S(2)}) collective-permute-start(bf16[96,1024]{1,0:T(8,128)(2,1)S(1)} %get-tuple-element.48), channel_id=1, source_target_pairs={{0,1},{1,0},{2,3},{3,2},{4,5},{5,4},{6,7},{7,6},{8,9},{9,8},{10,11... | collective-permute-start | bytes 589832 | tf_op jit(solution)/shard_map/ppermute | solution.py:566
  131.1 1.8 %collective-permute-start.13 = (bf16[192,1024]{1,0:T(8,128)(2,1)S(1)}, bf16[192,1024]{1,0:T(8,128)(2,1)S(1)}, u32[]{:S(2)}, u32[]{:S(2)}) collective-permute-start(bf16[192,1024]{1,0:T(8,128)(2,1)S(1)} %get-tuple-element.50), channel_id=1, source_target_pairs={{0,1},{1,0},{2,3},{3,2},{4,5},{5,4},{6,7},{7,6},{8,9},{9,8},{10,11... | collective-permute-start | bytes 1179656 | tf_op jit(solution)/shard_map/ppermute | solution.py:574

commit v6 on v5

--- a/solution.py
+++ b/solution.py
@@ -319,9 +319,9 @@
     p_ref[:, p_ref.shape[1] - 1] = tail_ref[...].astype(BF16)
 
 
-def combine_kernel(code_ref, r_ref, _, keep_ref, kmf_ref, *refs, capacity, side):
+def combine_kernel(code_ref, r_ref, _, *refs, capacity, side, split):
     _, core, _ = place_of(side)
-    *send_refs, r_scr, scr = refs
+    *outs, r_scr, scr = refs
     n_buckets, rows = code_ref.shape
     width = scr.shape[1]
     half = rows // 2
@@ -355,15 +355,20 @@
     over = (((0,), (0,)), ((), ()))
     pooled = lax.dot_general(high, r, over, preferred_element_type=F32)
     scr[...] = pooled + lax.dot_general(low, r, over, preferred_element_type=F32)
-    keep_ref[...] = scr[pl.ds(pl.multiple_of(core * half, 16), half), :]
-    start = 0
-    for ref in send_refs:
-        count = min(ref.shape[0], half - start)
-        at = pl.ds(pl.multiple_of((1 - core) * half + start, 16), count)
-        ref[:count, :] = scr[at, :].astype(BF16)
-        start = start + count
-    send_refs[-1][count:, :] = extra_rows(margin_row, forward_row, width)
-    kmf_ref[...] = jnp.concatenate([margin_row, forward_row, jnp.zeros((6, rows), F32)], axis=0)
+    last = extra_rows(margin_row, forward_row, width)
+    if split:
+        keep_ref, kmf_ref, send_ref = outs
+        keep_ref[...] = scr[pl.ds(pl.multiple_of(core * half, 16), half), :]
+        send_ref[:half, :] = scr[pl.ds(pl.multiple_of((1 - core) * half, 16), half), :].astype(BF16)
+        send_ref[half:, :] = last
+        kmf_ref[...] = jnp.concatenate([margin_row, forward_row, jnp.zeros((6, rows), F32)], axis=0)
+    else:
+        start = 0
+        for ref in outs:
+            count = min(ref.shape[0], rows - start)
+            ref[:count, :] = scr[start : start + count, :].astype(BF16)
+            start = start + count
+        outs[-1][count:, :] = last
 
 
 def log_sum(first, second, third=None):
@@ -390,24 +395,33 @@
     out_ref[half:, :] = extra_rows(margin_all, forward_all, width)
 
 
-def merge_last(keep_ref, kmf_ref, got_ref, last_ref, far_ref, out_ref, conf_ref, scr, *, side):
+def merge_last(*refs, n_pieces, side):
     _, core, _ = place_of(side)
-    half, width = keep_ref.shape
-    rows = kmf_ref.shape[1]
-    margin, forward = kmf_ref[0:1, :], kmf_ref[1:2, :]
-    first = got_ref.shape[0]
-    margin_b, forward_b = read_extra(last_ref, half - first, rows)
-    margin_c, forward_c = read_extra(far_ref, half, rows)
-    margin_all = log_sum(margin, margin_b, margin_c)
-    forward_all = log_sum(forward, forward_b, forward_c)
-    scr[...] = columns(
-        [jnp.exp2(margin - margin_all), jnp.exp2(margin_b - margin_all), jnp.exp2(margin_c - margin_all)], rows
-    )
-    factors = scr[pl.ds(pl.multiple_of(core * half, 16), half), :]
-    for at, ref in ((slice(0, first), got_ref), (slice(first, half), last_ref)):
-        out = keep_ref[at, :] * factors[at, 0:1] + ref[: at.stop - at.start, :].astype(F32) * factors[at, 1:2]
-        out_ref[at, :] = (out + far_ref[at, :].astype(F32) * factors[at, 2:3]).astype(BF16)
+    own, got = refs[:n_pieces], refs[n_pieces : 2 * n_pieces]
+    mine_ref, other_ref, out_ref, conf_ref, far_scr = refs[2 * n_pieces :]
+    rows, width = out_ref.shape
+    half = rows // 2
+    first_core = core == 0
+    far_scr[pl.ds(pl.multiple_of(core * half, 16), half), :] = mine_ref[:half, :]
+    far_scr[pl.ds(pl.multiple_of((1 - core) * half, 16), half), :] = other_ref[:half, :]
+    last = own[-1].shape[0] - EXTRA
+    pair = read_extra(own[-1], last, rows), read_extra(got[-1], last, rows)
+    margin_a, forward_a = [jnp.where(first_core, x, y) for x, y in zip(*pair)]
+    margin_b, forward_b = [jnp.where(first_core, y, x) for x, y in zip(*pair)]
+    margin_c, forward_c = read_extra(mine_ref, half, rows)
+    margin_all = log_sum(margin_a, margin_b, margin_c)
+    forward_all = log_sum(forward_a, forward_b, forward_c)
     conf_ref[...] = (margin_all - 0.5 * forward_all) * LN2
+    factors = columns([jnp.exp2(x - margin_all) for x in (margin_a, margin_b, margin_c)], rows)
+    start = 0
+    for x_ref, y_ref in zip(own, got):
+        count = min(x_ref.shape[0], rows - start)
+        at = slice(start, start + count)
+        x, y = x_ref[:count, :], y_ref[:count, :]
+        a = jnp.where(first_core, x, y).astype(F32) * factors[at, 0:1]
+        b = jnp.where(first_core, y, x).astype(F32) * factors[at, 1:2]
+        out_ref[at, :] = (a + b + far_scr[at, :].astype(F32) * factors[at, 2:3]).astype(BF16)
+        start = start + count
 
 
 def shards(sources, targets, picks, cluster_home, row_count):
@@ -479,11 +493,10 @@
     near_in = exchange(near_q)
     *far_q, far_code = call(
         functools.partial(gather_partner, n_picks=n_picks, **sizes),
-        tuple([sds((message, width), BF16)] * side) + gather_out[1:],
+        tuple([pltpu.HBM((message, width), BF16)] * side) + (pltpu.HBM((n_buckets, rows), F32),),
         gather_scratch + [pltpu.VMEM((rows, width), BF16)],
         flops=HIDE,
         moved=moved,
-        limit=FULL,
         in_specs=[vmem] * 3,
         out_specs=tuple([hbm] * (side + 1)),
     )(home, far_mine, far_other)
@@ -542,39 +555,41 @@
     )(near_s, reverse, near_fwd, targets)
     back_near = exchange(near_pool)
 
-    def combine(code, back, after, pieces, weight):
+    def combine(code, back, after, outs, weight, split):
         return call(
-            functools.partial(combine_kernel, capacity=capacity, side=side),
-            (sds((half, width), F32), sds((8, rows), F32)) + tuple(sds((n, width), BF16) for n in pieces),
+            functools.partial(combine_kernel, capacity=capacity, side=side, split=split),
+            outs,
             [pltpu.VMEM((n_slots, width), BF16), pltpu.VMEM((rows, width), F32)],
             flops=weight * 4 * n_slots * rows * width,
             moved=weight * 2 * (n_slots + 2 * rows) * width,
             in_specs=[vmem, vmem, unread],
-            out_specs=tuple([vmem] * (2 + len(pieces))),
+            out_specs=tuple([vmem] * len(outs)),
         )(code, back, after)
 
-    keep, kmf, send = combine(far_code, back_far, near_code, [half + EXTRA], 1)
+    outs = (sds((half, width), F32), sds((8, rows), F32), letter)
+    keep, kmf, send = combine(far_code, back_far, near_code, outs, 1, True)
     got = lax.ppermute(send, "tgt", twin)
-    factors = [pltpu.VMEM((rows, 128), F32)]
     joined = call(
-        functools.partial(merge_pair, side=side), letter, factors, n_in=3, moved=10 * half * width
+        functools.partial(merge_pair, side=side),
+        letter,
+        [pltpu.VMEM((rows, 128), F32)],
+        n_in=3,
+        moved=10 * half * width,
     )(keep, kmf, got)
     from_far = lax.ppermute(joined, "src", partner)
-
-    first = half // 32 * 16
-    keep, kmf, *send = combine(near_code, back_near, joined, [first, half - first + EXTRA], 0)
-    got = [lax.ppermute(piece, "tgt", twin) for piece in send]
-    mine, confidence = call(
-        functools.partial(merge_last, side=side),
-        (sds((half, width), BF16), sds((1, rows), F32)),
-        factors,
-        n_in=5,
-        moved=10 * half * width,
-    )(keep, kmf, *got, from_far)
-    other = lax.ppermute(mine, "tgt", twin)
-    first = jnp.where(core == 0, mine, other)
-    second = jnp.where(core == 0, other, mine)
-    return (jnp.concatenate([first, second], axis=0), confidence[0].astype(BF16))
+    from_far_other = lax.ppermute(from_far, "tgt", twin)
+
+    pieces = [rows // 4] * 3 + [rows // 4 + EXTRA]
+    own = combine(near_code, back_near, joined, tuple(sds((n, width), BF16) for n in pieces), 0, False)
+    got = [lax.ppermute(piece, "tgt", twin) for piece in own]
+    pooled, confidence = call(
+        functools.partial(merge_last, n_pieces=len(pieces), side=side),
+        (sds((rows, width), BF16), sds((1, rows), F32)),
+        [pltpu.VMEM((rows, width), BF16)],
+        n_in=2 * len(pieces) + 2,
+        moved=10 * rows * width,
+    )(*own, *got, from_far, from_far_other)
+    return (pooled, confidence[0].astype(BF16))
 
 
 def solution(mesh):

time: 134 us -> 134 us (level)
  starting transfers between devices: 27.1 us -> 24.8 us
  waiting for transfers between devices: 62.9 us -> 65 us
  local copies, waits for them, and re-layouts: 7.36 us -> 9.19 us
  Pallas kernels: 34 us -> 32.6 us
    all_to_all x3, waiting for transfers between devices: 35.9 us -> 13.9 us  [exchange(): lax.all_to_all(x, 'src', split_axis=0, concat_axis=0, axis_index_groups=h...]
    ppermute x1, waiting for transfers between devices: 0.01 us -> 22 us  [shards(): from_far = lax.ppermute(joined, 'src', partner)]
    ppermute x7, waiting for transfers between devices: 9.89 us -> 12.9 us  [shards(): lax.ppermute(far_q[k], 'src', [(i, i ^ k) for i in range(n_src)])]
    ppermute x7, starting transfers between devices: 9.18 us -> 6.56 us  [shards(): lax.ppermute(far_q[k], 'src', [(i, i ^ k) for i in range(n_src)])]
    unnamed x30, local copies, waits for them, and re-layouts: 7.36 us -> 9.19 us
  transfers between devices with their start and end apart: 17 -> 19, of which waited for: 11 -> 12; matrix products, arithmetic and copies ran while one was open for 1% -> 0% of each run, Pallas kernels for 17% -> 16%
where the time goes in v6:
time: 134 us; the launch traced here: 133 us
  waiting for transfers between devices  65 us (49%)
  Pallas kernels  32.6 us (24%)
  starting transfers between devices  24.8 us (19%)
  local copies, waits for them, and re-layouts  9.19 us (7%)
    ppermute x1, waiting for transfers between devices, shards(): from_far = lax.ppermute(joined, 'src', partner)  22 us
    all_to_all x3, waiting for transfers between devices, exchange(): lax.all_to_all(x, 'src', split_axis=0, concat_axis=0, axis_index_groups=h...  13.9 us
    all_to_all x3, starting transfers between devices, exchange(): lax.all_to_all(x, 'src', split_axis=0, concat_axis=0, axis_index_groups=h...  12.9 us
    ppermute x7, waiting for transfers between devices, shards(): lax.ppermute(far_q[k], 'src', [(i, i ^ k) for i in range(n_src)])  12.9 us
    ppermute x1, waiting for transfers between devices, shards(): far_mine = lax.ppermute(mine, 'src', partner)  11.3 us
    unnamed x30, local copies, waits for them, and re-layouts  9.19 us
    pallas_call x1, Pallas kernels, shards(): call(functools.partial(far_owner, block=row_block, side=side), (pltpu.HBM...  8.41 us
    pallas_call x2, Pallas kernels, combine(): call(functools.partial(combine_kernel, capacity=capacity, side=side, spli...  6.79 us
  transfers between devices with their start and end apart: 19, of which 12 were waited for; matrix products, arithmetic and copies ran while one was open for 0% of the time, Pallas kernels for 16%

profile of v6, /device:TPU:0, one launch (start us, length us, event | category | flops | bytes accessed | tf_op | source)
XLA Modules:
  0.0 133.1 jit_solution(13249640875516521892)
XLA Ops:
  0.6 1.8 %shard_map.70 = bf16[208,1024]{1,0:T(8,128)(2,1)} custom-call(s32[4,384]{1,0:T(4,128)} %bitcast.4, bf16[384,1024]{1,0:T(8,128)(2,1)} %src_hbm.3), custom_call_target="tpu_custom_call" | custom-call | bytes 786432 | tf_op jit(solution)/shard_map/pallas_call | solution.py:457
  2.4 4.1 %collective-permute-start = (bf16[208,1024]{1,0:T(8,128)(2,1)}, bf16[208,1024]{1,0:T(8,128)(2,1)S(1)}, u32[]{:S(2)}, u32[]{:S(2)}) collective-permute-start(bf16[208,1024]{1,0:T(8,128)(2,1)} %shard_map.70), channel_id=1, source_target_pairs={{0,16},{2,18},{4,20},{6,22},{8,24},{10,26},{12,28},{14,30},{16,0},... | collective-permute-start | bytes 1277960 | tf_op jit(solution)/shard_map/ppermute | solution.py:466
  6.5 3.2 %shard_map.68 = (bf16[8,96,1024]{2,1,0:T(8,128)(2,1)}, f32[16,384]{1,0:T(8,128)}) custom-call(s32[4,384]{1,0:T(4,128)} %bitcast.5, s32[1,64]{1,0:T(1,128)} %bitcast.2, bf16[384,1024]{1,0:T(8,128)(2,1)} %src_hbm.3), custom_call_target="tpu_custom_call" | custom-call | flops 603979776 | bytes 2359296 | tf_op jit(solution)/shard_map/pallas_call | solution.py:477
  9.7 0.0 copy-start.7
  9.7 4.8 %all-to-all-start = ((bf16[8,96,1024]{2,1,0:T(8,128)(2,1)}), bf16[8,96,1024]{2,1,0:T(8,128)(2,1)S(1)}, u32[]{:S(2)}, u32[]{:S(2)}) async-start(bf16[8,96,1024]{2,1,0:T(8,128)(2,1)} %get-tuple-element.28), calls=%async_computation | async-start | bytes 3145728 | tf_op jit(solution)/shard_map/all_to_all | solution.py:448
  14.5 11.3 %collective-permute-done.mine_ref = bf16[208,1024]{1,0:T(8,128)(2,1)S(1)} collective-permute-done((bf16[208,1024]{1,0:T(8,128)(2,1)}, bf16[208,1024]{1,0:T(8,128)(2,1)S(1)}, u32[]{:S(2)}, u32[]{:S(2)}) %collective-permute-start) | collective-permute-done | bytes 426016 | tf_op jit(solution)/shard_map/ppermute | solution.py:466
  25.8 0.0 collective-permute-start.1
  25.8 1.8 %collective-permute-done.1.other_ref = bf16[208,1024]{1,0:T(8,128)(2,1)S(1)} collective-permute-done((bf16[208,1024]{1,0:T(8,128)(2,1)S(1)}, bf16[208,1024]{1,0:T(8,128)(2,1)S(1)}, u32[]{:S(2)}, u32[]{:S(2)}) %collective-permute-start.1) | collective-permute-done | bytes 426016 | tf_op jit(solution)/shard_map/ppermute | solution.py:467
  27.6 0.0 copy-done.7
  27.6 2.4 %shard_map.71 = (bf16[96,1024]{1,0:T(8,128)(2,1)}, bf16[96,1024]{1,0:T(8,128)(2,1)}, bf16[96,1024]{1,0:T(8,128)(2,1)}, bf16[96,1024]{1,0:T(8,128)(2,1)}, bf16[96...) custom-call(s32[1,64]{1,0:T(1,128)S(1)} %bitcast.3, ...), custom_call_target="tpu_custom_call" | custom-call | flops 20000000000 | bytes 2359296 | tf_op jit(solution)/shard_map/pallas_call | solution.py:494
  29.9 1.6 %collective-permute-start.2 = (bf16[96,1024]{1,0:T(8,128)(2,1)}, bf16[96,1024]{1,0:T(8,128)(2,1)S(1)}, u32[]{:S(2)}, u32[]{:S(2)}) collective-permute-start(bf16[96,1024]{1,0:T(8,128)(2,1)} %get-tuple-element.32), channel_id=1, source_target_pairs={{0,2},{2,0},{4,6},{6,4},{8,10},{10,8},{12,14},{14,12},{16,18},{18,... | collective-permute-start | bytes 589832 | tf_op jit(solution)/shard_map/ppermute | solution.py:504
  31.5 1.5 %collective-permute-start.3 = (bf16[96,1024]{1,0:T(8,128)(2,1)}, bf16[96,1024]{1,0:T(8,128)(2,1)S(1)}, u32[]{:S(2)}, u32[]{:S(2)}) collective-permute-start(bf16[96,1024]{1,0:T(8,128)(2,1)} %get-tuple-element.33), channel_id=1, source_target_pairs={{0,4},{2,6},{4,0},{6,2},{8,12},{10,14},{12,8},{14,10},{16,20},{18,... | collective-permute-start | bytes 589832 | tf_op jit(solution)/shard_map/ppermute | solution.py:504
  33.1 0.4 collective-permute-start.4
  33.5 0.8 collective-permute-start.5
  34.3 2.2 %collective-permute-start.6 = (bf16[96,1024]{1,0:T(8,128)(2,1)}, bf16[96,1024]{1,0:T(8,128)(2,1)}, u32[]{:S(2)}, u32[]{:S(2)}) collective-permute-start(bf16[96,1024]{1,0:T(8,128)(2,1)} %get-tuple-element.36), channel_id=1, source_target_pairs={{0,10},{2,8},{4,14},{6,12},{8,2},{10,0},{12,6},{14,4},{16,26},{18,... | collective-permute-start | bytes 589832 | tf_op jit(solution)/shard_map/ppermute | solution.py:504
  36.5 5.2 %collective-permute-done.2.refs_1_ = bf16[96,1024]{1,0:T(8,128)(2,1)S(1)} collective-permute-done((bf16[96,1024]{1,0:T(8,128)(2,1)}, bf16[96,1024]{1,0:T(8,128)(2,1)S(1)}, u32[]{:S(2)}, u32[]{:S(2)}) %collective-permute-start.2) | collective-permute-done | bytes 196640 | tf_op jit(solution)/shard_map/ppermute | solution.py:504
  41.7 0.7 copy-done.8
  42.4 0.0 collective-permute-start.7
  42.4 4.6 %collective-permute-done.3.refs_2_ = bf16[96,1024]{1,0:T(8,128)(2,1)S(1)} collective-permute-done((bf16[96,1024]{1,0:T(8,128)(2,1)}, bf16[96,1024]{1,0:T(8,128)(2,1)S(1)}, u32[]{:S(2)}, u32[]{:S(2)}) %collective-permute-start.3) | collective-permute-done | bytes 196640 | tf_op jit(solution)/shard_map/ppermute | solution.py:504
  47.0 0.7 copy-done.10
  47.6 0.0 collective-permute-start.8
  47.6 0.0 copy-done.14
  47.6 0.2 fusion.count_ref
  47.8 0.0 all-to-all-done.q_ref
  47.8 0.0 copy-start.3
  47.8 1.2 copy-done.3
  49.0 2.2 %copy-done = bf16[2,1024,1024]{2,1,0:T(8,128)(2,1)S(1)} copy-done((bf16[2,1024,1024]{2,1,0:T(8,128)(2,1)S(1)}, bf16[2,1024,1024]{2,1,0:T(8,128)(2,1)}, u32[]{:S(2)}) %copy-start) | copy-done | bytes 4194328
  51.2 1.4 %copy-done.4 = bf16[8,96,1024]{2,1,0:T(8,128)(2,1)S(1)} copy-done((bf16[8,96,1024]{2,1,0:T(8,128)(2,1)S(1)}, bf16[8,96,1024]{2,1,0:T(8,128)(2,1)}, u32[]{:S(2)}) %copy-start.4) | copy-done | bytes 1572888
  52.6 4.4 %shard_map.69 = (f32[2,384,1024]{2,1,0:T(8,128)S(1)}, f32[2,8,1024]{2,1,0:T(8,128)S(1)}, f32[2,384,128]{2,1,0:T(8,128)S(1)}) custom-call(s32[2]{0:T(128)S(1)} %fusion.count_ref, bf16[8,96,1024]{2,1,0:T(8,128)(2,1)S(1)} %copy-done.4, bf16[2,1024,1024]{2,1,0:T(8,128)(2,1)S(1)} %copy-done), custom_call_target="tpu_custom_call" | custom-call | flops 1610612736 | bytes 5767168 | tf_op jit(solution)/shard_map/pallas_call | solution.py:515
  57.1 0.0 collective-permute-done.4.refs_3_
  57.1 0.0 collective-permute-done.5.refs_4_
  57.1 0.0 collective-permute-done.6.refs_5_
  57.1 0.0 collective-permute-done.7.refs_6_
  57.1 3.1 %collective-permute-done.8.refs_7_ = bf16[96,1024]{1,0:T(8,128)(2,1)} collective-permute-done((bf16[96,1024]{1,0:T(8,128)(2,1)}, bf16[96,1024]{1,0:T(8,128)(2,1)}, u32[]{:S(2)}, u32[]{:S(2)}) %collective-permute-start.8) | collective-permute-done | bytes 196640 | tf_op jit(solution)/shard_map/ppermute | solution.py:504
  60.2 0.0 copy-done.1
  60.2 0.0 copy-done.11
  60.2 8.4 %shard_map.72 = (bf16[8,49,16,128]{3,2,1,0:T(8,128)(2,1)}, f32[2,8,1024]{2,1,0:T(8,128)}) custom-call(s32[2]{0:T(128)S(1)} %fusion.count_ref, f32[2,8,1024]{2,1,0:T(8,128)S(1)} %get-tuple-element.30.col_ref, bf16[2,1024,1024]{2,1,0:T(8,128)(2,1)S(1)} %copy-done.1, bf16[96,1024]{1,0:T(8,128)(2,1)S(1)} %copy-done.12, bf16[96,1024]{1,0:T(8,128)(2,1)S(1)} %copy-done.9, ...), custom_call_target="tpu_custom_call" | custom-call | flops 1610612736 | bytes 5767168 | tf_op jit(solution)/shard_map/pallas_call | solution.py:528
  68.6 4.5 %all-to-all-start.2 = ((bf16[8,49,16,128]{3,2,1,0:T(8,128)(2,1)}), bf16[8,49,16,128]{3,2,1,0:T(8,128)(2,1)}, u32[]{:S(2)}, u32[]{:S(2)}) async-start(bf16[8,49,16,128]{3,2,1,0:T(8,128)(2,1)} %get-tuple-element.42), calls=%async_computation.2 | async-start | bytes 3211264 | tf_op jit(solution)/shard_map/all_to_all | solution.py:448
  73.1 0.0 copy-start.2
  73.1 2.2 %copy-done.2 = bf16[2,1024,1024]{2,1,0:T(8,128)(2,1)S(1)} copy-done((bf16[2,1024,1024]{2,1,0:T(8,128)(2,1)S(1)}, bf16[2,1024,1024]{2,1,0:T(8,128)(2,1)}, u32[]{:S(2)}) %copy-start.2) | copy-done | bytes 4194328
  75.3 0.8 copy-done.5
  76.2 3.6 %shard_map.73 = bf16[8,49,16,128]{3,2,1,0:T(8,128)(2,1)} custom-call(f32[2,384,1024]{2,1,0:T(8,128)S(1)} %get-tuple-element.29.s_ref, f32[2,8,1024]{2,1,0:T(8,128)S(1)} %copy-done.5, f32[2,384,128]{2,1,0:T(8,128)S(1)} %get-tuple-element.40.fwd_ref, bf16[2,1024,1024]{2,1,0:T(8,128)(2,1)S(1)} %copy-done.2), custom_call_target="tpu_custom_call" | custom-call | flops 1610612736 | bytes 5767168 | tf_op jit(solution)/shard_map/pallas_call | solution.py:548
  79.8 13.6 %all-to-all-done.2.r_ref = bf16[8,49,16,128]{3,2,1,0:T(8,128)(2,1)} async-done(((bf16[8,49,16,128]{3,2,1,0:T(8,128)(2,1)}), bf16[8,49,16,128]{3,2,1,0:T(8,128)(2,1)}, u32[]{:S(2)}, u32[]{:S(2)}) %all-to-all-start.2) | async-done | bytes 1605664 | tf_op jit(solution)/shard_map/all_to_all | solution.py:448
  93.4 3.6 %all-to-all-start.1 = ((bf16[8,49,16,128]{3,2,1,0:T(8,128)(2,1)}), bf16[8,49,16,128]{3,2,1,0:T(8,128)(2,1)S(1)}, u32[]{:S(2)}, u32[]{:S(2)}) async-start(bf16[8,49,16,128]{3,2,1,0:T(8,128)(2,1)} %shard_map.73), calls=%async_computation.1 | async-start | bytes 3211264 | tf_op jit(solution)/shard_map/all_to_all | solution.py:448
  97.0 4.3 %shard_map.74 = (f32[192,1024]{1,0:T(8,128)S(1)}, f32[8,384]{1,0:T(8,128)S(1)}, bf16[208,1024]{1,0:T(8,128)(2,1)S(1)}) custom-call(f32[16,384]{1,0:T(8,128)S(1)} %copy-done.13, bf16[8,49,16,128]{3,2,1,0:T(8,128)(2,1)} %all-to-all-done.2.r_ref, f32[16,384]{1,0:T(8,128)S(1)} %copy-done.6), custom_call_target="tpu_custom_call" | custom-call | flops 1207959552 | bytes 3145728 | tf_op jit(solution)/shard_map/pallas_call | solution.py:559
  101.3 0.1 collective-permute-start.9
  101.4 1.8 %collective-permute-done.9.got_ref = bf16[208,1024]{1,0:T(8,128)(2,1)S(1)} collective-permute-done((bf16[208,1024]{1,0:T(8,128)(2,1)S(1)}, bf16[208,1024]{1,0:T(8,128)(2,1)S(1)}, u32[]{:S(2)}, u32[]{:S(2)}) %collective-permute-start.9) | collective-permute-done | bytes 426016 | tf_op jit(solution)/shard_map/ppermute | solution.py:571
  103.1 0.4 shard_map.75._
  103.5 0.1 collective-permute-start.14
  103.6 22.0 %collective-permute-done.14.refs_8_ = bf16[208,1024]{1,0:T(8,128)(2,1)S(1)} collective-permute-done((bf16[208,1024]{1,0:T(8,128)(2,1)S(1)}, bf16[208,1024]{1,0:T(8,128)(2,1)S(1)}, u32[]{:S(2)}, u32[]{:S(2)}) %collective-permute-start.14) | collective-permute-done | bytes 426016 | tf_op jit(solution)/shard_map/ppermute | solution.py:579
  125.6 0.0 collective-permute-start.15
  125.6 0.3 all-to-all-done.1.r_ref
  126.0 2.5 %shard_map.76 = (bf16[96,1024]{1,0:T(8,128)(2,1)S(1)}, bf16[96,1024]{1,0:T(8,128)(2,1)S(1)}, bf16[96,1024]{1,0:T(8,128)(2,1)S(1)}, bf16[112,1024]{1,0:T(8,128)(2,1)S(1)}) custom-call(f32[16,384]{1,0:T(8,128)S(1)} %copy-done.6, bf16[8,49,16,128]{3,2,1,0:T(8,128)(2,1)S(1)} %all-to-all-done.1.r_ref, bf16[208,1024]{1,0:T(8,128)(2,1)S(1)} %shard_map.75._), custom_call_target="tpu_custom_call" | custom-call | tf_op jit(solution)/shard_map/pallas_call | solution.py:559
  128.5 0.2 collective-permute-start.13
  128.7 0.3 collective-permute-start.10
  129.1 0.2 collective-permute-start.11
  129.3 0.3 collective-permute-start.12
  129.6 0.7 collective-permute-done.10.refs_4_
  130.3 0.3 collective-permute-done.11.refs_5_
  130.6 0.3 collective-permute-done.12.refs_6_
  130.9 0.0 collective-permute-done.13.refs_7_
  130.9 0.0 collective-permute-done.15.refs_9_
  130.9 1.6 %shard_map.77 = (bf16[384,1024]{1,0:T(8,128)(2,1)}, f32[1,384]{1,0:T(1,128)S(1)}) custom-call(bf16[96,1024]{1,0:T(8,128)(2,1)S(1)} %get-tuple-element.46.refs_0_, bf16[96,1024]{1,0:T(8,128)(2,1)S(1)} %get-tuple-element.47.refs_1_, bf16[96,1024]{1,0:T(8,128)(2,1)S(1)} %get-tuple-element.48.refs_2_, bf16[112,1024]{1,0:T(8,128)(2,1)S(1)} %get-tuple-element.49.refs_3_, ...), custom_call_target="tpu_custom_call" | custom-call | bytes 3932160 | tf_op jit(solution)/shard_map/pallas_call | solution.py:585
  132.5 0.6 convert_reduce_fusion
  (17 shorter events, 0.0 us)
Async XLA Ops:
  2.4 23.4 %collective-permute-start = (bf16[208,1024]{1,0:T(8,128)(2,1)}, bf16[208,1024]{1,0:T(8,128)(2,1)S(1)}, u32[]{:S(2)}, u32[]{:S(2)}) collective-permute-start(bf16[208,1024]{1,0:T(8,128)(2,1)} %shard_map.70), channel_id=1, source_target_pairs={{0,16},{2,18},{4,20},{6,22},{8,24},{10,26},{12,28},{14,30},{16,0},... | collective-permute-start | bytes 1277960 | tf_op jit(solution)/shard_map/ppermute | solution.py:466
  9.7 17.9 %copy-start.7 = (s32[64]{0:T(128)S(1)}, s32[64]{0:T(128)}, u32[]{:S(2)}) copy-start(s32[64]{0:T(128)} %param.8) | copy-start | bytes 772
  9.7 38.1 %all-to-all-start = ((bf16[8,96,1024]{2,1,0:T(8,128)(2,1)}), bf16[8,96,1024]{2,1,0:T(8,128)(2,1)S(1)}, u32[]{:S(2)}, u32[]{:S(2)}) async-start(bf16[8,96,1024]{2,1,0:T(8,128)(2,1)} %get-tuple-element.28), calls=%async_computation | async-start | bytes 3145728 | tf_op jit(solution)/shard_map/all_to_all | solution.py:448
  14.5 33.2 %copy-start.14 = (s32[64]{0:T(128)S(1)}, s32[64]{0:T(128)}, u32[]{:S(2)}) copy-start(s32[64]{0:T(128)} %param.9) | copy-start | bytes 772
  25.8 1.8 %collective-permute-start.1 = (bf16[208,1024]{1,0:T(8,128)(2,1)S(1)}, bf16[208,1024]{1,0:T(8,128)(2,1)S(1)}, u32[]{:S(2)}, u32[]{:S(2)}) collective-permute-start(bf16[208,1024]{1,0:T(8,128)(2,1)S(1)} %collective-permute-done.mine_ref), channel_id=1, source_target_pairs={{0,1},{1,0},{2,3},{3,2},{4,5},{5,4},{6,7},{7,6},{8,9},{9,8},{10,11... | collective-permute-start | bytes 1277960 | tf_op jit(solution)/shard_map/ppermute | solution.py:467
  29.9 11.8 %collective-permute-start.2 = (bf16[96,1024]{1,0:T(8,128)(2,1)}, bf16[96,1024]{1,0:T(8,128)(2,1)S(1)}, u32[]{:S(2)}, u32[]{:S(2)}) collective-permute-start(bf16[96,1024]{1,0:T(8,128)(2,1)} %get-tuple-element.32), channel_id=1, source_target_pairs={{0,2},{2,0},{4,6},{6,4},{8,10},{10,8},{12,14},{14,12},{16,18},{18,... | collective-permute-start | bytes 589832 | tf_op jit(solution)/shard_map/ppermute | solution.py:504
  31.5 15.4 %collective-permute-start.3 = (bf16[96,1024]{1,0:T(8,128)(2,1)}, bf16[96,1024]{1,0:T(8,128)(2,1)S(1)}, u32[]{:S(2)}, u32[]{:S(2)}) collective-permute-start(bf16[96,1024]{1,0:T(8,128)(2,1)} %get-tuple-element.33), channel_id=1, source_target_pairs={{0,4},{2,6},{4,0},{6,2},{8,12},{10,14},{12,8},{14,10},{16,20},{18,... | collective-permute-start | bytes 589832 | tf_op jit(solution)/shard_map/ppermute | solution.py:504
  33.1 24.0 %collective-permute-start.4 = (bf16[96,1024]{1,0:T(8,128)(2,1)}, bf16[96,1024]{1,0:T(8,128)(2,1)}, u32[]{:S(2)}, u32[]{:S(2)}) collective-permute-start(bf16[96,1024]{1,0:T(8,128)(2,1)} %get-tuple-element.34), channel_id=1, source_target_pairs={{0,6},{2,4},{4,2},{6,0},{8,14},{10,12},{12,10},{14,8},{16,22},{18,... | collective-permute-start | bytes 589832 | tf_op jit(solution)/shard_map/ppermute | solution.py:504
  33.5 23.6 %collective-permute-start.5 = (bf16[96,1024]{1,0:T(8,128)(2,1)}, bf16[96,1024]{1,0:T(8,128)(2,1)}, u32[]{:S(2)}, u32[]{:S(2)}) collective-permute-start(bf16[96,1024]{1,0:T(8,128)(2,1)} %get-tuple-element.35), channel_id=1, source_target_pairs={{0,8},{2,10},{4,12},{6,14},{8,0},{10,2},{12,4},{14,6},{16,24},{18,... | collective-permute-start | bytes 589832 | tf_op jit(solution)/shard_map/ppermute | solution.py:504
  34.3 22.8 %collective-permute-start.6 = (bf16[96,1024]{1,0:T(8,128)(2,1)}, bf16[96,1024]{1,0:T(8,128)(2,1)}, u32[]{:S(2)}, u32[]{:S(2)}) collective-permute-start(bf16[96,1024]{1,0:T(8,128)(2,1)} %get-tuple-element.36), channel_id=1, source_target_pairs={{0,10},{2,8},{4,14},{6,12},{8,2},{10,0},{12,6},{14,4},{16,26},{18,... | collective-permute-start | bytes 589832 | tf_op jit(solution)/shard_map/ppermute | solution.py:504
  41.7 0.7 copy-start.8
  42.4 14.7 %collective-permute-start.7 = (bf16[96,1024]{1,0:T(8,128)(2,1)}, bf16[96,1024]{1,0:T(8,128)(2,1)}, u32[]{:S(2)}, u32[]{:S(2)}) collective-permute-start(bf16[96,1024]{1,0:T(8,128)(2,1)} %get-tuple-element.37), channel_id=1, source_target_pairs={{0,12},{2,14},{4,8},{6,10},{8,4},{10,6},{12,0},{14,2},{16,28},{18,... | collective-permute-start | bytes 589832 | tf_op jit(solution)/shard_map/ppermute | solution.py:504
  47.0 0.7 copy-start.10
  47.6 12.6 %collective-permute-start.8 = (bf16[96,1024]{1,0:T(8,128)(2,1)}, bf16[96,1024]{1,0:T(8,128)(2,1)}, u32[]{:S(2)}, u32[]{:S(2)}) collective-permute-start(bf16[96,1024]{1,0:T(8,128)(2,1)} %get-tuple-element.38), channel_id=1, source_target_pairs={{0,14},{2,12},{4,10},{6,8},{8,6},{10,4},{12,2},{14,0},{16,30},{18,... | collective-permute-start | bytes 589832 | tf_op jit(solution)/shard_map/ppermute | solution.py:504
  47.8 1.2 copy-start.3
  49.0 2.2 %copy-start = (bf16[2,1024,1024]{2,1,0:T(8,128)(2,1)S(1)}, bf16[2,1024,1024]{2,1,0:T(8,128)(2,1)}, u32[]{:S(2)}) copy-start(bf16[2,1024,1024]{2,1,0:T(8,128)(2,1)} %t_ref.5) | copy-start | bytes 12582916
  51.2 1.4 %copy-start.4 = (bf16[8,96,1024]{2,1,0:T(8,128)(2,1)S(1)}, bf16[8,96,1024]{2,1,0:T(8,128)(2,1)}, u32[]{:S(2)}) copy-start(bf16[8,96,1024]{2,1,0:T(8,128)(2,1)} %copy-done.3) | copy-start | bytes 4718596
  52.6 7.6 %copy-start.1 = (bf16[2,1024,1024]{2,1,0:T(8,128)(2,1)S(1)}, bf16[2,1024,1024]{2,1,0:T(8,128)(2,1)}, u32[]{:S(2)}) copy-start(bf16[2,1024,1024]{2,1,0:T(8,128)(2,1)} %t_ref.5) | copy-start | bytes 12582916
  52.6 7.6 %copy-start.9 = (bf16[96,1024]{1,0:T(8,128)(2,1)S(1)}, bf16[96,1024]{1,0:T(8,128)(2,1)}, u32[]{:S(2)}) copy-start(bf16[96,1024]{1,0:T(8,128)(2,1)} %copy-done.8) | copy-start | bytes 589828
  52.6 7.6 %copy-start.11 = (bf16[96,1024]{1,0:T(8,128)(2,1)S(1)}, bf16[96,1024]{1,0:T(8,128)(2,1)}, u32[]{:S(2)}) copy-start(bf16[96,1024]{1,0:T(8,128)(2,1)} %copy-done.10) | copy-start | bytes 589828
  52.6 7.6 %copy-start.12 = (bf16[96,1024]{1,0:T(8,128)(2,1)S(1)}, bf16[96,1024]{1,0:T(8,128)(2,1)}, u32[]{:S(2)}) copy-start(bf16[96,1024]{1,0:T(8,128)(2,1)} %get-tuple-element.31.refs_0_) | copy-start | bytes 589828
  68.6 24.7 %all-to-all-start.2 = ((bf16[8,49,16,128]{3,2,1,0:T(8,128)(2,1)}), bf16[8,49,16,128]{3,2,1,0:T(8,128)(2,1)}, u32[]{:S(2)}, u32[]{:S(2)}) async-start(bf16[8,49,16,128]{3,2,1,0:T(8,128)(2,1)} %get-tuple-element.42), calls=%async_computation.2 | async-start | bytes 3211264 | tf_op jit(solution)/shard_map/all_to_all | solution.py:448
  73.1 2.2 %copy-start.2 = (bf16[2,1024,1024]{2,1,0:T(8,128)(2,1)S(1)}, bf16[2,1024,1024]{2,1,0:T(8,128)(2,1)}, u32[]{:S(2)}) copy-start(bf16[2,1024,1024]{2,1,0:T(8,128)(2,1)} %t_ref.5) | copy-start | bytes 12582916
  75.3 0.8 copy-start.5
  79.8 17.2 %copy-start.6 = (f32[16,384]{1,0:T(8,128)S(1)}, f32[16,384]{1,0:T(8,128)}, u32[]{:S(2)}) copy-start(f32[16,384]{1,0:T(8,128)} %get-tuple-element.27._.code_ref) | copy-start | bytes 73732
  79.8 17.2 %copy-start.13 = (f32[16,384]{1,0:T(8,128)S(1)}, f32[16,384]{1,0:T(8,128)}, u32[]{:S(2)}) copy-start(f32[16,384]{1,0:T(8,128)} %get-tuple-element.41.code_ref) | copy-start | bytes 73732
  93.4 32.6 %all-to-all-start.1 = ((bf16[8,49,16,128]{3,2,1,0:T(8,128)(2,1)}), bf16[8,49,16,128]{3,2,1,0:T(8,128)(2,1)S(1)}, u32[]{:S(2)}, u32[]{:S(2)}) async-start(bf16[8,49,16,128]{3,2,1,0:T(8,128)(2,1)} %shard_map.73), calls=%async_computation.1 | async-start | bytes 3211264 | tf_op jit(solution)/shard_map/all_to_all | solution.py:448
  101.3 1.8 %collective-permute-start.9 = (bf16[208,1024]{1,0:T(8,128)(2,1)S(1)}, bf16[208,1024]{1,0:T(8,128)(2,1)S(1)}, u32[]{:S(2)}, u32[]{:S(2)}) collective-permute-start(bf16[208,1024]{1,0:T(8,128)(2,1)S(1)} %get-tuple-element.45), channel_id=1, source_target_pairs={{0,1},{1,0},{2,3},{3,2},{4,5},{5,4},{6,7},{7,6},{8,9},{9,8},{10,11... | collective-permute-start | bytes 1277960 | tf_op jit(solution)/shard_map/ppermute | solution.py:571
  103.5 22.1 %collective-permute-start.14 = (bf16[208,1024]{1,0:T(8,128)(2,1)S(1)}, bf16[208,1024]{1,0:T(8,128)(2,1)S(1)}, u32[]{:S(2)}, u32[]{:S(2)}) collective-permute-start(bf16[208,1024]{1,0:T(8,128)(2,1)S(1)} %shard_map.75._), channel_id=1, source_target_pairs={{0,16},{2,18},{4,20},{6,22},{8,24},{10,26},{12,28},{14,30},{16,0},... | collective-permute-start | bytes 1277960 | tf_op jit(solution)/shard_map/ppermute | solution.py:579
  125.6 5.3 %collective-permute-start.15 = (bf16[208,1024]{1,0:T(8,128)(2,1)S(1)}, bf16[208,1024]{1,0:T(8,128)(2,1)S(1)}, u32[]{:S(2)}, u32[]{:S(2)}) collective-permute-start(bf16[208,1024]{1,0:T(8,128)(2,1)S(1)} %collective-permute-done.14.refs_8_), channel_id=1, source_target_pairs={{0,1},{1,0},{2,3},{3,2},{4,5},{5,4},{6,7},{7,6},{8,9},{9,8},{10,11... | collective-permute-start | bytes 1277960 | tf_op jit(solution)/shard_map/ppermute | solution.py:580
  128.5 2.4 %collective-permute-start.13 = (bf16[112,1024]{1,0:T(8,128)(2,1)S(1)}, bf16[112,1024]{1,0:T(8,128)(2,1)S(1)}, u32[]{:S(2)}, u32[]{:S(2)}) collective-permute-start(bf16[112,1024]{1,0:T(8,128)(2,1)S(1)} %get-tuple-element.49.refs_3_), channel_id=1, source_target_pairs={{0,1},{1,0},{2,3},{3,2},{4,5},{5,4},{6,7},{7,6},{8,9},{9,8},{10,11... | collective-permute-start | bytes 688136 | tf_op jit(solution)/shard_map/ppermute | solution.py:584
  128.7 1.6 %collective-permute-start.10 = (bf16[96,1024]{1,0:T(8,128)(2,1)S(1)}, bf16[96,1024]{1,0:T(8,128)(2,1)S(1)}, u32[]{:S(2)}, u32[]{:S(2)}) collective-permute-start(bf16[96,1024]{1,0:T(8,128)(2,1)S(1)} %get-tuple-element.46.refs_0_), channel_id=1, source_target_pairs={{0,1},{1,0},{2,3},{3,2},{4,5},{5,4},{6,7},{7,6},{8,9},{9,8},{10,11... | collective-permute-start | bytes 589832 | tf_op jit(solution)/shard_map/ppermute | solution.py:584
  129.1 1.5 %collective-permute-start.11 = (bf16[96,1024]{1,0:T(8,128)(2,1)S(1)}, bf16[96,1024]{1,0:T(8,128)(2,1)S(1)}, u32[]{:S(2)}, u32[]{:S(2)}) collective-permute-start(bf16[96,1024]{1,0:T(8,128)(2,1)S(1)} %get-tuple-element.47.refs_1_), channel_id=1, source_target_pairs={{0,1},{1,0},{2,3},{3,2},{4,5},{5,4},{6,7},{7,6},{8,9},{9,8},{10,11... | collective-permute-start | bytes 589832 | tf_op jit(solution)/shard_map/ppermute | solution.py:584
  129.3 1.6 %collective-permute-start.12 = (bf16[96,1024]{1,0:T(8,128)(2,1)S(1)}, bf16[96,1024]{1,0:T(8,128)(2,1)S(1)}, u32[]{:S(2)}, u32[]{:S(2)}) collective-permute-start(bf16[96,1024]{1,0:T(8,128)(2,1)S(1)} %get-tuple-element.48.refs_2_), channel_id=1, source_target_pairs={{0,1},{1,0},{2,3},{3,2},{4,5},{5,4},{6,7},{7,6},{8,9},{9,8},{10,11... | collective-permute-start | bytes 589832 | tf_op jit(solution)/shard_map/ppermute | solution.py:584

commit v7 on v6

--- a/solution.py
+++ b/solution.py
@@ -131,38 +131,37 @@
         copy.wait()
 
 
-def half_with_picks(picks_hbm, src_hbm, out_ref, picks_ref, sems, *, side):
-    _, core, _ = place_of(side)
-    n_picks, rows = picks_ref.shape
-    width = src_hbm.shape[1]
-    half = rows // 2
-    mine = pl.ds(pl.multiple_of(core * half, 16), half)
-    names = pltpu.make_async_copy(picks_hbm, picks_ref, sems.at[0])
-    names.start()
-    body = pltpu.make_async_copy(src_hbm.at[mine, :], out_ref.at[pl.ds(0, half), :], sems.at[1])
-    body.start()
-    names.wait()
-    names = jnp.concatenate([picks_ref[...].astype(F32), jnp.zeros((EXTRA - n_picks, rows), F32)], axis=0)
-    rest = jnp.zeros((EXTRA, width - rows), F32)
-    out_ref[half:, :] = jnp.concatenate([names, rest], axis=1).astype(BF16)
-    body.wait()
-
-
-def gather_own(picks_hbm, home_hbm, src_hbm, *refs, side, **sizes):
-    *refs, picks_ref, home_ref, src_ref, sems = refs
+def gather_own(picks_hbm, home_hbm, src_hbm, letter_hbm, *refs, side, **sizes):
+    *refs, picks_ref, home_ref, src_ref, last_ref, sems = refs
+    info = place_of(side)
     copies = []
     for i, (here, there) in enumerate(((picks_hbm, picks_ref), (home_hbm, home_ref), (src_hbm, src_ref))):
         copies.append(pltpu.make_async_copy(here, there, sems.at[i]))
         copies[-1].start()
     copies[0].wait()
     copies[1].wait()
-    picks = [picks_ref[k : k + 1, :].astype(F32) for k in range(picks_ref.shape[0])]
+    n_picks, rows = picks_ref.shape
+    width = src_ref.shape[1]
+    half = rows // 2
+    names = picks_ref[...].astype(F32)
+    picks = [names[k : k + 1, :] for k in range(n_picks)]
+    names = jnp.concatenate([names, jnp.zeros((EXTRA - n_picks, rows), F32)], axis=0)
+    last_ref[...] = jnp.concatenate([names, jnp.zeros((EXTRA, width - rows), F32)], axis=1).astype(BF16)
+    mine = pl.ds(pl.multiple_of(info[1] * half, 16), half)
+    letter = [
+        pltpu.make_async_copy(last_ref, letter_hbm.at[pl.ds(half, EXTRA), :], sems.at[3]),
+        pltpu.make_async_copy(src_ref.at[mine, :], letter_hbm.at[pl.ds(0, half), :], sems.at[4]),
+    ]
+    letter[0].start()
 
     def load():
         copies[2].wait()
+        letter[1].start()
         return src_ref[...]
 
-    gather_body(place_of(side), None, picks, home_ref, load, *refs, **sizes)
+    gather_body(info, None, picks, home_ref, load, *refs, **sizes)
+    for copy in letter:
+        copy.wait()
 
 
 def gather_partner(home_ref, mine_ref, other_ref, *refs, n_picks, side, **sizes):
@@ -454,18 +453,6 @@
     vmem = pl.BlockSpec(memory_space=pltpu.VMEM)
     smem = pl.BlockSpec(memory_space=pltpu.SMEM)
     unread = pl.BlockSpec(memory_space=pl.ANY)
-    mine = call(
-        functools.partial(half_with_picks, side=side),
-        letter,
-        [pltpu.VMEM((n_picks, rows), jnp.int32), pltpu.SemaphoreType.DMA((2,))],
-        moved=4 * half * width,
-        limit=FULL,
-        in_specs=[hbm, hbm],
-        out_specs=vmem,
-    )(picks_t, sources)
-    far_mine = lax.ppermute(mine, "src", partner)
-    far_other = lax.ppermute(far_mine, "tgt", twin)
-
     sizes = dict(side=side, n_tgt=n_tgt, per_device=per_device, capacity=capacity, group=group)
     gather_out = (sds((side, message, width), BF16), sds((n_buckets, rows), F32))
     moved = 2 * (n_slots + rows) * width
@@ -474,22 +461,25 @@
         pltpu.VMEM((n_buckets, rows), F32),
         pltpu.SemaphoreType.DMA((1 + side,)),
     ]
-    near_q, near_code = call(
+    mine, near_q, near_code = call(
         functools.partial(gather_own, **sizes),
-        gather_out,
+        (letter,) + gather_out,
         gather_scratch
         + [
             pltpu.VMEM((n_picks, rows), jnp.int32),
             pltpu.VMEM((1, n_clusters), jnp.int32),
             pltpu.VMEM((rows, width), BF16),
-            pltpu.SemaphoreType.DMA((3,)),
+            pltpu.VMEM((EXTRA, width), BF16),
+            pltpu.SemaphoreType.DMA((5,)),
         ],
         flops=2 * n_slots * rows * width,
         moved=moved,
         limit=FULL,
         in_specs=[hbm] * 3,
-        out_specs=(hbm, hbm),
+        out_specs=(hbm, hbm, hbm),
     )(picks_t, home, sources)
+    far_mine = lax.ppermute(mine, "src", partner)
+    far_other = lax.ppermute(far_mine, "tgt", twin)
     near_in = exchange(near_q)
     *far_q, far_code = call(
         functools.partial(gather_partner, n_picks=n_picks, **sizes),

time: 134 us -> 131 us (0.978)
  waiting for transfers between devices: 65 us -> 62 us
  starting transfers between devices: 24.8 us -> 27 us
  Pallas kernels: 32.6 us -> 30.8 us
    ppermute x7, waiting for transfers between devices: 12.9 us -> 7.57 us  [shards(): lax.ppermute(far_q[k], 'src', [(i, i ^ k) for i in range(n_src)])]
    ppermute x1, waiting for transfers between devices: 11.3 us -> 14.5 us  [shards(): far_mine = lax.ppermute(mine, 'src', partner)]
    ppermute x7, starting transfers between devices: 6.56 us -> 8.72 us  [shards(): lax.ppermute(far_q[k], 'src', [(i, i ^ k) for i in range(n_src)])]
    pallas_call x2 -> x1, Pallas kernels: 4.95 us -> 3.21 us  [shards(): call(functools.partial(gather_own, **sizes), (letter,) + gather_out, gath...]
  transfers between devices with their start and end apart: 19 -> 19, of which waited for: 12 -> 11; matrix products, arithmetic and copies ran while one was open for 0% -> 0% of each run, Pallas kernels for 16% -> 13%
where the time goes in v7:
time: 131 us
  waiting for transfers between devices  62 us (47%)
  Pallas kernels  30.8 us (24%)
  starting transfers between devices  27 us (21%)
  local copies, waits for them, and re-layouts  9.19 us (7%)
    ppermute x1, waiting for transfers between devices, shards(): from_far = lax.ppermute(joined, 'src', partner)  22 us
    ppermute x1, waiting for transfers between devices, shards(): far_mine = lax.ppermute(mine, 'src', partner)  14.5 us
    all_to_all x3, waiting for transfers between devices, exchange(): lax.all_to_all(x, 'src', split_axis=0, concat_axis=0, axis_index_groups=h...  13 us
    all_to_all x3, starting transfers between devices, exchange(): lax.all_to_all(x, 'src', split_axis=0, concat_axis=0, axis_index_groups=h...  12.9 us
    unnamed x30, local copies, waits for them, and re-layouts  9.19 us
    ppermute x7, starting transfers between devices, shards(): lax.ppermute(far_q[k], 'src', [(i, i ^ k) for i in range(n_src)])  8.72 us
    pallas_call x1, Pallas kernels, shards(): call(functools.partial(far_owner, block=row_block, side=side), (pltpu.HBM...  8.41 us
    ppermute x7, waiting for transfers between devices, shards(): lax.ppermute(far_q[k], 'src', [(i, i ^ k) for i in range(n_src)])  7.57 us
  transfers between devices with their start and end apart: 19, of which 11 were waited for; matrix products, arithmetic and copies ran while one was open for 0% of the time, Pallas kernels for 13%

profile of v7, /device:TPU:0, one launch (start us, length us, event | category | flops | bytes accessed | tf_op | source)
XLA Modules:
  0.0 130.6 jit_solution(6470157756616659372)
XLA Ops:
  0.6 3.2 %shard_map.68 = (bf16[208,1024]{1,0:T(8,128)(2,1)}, bf16[8,96,1024]{2,1,0:T(8,128)(2,1)}, f32[16,384]{1,0:T(8,128)}) custom-call(s32[4,384]{1,0:T(4,128)} %bitcast.4, s32[1,64]{1,0:T(1,128)} %bitcast.2, bf16[384,1024]{1,0:T(8,128)(2,1)} %src_hbm.1), custom_call_target="tpu_custom_call" | custom-call | flops 603979776 | bytes 2359296 | tf_op jit(solution)/shard_map/pallas_call | solution.py:464
  3.8 0.0 copy-start.7
  3.9 4.1 %collective-permute-start = (bf16[208,1024]{1,0:T(8,128)(2,1)}, bf16[208,1024]{1,0:T(8,128)(2,1)S(1)}, u32[]{:S(2)}, u32[]{:S(2)}) collective-permute-start(bf16[208,1024]{1,0:T(8,128)(2,1)} %get-tuple-element.32), channel_id=1, source_target_pairs={{0,16},{2,18},{4,20},{6,22},{8,24},{10,26},{12,28},{14,30},{16,0},... | collective-permute-start | bytes 1277960 | tf_op jit(solution)/shard_map/ppermute | solution.py:481
  7.9 4.7 %all-to-all-start = ((bf16[8,96,1024]{2,1,0:T(8,128)(2,1)}), bf16[8,96,1024]{2,1,0:T(8,128)(2,1)S(1)}, u32[]{:S(2)}, u32[]{:S(2)}) async-start(bf16[8,96,1024]{2,1,0:T(8,128)(2,1)} %get-tuple-element.29), calls=%async_computation | async-start | bytes 3145728 | tf_op jit(solution)/shard_map/all_to_all | solution.py:447
  12.7 14.5 %collective-permute-done.mine_ref = bf16[208,1024]{1,0:T(8,128)(2,1)S(1)} collective-permute-done((bf16[208,1024]{1,0:T(8,128)(2,1)}, bf16[208,1024]{1,0:T(8,128)(2,1)S(1)}, u32[]{:S(2)}, u32[]{:S(2)}) %collective-permute-start) | collective-permute-done | bytes 426016 | tf_op jit(solution)/shard_map/ppermute | solution.py:481
  27.2 0.0 collective-permute-start.1
  27.2 1.8 %collective-permute-done.1.other_ref = bf16[208,1024]{1,0:T(8,128)(2,1)S(1)} collective-permute-done((bf16[208,1024]{1,0:T(8,128)(2,1)S(1)}, bf16[208,1024]{1,0:T(8,128)(2,1)S(1)}, u32[]{:S(2)}, u32[]{:S(2)}) %collective-permute-start.1) | collective-permute-done | bytes 426016 | tf_op jit(solution)/shard_map/ppermute | solution.py:482
  29.0 0.0 copy-done.7
  29.0 2.4 %shard_map.70 = (bf16[96,1024]{1,0:T(8,128)(2,1)}, bf16[96,1024]{1,0:T(8,128)(2,1)}, bf16[96,1024]{1,0:T(8,128)(2,1)}, bf16[96,1024]{1,0:T(8,128)(2,1)}, bf16[96...) custom-call(s32[1,64]{1,0:T(1,128)S(1)} %bitcast.3, ...), custom_call_target="tpu_custom_call" | custom-call | flops 20000000000 | bytes 2359296 | tf_op jit(solution)/shard_map/pallas_call | solution.py:484
  31.3 1.6 %collective-permute-start.2 = (bf16[96,1024]{1,0:T(8,128)(2,1)}, bf16[96,1024]{1,0:T(8,128)(2,1)S(1)}, u32[]{:S(2)}, u32[]{:S(2)}) collective-permute-start(bf16[96,1024]{1,0:T(8,128)(2,1)} %get-tuple-element.34), channel_id=1, source_target_pairs={{0,2},{2,0},{4,6},{6,4},{8,10},{10,8},{12,14},{14,12},{16,18},{18,... | collective-permute-start | bytes 589832 | tf_op jit(solution)/shard_map/ppermute | solution.py:494
  32.9 1.6 %collective-permute-start.3 = (bf16[96,1024]{1,0:T(8,128)(2,1)}, bf16[96,1024]{1,0:T(8,128)(2,1)S(1)}, u32[]{:S(2)}, u32[]{:S(2)}) collective-permute-start(bf16[96,1024]{1,0:T(8,128)(2,1)} %get-tuple-element.35), channel_id=1, source_target_pairs={{0,4},{2,6},{4,0},{6,2},{8,12},{10,14},{12,8},{14,10},{16,20},{18,... | collective-permute-start | bytes 589832 | tf_op jit(solution)/shard_map/ppermute | solution.py:494
  34.5 0.4 collective-permute-start.4
  34.9 0.8 collective-permute-start.5
  35.7 2.2 %collective-permute-start.6 = (bf16[96,1024]{1,0:T(8,128)(2,1)}, bf16[96,1024]{1,0:T(8,128)(2,1)}, u32[]{:S(2)}, u32[]{:S(2)}) collective-permute-start(bf16[96,1024]{1,0:T(8,128)(2,1)} %get-tuple-element.38), channel_id=1, source_target_pairs={{0,10},{2,8},{4,14},{6,12},{8,2},{10,0},{12,6},{14,4},{16,26},{18,... | collective-permute-start | bytes 589832 | tf_op jit(solution)/shard_map/ppermute | solution.py:494
  37.9 2.9 %collective-permute-done.2.refs_1_ = bf16[96,1024]{1,0:T(8,128)(2,1)S(1)} collective-permute-done((bf16[96,1024]{1,0:T(8,128)(2,1)}, bf16[96,1024]{1,0:T(8,128)(2,1)S(1)}, u32[]{:S(2)}, u32[]{:S(2)}) %collective-permute-start.2) | collective-permute-done | bytes 196640 | tf_op jit(solution)/shard_map/ppermute | solution.py:494
  40.8 0.7 copy-done.8
  41.5 0.3 collective-permute-start.7
  41.8 1.2 collective-permute-done.3.refs_2_
  43.0 0.7 copy-done.10
  43.7 1.9 %collective-permute-start.8 = (bf16[96,1024]{1,0:T(8,128)(2,1)}, bf16[96,1024]{1,0:T(8,128)(2,1)}, u32[]{:S(2)}, u32[]{:S(2)}) collective-permute-start(bf16[96,1024]{1,0:T(8,128)(2,1)} %get-tuple-element.40), channel_id=1, source_target_pairs={{0,14},{2,12},{4,10},{6,8},{8,6},{10,4},{12,2},{14,0},{16,30},{18,... | collective-permute-start | bytes 589832 | tf_op jit(solution)/shard_map/ppermute | solution.py:494
  45.6 0.0 copy-done.14
  45.6 0.2 fusion.count_ref
  45.7 0.0 all-to-all-done.q_ref
  45.7 0.0 copy-start.3
  45.8 1.2 copy-done.3
  47.0 2.2 %copy-done = bf16[2,1024,1024]{2,1,0:T(8,128)(2,1)S(1)} copy-done((bf16[2,1024,1024]{2,1,0:T(8,128)(2,1)S(1)}, bf16[2,1024,1024]{2,1,0:T(8,128)(2,1)}, u32[]{:S(2)}) %copy-start) | copy-done | bytes 4194328
  49.1 1.4 %copy-done.4 = bf16[8,96,1024]{2,1,0:T(8,128)(2,1)S(1)} copy-done((bf16[8,96,1024]{2,1,0:T(8,128)(2,1)S(1)}, bf16[8,96,1024]{2,1,0:T(8,128)(2,1)}, u32[]{:S(2)}) %copy-start.4) | copy-done | bytes 1572888
  50.6 4.4 %shard_map.69 = (f32[2,384,1024]{2,1,0:T(8,128)S(1)}, f32[2,8,1024]{2,1,0:T(8,128)S(1)}, f32[2,384,128]{2,1,0:T(8,128)S(1)}) custom-call(s32[2]{0:T(128)S(1)} %fusion.count_ref, bf16[8,96,1024]{2,1,0:T(8,128)(2,1)S(1)} %copy-done.4, bf16[2,1024,1024]{2,1,0:T(8,128)(2,1)S(1)} %copy-done), custom_call_target="tpu_custom_call" | custom-call | flops 1610612736 | bytes 5767168 | tf_op jit(solution)/shard_map/pallas_call | solution.py:505
  55.0 0.0 collective-permute-done.4.refs_3_
  55.0 0.0 collective-permute-done.5.refs_4_
  55.0 0.0 collective-permute-done.6.refs_5_
  55.0 0.0 collective-permute-done.7.refs_6_
  55.0 3.4 %collective-permute-done.8.refs_7_ = bf16[96,1024]{1,0:T(8,128)(2,1)} collective-permute-done((bf16[96,1024]{1,0:T(8,128)(2,1)}, bf16[96,1024]{1,0:T(8,128)(2,1)}, u32[]{:S(2)}, u32[]{:S(2)}) %collective-permute-start.8) | collective-permute-done | bytes 196640 | tf_op jit(solution)/shard_map/ppermute | solution.py:494
  58.4 0.0 copy-done.1
  58.5 0.0 copy-done.9
  58.5 0.0 copy-done.12
  58.5 8.4 %shard_map.71 = (bf16[8,49,16,128]{3,2,1,0:T(8,128)(2,1)}, f32[2,8,1024]{2,1,0:T(8,128)}) custom-call(s32[2]{0:T(128)S(1)} %fusion.count_ref, f32[2,8,1024]{2,1,0:T(8,128)S(1)} %get-tuple-element.31.col_ref, bf16[2,1024,1024]{2,1,0:T(8,128)(2,1)S(1)} %copy-done.1, bf16[96,1024]{1,0:T(8,128)(2,1)S(1)} %copy-done.12, bf16[96,1024]{1,0:T(8,128)(2,1)S(1)} %copy-done.9, ...), custom_call_target="tpu_custom_call" | custom-call | flops 1610612736 | bytes 5767168 | tf_op jit(solution)/shard_map/pallas_call | solution.py:518
  66.9 4.5 %all-to-all-start.2 = ((bf16[8,49,16,128]{3,2,1,0:T(8,128)(2,1)}), bf16[8,49,16,128]{3,2,1,0:T(8,128)(2,1)}, u32[]{:S(2)}, u32[]{:S(2)}) async-start(bf16[8,49,16,128]{3,2,1,0:T(8,128)(2,1)} %get-tuple-element.44), calls=%async_computation.2 | async-start | bytes 3211264 | tf_op jit(solution)/shard_map/all_to_all | solution.py:447
  71.4 0.0 copy-start.2
  71.4 2.2 %copy-done.2 = bf16[2,1024,1024]{2,1,0:T(8,128)(2,1)S(1)} copy-done((bf16[2,1024,1024]{2,1,0:T(8,128)(2,1)S(1)}, bf16[2,1024,1024]{2,1,0:T(8,128)(2,1)}, u32[]{:S(2)}) %copy-start.2) | copy-done | bytes 4194328
  73.6 0.8 copy-done.5
  74.4 3.6 %shard_map.72 = bf16[8,49,16,128]{3,2,1,0:T(8,128)(2,1)} custom-call(f32[2,384,1024]{2,1,0:T(8,128)S(1)} %get-tuple-element.30.s_ref, f32[2,8,1024]{2,1,0:T(8,128)S(1)} %copy-done.5, f32[2,384,128]{2,1,0:T(8,128)S(1)} %get-tuple-element.42.fwd_ref, bf16[2,1024,1024]{2,1,0:T(8,128)(2,1)S(1)} %copy-done.2), custom_call_target="tpu_custom_call" | custom-call | flops 1610612736 | bytes 5767168 | tf_op jit(solution)/shard_map/pallas_call | solution.py:538
  78.0 13.0 %all-to-all-done.2.r_ref = bf16[8,49,16,128]{3,2,1,0:T(8,128)(2,1)} async-done(((bf16[8,49,16,128]{3,2,1,0:T(8,128)(2,1)}), bf16[8,49,16,128]{3,2,1,0:T(8,128)(2,1)}, u32[]{:S(2)}, u32[]{:S(2)}) %all-to-all-start.2) | async-done | bytes 1605664 | tf_op jit(solution)/shard_map/all_to_all | solution.py:447
  91.0 3.7 %all-to-all-start.1 = ((bf16[8,49,16,128]{3,2,1,0:T(8,128)(2,1)}), bf16[8,49,16,128]{3,2,1,0:T(8,128)(2,1)S(1)}, u32[]{:S(2)}, u32[]{:S(2)}) async-start(bf16[8,49,16,128]{3,2,1,0:T(8,128)(2,1)} %shard_map.72), calls=%async_computation.1 | async-start | bytes 3211264 | tf_op jit(solution)/shard_map/all_to_all | solution.py:447
  94.7 4.3 %shard_map.73 = (f32[192,1024]{1,0:T(8,128)S(1)}, f32[8,384]{1,0:T(8,128)S(1)}, bf16[208,1024]{1,0:T(8,128)(2,1)S(1)}) custom-call(f32[16,384]{1,0:T(8,128)S(1)} %copy-done.13, bf16[8,49,16,128]{3,2,1,0:T(8,128)(2,1)} %all-to-all-done.2.r_ref, f32[16,384]{1,0:T(8,128)S(1)} %copy-done.6), custom_call_target="tpu_custom_call" | custom-call | flops 1207959552 | bytes 3145728 | tf_op jit(solution)/shard_map/pallas_call | solution.py:549
  99.0 0.1 collective-permute-start.9
  99.1 1.8 %collective-permute-done.9.got_ref = bf16[208,1024]{1,0:T(8,128)(2,1)S(1)} collective-permute-done((bf16[208,1024]{1,0:T(8,128)(2,1)S(1)}, bf16[208,1024]{1,0:T(8,128)(2,1)S(1)}, u32[]{:S(2)}, u32[]{:S(2)}) %collective-permute-start.9) | collective-permute-done | bytes 426016 | tf_op jit(solution)/shard_map/ppermute | solution.py:561
  100.8 0.4 shard_map.74._
  101.2 0.1 collective-permute-start.14
  101.3 22.0 %collective-permute-done.14.refs_8_ = bf16[208,1024]{1,0:T(8,128)(2,1)S(1)} collective-permute-done((bf16[208,1024]{1,0:T(8,128)(2,1)S(1)}, bf16[208,1024]{1,0:T(8,128)(2,1)S(1)}, u32[]{:S(2)}, u32[]{:S(2)}) %collective-permute-start.14) | collective-permute-done | bytes 426016 | tf_op jit(solution)/shard_map/ppermute | solution.py:569
  123.3 0.0 collective-permute-start.15
  123.3 0.0 all-to-all-done.1.r_ref
  123.3 2.5 %shard_map.75 = (bf16[96,1024]{1,0:T(8,128)(2,1)S(1)}, bf16[96,1024]{1,0:T(8,128)(2,1)S(1)}, bf16[96,1024]{1,0:T(8,128)(2,1)S(1)}, bf16[112,1024]{1,0:T(8,128)(2,1)S(1)}) custom-call(f32[16,384]{1,0:T(8,128)S(1)} %copy-done.6, bf16[8,49,16,128]{3,2,1,0:T(8,128)(2,1)S(1)} %all-to-all-done.1.r_ref, bf16[208,1024]{1,0:T(8,128)(2,1)S(1)} %shard_map.74._), custom_call_target="tpu_custom_call" | custom-call | tf_op jit(solution)/shard_map/pallas_call | solution.py:549
  125.8 0.6 collective-permute-start.13
  126.4 0.1 collective-permute-start.10
  126.5 0.4 collective-permute-start.11
  126.9 0.1 collective-permute-start.12
  127.0 0.9 collective-permute-done.10.refs_4_
  127.9 0.3 collective-permute-done.11.refs_5_
  128.1 0.3 collective-permute-done.12.refs_6_
  128.4 0.0 collective-permute-done.13.refs_7_
  128.4 0.0 collective-permute-done.15.refs_9_
  128.4 1.6 %shard_map.76 = (bf16[384,1024]{1,0:T(8,128)(2,1)}, f32[1,384]{1,0:T(1,128)S(1)}) custom-call(bf16[96,1024]{1,0:T(8,128)(2,1)S(1)} %get-tuple-element.48.refs_0_, bf16[96,1024]{1,0:T(8,128)(2,1)S(1)} %get-tuple-element.49.refs_1_, bf16[96,1024]{1,0:T(8,128)(2,1)S(1)} %get-tuple-element.50.refs_2_, bf16[112,1024]{1,0:T(8,128)(2,1)S(1)} %get-tuple-element.51.refs_3_, ...), custom_call_target="tpu_custom_call" | custom-call | bytes 3932160 | tf_op jit(solution)/shard_map/pallas_call | solution.py:575
  130.0 0.6 convert_reduce_fusion
  (16 shorter events, 0.0 us)
Async XLA Ops:
  3.8 25.1 %copy-start.7 = (s32[64]{0:T(128)S(1)}, s32[64]{0:T(128)}, u32[]{:S(2)}) copy-start(s32[64]{0:T(128)} %param.8) | copy-start | bytes 772
  3.9 23.3 %collective-permute-start = (bf16[208,1024]{1,0:T(8,128)(2,1)}, bf16[208,1024]{1,0:T(8,128)(2,1)S(1)}, u32[]{:S(2)}, u32[]{:S(2)}) collective-permute-start(bf16[208,1024]{1,0:T(8,128)(2,1)} %get-tuple-element.32), channel_id=1, source_target_pairs={{0,16},{2,18},{4,20},{6,22},{8,24},{10,26},{12,28},{14,30},{16,0},... | collective-permute-start | bytes 1277960 | tf_op jit(solution)/shard_map/ppermute | solution.py:481
  7.9 37.8 %all-to-all-start = ((bf16[8,96,1024]{2,1,0:T(8,128)(2,1)}), bf16[8,96,1024]{2,1,0:T(8,128)(2,1)S(1)}, u32[]{:S(2)}, u32[]{:S(2)}) async-start(bf16[8,96,1024]{2,1,0:T(8,128)(2,1)} %get-tuple-element.29), calls=%async_computation | async-start | bytes 3145728 | tf_op jit(solution)/shard_map/all_to_all | solution.py:447
  12.7 32.9 %copy-start.14 = (s32[64]{0:T(128)S(1)}, s32[64]{0:T(128)}, u32[]{:S(2)}) copy-start(s32[64]{0:T(128)} %param.9) | copy-start | bytes 772
  27.2 1.8 %collective-permute-start.1 = (bf16[208,1024]{1,0:T(8,128)(2,1)S(1)}, bf16[208,1024]{1,0:T(8,128)(2,1)S(1)}, u32[]{:S(2)}, u32[]{:S(2)}) collective-permute-start(bf16[208,1024]{1,0:T(8,128)(2,1)S(1)} %collective-permute-done.mine_ref), channel_id=1, source_target_pairs={{0,1},{1,0},{2,3},{3,2},{4,5},{5,4},{6,7},{7,6},{8,9},{9,8},{10,11... | collective-permute-start | bytes 1277960 | tf_op jit(solution)/shard_map/ppermute | solution.py:482
  31.3 9.5 %collective-permute-start.2 = (bf16[96,1024]{1,0:T(8,128)(2,1)}, bf16[96,1024]{1,0:T(8,128)(2,1)S(1)}, u32[]{:S(2)}, u32[]{:S(2)}) collective-permute-start(bf16[96,1024]{1,0:T(8,128)(2,1)} %get-tuple-element.34), channel_id=1, source_target_pairs={{0,2},{2,0},{4,6},{6,4},{8,10},{10,8},{12,14},{14,12},{16,18},{18,... | collective-permute-start | bytes 589832 | tf_op jit(solution)/shard_map/ppermute | solution.py:494
  32.9 10.0 %collective-permute-start.3 = (bf16[96,1024]{1,0:T(8,128)(2,1)}, bf16[96,1024]{1,0:T(8,128)(2,1)S(1)}, u32[]{:S(2)}, u32[]{:S(2)}) collective-permute-start(bf16[96,1024]{1,0:T(8,128)(2,1)} %get-tuple-element.35), channel_id=1, source_target_pairs={{0,4},{2,6},{4,0},{6,2},{8,12},{10,14},{12,8},{14,10},{16,20},{18,... | collective-permute-start | bytes 589832 | tf_op jit(solution)/shard_map/ppermute | solution.py:494
  34.5 20.5 %collective-permute-start.4 = (bf16[96,1024]{1,0:T(8,128)(2,1)}, bf16[96,1024]{1,0:T(8,128)(2,1)}, u32[]{:S(2)}, u32[]{:S(2)}) collective-permute-start(bf16[96,1024]{1,0:T(8,128)(2,1)} %get-tuple-element.36), channel_id=1, source_target_pairs={{0,6},{2,4},{4,2},{6,0},{8,14},{10,12},{12,10},{14,8},{16,22},{18,... | collective-permute-start | bytes 589832 | tf_op jit(solution)/shard_map/ppermute | solution.py:494
  34.9 20.1 %collective-permute-start.5 = (bf16[96,1024]{1,0:T(8,128)(2,1)}, bf16[96,1024]{1,0:T(8,128)(2,1)}, u32[]{:S(2)}, u32[]{:S(2)}) collective-permute-start(bf16[96,1024]{1,0:T(8,128)(2,1)} %get-tuple-element.37), channel_id=1, source_target_pairs={{0,8},{2,10},{4,12},{6,14},{8,0},{10,2},{12,4},{14,6},{16,24},{18,... | collective-permute-start | bytes 589832 | tf_op jit(solution)/shard_map/ppermute | solution.py:494
  35.7 19.4 %collective-permute-start.6 = (bf16[96,1024]{1,0:T(8,128)(2,1)}, bf16[96,1024]{1,0:T(8,128)(2,1)}, u32[]{:S(2)}, u32[]{:S(2)}) collective-permute-start(bf16[96,1024]{1,0:T(8,128)(2,1)} %get-tuple-element.38), channel_id=1, source_target_pairs={{0,10},{2,8},{4,14},{6,12},{8,2},{10,0},{12,6},{14,4},{16,26},{18,... | collective-permute-start | bytes 589832 | tf_op jit(solution)/shard_map/ppermute | solution.py:494
  40.8 0.7 copy-start.8
  41.5 13.5 %collective-permute-start.7 = (bf16[96,1024]{1,0:T(8,128)(2,1)}, bf16[96,1024]{1,0:T(8,128)(2,1)}, u32[]{:S(2)}, u32[]{:S(2)}) collective-permute-start(bf16[96,1024]{1,0:T(8,128)(2,1)} %get-tuple-element.39), channel_id=1, source_target_pairs={{0,12},{2,14},{4,8},{6,10},{8,4},{10,6},{12,0},{14,2},{16,28},{18,... | collective-permute-start | bytes 589832 | tf_op jit(solution)/shard_map/ppermute | solution.py:494
  43.0 0.7 copy-start.10
  43.7 14.8 %collective-permute-start.8 = (bf16[96,1024]{1,0:T(8,128)(2,1)}, bf16[96,1024]{1,0:T(8,128)(2,1)}, u32[]{:S(2)}, u32[]{:S(2)}) collective-permute-start(bf16[96,1024]{1,0:T(8,128)(2,1)} %get-tuple-element.40), channel_id=1, source_target_pairs={{0,14},{2,12},{4,10},{6,8},{8,6},{10,4},{12,2},{14,0},{16,30},{18,... | collective-permute-start | bytes 589832 | tf_op jit(solution)/shard_map/ppermute | solution.py:494
  45.7 1.2 copy-start.3
  47.0 2.2 %copy-start = (bf16[2,1024,1024]{2,1,0:T(8,128)(2,1)S(1)}, bf16[2,1024,1024]{2,1,0:T(8,128)(2,1)}, u32[]{:S(2)}) copy-start(bf16[2,1024,1024]{2,1,0:T(8,128)(2,1)} %t_ref.5) | copy-start | bytes 12582916
  49.1 1.4 %copy-start.4 = (bf16[8,96,1024]{2,1,0:T(8,128)(2,1)S(1)}, bf16[8,96,1024]{2,1,0:T(8,128)(2,1)}, u32[]{:S(2)}) copy-start(bf16[8,96,1024]{2,1,0:T(8,128)(2,1)} %copy-done.3) | copy-start | bytes 4718596
  50.5 7.9 %copy-start.1 = (bf16[2,1024,1024]{2,1,0:T(8,128)(2,1)S(1)}, bf16[2,1024,1024]{2,1,0:T(8,128)(2,1)}, u32[]{:S(2)}) copy-start(bf16[2,1024,1024]{2,1,0:T(8,128)(2,1)} %t_ref.5) | copy-start | bytes 12582916
  50.5 7.9 %copy-start.9 = (bf16[96,1024]{1,0:T(8,128)(2,1)S(1)}, bf16[96,1024]{1,0:T(8,128)(2,1)}, u32[]{:S(2)}) copy-start(bf16[96,1024]{1,0:T(8,128)(2,1)} %copy-done.8) | copy-start | bytes 589828
  50.6 7.9 %copy-start.11 = (bf16[96,1024]{1,0:T(8,128)(2,1)S(1)}, bf16[96,1024]{1,0:T(8,128)(2,1)}, u32[]{:S(2)}) copy-start(bf16[96,1024]{1,0:T(8,128)(2,1)} %copy-done.10) | copy-start | bytes 589828
  50.6 7.9 %copy-start.12 = (bf16[96,1024]{1,0:T(8,128)(2,1)S(1)}, bf16[96,1024]{1,0:T(8,128)(2,1)}, u32[]{:S(2)}) copy-start(bf16[96,1024]{1,0:T(8,128)(2,1)} %get-tuple-element.33.refs_0_) | copy-start | bytes 589828
  66.9 24.1 %all-to-all-start.2 = ((bf16[8,49,16,128]{3,2,1,0:T(8,128)(2,1)}), bf16[8,49,16,128]{3,2,1,0:T(8,128)(2,1)}, u32[]{:S(2)}, u32[]{:S(2)}) async-start(bf16[8,49,16,128]{3,2,1,0:T(8,128)(2,1)} %get-tuple-element.44), calls=%async_computation.2 | async-start | bytes 3211264 | tf_op jit(solution)/shard_map/all_to_all | solution.py:447
  71.4 2.2 %copy-start.2 = (bf16[2,1024,1024]{2,1,0:T(8,128)(2,1)S(1)}, bf16[2,1024,1024]{2,1,0:T(8,128)(2,1)}, u32[]{:S(2)}) copy-start(bf16[2,1024,1024]{2,1,0:T(8,128)(2,1)} %t_ref.5) | copy-start | bytes 12582916
  73.6 0.8 copy-start.5
  78.0 16.7 %copy-start.6 = (f32[16,384]{1,0:T(8,128)S(1)}, f32[16,384]{1,0:T(8,128)}, u32[]{:S(2)}) copy-start(f32[16,384]{1,0:T(8,128)} %get-tuple-element.28._.code_ref) | copy-start | bytes 73732
  78.0 16.7 %copy-start.13 = (f32[16,384]{1,0:T(8,128)S(1)}, f32[16,384]{1,0:T(8,128)}, u32[]{:S(2)}) copy-start(f32[16,384]{1,0:T(8,128)} %get-tuple-element.43.code_ref) | copy-start | bytes 73732
  91.0 32.3 %all-to-all-start.1 = ((bf16[8,49,16,128]{3,2,1,0:T(8,128)(2,1)}), bf16[8,49,16,128]{3,2,1,0:T(8,128)(2,1)S(1)}, u32[]{:S(2)}, u32[]{:S(2)}) async-start(bf16[8,49,16,128]{3,2,1,0:T(8,128)(2,1)} %shard_map.72), calls=%async_computation.1 | async-start | bytes 3211264 | tf_op jit(solution)/shard_map/all_to_all | solution.py:447
  99.0 1.8 %collective-permute-start.9 = (bf16[208,1024]{1,0:T(8,128)(2,1)S(1)}, bf16[208,1024]{1,0:T(8,128)(2,1)S(1)}, u32[]{:S(2)}, u32[]{:S(2)}) collective-permute-start(bf16[208,1024]{1,0:T(8,128)(2,1)S(1)} %get-tuple-element.47), channel_id=1, source_target_pairs={{0,1},{1,0},{2,3},{3,2},{4,5},{5,4},{6,7},{7,6},{8,9},{9,8},{10,11... | collective-permute-start | bytes 1277960 | tf_op jit(solution)/shard_map/ppermute | solution.py:561
  101.2 22.1 %collective-permute-start.14 = (bf16[208,1024]{1,0:T(8,128)(2,1)S(1)}, bf16[208,1024]{1,0:T(8,128)(2,1)S(1)}, u32[]{:S(2)}, u32[]{:S(2)}) collective-permute-start(bf16[208,1024]{1,0:T(8,128)(2,1)S(1)} %shard_map.74._), channel_id=1, source_target_pairs={{0,16},{2,18},{4,20},{6,22},{8,24},{10,26},{12,28},{14,30},{16,0},... | collective-permute-start | bytes 1277960 | tf_op jit(solution)/shard_map/ppermute | solution.py:569
  123.3 5.1 %collective-permute-start.15 = (bf16[208,1024]{1,0:T(8,128)(2,1)S(1)}, bf16[208,1024]{1,0:T(8,128)(2,1)S(1)}, u32[]{:S(2)}, u32[]{:S(2)}) collective-permute-start(bf16[208,1024]{1,0:T(8,128)(2,1)S(1)} %collective-permute-done.14.refs_8_), channel_id=1, source_target_pairs={{0,1},{1,0},{2,3},{3,2},{4,5},{5,4},{6,7},{7,6},{8,9},{9,8},{10,11... | collective-permute-start | bytes 1277960 | tf_op jit(solution)/shard_map/ppermute | solution.py:570
  125.8 2.6 %collective-permute-start.13 = (bf16[112,1024]{1,0:T(8,128)(2,1)S(1)}, bf16[112,1024]{1,0:T(8,128)(2,1)S(1)}, u32[]{:S(2)}, u32[]{:S(2)}) collective-permute-start(bf16[112,1024]{1,0:T(8,128)(2,1)S(1)} %get-tuple-element.51.refs_3_), channel_id=1, source_target_pairs={{0,1},{1,0},{2,3},{3,2},{4,5},{5,4},{6,7},{7,6},{8,9},{9,8},{10,11... | collective-permute-start | bytes 688136 | tf_op jit(solution)/shard_map/ppermute | solution.py:574
  126.4 1.4 %collective-permute-start.10 = (bf16[96,1024]{1,0:T(8,128)(2,1)S(1)}, bf16[96,1024]{1,0:T(8,128)(2,1)S(1)}, u32[]{:S(2)}, u32[]{:S(2)}) collective-permute-start(bf16[96,1024]{1,0:T(8,128)(2,1)S(1)} %get-tuple-element.48.refs_0_), channel_id=1, source_target_pairs={{0,1},{1,0},{2,3},{3,2},{4,5},{5,4},{6,7},{7,6},{8,9},{9,8},{10,11... | collective-permute-start | bytes 589832 | tf_op jit(solution)/shard_map/ppermute | solution.py:574
  126.5 1.6 %collective-permute-start.11 = (bf16[96,1024]{1,0:T(8,128)(2,1)S(1)}, bf16[96,1024]{1,0:T(8,128)(2,1)S(1)}, u32[]{:S(2)}, u32[]{:S(2)}) collective-permute-start(bf16[96,1024]{1,0:T(8,128)(2,1)S(1)} %get-tuple-element.49.refs_1_), channel_id=1, source_target_pairs={{0,1},{1,0},{2,3},{3,2},{4,5},{5,4},{6,7},{7,6},{8,9},{9,8},{10,11... | collective-permute-start | bytes 589832 | tf_op jit(solution)/shard_map/ppermute | solution.py:574
  126.9 1.5 %collective-permute-start.12 = (bf16[96,1024]{1,0:T(8,128)(2,1)S(1)}, bf16[96,1024]{1,0:T(8,128)(2,1)S(1)}, u32[]{:S(2)}, u32[]{:S(2)}) collective-permute-start(bf16[96,1024]{1,0:T(8,128)(2,1)S(1)} %get-tuple-element.50.refs_2_), channel_id=1, source_target_pairs={{0,1},{1,0},{2,3},{3,2},{4,5},{5,4},{6,7},{7,6},{8,9},{9,8},{10,11... | collective-permute-start | bytes 589832 | tf_op jit(solution)/shard_map/ppermute | solution.py:574

commit v8 on v7

--- a/solution.py
+++ b/solution.py
@@ -16,7 +16,7 @@
 LOG2E = math.log2(math.e)
 LN2 = math.log(2.0)
 BLOCK = 128
-ROW_GROUPS = 8
+ROW_GROUPS = 4
 LIMIT = 24
 FULL = 63
 HIDE = 20_000_000_000
@@ -255,44 +255,63 @@
         lax.fori_loop(0, n_half // block, forward, 0)
 
 
-def far_owner(count_ref, col_ref, t_ref, *refs, block, side):
+def join_columns(first, second):
+    top = jnp.maximum(first[0], second[0])
+    return top, first[1] * jnp.exp2(first[0] - top) + second[1] * jnp.exp2(second[0] - top)
+
+
+def early_scores(count_ref, near_ref, t_ref, *refs, capacity, block):
+    *q_refs, s_ref, col_ref = refs
+    per_device, _, n_cols = s_ref.shape
+    for l in range(per_device):
+        q = jnp.concatenate([ref[l * capacity : (l + 1) * capacity, :] for ref in q_refs], axis=0)
+        s = scores_of(q, t_ref[l], count_ref[l])
+        s_ref[l] = s
+        highest = jnp.max(s, axis=0, keepdims=True)
+        part = highest, column_part(s_ref.at[l], highest, block)
+        top, total = join_columns(part, (near_ref[l, 0:1, :], near_ref[l, 1:2, :]))
+        col_ref[l] = jnp.concatenate([top, total, jnp.zeros((6, n_cols), F32)], axis=0)
+
+
+def far_owner(count_ref, col_ref, t_ref, early_ref, *refs, block, side):
     _, _, here = place_of(side)
     *q_hbm, p_hbm, rev_hbm, q_ref, s_ref, w_ref, p_ref, tail_ref, rev_ref, q_sem, p_sem, rev_sem = refs
-    per_device, n_msg, capacity, width = q_ref.shape
-    _, n_half, n_cols = s_ref.shape
+    per_device, n_late, capacity, width = q_ref.shape
+    _, n_rows, n_cols = s_ref.shape
+    n_msg = p_ref.shape[0]
+    n_early = early_ref.shape[1]
     tiles = capacity * width // 2048
     arrive, leave = [], []
     for l in range(per_device):
         at = pl.ds(l * capacity, capacity)
-        arrive.append([pltpu.make_async_copy(q_hbm[k].at[at, :], q_ref.at[l, k], q_sem.at[l, k]) for k in range(n_msg)])
+        arrive.append([pltpu.make_async_copy(q_hbm[k].at[at, :], q_ref.at[l, k], q_sem.at[l, k]) for k in range(n_late)])
         at = pl.ds(l * tiles, tiles + l // (per_device - 1))
         to = [p_hbm.at[lax.bitwise_xor(here, k), at] for k in range(n_msg)]
         leave.append([pltpu.make_async_copy(p_ref.at[k, at], to[k], p_sem.at[l, k]) for k in range(n_msg)])
-    for copy in arrive[0]:
+    for copy in sum(arrive, []):
         copy.start()
     rev_leave = pltpu.make_async_copy(rev_ref, rev_hbm, rev_sem)
     half_reverse = []
     for l in range(per_device):
         for copy in arrive[l]:
             copy.wait()
-        for copy in arrive[l + 1] if l + 1 < per_device else []:
-            copy.start()
-        s = scores_of(q_ref[l].reshape(n_half, width), t_ref[l], count_ref[l])
+        s = scores_of(q_ref[l].reshape(n_rows, width), t_ref[l], count_ref[l])
         s_ref[l] = s
         highest = jnp.max(s, axis=0, keepdims=True)
-        total = column_part(s_ref.at[l], highest, block)
-        top = jnp.maximum(highest, col_ref[l, 0:1, :])
-        total = total * jnp.exp2(highest - top) + col_ref[l, 1:2, :] * jnp.exp2(col_ref[l, 0:1, :] - top)
+        part = highest, column_part(s_ref.at[l], highest, block)
+        top, total = join_columns(part, (col_ref[l, 0:1, :], col_ref[l, 1:2, :]))
         half_reverse.append(0.5 * (top + jnp.log2(total)))
         rev_ref[l] = jnp.broadcast_to(half_reverse[l], (8, n_cols))
     rev_leave.start()
     for l in range(per_device):
-        for start in range(0, n_half, block):
-            at = slice(start, start + block)
-            s = s_ref[l, at, :]
+        for start in range(0, n_early + n_rows, block):
+            if start < n_early:
+                s = early_ref[l, start : start + block, :]
+            else:
+                s = s_ref[l, start - n_early : start - n_early + block, :]
             forward = row_log_sum(s)
             w, margin = weigh(s, half_reverse[l])
-            w_ref[l, at, :] = w
+            w_ref[l, start : start + block, :] = w
             put_tail(tail_ref, l, start // capacity, margin, forward, capacity)
         p = jnp.dot(w_ref[l], t_ref[l], preferred_element_type=F32).astype(BF16)
         put_pool(p_ref, l, p, capacity)
@@ -515,25 +534,36 @@
         **work,
     )(counts, near_in, targets)
     tails = pltpu.VMEM((side, 16, 128), F32)
+    early = side // 2
+    n_early = early * capacity
+    late_block = capacity * math.gcd(early, ROW_GROUPS)
+    early_s, early_col = call(
+        functools.partial(early_scores, capacity=capacity, block=late_block),
+        (sds((per_device, n_early, n_cols), F32), sds((per_device, 8, n_cols), F32)),
+        exps=n_slots * n_cols // 2,
+        in_specs=[smem] + [vmem] * (2 + early),
+        out_specs=(vmem, vmem),
+        **work,
+    )(counts, near_col, targets, *far_in[:early])
     far_pool, reverse = call(
-        functools.partial(far_owner, block=row_block, side=side),
+        functools.partial(far_owner, block=late_block, side=side),
         (pltpu.HBM(pooled.shape, BF16), pltpu.HBM((per_device, 8, n_cols), F32)),
         [
-            pltpu.VMEM((per_device, side, capacity, width), BF16),
-            pltpu.VMEM((per_device, n_half, n_cols), F32),
+            pltpu.VMEM((per_device, side - early, capacity, width), BF16),
+            pltpu.VMEM((per_device, n_half - n_early, n_cols), F32),
             pltpu.VMEM((per_device, n_half, n_cols), BF16),
             pltpu.VMEM((side, n_tiles, 16, 128), BF16),
             tails,
             pltpu.VMEM((per_device, 8, n_cols), F32),
-            pltpu.SemaphoreType.DMA((per_device, side)),
+            pltpu.SemaphoreType.DMA((per_device, side - early)),
             pltpu.SemaphoreType.DMA((per_device, side)),
             pltpu.SemaphoreType.DMA,
         ],
         exps=3 * n_slots * n_cols,
-        in_specs=[smem, vmem, vmem] + [hbm] * side,
+        in_specs=[smem, vmem, vmem, vmem] + [hbm] * (side - early),
         out_specs=(hbm, hbm),
         **work,
-    )(counts, near_col, targets, *far_in)
+    )(counts, early_col, targets, early_s, *far_in[early:])
     back_far = exchange(far_pool)
     near_pool = call(
         functools.partial(near_owner, capacity=capacity, block=row_block),

time: 131 us -> 130 us (level)
  waiting for transfers between devices: 62 us -> 58.6 us
    ppermute x1, waiting for transfers between devices: 22 us -> 19.2 us  [shards(): from_far = lax.ppermute(joined, 'src', partner)]
    ppermute x7, waiting for transfers between devices: 7.57 us -> 4.85 us  [shards(): lax.ppermute(far_q[k], 'src', [(i, i ^ k) for i in range(n_src)])]
    all_to_all x3, waiting for transfers between devices: 13 us -> 15.2 us  [exchange(): lax.all_to_all(x, 'src', split_axis=0, concat_axis=0, axis_index_groups=h...]
    pallas_call x1 -> x2, Pallas kernels: 8.41 us -> 9.71 us  [the longest x1 7.08 us: shards(): call(functools.partial(far_owner, block=late_block, side=side), (pltpu.HB...]
  transfers between devices with their start and end apart: 19 -> 19, of which waited for: 11 -> 12; matrix products, arithmetic and copies ran while one was open for 0% -> 0% of each run, Pallas kernels for 13% -> 16%
where the time goes in v8:
time: 130 us; the launch traced here: 129 us
  waiting for transfers between devices  58.6 us (45%)
  Pallas kernels  32.1 us (25%)
  starting transfers between devices  27.6 us (21%)
  local copies, waits for them, and re-layouts  9.18 us (7%)
    ppermute x1, waiting for transfers between devices, shards(): from_far = lax.ppermute(joined, 'src', partner)  19.2 us
    all_to_all x3, waiting for transfers between devices, exchange(): lax.all_to_all(x, 'src', split_axis=0, concat_axis=0, axis_index_groups=h...  15.2 us
    ppermute x1, waiting for transfers between devices, shards(): far_mine = lax.ppermute(mine, 'src', partner)  14.5 us
    all_to_all x3, starting transfers between devices, exchange(): lax.all_to_all(x, 'src', split_axis=0, concat_axis=0, axis_index_groups=h...  12.9 us
    unnamed x30, local copies, waits for them, and re-layouts  9.18 us
    ppermute x7, starting transfers between devices, shards(): lax.ppermute(far_q[k], 'src', [(i, i ^ k) for i in range(n_src)])  8.76 us
    pallas_call x1, Pallas kernels, shards(): call(functools.partial(far_owner, block=late_block, side=side), (pltpu.HB...  7.08 us
    pallas_call x2, Pallas kernels, combine(): call(functools.partial(combine_kernel, capacity=capacity, side=side, spli...  6.75 us
  transfers between devices with their start and end apart: 19, of which 12 were waited for; matrix products, arithmetic and copies ran while one was open for 0% of the time, Pallas kernels for 16%

profile of v8, /device:TPU:0, one launch (start us, length us, event | category | flops | bytes accessed | tf_op | source)
XLA Modules:
  0.0 129.0 jit_solution(10835294563871785988)
XLA Ops:
  0.6 3.2 %shard_map.68 = (bf16[208,1024]{1,0:T(8,128)(2,1)}, bf16[8,96,1024]{2,1,0:T(8,128)(2,1)}, f32[16,384]{1,0:T(8,128)}) custom-call(s32[4,384]{1,0:T(4,128)} %bitcast.4, s32[1,64]{1,0:T(1,128)} %bitcast.2, bf16[384,1024]{1,0:T(8,128)(2,1)} %src_hbm.1), custom_call_target="tpu_custom_call" | custom-call | flops 603979776 | bytes 2359296 | tf_op jit(solution)/shard_map/pallas_call | solution.py:483
  3.8 0.0 copy-start.7
  3.9 4.1 %collective-permute-start = (bf16[208,1024]{1,0:T(8,128)(2,1)}, bf16[208,1024]{1,0:T(8,128)(2,1)S(1)}, u32[]{:S(2)}, u32[]{:S(2)}) collective-permute-start(bf16[208,1024]{1,0:T(8,128)(2,1)} %get-tuple-element.34), channel_id=1, source_target_pairs={{0,16},{2,18},{4,20},{6,22},{8,24},{10,26},{12,28},{14,30},{16,0},... | collective-permute-start | bytes 1277960 | tf_op jit(solution)/shard_map/ppermute | solution.py:500
  7.9 4.7 %all-to-all-start = ((bf16[8,96,1024]{2,1,0:T(8,128)(2,1)}), bf16[8,96,1024]{2,1,0:T(8,128)(2,1)S(1)}, u32[]{:S(2)}, u32[]{:S(2)}) async-start(bf16[8,96,1024]{2,1,0:T(8,128)(2,1)} %get-tuple-element.31), calls=%async_computation | async-start | bytes 3145728 | tf_op jit(solution)/shard_map/all_to_all | solution.py:466
  12.7 14.5 %collective-permute-done.mine_ref = bf16[208,1024]{1,0:T(8,128)(2,1)S(1)} collective-permute-done((bf16[208,1024]{1,0:T(8,128)(2,1)}, bf16[208,1024]{1,0:T(8,128)(2,1)S(1)}, u32[]{:S(2)}, u32[]{:S(2)}) %collective-permute-start) | collective-permute-done | bytes 426016 | tf_op jit(solution)/shard_map/ppermute | solution.py:500
  27.2 0.0 collective-permute-start.1
  27.2 1.8 %collective-permute-done.1.other_ref = bf16[208,1024]{1,0:T(8,128)(2,1)S(1)} collective-permute-done((bf16[208,1024]{1,0:T(8,128)(2,1)S(1)}, bf16[208,1024]{1,0:T(8,128)(2,1)S(1)}, u32[]{:S(2)}, u32[]{:S(2)}) %collective-permute-start.1) | collective-permute-done | bytes 426016 | tf_op jit(solution)/shard_map/ppermute | solution.py:501
  29.0 0.0 copy-done.7
  29.0 2.4 %shard_map.70 = (bf16[96,1024]{1,0:T(8,128)(2,1)}, bf16[96,1024]{1,0:T(8,128)(2,1)}, bf16[96,1024]{1,0:T(8,128)(2,1)}, bf16[96,1024]{1,0:T(8,128)(2,1)}, bf16[96...) custom-call(s32[1,64]{1,0:T(1,128)S(1)} %bitcast.3, ...), custom_call_target="tpu_custom_call" | custom-call | flops 20000000000 | bytes 2359296 | tf_op jit(solution)/shard_map/pallas_call | solution.py:503
  31.3 1.6 %collective-permute-start.2 = (bf16[96,1024]{1,0:T(8,128)(2,1)}, bf16[96,1024]{1,0:T(8,128)(2,1)S(1)}, u32[]{:S(2)}, u32[]{:S(2)}) collective-permute-start(bf16[96,1024]{1,0:T(8,128)(2,1)} %get-tuple-element.36), channel_id=1, source_target_pairs={{0,2},{2,0},{4,6},{6,4},{8,10},{10,8},{12,14},{14,12},{16,18},{18,... | collective-permute-start | bytes 589832 | tf_op jit(solution)/shard_map/ppermute | solution.py:513
  32.9 1.6 %collective-permute-start.3 = (bf16[96,1024]{1,0:T(8,128)(2,1)}, bf16[96,1024]{1,0:T(8,128)(2,1)S(1)}, u32[]{:S(2)}, u32[]{:S(2)}) collective-permute-start(bf16[96,1024]{1,0:T(8,128)(2,1)} %get-tuple-element.37), channel_id=1, source_target_pairs={{0,4},{2,6},{4,0},{6,2},{8,12},{10,14},{12,8},{14,10},{16,20},{18,... | collective-permute-start | bytes 589832 | tf_op jit(solution)/shard_map/ppermute | solution.py:513
  34.5 0.4 collective-permute-start.4
  34.9 0.2 fusion.count_ref
  35.1 0.8 collective-permute-start.5
  35.9 2.2 %collective-permute-start.6 = (bf16[96,1024]{1,0:T(8,128)(2,1)}, bf16[96,1024]{1,0:T(8,128)(2,1)}, u32[]{:S(2)}, u32[]{:S(2)}) collective-permute-start(bf16[96,1024]{1,0:T(8,128)(2,1)} %get-tuple-element.42), channel_id=1, source_target_pairs={{0,10},{2,8},{4,14},{6,12},{8,2},{10,0},{12,6},{14,4},{16,26},{18,... | collective-permute-start | bytes 589832 | tf_op jit(solution)/shard_map/ppermute | solution.py:513
  38.1 2.7 %collective-permute-done.2.refs_1_ = bf16[96,1024]{1,0:T(8,128)(2,1)S(1)} collective-permute-done((bf16[96,1024]{1,0:T(8,128)(2,1)}, bf16[96,1024]{1,0:T(8,128)(2,1)S(1)}, u32[]{:S(2)}, u32[]{:S(2)}) %collective-permute-start.2) | collective-permute-done | bytes 196640 | tf_op jit(solution)/shard_map/ppermute | solution.py:513
  40.8 0.7 copy-done.8
  41.5 0.3 collective-permute-start.7
  41.8 1.2 collective-permute-done.3.refs_2_
  43.0 0.7 copy-done.10
  43.7 1.9 %collective-permute-start.8 = (bf16[96,1024]{1,0:T(8,128)(2,1)}, bf16[96,1024]{1,0:T(8,128)(2,1)}, u32[]{:S(2)}, u32[]{:S(2)}) collective-permute-start(bf16[96,1024]{1,0:T(8,128)(2,1)} %get-tuple-element.44), channel_id=1, source_target_pairs={{0,14},{2,12},{4,10},{6,8},{8,6},{10,4},{12,2},{14,0},{16,30},{18,... | collective-permute-start | bytes 589832 | tf_op jit(solution)/shard_map/ppermute | solution.py:513
  45.5 0.0 all-to-all-done.q_ref
  45.6 1.2 copy-done.3
  46.7 2.2 %copy-done = bf16[2,1024,1024]{2,1,0:T(8,128)(2,1)S(1)} copy-done((bf16[2,1024,1024]{2,1,0:T(8,128)(2,1)S(1)}, bf16[2,1024,1024]{2,1,0:T(8,128)(2,1)}, u32[]{:S(2)}) %copy-start) | copy-done | bytes 4194328
  48.9 1.4 %copy-done.4 = bf16[8,96,1024]{2,1,0:T(8,128)(2,1)S(1)} copy-done((bf16[8,96,1024]{2,1,0:T(8,128)(2,1)S(1)}, bf16[8,96,1024]{2,1,0:T(8,128)(2,1)}, u32[]{:S(2)}) %copy-start.4) | copy-done | bytes 1572888
  50.4 4.4 %shard_map.69 = (f32[2,384,1024]{2,1,0:T(8,128)S(1)}, f32[2,8,1024]{2,1,0:T(8,128)S(1)}, f32[2,384,128]{2,1,0:T(8,128)S(1)}) custom-call(s32[2]{0:T(128)S(1)} %fusion.count_ref, bf16[8,96,1024]{2,1,0:T(8,128)(2,1)S(1)} %copy-done.4, bf16[2,1024,1024]{2,1,0:T(8,128)(2,1)S(1)} %copy-done), custom_call_target="tpu_custom_call" | custom-call | flops 1610612736 | bytes 5767168 | tf_op jit(solution)/shard_map/pallas_call | solution.py:524
  54.8 0.0 collective-permute-done.4.refs_3_
  54.8 0.0 copy-done.1
  54.8 0.0 copy-done.9
  54.8 0.0 copy-done.11
  54.8 0.0 copy-done.12
  54.9 2.6 %shard_map.71 = (f32[2,192,1024]{2,1,0:T(8,128)S(1)}, f32[2,8,1024]{2,1,0:T(8,128)S(1)}) custom-call(s32[2]{0:T(128)S(1)} %fusion.count_ref, f32[2,8,1024]{2,1,0:T(8,128)S(1)} %get-tuple-element.33.near_ref, bf16[2,1024,1024]{2,1,0:T(8,128)(2,1)S(1)} %copy-done.1, bf16[96,1024]{1,0:T(8,128)(2,1)S(1)} %copy-done.12, bf16[96,1024]{1,0:T(8,128)(2,1)S(1)} %copy-done.9, ...), custom_call_target="tpu_custom_call" | custom-call | flops 1610612736 | bytes 5767168 | tf_op jit(solution)/shard_map/pallas_call | solution.py:540
  57.5 0.0 collective-permute-done.5.refs_0_
  57.5 0.0 collective-permute-done.6.refs_1_
  57.5 0.0 collective-permute-done.7.refs_2_
  57.5 0.9 collective-permute-done.8.refs_3_
  58.4 7.1 %shard_map.72 = (bf16[8,49,16,128]{3,2,1,0:T(8,128)(2,1)}, f32[2,8,1024]{2,1,0:T(8,128)}) custom-call(s32[2]{0:T(128)S(1)} %fusion.count_ref, f32[2,8,1024]{2,1,0:T(8,128)S(1)} %get-tuple-element.39.col_ref, bf16[2,1024,1024]{2,1,0:T(8,128)(2,1)S(1)} %copy-done.1, f32[2,192,1024]{2,1,0:T(8,128)S(1)} %get-tuple-element.40.early_ref, ...), custom_call_target="tpu_custom_call" | custom-call | flops 1610612736 | bytes 5767168 | tf_op jit(solution)/shard_map/pallas_call | solution.py:548
  65.5 4.5 %all-to-all-start.2 = ((bf16[8,49,16,128]{3,2,1,0:T(8,128)(2,1)}), bf16[8,49,16,128]{3,2,1,0:T(8,128)(2,1)}, u32[]{:S(2)}, u32[]{:S(2)}) async-start(bf16[8,49,16,128]{3,2,1,0:T(8,128)(2,1)} %get-tuple-element.48), calls=%async_computation.2 | async-start | bytes 3211264 | tf_op jit(solution)/shard_map/all_to_all | solution.py:466
  70.0 0.0 copy-start.2
  70.0 2.2 %copy-done.2 = bf16[2,1024,1024]{2,1,0:T(8,128)(2,1)S(1)} copy-done((bf16[2,1024,1024]{2,1,0:T(8,128)(2,1)S(1)}, bf16[2,1024,1024]{2,1,0:T(8,128)(2,1)}, u32[]{:S(2)}) %copy-start.2) | copy-done | bytes 4194328
  72.2 0.8 copy-done.5
  73.1 3.6 %shard_map.73 = bf16[8,49,16,128]{3,2,1,0:T(8,128)(2,1)} custom-call(f32[2,384,1024]{2,1,0:T(8,128)S(1)} %get-tuple-element.32.s_ref, f32[2,8,1024]{2,1,0:T(8,128)S(1)} %copy-done.5, f32[2,384,128]{2,1,0:T(8,128)S(1)} %get-tuple-element.46.fwd_ref, bf16[2,1024,1024]{2,1,0:T(8,128)(2,1)S(1)} %copy-done.2), custom_call_target="tpu_custom_call" | custom-call | flops 1610612736 | bytes 5767168 | tf_op jit(solution)/shard_map/pallas_call | solution.py:568
  76.7 13.0 %all-to-all-done.2.r_ref = bf16[8,49,16,128]{3,2,1,0:T(8,128)(2,1)} async-done(((bf16[8,49,16,128]{3,2,1,0:T(8,128)(2,1)}), bf16[8,49,16,128]{3,2,1,0:T(8,128)(2,1)}, u32[]{:S(2)}, u32[]{:S(2)}) %all-to-all-start.2) | async-done | bytes 1605664 | tf_op jit(solution)/shard_map/all_to_all | solution.py:466
  89.7 3.7 %all-to-all-start.1 = ((bf16[8,49,16,128]{3,2,1,0:T(8,128)(2,1)}), bf16[8,49,16,128]{3,2,1,0:T(8,128)(2,1)S(1)}, u32[]{:S(2)}, u32[]{:S(2)}) async-start(bf16[8,49,16,128]{3,2,1,0:T(8,128)(2,1)} %shard_map.73), calls=%async_computation.1 | async-start | bytes 3211264 | tf_op jit(solution)/shard_map/all_to_all | solution.py:466
  93.4 4.3 %shard_map.74 = (f32[192,1024]{1,0:T(8,128)S(1)}, f32[8,384]{1,0:T(8,128)S(1)}, bf16[208,1024]{1,0:T(8,128)(2,1)S(1)}) custom-call(f32[16,384]{1,0:T(8,128)S(1)} %copy-done.13, bf16[8,49,16,128]{3,2,1,0:T(8,128)(2,1)} %all-to-all-done.2.r_ref, f32[16,384]{1,0:T(8,128)S(1)} %copy-done.6), custom_call_target="tpu_custom_call" | custom-call | flops 1207959552 | bytes 3145728 | tf_op jit(solution)/shard_map/pallas_call | solution.py:579
  97.7 0.1 collective-permute-start.9
  97.7 1.8 %collective-permute-done.9.got_ref = bf16[208,1024]{1,0:T(8,128)(2,1)S(1)} collective-permute-done((bf16[208,1024]{1,0:T(8,128)(2,1)S(1)}, bf16[208,1024]{1,0:T(8,128)(2,1)S(1)}, u32[]{:S(2)}, u32[]{:S(2)}) %collective-permute-start.9) | collective-permute-done | bytes 426016 | tf_op jit(solution)/shard_map/ppermute | solution.py:591
  99.5 0.4 shard_map.75._
  99.9 0.7 collective-permute-start.14
  100.6 19.2 %collective-permute-done.14.refs_8_ = bf16[208,1024]{1,0:T(8,128)(2,1)S(1)} collective-permute-done((bf16[208,1024]{1,0:T(8,128)(2,1)S(1)}, bf16[208,1024]{1,0:T(8,128)(2,1)S(1)}, u32[]{:S(2)}, u32[]{:S(2)}) %collective-permute-start.14) | collective-permute-done | bytes 426016 | tf_op jit(solution)/shard_map/ppermute | solution.py:599
  119.8 0.0 collective-permute-start.15
  119.8 2.2 %all-to-all-done.1.r_ref = bf16[8,49,16,128]{3,2,1,0:T(8,128)(2,1)S(1)} async-done(((bf16[8,49,16,128]{3,2,1,0:T(8,128)(2,1)}), bf16[8,49,16,128]{3,2,1,0:T(8,128)(2,1)S(1)}, u32[]{:S(2)}, u32[]{:S(2)}) %all-to-all-start.1) | async-done | bytes 1605664 | tf_op jit(solution)/shard_map/all_to_all | solution.py:466
  122.0 2.5 %shard_map.76 = (bf16[96,1024]{1,0:T(8,128)(2,1)S(1)}, bf16[96,1024]{1,0:T(8,128)(2,1)S(1)}, bf16[96,1024]{1,0:T(8,128)(2,1)S(1)}, bf16[112,1024]{1,0:T(8,128)(2,1)S(1)}) custom-call(f32[16,384]{1,0:T(8,128)S(1)} %copy-done.6, bf16[8,49,16,128]{3,2,1,0:T(8,128)(2,1)S(1)} %all-to-all-done.1.r_ref, bf16[208,1024]{1,0:T(8,128)(2,1)S(1)} %shard_map.75._), custom_call_target="tpu_custom_call" | custom-call | tf_op jit(solution)/shard_map/pallas_call | solution.py:579
  124.4 0.1 collective-permute-start.13
  124.5 0.5 collective-permute-start.10
  125.0 0.1 collective-permute-start.11
  125.1 0.4 collective-permute-start.12
  125.5 0.7 collective-permute-done.10.refs_4_
  126.3 0.3 collective-permute-done.11.refs_5_
  126.6 0.3 collective-permute-done.12.refs_6_
  126.8 0.0 collective-permute-done.13.refs_7_
  126.8 0.0 collective-permute-done.15.refs_9_
  126.9 1.6 %shard_map.77 = (bf16[384,1024]{1,0:T(8,128)(2,1)}, f32[1,384]{1,0:T(1,128)S(1)}) custom-call(bf16[96,1024]{1,0:T(8,128)(2,1)S(1)} %get-tuple-element.52.refs_0_, bf16[96,1024]{1,0:T(8,128)(2,1)S(1)} %get-tuple-element.53.refs_1_, bf16[96,1024]{1,0:T(8,128)(2,1)S(1)} %get-tuple-element.54.refs_2_, bf16[112,1024]{1,0:T(8,128)(2,1)S(1)} %get-tuple-element.55.refs_3_, ...), custom_call_target="tpu_custom_call" | custom-call | bytes 3932160 | tf_op jit(solution)/shard_map/pallas_call | solution.py:605
  128.5 0.6 convert_reduce_fusion
  (17 shorter events, 0.0 us)
Async XLA Ops:
  3.8 25.1 %copy-start.7 = (s32[64]{0:T(128)S(1)}, s32[64]{0:T(128)}, u32[]{:S(2)}) copy-start(s32[64]{0:T(128)} %param.8) | copy-start | bytes 772
  3.9 23.3 %collective-permute-start = (bf16[208,1024]{1,0:T(8,128)(2,1)}, bf16[208,1024]{1,0:T(8,128)(2,1)S(1)}, u32[]{:S(2)}, u32[]{:S(2)}) collective-permute-start(bf16[208,1024]{1,0:T(8,128)(2,1)} %get-tuple-element.34), channel_id=1, source_target_pairs={{0,16},{2,18},{4,20},{6,22},{8,24},{10,26},{12,28},{14,30},{16,0},... | collective-permute-start | bytes 1277960 | tf_op jit(solution)/shard_map/ppermute | solution.py:500
  7.9 37.6 %all-to-all-start = ((bf16[8,96,1024]{2,1,0:T(8,128)(2,1)}), bf16[8,96,1024]{2,1,0:T(8,128)(2,1)S(1)}, u32[]{:S(2)}, u32[]{:S(2)}) async-start(bf16[8,96,1024]{2,1,0:T(8,128)(2,1)} %get-tuple-element.31), calls=%async_computation | async-start | bytes 3145728 | tf_op jit(solution)/shard_map/all_to_all | solution.py:466
  27.2 1.8 %collective-permute-start.1 = (bf16[208,1024]{1,0:T(8,128)(2,1)S(1)}, bf16[208,1024]{1,0:T(8,128)(2,1)S(1)}, u32[]{:S(2)}, u32[]{:S(2)}) collective-permute-start(bf16[208,1024]{1,0:T(8,128)(2,1)S(1)} %collective-permute-done.mine_ref), channel_id=1, source_target_pairs={{0,1},{1,0},{2,3},{3,2},{4,5},{5,4},{6,7},{7,6},{8,9},{9,8},{10,11... | collective-permute-start | bytes 1277960 | tf_op jit(solution)/shard_map/ppermute | solution.py:501
  27.2 7.7 %copy-start.14 = (s32[64]{0:T(128)S(1)}, s32[64]{0:T(128)}, u32[]{:S(2)}) copy-start(s32[64]{0:T(128)} %param.9) | copy-start | bytes 772
  31.3 9.5 %collective-permute-start.2 = (bf16[96,1024]{1,0:T(8,128)(2,1)}, bf16[96,1024]{1,0:T(8,128)(2,1)S(1)}, u32[]{:S(2)}, u32[]{:S(2)}) collective-permute-start(bf16[96,1024]{1,0:T(8,128)(2,1)} %get-tuple-element.36), channel_id=1, source_target_pairs={{0,2},{2,0},{4,6},{6,4},{8,10},{10,8},{12,14},{14,12},{16,18},{18,... | collective-permute-start | bytes 589832 | tf_op jit(solution)/shard_map/ppermute | solution.py:513
  32.9 10.0 %collective-permute-start.3 = (bf16[96,1024]{1,0:T(8,128)(2,1)}, bf16[96,1024]{1,0:T(8,128)(2,1)S(1)}, u32[]{:S(2)}, u32[]{:S(2)}) collective-permute-start(bf16[96,1024]{1,0:T(8,128)(2,1)} %get-tuple-element.37), channel_id=1, source_target_pairs={{0,4},{2,6},{4,0},{6,2},{8,12},{10,14},{12,8},{14,10},{16,20},{18,... | collective-permute-start | bytes 589832 | tf_op jit(solution)/shard_map/ppermute | solution.py:513
  34.5 20.3 %collective-permute-start.4 = (bf16[96,1024]{1,0:T(8,128)(2,1)}, bf16[96,1024]{1,0:T(8,128)(2,1)}, u32[]{:S(2)}, u32[]{:S(2)}) collective-permute-start(bf16[96,1024]{1,0:T(8,128)(2,1)} %get-tuple-element.38), channel_id=1, source_target_pairs={{0,6},{2,4},{4,2},{6,0},{8,14},{10,12},{12,10},{14,8},{16,22},{18,... | collective-permute-start | bytes 589832 | tf_op jit(solution)/shard_map/ppermute | solution.py:513
  35.1 22.4 %collective-permute-start.5 = (bf16[96,1024]{1,0:T(8,128)(2,1)}, bf16[96,1024]{1,0:T(8,128)(2,1)}, u32[]{:S(2)}, u32[]{:S(2)}) collective-permute-start(bf16[96,1024]{1,0:T(8,128)(2,1)} %get-tuple-element.41), channel_id=1, source_target_pairs={{0,8},{2,10},{4,12},{6,14},{8,0},{10,2},{12,4},{14,6},{16,24},{18,... | collective-permute-start | bytes 589832 | tf_op jit(solution)/shard_map/ppermute | solution.py:513
  35.9 21.6 %collective-permute-start.6 = (bf16[96,1024]{1,0:T(8,128)(2,1)}, bf16[96,1024]{1,0:T(8,128)(2,1)}, u32[]{:S(2)}, u32[]{:S(2)}) collective-permute-start(bf16[96,1024]{1,0:T(8,128)(2,1)} %get-tuple-element.42), channel_id=1, source_target_pairs={{0,10},{2,8},{4,14},{6,12},{8,2},{10,0},{12,6},{14,4},{16,26},{18,... | collective-permute-start | bytes 589832 | tf_op jit(solution)/shard_map/ppermute | solution.py:513
  40.8 0.7 copy-start.8
  41.5 16.0 %collective-permute-start.7 = (bf16[96,1024]{1,0:T(8,128)(2,1)}, bf16[96,1024]{1,0:T(8,128)(2,1)}, u32[]{:S(2)}, u32[]{:S(2)}) collective-permute-start(bf16[96,1024]{1,0:T(8,128)(2,1)} %get-tuple-element.43), channel_id=1, source_target_pairs={{0,12},{2,14},{4,8},{6,10},{8,4},{10,6},{12,0},{14,2},{16,28},{18,... | collective-permute-start | bytes 589832 | tf_op jit(solution)/shard_map/ppermute | solution.py:513
  43.0 0.7 copy-start.10
  43.7 14.8 %collective-permute-start.8 = (bf16[96,1024]{1,0:T(8,128)(2,1)}, bf16[96,1024]{1,0:T(8,128)(2,1)}, u32[]{:S(2)}, u32[]{:S(2)}) collective-permute-start(bf16[96,1024]{1,0:T(8,128)(2,1)} %get-tuple-element.44), channel_id=1, source_target_pairs={{0,14},{2,12},{4,10},{6,8},{8,6},{10,4},{12,2},{14,0},{16,30},{18,... | collective-permute-start | bytes 589832 | tf_op jit(solution)/shard_map/ppermute | solution.py:513
  45.6 1.2 copy-start.3
  46.7 2.2 %copy-start = (bf16[2,1024,1024]{2,1,0:T(8,128)(2,1)S(1)}, bf16[2,1024,1024]{2,1,0:T(8,128)(2,1)}, u32[]{:S(2)}) copy-start(bf16[2,1024,1024]{2,1,0:T(8,128)(2,1)} %t_ref.7) | copy-start | bytes 12582916
  48.9 1.4 %copy-start.4 = (bf16[8,96,1024]{2,1,0:T(8,128)(2,1)S(1)}, bf16[8,96,1024]{2,1,0:T(8,128)(2,1)}, u32[]{:S(2)}) copy-start(bf16[8,96,1024]{2,1,0:T(8,128)(2,1)} %copy-done.3) | copy-start | bytes 4718596
  50.3 4.5 %copy-start.1 = (bf16[2,1024,1024]{2,1,0:T(8,128)(2,1)S(1)}, bf16[2,1024,1024]{2,1,0:T(8,128)(2,1)}, u32[]{:S(2)}) copy-start(bf16[2,1024,1024]{2,1,0:T(8,128)(2,1)} %t_ref.7) | copy-start | bytes 12582916
  50.3 4.5 %copy-start.9 = (bf16[96,1024]{1,0:T(8,128)(2,1)S(1)}, bf16[96,1024]{1,0:T(8,128)(2,1)}, u32[]{:S(2)}) copy-start(bf16[96,1024]{1,0:T(8,128)(2,1)} %copy-done.8) | copy-start | bytes 589828
  50.3 4.5 %copy-start.11 = (bf16[96,1024]{1,0:T(8,128)(2,1)S(1)}, bf16[96,1024]{1,0:T(8,128)(2,1)}, u32[]{:S(2)}) copy-start(bf16[96,1024]{1,0:T(8,128)(2,1)} %copy-done.10) | copy-start | bytes 589828
  50.3 4.5 %copy-start.12 = (bf16[96,1024]{1,0:T(8,128)(2,1)S(1)}, bf16[96,1024]{1,0:T(8,128)(2,1)}, u32[]{:S(2)}) copy-start(bf16[96,1024]{1,0:T(8,128)(2,1)} %get-tuple-element.35.refs_0_) | copy-start | bytes 589828
  65.5 24.1 %all-to-all-start.2 = ((bf16[8,49,16,128]{3,2,1,0:T(8,128)(2,1)}), bf16[8,49,16,128]{3,2,1,0:T(8,128)(2,1)}, u32[]{:S(2)}, u32[]{:S(2)}) async-start(bf16[8,49,16,128]{3,2,1,0:T(8,128)(2,1)} %get-tuple-element.48), calls=%async_computation.2 | async-start | bytes 3211264 | tf_op jit(solution)/shard_map/all_to_all | solution.py:466
  70.0 2.2 %copy-start.2 = (bf16[2,1024,1024]{2,1,0:T(8,128)(2,1)S(1)}, bf16[2,1024,1024]{2,1,0:T(8,128)(2,1)}, u32[]{:S(2)}) copy-start(bf16[2,1024,1024]{2,1,0:T(8,128)(2,1)} %t_ref.7) | copy-start | bytes 12582916
  72.2 0.8 copy-start.5
  76.7 16.7 %copy-start.6 = (f32[16,384]{1,0:T(8,128)S(1)}, f32[16,384]{1,0:T(8,128)}, u32[]{:S(2)}) copy-start(f32[16,384]{1,0:T(8,128)} %get-tuple-element.30._.code_ref) | copy-start | bytes 73732
  76.7 16.7 %copy-start.13 = (f32[16,384]{1,0:T(8,128)S(1)}, f32[16,384]{1,0:T(8,128)}, u32[]{:S(2)}) copy-start(f32[16,384]{1,0:T(8,128)} %get-tuple-element.47.code_ref) | copy-start | bytes 73732
  89.7 32.3 %all-to-all-start.1 = ((bf16[8,49,16,128]{3,2,1,0:T(8,128)(2,1)}), bf16[8,49,16,128]{3,2,1,0:T(8,128)(2,1)S(1)}, u32[]{:S(2)}, u32[]{:S(2)}) async-start(bf16[8,49,16,128]{3,2,1,0:T(8,128)(2,1)} %shard_map.73), calls=%async_computation.1 | async-start | bytes 3211264 | tf_op jit(solution)/shard_map/all_to_all | solution.py:466
  97.7 1.8 %collective-permute-start.9 = (bf16[208,1024]{1,0:T(8,128)(2,1)S(1)}, bf16[208,1024]{1,0:T(8,128)(2,1)S(1)}, u32[]{:S(2)}, u32[]{:S(2)}) collective-permute-start(bf16[208,1024]{1,0:T(8,128)(2,1)S(1)} %get-tuple-element.51), channel_id=1, source_target_pairs={{0,1},{1,0},{2,3},{3,2},{4,5},{5,4},{6,7},{7,6},{8,9},{9,8},{10,11... | collective-permute-start | bytes 1277960 | tf_op jit(solution)/shard_map/ppermute | solution.py:591
  99.9 19.9 %collective-permute-start.14 = (bf16[208,1024]{1,0:T(8,128)(2,1)S(1)}, bf16[208,1024]{1,0:T(8,128)(2,1)S(1)}, u32[]{:S(2)}, u32[]{:S(2)}) collective-permute-start(bf16[208,1024]{1,0:T(8,128)(2,1)S(1)} %shard_map.75._), channel_id=1, source_target_pairs={{0,16},{2,18},{4,20},{6,22},{8,24},{10,26},{12,28},{14,30},{16,0},... | collective-permute-start | bytes 1277960 | tf_op jit(solution)/shard_map/ppermute | solution.py:599
  119.8 7.1 %collective-permute-start.15 = (bf16[208,1024]{1,0:T(8,128)(2,1)S(1)}, bf16[208,1024]{1,0:T(8,128)(2,1)S(1)}, u32[]{:S(2)}, u32[]{:S(2)}) collective-permute-start(bf16[208,1024]{1,0:T(8,128)(2,1)S(1)} %collective-permute-done.14.refs_8_), channel_id=1, source_target_pairs={{0,1},{1,0},{2,3},{3,2},{4,5},{5,4},{6,7},{7,6},{8,9},{9,8},{10,11... | collective-permute-start | bytes 1277960 | tf_op jit(solution)/shard_map/ppermute | solution.py:600
  124.4 2.4 %collective-permute-start.13 = (bf16[112,1024]{1,0:T(8,128)(2,1)S(1)}, bf16[112,1024]{1,0:T(8,128)(2,1)S(1)}, u32[]{:S(2)}, u32[]{:S(2)}) collective-permute-start(bf16[112,1024]{1,0:T(8,128)(2,1)S(1)} %get-tuple-element.55.refs_3_), channel_id=1, source_target_pairs={{0,1},{1,0},{2,3},{3,2},{4,5},{5,4},{6,7},{7,6},{8,9},{9,8},{10,11... | collective-permute-start | bytes 688136 | tf_op jit(solution)/shard_map/ppermute | solution.py:604
  124.5 1.8 %collective-permute-start.10 = (bf16[96,1024]{1,0:T(8,128)(2,1)S(1)}, bf16[96,1024]{1,0:T(8,128)(2,1)S(1)}, u32[]{:S(2)}, u32[]{:S(2)}) collective-permute-start(bf16[96,1024]{1,0:T(8,128)(2,1)S(1)} %get-tuple-element.52.refs_0_), channel_id=1, source_target_pairs={{0,1},{1,0},{2,3},{3,2},{4,5},{5,4},{6,7},{7,6},{8,9},{9,8},{10,11... | collective-permute-start | bytes 589832 | tf_op jit(solution)/shard_map/ppermute | solution.py:604
  125.0 1.5 %collective-permute-start.11 = (bf16[96,1024]{1,0:T(8,128)(2,1)S(1)}, bf16[96,1024]{1,0:T(8,128)(2,1)S(1)}, u32[]{:S(2)}, u32[]{:S(2)}) collective-permute-start(bf16[96,1024]{1,0:T(8,128)(2,1)S(1)} %get-tuple-element.53.refs_1_), channel_id=1, source_target_pairs={{0,1},{1,0},{2,3},{3,2},{4,5},{5,4},{6,7},{7,6},{8,9},{9,8},{10,11... | collective-permute-start | bytes 589832 | tf_op jit(solution)/shard_map/ppermute | solution.py:604
  125.1 1.7 %collective-permute-start.12 = (bf16[96,1024]{1,0:T(8,128)(2,1)S(1)}, bf16[96,1024]{1,0:T(8,128)(2,1)S(1)}, u32[]{:S(2)}, u32[]{:S(2)}) collective-permute-start(bf16[96,1024]{1,0:T(8,128)(2,1)S(1)} %get-tuple-element.54.refs_2_), channel_id=1, source_target_pairs={{0,1},{1,0},{2,3},{3,2},{4,5},{5,4},{6,7},{7,6},{8,9},{9,8},{10,11... | collective-permute-start | bytes 589832 | tf_op jit(solution)/shard_map/ppermute | solution.py:604

commit v9 on v8

--- a/solution.py
+++ b/solution.py
@@ -103,12 +103,10 @@
         rank = jnp.dot(inside.astype(BF16), earlier, preferred_element_type=F32)
         return jnp.where(inside > 0.5, rank, -1.0)
 
-    code = ranks(0)
+    code = ranks(0 if flip is None else flip)
     code_ref[...] = code
     leave = [pltpu.make_async_copy(code_ref, code_hbm, sem.at[0])]
     leave[0].start()
-    if flip is not None:
-        code = ranks(flip)
     source = load()
     for start in range(0, n_buckets, group):
         slots = one_hot_slots(code, start, group, capacity)
@@ -338,7 +336,7 @@
 
 
 def combine_kernel(code_ref, r_ref, _, *refs, capacity, side, split):
-    _, core, _ = place_of(side)
+    _, core, here = place_of(side)
     *outs, r_scr, scr = refs
     n_buckets, rows = code_ref.shape
     width = scr.shape[1]
@@ -348,14 +346,15 @@
     strips = n_tiles // cols
     margin, forward = [], []
     for j in range(n_msg):
-        last = r_ref[j, n_tiles - 1].astype(F32)
+        owner = lax.bitwise_xor(here, j) if split else j
+        last = r_ref[owner, n_tiles - 1].astype(F32)
         last = (last + pltpu.roll(last, 127, 1)) + pltpu.roll(last, 126, 1)
         for r in range(strips):
             margin.append(jnp.broadcast_to(last[:, 6 * r : 6 * r + 1], (16, 128)))
             forward.append(jnp.broadcast_to(last[:, 6 * r + 3 : 6 * r + 4], (16, 128)))
             at = slice((j * strips + r) * 16, (j * strips + r + 1) * 16)
             for c in range(cols):
-                r_scr[at, 128 * c : 128 * (c + 1)] = r_ref[j, r * cols + c]
+                r_scr[at, 128 * c : 128 * (c + 1)] = r_ref[owner, r * cols + c]
     margin = jnp.concatenate([jnp.concatenate(margin, axis=0)] * (rows // 128), axis=1)
     forward = jnp.concatenate([jnp.concatenate(forward, axis=0)] * (rows // 128), axis=1)
     slots = one_hot_slots(code_ref[...], 0, n_buckets, capacity) > 0.5
@@ -534,7 +533,7 @@
         **work,
     )(counts, near_in, targets)
     tails = pltpu.VMEM((side, 16, 128), F32)
-    early = side // 2
+    early = side * 3 // 4
     n_early = early * capacity
     late_block = capacity * math.gcd(early, ROW_GROUPS)
     early_s, early_col = call(

time: 130 us -> 129 us (level)
  no operation moved by 1% of the time
where the time goes in v9:
time: 129 us
  waiting for transfers between devices  58.3 us (45%)
  Pallas kernels  31.8 us (25%)
  starting transfers between devices  27.8 us (22%)
  local copies, waits for them, and re-layouts  9.18 us (7%)
    ppermute x1, waiting for transfers between devices, shards(): from_far = lax.ppermute(joined, 'src', partner)  19 us
    all_to_all x3, waiting for transfers between devices, exchange(): lax.all_to_all(x, 'src', split_axis=0, concat_axis=0, axis_index_groups=h...  15.2 us
    ppermute x1, waiting for transfers between devices, shards(): far_mine = lax.ppermute(mine, 'src', partner)  14.5 us
    all_to_all x3, starting transfers between devices, exchange(): lax.all_to_all(x, 'src', split_axis=0, concat_axis=0, axis_index_groups=h...  12.9 us
    unnamed x30, local copies, waits for them, and re-layouts  9.18 us
    ppermute x7, starting transfers between devices, shards(): lax.ppermute(far_q[k], 'src', [(i, i ^ k) for i in range(n_src)])  8.74 us
    pallas_call x2, Pallas kernels, combine(): call(functools.partial(combine_kernel, capacity=capacity, side=side, spli...  6.82 us
    pallas_call x1, Pallas kernels, shards(): call(functools.partial(far_owner, block=late_block, side=side), (pltpu.HB...  6.6 us
  transfers between devices with their start and end apart: 19, of which 12 were waited for; matrix products, arithmetic and copies ran while one was open for 0% of the time, Pallas kernels for 16%

profile of v9, /device:TPU:0, one launch (start us, length us, event | category | flops | bytes accessed | tf_op | source)
XLA Modules:
  0.0 128.6 jit_solution(4246496109186750364)
XLA Ops:
  0.6 3.2 %shard_map.68 = (bf16[208,1024]{1,0:T(8,128)(2,1)}, bf16[8,96,1024]{2,1,0:T(8,128)(2,1)}, f32[16,384]{1,0:T(8,128)}) custom-call(s32[4,384]{1,0:T(4,128)} %bitcast.4, s32[1,64]{1,0:T(1,128)} %bitcast.2, bf16[384,1024]{1,0:T(8,128)(2,1)} %src_hbm.1), custom_call_target="tpu_custom_call" | custom-call | flops 603979776 | bytes 2359296 | tf_op jit(solution)/shard_map/pallas_call | solution.py:482
  3.8 0.0 copy-start.7
  3.9 4.1 %collective-permute-start = (bf16[208,1024]{1,0:T(8,128)(2,1)}, bf16[208,1024]{1,0:T(8,128)(2,1)S(1)}, u32[]{:S(2)}, u32[]{:S(2)}) collective-permute-start(bf16[208,1024]{1,0:T(8,128)(2,1)} %get-tuple-element.34), channel_id=1, source_target_pairs={{0,16},{2,18},{4,20},{6,22},{8,24},{10,26},{12,28},{14,30},{16,0},... | collective-permute-start | bytes 1277960 | tf_op jit(solution)/shard_map/ppermute | solution.py:499
  7.9 4.7 %all-to-all-start = ((bf16[8,96,1024]{2,1,0:T(8,128)(2,1)}), bf16[8,96,1024]{2,1,0:T(8,128)(2,1)S(1)}, u32[]{:S(2)}, u32[]{:S(2)}) async-start(bf16[8,96,1024]{2,1,0:T(8,128)(2,1)} %get-tuple-element.31), calls=%async_computation | async-start | bytes 3145728 | tf_op jit(solution)/shard_map/all_to_all | solution.py:465
  12.7 14.5 %collective-permute-done.mine_ref = bf16[208,1024]{1,0:T(8,128)(2,1)S(1)} collective-permute-done((bf16[208,1024]{1,0:T(8,128)(2,1)}, bf16[208,1024]{1,0:T(8,128)(2,1)S(1)}, u32[]{:S(2)}, u32[]{:S(2)}) %collective-permute-start) | collective-permute-done | bytes 426016 | tf_op jit(solution)/shard_map/ppermute | solution.py:499
  27.2 0.0 collective-permute-start.1
  27.2 1.8 %collective-permute-done.1.other_ref = bf16[208,1024]{1,0:T(8,128)(2,1)S(1)} collective-permute-done((bf16[208,1024]{1,0:T(8,128)(2,1)S(1)}, bf16[208,1024]{1,0:T(8,128)(2,1)S(1)}, u32[]{:S(2)}, u32[]{:S(2)}) %collective-permute-start.1) | collective-permute-done | bytes 426016 | tf_op jit(solution)/shard_map/ppermute | solution.py:500
  29.0 0.0 copy-done.7
  29.0 2.3 %shard_map.70 = (bf16[96,1024]{1,0:T(8,128)(2,1)}, bf16[96,1024]{1,0:T(8,128)(2,1)}, bf16[96,1024]{1,0:T(8,128)(2,1)}, bf16[96,1024]{1,0:T(8,128)(2,1)}, bf16[96...) custom-call(s32[1,64]{1,0:T(1,128)S(1)} %bitcast.3, ...), custom_call_target="tpu_custom_call" | custom-call | flops 20000000000 | bytes 2359296 | tf_op jit(solution)/shard_map/pallas_call | solution.py:502
  31.2 1.6 %collective-permute-start.2 = (bf16[96,1024]{1,0:T(8,128)(2,1)}, bf16[96,1024]{1,0:T(8,128)(2,1)S(1)}, u32[]{:S(2)}, u32[]{:S(2)}) collective-permute-start(bf16[96,1024]{1,0:T(8,128)(2,1)} %get-tuple-element.36), channel_id=1, source_target_pairs={{0,2},{2,0},{4,6},{6,4},{8,10},{10,8},{12,14},{14,12},{16,18},{18,... | collective-permute-start | bytes 589832 | tf_op jit(solution)/shard_map/ppermute | solution.py:512
  32.8 1.6 %collective-permute-start.3 = (bf16[96,1024]{1,0:T(8,128)(2,1)}, bf16[96,1024]{1,0:T(8,128)(2,1)S(1)}, u32[]{:S(2)}, u32[]{:S(2)}) collective-permute-start(bf16[96,1024]{1,0:T(8,128)(2,1)} %get-tuple-element.37), channel_id=1, source_target_pairs={{0,4},{2,6},{4,0},{6,2},{8,12},{10,14},{12,8},{14,10},{16,20},{18,... | collective-permute-start | bytes 589832 | tf_op jit(solution)/shard_map/ppermute | solution.py:512
  34.4 0.4 collective-permute-start.4
  34.8 0.8 collective-permute-start.5
  35.6 2.2 %collective-permute-start.6 = (bf16[96,1024]{1,0:T(8,128)(2,1)}, bf16[96,1024]{1,0:T(8,128)(2,1)}, u32[]{:S(2)}, u32[]{:S(2)}) collective-permute-start(bf16[96,1024]{1,0:T(8,128)(2,1)} %get-tuple-element.40), channel_id=1, source_target_pairs={{0,10},{2,8},{4,14},{6,12},{8,2},{10,0},{12,6},{14,4},{16,26},{18,... | collective-permute-start | bytes 589832 | tf_op jit(solution)/shard_map/ppermute | solution.py:512
  37.8 0.0 copy-done.14
  37.8 0.2 fusion.count_ref
  38.0 2.8 %collective-permute-done.2.refs_1_ = bf16[96,1024]{1,0:T(8,128)(2,1)S(1)} collective-permute-done((bf16[96,1024]{1,0:T(8,128)(2,1)}, bf16[96,1024]{1,0:T(8,128)(2,1)S(1)}, u32[]{:S(2)}, u32[]{:S(2)}) %collective-permute-start.2) | collective-permute-done | bytes 196640 | tf_op jit(solution)/shard_map/ppermute | solution.py:512
  40.8 0.7 copy-done.8
  41.4 0.2 collective-permute-start.7
  41.7 1.2 collective-permute-done.3.refs_2_
  42.9 0.7 copy-done.10
  43.5 2.0 %collective-permute-start.8 = (bf16[96,1024]{1,0:T(8,128)(2,1)}, bf16[96,1024]{1,0:T(8,128)(2,1)}, u32[]{:S(2)}, u32[]{:S(2)}) collective-permute-start(bf16[96,1024]{1,0:T(8,128)(2,1)} %get-tuple-element.44), channel_id=1, source_target_pairs={{0,14},{2,12},{4,10},{6,8},{8,6},{10,4},{12,2},{14,0},{16,30},{18,... | collective-permute-start | bytes 589832 | tf_op jit(solution)/shard_map/ppermute | solution.py:512
  45.5 0.0 all-to-all-done.q_ref
  45.5 1.2 copy-done.3
  46.7 2.2 %copy-done = bf16[2,1024,1024]{2,1,0:T(8,128)(2,1)S(1)} copy-done((bf16[2,1024,1024]{2,1,0:T(8,128)(2,1)S(1)}, bf16[2,1024,1024]{2,1,0:T(8,128)(2,1)}, u32[]{:S(2)}) %copy-start) | copy-done | bytes 4194328
  48.9 1.4 %copy-done.4 = bf16[8,96,1024]{2,1,0:T(8,128)(2,1)S(1)} copy-done((bf16[8,96,1024]{2,1,0:T(8,128)(2,1)S(1)}, bf16[8,96,1024]{2,1,0:T(8,128)(2,1)}, u32[]{:S(2)}) %copy-start.4) | copy-done | bytes 1572888
  50.3 4.4 %shard_map.69 = (f32[2,384,1024]{2,1,0:T(8,128)S(1)}, f32[2,8,1024]{2,1,0:T(8,128)S(1)}, f32[2,384,128]{2,1,0:T(8,128)S(1)}) custom-call(s32[2]{0:T(128)S(1)} %fusion.count_ref, bf16[8,96,1024]{2,1,0:T(8,128)(2,1)S(1)} %copy-done.4, bf16[2,1024,1024]{2,1,0:T(8,128)(2,1)S(1)} %copy-done), custom_call_target="tpu_custom_call" | custom-call | flops 1610612736 | bytes 5767168 | tf_op jit(solution)/shard_map/pallas_call | solution.py:523
  54.7 0.0 collective-permute-done.4.refs_3_
  54.8 0.0 collective-permute-done.5.refs_4_
  54.8 0.0 collective-permute-done.6.refs_5_
  54.8 0.0 copy-done.1
  54.8 0.0 copy-done.9
  54.8 0.0 copy-done.11
  54.8 2.9 %shard_map.71 = (f32[2,288,1024]{2,1,0:T(8,128)S(1)}, f32[2,8,1024]{2,1,0:T(8,128)S(1)}) custom-call(s32[2]{0:T(128)S(1)} %fusion.count_ref, f32[2,8,1024]{2,1,0:T(8,128)S(1)} %get-tuple-element.33.near_ref, bf16[2,1024,1024]{2,1,0:T(8,128)(2,1)S(1)} %copy-done.1, bf16[96,1024]{1,0:T(8,128)(2,1)S(1)} %copy-done.12, bf16[96,1024]{1,0:T(8,128)(2,1)S(1)} %copy-done.9, ...), custom_call_target="tpu_custom_call" | custom-call | flops 1610612736 | bytes 5767168 | tf_op jit(solution)/shard_map/pallas_call | solution.py:539
  57.7 0.0 collective-permute-done.7.refs_0_
  57.7 0.8 collective-permute-done.8.refs_1_
  58.4 6.6 %shard_map.72 = (bf16[8,49,16,128]{3,2,1,0:T(8,128)(2,1)}, f32[2,8,1024]{2,1,0:T(8,128)}) custom-call(s32[2]{0:T(128)S(1)} %fusion.count_ref, f32[2,8,1024]{2,1,0:T(8,128)S(1)} %get-tuple-element.41.col_ref, bf16[2,1024,1024]{2,1,0:T(8,128)(2,1)S(1)} %copy-done.1, f32[2,288,1024]{2,1,0:T(8,128)S(1)} %get-tuple-element.42.early_ref, ...), custom_call_target="tpu_custom_call" | custom-call | flops 1610612736 | bytes 5767168 | tf_op jit(solution)/shard_map/pallas_call | solution.py:547
  65.1 4.5 %all-to-all-start.2 = ((bf16[8,49,16,128]{3,2,1,0:T(8,128)(2,1)}), bf16[8,49,16,128]{3,2,1,0:T(8,128)(2,1)}, u32[]{:S(2)}, u32[]{:S(2)}) async-start(bf16[8,49,16,128]{3,2,1,0:T(8,128)(2,1)} %get-tuple-element.48), calls=%async_computation.2 | async-start | bytes 3211264 | tf_op jit(solution)/shard_map/all_to_all | solution.py:465
  69.6 0.0 copy-start.2
  69.6 2.2 %copy-done.2 = bf16[2,1024,1024]{2,1,0:T(8,128)(2,1)S(1)} copy-done((bf16[2,1024,1024]{2,1,0:T(8,128)(2,1)S(1)}, bf16[2,1024,1024]{2,1,0:T(8,128)(2,1)}, u32[]{:S(2)}) %copy-start.2) | copy-done | bytes 4194328
  71.7 0.8 copy-done.5
  72.6 3.6 %shard_map.73 = bf16[8,49,16,128]{3,2,1,0:T(8,128)(2,1)} custom-call(f32[2,384,1024]{2,1,0:T(8,128)S(1)} %get-tuple-element.32.s_ref, f32[2,8,1024]{2,1,0:T(8,128)S(1)} %copy-done.5, f32[2,384,128]{2,1,0:T(8,128)S(1)} %get-tuple-element.46.fwd_ref, bf16[2,1024,1024]{2,1,0:T(8,128)(2,1)S(1)} %copy-done.2), custom_call_target="tpu_custom_call" | custom-call | flops 1610612736 | bytes 5767168 | tf_op jit(solution)/shard_map/pallas_call | solution.py:567
  76.2 13.0 %all-to-all-done.2.r_ref = bf16[8,49,16,128]{3,2,1,0:T(8,128)(2,1)} async-done(((bf16[8,49,16,128]{3,2,1,0:T(8,128)(2,1)}), bf16[8,49,16,128]{3,2,1,0:T(8,128)(2,1)}, u32[]{:S(2)}, u32[]{:S(2)}) %all-to-all-start.2) | async-done | bytes 1605664 | tf_op jit(solution)/shard_map/all_to_all | solution.py:465
  89.2 3.7 %all-to-all-start.1 = ((bf16[8,49,16,128]{3,2,1,0:T(8,128)(2,1)}), bf16[8,49,16,128]{3,2,1,0:T(8,128)(2,1)S(1)}, u32[]{:S(2)}, u32[]{:S(2)}) async-start(bf16[8,49,16,128]{3,2,1,0:T(8,128)(2,1)} %shard_map.73), calls=%async_computation.1 | async-start | bytes 3211264 | tf_op jit(solution)/shard_map/all_to_all | solution.py:465
  92.9 4.3 %shard_map.74 = (f32[192,1024]{1,0:T(8,128)S(1)}, f32[8,384]{1,0:T(8,128)S(1)}, bf16[208,1024]{1,0:T(8,128)(2,1)S(1)}) custom-call(f32[16,384]{1,0:T(8,128)S(1)} %copy-done.13, bf16[8,49,16,128]{3,2,1,0:T(8,128)(2,1)} %all-to-all-done.2.r_ref, f32[16,384]{1,0:T(8,128)S(1)} %copy-done.6), custom_call_target="tpu_custom_call" | custom-call | flops 1207959552 | bytes 3145728 | tf_op jit(solution)/shard_map/pallas_call | solution.py:578
  97.2 0.1 collective-permute-start.9
  97.3 1.8 %collective-permute-done.9.got_ref = bf16[208,1024]{1,0:T(8,128)(2,1)S(1)} collective-permute-done((bf16[208,1024]{1,0:T(8,128)(2,1)S(1)}, bf16[208,1024]{1,0:T(8,128)(2,1)S(1)}, u32[]{:S(2)}, u32[]{:S(2)}) %collective-permute-start.9) | collective-permute-done | bytes 426016 | tf_op jit(solution)/shard_map/ppermute | solution.py:590
  99.1 0.4 shard_map.75._
  99.5 0.9 collective-permute-start.14
  100.3 19.0 %collective-permute-done.14.refs_8_ = bf16[208,1024]{1,0:T(8,128)(2,1)S(1)} collective-permute-done((bf16[208,1024]{1,0:T(8,128)(2,1)S(1)}, bf16[208,1024]{1,0:T(8,128)(2,1)S(1)}, u32[]{:S(2)}, u32[]{:S(2)}) %collective-permute-start.14) | collective-permute-done | bytes 426016 | tf_op jit(solution)/shard_map/ppermute | solution.py:598
  119.4 0.0 collective-permute-start.15
  119.4 2.1 %all-to-all-done.1.r_ref = bf16[8,49,16,128]{3,2,1,0:T(8,128)(2,1)S(1)} async-done(((bf16[8,49,16,128]{3,2,1,0:T(8,128)(2,1)}), bf16[8,49,16,128]{3,2,1,0:T(8,128)(2,1)S(1)}, u32[]{:S(2)}, u32[]{:S(2)}) %all-to-all-start.1) | async-done | bytes 1605664 | tf_op jit(solution)/shard_map/all_to_all | solution.py:465
  121.5 2.5 %shard_map.76 = (bf16[96,1024]{1,0:T(8,128)(2,1)S(1)}, bf16[96,1024]{1,0:T(8,128)(2,1)S(1)}, bf16[96,1024]{1,0:T(8,128)(2,1)S(1)}, bf16[112,1024]{1,0:T(8,128)(2,1)S(1)}) custom-call(f32[16,384]{1,0:T(8,128)S(1)} %copy-done.6, bf16[8,49,16,128]{3,2,1,0:T(8,128)(2,1)S(1)} %all-to-all-done.1.r_ref, bf16[208,1024]{1,0:T(8,128)(2,1)S(1)} %shard_map.75._), custom_call_target="tpu_custom_call" | custom-call | tf_op jit(solution)/shard_map/pallas_call | solution.py:578
  124.0 0.1 collective-permute-start.13
  124.1 0.5 collective-permute-start.10
  124.6 0.1 collective-permute-start.11
  124.7 0.4 collective-permute-start.12
  125.1 0.7 collective-permute-done.10.refs_4_
  125.9 0.3 collective-permute-done.11.refs_5_
  126.2 0.3 collective-permute-done.12.refs_6_
  126.4 0.0 collective-permute-done.13.refs_7_
  126.4 0.0 collective-permute-done.15.refs_9_
  126.4 1.6 %shard_map.77 = (bf16[384,1024]{1,0:T(8,128)(2,1)}, f32[1,384]{1,0:T(1,128)S(1)}) custom-call(bf16[96,1024]{1,0:T(8,128)(2,1)S(1)} %get-tuple-element.52.refs_0_, bf16[96,1024]{1,0:T(8,128)(2,1)S(1)} %get-tuple-element.53.refs_1_, bf16[96,1024]{1,0:T(8,128)(2,1)S(1)} %get-tuple-element.54.refs_2_, bf16[112,1024]{1,0:T(8,128)(2,1)S(1)} %get-tuple-element.55.refs_3_, ...), custom_call_target="tpu_custom_call" | custom-call | bytes 3932160 | tf_op jit(solution)/shard_map/pallas_call | solution.py:604
  128.1 0.6 convert_reduce_fusion
  (17 shorter events, 0.0 us)
Async XLA Ops:
  3.8 25.1 %copy-start.7 = (s32[64]{0:T(128)S(1)}, s32[64]{0:T(128)}, u32[]{:S(2)}) copy-start(s32[64]{0:T(128)} %param.8) | copy-start | bytes 772
  3.9 23.3 %collective-permute-start = (bf16[208,1024]{1,0:T(8,128)(2,1)}, bf16[208,1024]{1,0:T(8,128)(2,1)S(1)}, u32[]{:S(2)}, u32[]{:S(2)}) collective-permute-start(bf16[208,1024]{1,0:T(8,128)(2,1)} %get-tuple-element.34), channel_id=1, source_target_pairs={{0,16},{2,18},{4,20},{6,22},{8,24},{10,26},{12,28},{14,30},{16,0},... | collective-permute-start | bytes 1277960 | tf_op jit(solution)/shard_map/ppermute | solution.py:499
  7.9 37.6 %all-to-all-start = ((bf16[8,96,1024]{2,1,0:T(8,128)(2,1)}), bf16[8,96,1024]{2,1,0:T(8,128)(2,1)S(1)}, u32[]{:S(2)}, u32[]{:S(2)}) async-start(bf16[8,96,1024]{2,1,0:T(8,128)(2,1)} %get-tuple-element.31), calls=%async_computation | async-start | bytes 3145728 | tf_op jit(solution)/shard_map/all_to_all | solution.py:465
  27.2 1.8 %collective-permute-start.1 = (bf16[208,1024]{1,0:T(8,128)(2,1)S(1)}, bf16[208,1024]{1,0:T(8,128)(2,1)S(1)}, u32[]{:S(2)}, u32[]{:S(2)}) collective-permute-start(bf16[208,1024]{1,0:T(8,128)(2,1)S(1)} %collective-permute-done.mine_ref), channel_id=1, source_target_pairs={{0,1},{1,0},{2,3},{3,2},{4,5},{5,4},{6,7},{7,6},{8,9},{9,8},{10,11... | collective-permute-start | bytes 1277960 | tf_op jit(solution)/shard_map/ppermute | solution.py:500
  27.2 10.6 %copy-start.14 = (s32[64]{0:T(128)S(1)}, s32[64]{0:T(128)}, u32[]{:S(2)}) copy-start(s32[64]{0:T(128)} %param.9) | copy-start | bytes 772
  31.2 9.5 %collective-permute-start.2 = (bf16[96,1024]{1,0:T(8,128)(2,1)}, bf16[96,1024]{1,0:T(8,128)(2,1)S(1)}, u32[]{:S(2)}, u32[]{:S(2)}) collective-permute-start(bf16[96,1024]{1,0:T(8,128)(2,1)} %get-tuple-element.36), channel_id=1, source_target_pairs={{0,2},{2,0},{4,6},{6,4},{8,10},{10,8},{12,14},{14,12},{16,18},{18,... | collective-permute-start | bytes 589832 | tf_op jit(solution)/shard_map/ppermute | solution.py:512
  32.8 10.0 %collective-permute-start.3 = (bf16[96,1024]{1,0:T(8,128)(2,1)}, bf16[96,1024]{1,0:T(8,128)(2,1)S(1)}, u32[]{:S(2)}, u32[]{:S(2)}) collective-permute-start(bf16[96,1024]{1,0:T(8,128)(2,1)} %get-tuple-element.37), channel_id=1, source_target_pairs={{0,4},{2,6},{4,0},{6,2},{8,12},{10,14},{12,8},{14,10},{16,20},{18,... | collective-permute-start | bytes 589832 | tf_op jit(solution)/shard_map/ppermute | solution.py:512
  34.4 20.3 %collective-permute-start.4 = (bf16[96,1024]{1,0:T(8,128)(2,1)}, bf16[96,1024]{1,0:T(8,128)(2,1)}, u32[]{:S(2)}, u32[]{:S(2)}) collective-permute-start(bf16[96,1024]{1,0:T(8,128)(2,1)} %get-tuple-element.38), channel_id=1, source_target_pairs={{0,6},{2,4},{4,2},{6,0},{8,14},{10,12},{12,10},{14,8},{16,22},{18,... | collective-permute-start | bytes 589832 | tf_op jit(solution)/shard_map/ppermute | solution.py:512
  34.8 20.0 %collective-permute-start.5 = (bf16[96,1024]{1,0:T(8,128)(2,1)}, bf16[96,1024]{1,0:T(8,128)(2,1)}, u32[]{:S(2)}, u32[]{:S(2)}) collective-permute-start(bf16[96,1024]{1,0:T(8,128)(2,1)} %get-tuple-element.39), channel_id=1, source_target_pairs={{0,8},{2,10},{4,12},{6,14},{8,0},{10,2},{12,4},{14,6},{16,24},{18,... | collective-permute-start | bytes 589832 | tf_op jit(solution)/shard_map/ppermute | solution.py:512
  35.6 19.2 %collective-permute-start.6 = (bf16[96,1024]{1,0:T(8,128)(2,1)}, bf16[96,1024]{1,0:T(8,128)(2,1)}, u32[]{:S(2)}, u32[]{:S(2)}) collective-permute-start(bf16[96,1024]{1,0:T(8,128)(2,1)} %get-tuple-element.40), channel_id=1, source_target_pairs={{0,10},{2,8},{4,14},{6,12},{8,2},{10,0},{12,6},{14,4},{16,26},{18,... | collective-permute-start | bytes 589832 | tf_op jit(solution)/shard_map/ppermute | solution.py:512
  40.8 0.7 copy-start.8
  41.4 16.2 %collective-permute-start.7 = (bf16[96,1024]{1,0:T(8,128)(2,1)}, bf16[96,1024]{1,0:T(8,128)(2,1)}, u32[]{:S(2)}, u32[]{:S(2)}) collective-permute-start(bf16[96,1024]{1,0:T(8,128)(2,1)} %get-tuple-element.43), channel_id=1, source_target_pairs={{0,12},{2,14},{4,8},{6,10},{8,4},{10,6},{12,0},{14,2},{16,28},{18,... | collective-permute-start | bytes 589832 | tf_op jit(solution)/shard_map/ppermute | solution.py:512
  42.9 0.7 copy-start.10
  43.5 14.9 %collective-permute-start.8 = (bf16[96,1024]{1,0:T(8,128)(2,1)}, bf16[96,1024]{1,0:T(8,128)(2,1)}, u32[]{:S(2)}, u32[]{:S(2)}) collective-permute-start(bf16[96,1024]{1,0:T(8,128)(2,1)} %get-tuple-element.44), channel_id=1, source_target_pairs={{0,14},{2,12},{4,10},{6,8},{8,6},{10,4},{12,2},{14,0},{16,30},{18,... | collective-permute-start | bytes 589832 | tf_op jit(solution)/shard_map/ppermute | solution.py:512
  45.5 1.2 copy-start.3
  46.7 2.2 %copy-start = (bf16[2,1024,1024]{2,1,0:T(8,128)(2,1)S(1)}, bf16[2,1024,1024]{2,1,0:T(8,128)(2,1)}, u32[]{:S(2)}) copy-start(bf16[2,1024,1024]{2,1,0:T(8,128)(2,1)} %t_ref.7) | copy-start | bytes 12582916
  48.9 1.4 %copy-start.4 = (bf16[8,96,1024]{2,1,0:T(8,128)(2,1)S(1)}, bf16[8,96,1024]{2,1,0:T(8,128)(2,1)}, u32[]{:S(2)}) copy-start(bf16[8,96,1024]{2,1,0:T(8,128)(2,1)} %copy-done.3) | copy-start | bytes 4718596
  50.3 4.5 %copy-start.1 = (bf16[2,1024,1024]{2,1,0:T(8,128)(2,1)S(1)}, bf16[2,1024,1024]{2,1,0:T(8,128)(2,1)}, u32[]{:S(2)}) copy-start(bf16[2,1024,1024]{2,1,0:T(8,128)(2,1)} %t_ref.7) | copy-start | bytes 12582916
  50.3 4.5 %copy-start.9 = (bf16[96,1024]{1,0:T(8,128)(2,1)S(1)}, bf16[96,1024]{1,0:T(8,128)(2,1)}, u32[]{:S(2)}) copy-start(bf16[96,1024]{1,0:T(8,128)(2,1)} %copy-done.8) | copy-start | bytes 589828
  50.3 4.5 %copy-start.11 = (bf16[96,1024]{1,0:T(8,128)(2,1)S(1)}, bf16[96,1024]{1,0:T(8,128)(2,1)}, u32[]{:S(2)}) copy-start(bf16[96,1024]{1,0:T(8,128)(2,1)} %copy-done.10) | copy-start | bytes 589828
  50.3 4.5 %copy-start.12 = (bf16[96,1024]{1,0:T(8,128)(2,1)S(1)}, bf16[96,1024]{1,0:T(8,128)(2,1)}, u32[]{:S(2)}) copy-start(bf16[96,1024]{1,0:T(8,128)(2,1)} %get-tuple-element.35.refs_0_) | copy-start | bytes 589828
  65.1 24.2 %all-to-all-start.2 = ((bf16[8,49,16,128]{3,2,1,0:T(8,128)(2,1)}), bf16[8,49,16,128]{3,2,1,0:T(8,128)(2,1)}, u32[]{:S(2)}, u32[]{:S(2)}) async-start(bf16[8,49,16,128]{3,2,1,0:T(8,128)(2,1)} %get-tuple-element.48), calls=%async_computation.2 | async-start | bytes 3211264 | tf_op jit(solution)/shard_map/all_to_all | solution.py:465
  69.6 2.2 %copy-start.2 = (bf16[2,1024,1024]{2,1,0:T(8,128)(2,1)S(1)}, bf16[2,1024,1024]{2,1,0:T(8,128)(2,1)}, u32[]{:S(2)}) copy-start(bf16[2,1024,1024]{2,1,0:T(8,128)(2,1)} %t_ref.7) | copy-start | bytes 12582916
  71.7 0.8 copy-start.5
  76.2 16.7 %copy-start.6 = (f32[16,384]{1,0:T(8,128)S(1)}, f32[16,384]{1,0:T(8,128)}, u32[]{:S(2)}) copy-start(f32[16,384]{1,0:T(8,128)} %get-tuple-element.30._.code_ref) | copy-start | bytes 73732
  76.2 16.7 %copy-start.13 = (f32[16,384]{1,0:T(8,128)S(1)}, f32[16,384]{1,0:T(8,128)}, u32[]{:S(2)}) copy-start(f32[16,384]{1,0:T(8,128)} %get-tuple-element.47.code_ref) | copy-start | bytes 73732
  89.2 32.3 %all-to-all-start.1 = ((bf16[8,49,16,128]{3,2,1,0:T(8,128)(2,1)}), bf16[8,49,16,128]{3,2,1,0:T(8,128)(2,1)S(1)}, u32[]{:S(2)}, u32[]{:S(2)}) async-start(bf16[8,49,16,128]{3,2,1,0:T(8,128)(2,1)} %shard_map.73), calls=%async_computation.1 | async-start | bytes 3211264 | tf_op jit(solution)/shard_map/all_to_all | solution.py:465
  97.2 1.8 %collective-permute-start.9 = (bf16[208,1024]{1,0:T(8,128)(2,1)S(1)}, bf16[208,1024]{1,0:T(8,128)(2,1)S(1)}, u32[]{:S(2)}, u32[]{:S(2)}) collective-permute-start(bf16[208,1024]{1,0:T(8,128)(2,1)S(1)} %get-tuple-element.51), channel_id=1, source_target_pairs={{0,1},{1,0},{2,3},{3,2},{4,5},{5,4},{6,7},{7,6},{8,9},{9,8},{10,11... | collective-permute-start | bytes 1277960 | tf_op jit(solution)/shard_map/ppermute | solution.py:590
  99.5 19.9 %collective-permute-start.14 = (bf16[208,1024]{1,0:T(8,128)(2,1)S(1)}, bf16[208,1024]{1,0:T(8,128)(2,1)S(1)}, u32[]{:S(2)}, u32[]{:S(2)}) collective-permute-start(bf16[208,1024]{1,0:T(8,128)(2,1)S(1)} %shard_map.75._), channel_id=1, source_target_pairs={{0,16},{2,18},{4,20},{6,22},{8,24},{10,26},{12,28},{14,30},{16,0},... | collective-permute-start | bytes 1277960 | tf_op jit(solution)/shard_map/ppermute | solution.py:598
  119.4 7.1 %collective-permute-start.15 = (bf16[208,1024]{1,0:T(8,128)(2,1)S(1)}, bf16[208,1024]{1,0:T(8,128)(2,1)S(1)}, u32[]{:S(2)}, u32[]{:S(2)}) collective-permute-start(bf16[208,1024]{1,0:T(8,128)(2,1)S(1)} %collective-permute-done.14.refs_8_), channel_id=1, source_target_pairs={{0,1},{1,0},{2,3},{3,2},{4,5},{5,4},{6,7},{7,6},{8,9},{9,8},{10,11... | collective-permute-start | bytes 1277960 | tf_op jit(solution)/shard_map/ppermute | solution.py:599
  124.0 2.4 %collective-permute-start.13 = (bf16[112,1024]{1,0:T(8,128)(2,1)S(1)}, bf16[112,1024]{1,0:T(8,128)(2,1)S(1)}, u32[]{:S(2)}, u32[]{:S(2)}) collective-permute-start(bf16[112,1024]{1,0:T(8,128)(2,1)S(1)} %get-tuple-element.55.refs_3_), channel_id=1, source_target_pairs={{0,1},{1,0},{2,3},{3,2},{4,5},{5,4},{6,7},{7,6},{8,9},{9,8},{10,11... | collective-permute-start | bytes 688136 | tf_op jit(solution)/shard_map/ppermute | solution.py:603
  124.1 1.8 %collective-permute-start.10 = (bf16[96,1024]{1,0:T(8,128)(2,1)S(1)}, bf16[96,1024]{1,0:T(8,128)(2,1)S(1)}, u32[]{:S(2)}, u32[]{:S(2)}) collective-permute-start(bf16[96,1024]{1,0:T(8,128)(2,1)S(1)} %get-tuple-element.52.refs_0_), channel_id=1, source_target_pairs={{0,1},{1,0},{2,3},{3,2},{4,5},{5,4},{6,7},{7,6},{8,9},{9,8},{10,11... | collective-permute-start | bytes 589832 | tf_op jit(solution)/shard_map/ppermute | solution.py:603
  124.6 1.5 %collective-permute-start.11 = (bf16[96,1024]{1,0:T(8,128)(2,1)S(1)}, bf16[96,1024]{1,0:T(8,128)(2,1)S(1)}, u32[]{:S(2)}, u32[]{:S(2)}) collective-permute-start(bf16[96,1024]{1,0:T(8,128)(2,1)S(1)} %get-tuple-element.53.refs_1_), channel_id=1, source_target_pairs={{0,1},{1,0},{2,3},{3,2},{4,5},{5,4},{6,7},{7,6},{8,9},{9,8},{10,11... | collective-permute-start | bytes 589832 | tf_op jit(solution)/shard_map/ppermute | solution.py:603
  124.7 1.7 %collective-permute-start.12 = (bf16[96,1024]{1,0:T(8,128)(2,1)S(1)}, bf16[96,1024]{1,0:T(8,128)(2,1)S(1)}, u32[]{:S(2)}, u32[]{:S(2)}) collective-permute-start(bf16[96,1024]{1,0:T(8,128)(2,1)S(1)} %get-tuple-element.54.refs_2_), channel_id=1, source_target_pairs={{0,1},{1,0},{2,3},{3,2},{4,5},{5,4},{6,7},{7,6},{8,9},{9,8},{10,11... | collective-permute-start | bytes 589832 | tf_op jit(solution)/shard_map/ppermute | solution.py:603
